TPU v7x, 32 devices: a whole 2x2x4 slice. The times are simulated.
32 devices in a mesh: section: 2 (over y), fsdp: 16 (over z, x, core).
Axes of the slice: x: 2, y: 2, z: 4, core: 2. Of those that a mesh axis runs over, the one named last changes fastest.
Arguments:
- block_input: bfloat16 [2, 4096, 1536], P(None, 'fsdp'), may hold values from -6 to 6
- cotangent: bfloat16 [2, 4096, 1536], P(None, 'fsdp'), may hold values from -6 to 6
- lengths: int32 [2, 16], P(None, 'fsdp'), may hold values from 128 to 256, as said below
- in_weight: bfloat16 [2, 1536, 6448], P('section', 'fsdp'), may hold values from -0.15625 to 0.15625
- out_weight: bfloat16 [2, 3072, 1536], P('section', 'fsdp'), may hold values from -0.109375 to 0.109375
- conv_weight: bfloat16 [2, 4, 3328], P('section', None, 'fsdp'), may hold values from -3 to 3
- conv_bias: bfloat16 [2, 3328], P('section', 'fsdp'), may hold values from -0.5 to 0.5
- norm_gain: bfloat16 [2, 1536], P('section', 'fsdp'), may hold values from 0.5 to 1.5
- gate_gain: bfloat16 [2, 3072], P('section', 'fsdp'), may hold values from 0.5 to 1.5
- dt_bias: float32 [2, 48], P('section'), may hold values from -6.5 to -2.3
- a_log: float32 [2, 48], P('section'), may hold values from 0 to 2.77
- skip_d: float32 [2, 48], P('section'), may hold values from 0.5 to 1.5
Outputs:
- layer_outputs: bfloat16 [2, 2, 4096, 1536], P('section', None, 'fsdp')
- input_grads: bfloat16 [2, 2, 4096, 1536], P('section', None, 'fsdp')
- in_weight_grad: float32 [2, 1536, 6448], P('section', 'fsdp')
- out_weight_grad: float32 [2, 3072, 1536], P('section', 'fsdp')
- conv_weight_grad: float32 [2, 4, 3328], P('section', None, 'fsdp')
- conv_bias_grad: float32 [2, 3328], P('section', 'fsdp')
- norm_gain_grad: float32 [2, 1536], P('section', 'fsdp')
- gate_gain_grad: float32 [2, 3072], P('section', 'fsdp')
- dt_bias_grad: float32 [2, 48], P('section')
- a_log_grad: float32 [2, 48], P('section')
- skip_d_grad: float32 [2, 48], P('section')
Inputs may be any that keep to these rules, and one draw needn't show every extreme that they name: Each slot's sequence fills its first lengths[b, f] rows; some entry equals 256 and some equals 128.
All inputs are finite; a program needn't handle non-finite values.
Results may differ from a plain program's by a relative error of at most 0.012.
The roundings to bfloat16 on the way count: a program that leaves them out, or rounds other values in their place, can miss the bound.
Values may be sent and summed in bfloat16 or wider, within the bound.
No kernel may reach another device: no remote copies, remote signals or barrier semaphores. Data moves between devices by JAX's collectives and lax.ppermute only.
A program may use at most 256 MiB of HBM per device.

v0:
```python
import jax
import jax.numpy as jnp
from jax import lax
from jax.sharding import PartitionSpec as P

INNER = 3072
HEADS = 48
HEAD_DIM = 64
STATE = 128
CONV = 4
SPAN = 256


EPS = 1e-05
exact_mode = lax.Precision.HIGHEST


def from_behind(value, axis, steps):
    count = lax.axis_size(axis)
    first, last = (max(0, -steps), min(count, count - steps))
    return lax.ppermute(value, axis, [(source, source + steps) for source in range(first, last)])


def rms_rows(values, scale_gain):
    factor = lax.rsqrt(jnp.mean(values * values, axis=-1, keepdims=True) + EPS)
    return values * factor * scale_gain


def ssd_blocks(x_heads, b_mat, c_mat, step_size, log_decay):
    row_count = x_heads.shape[0]
    block_count = row_count // SPAN
    pieces = (
        x_heads.reshape(block_count, SPAN, HEADS, HEAD_DIM),
        b_mat.reshape(block_count, SPAN, STATE),
        c_mat.reshape(block_count, SPAN, STATE),
        step_size.reshape(block_count, SPAN, HEADS),
        log_decay.reshape(block_count, SPAN, HEADS),
    )
    places = jnp.arange(SPAN, dtype=jnp.int32)
    causal = places[:, None] >= places[None, :]

    def one_block(carried_state, piece):
        x_block, b_block, c_block, step_block, decay_block = piece
        cumulative = jnp.cumsum(decay_block, axis=0).T
        spread_log = cumulative[:, :, None] - cumulative[:, None, :]
        decays = jnp.where(causal[None], jnp.exp(jnp.where(causal[None], spread_log, 0.0)), 0.0)
        contact = jnp.dot(c_block, b_block.T, precision=exact_mode)
        mixing = decays * contact[None] * step_block.T[:, None, :]
        local_part = jnp.einsum("hts,shp->thp", mixing, x_block, precision=exact_mode)
        from_state = jnp.einsum("tn,hpn->thp", c_block, carried_state, precision=exact_mode)
        from_state = from_state * jnp.exp(cumulative.T)[:, :, None]
        ending = cumulative[:, -1]
        tail_weight = jnp.exp(ending[None, :] - cumulative.T) * step_block
        fresh = jnp.einsum("sh,shp,sn->hpn", tail_weight, x_block, b_block, precision=exact_mode)
        next_state = carried_state * jnp.exp(ending)[:, None, None] + fresh
        return (next_state, local_part + from_state)

    start_state = jnp.zeros((HEADS, HEAD_DIM, STATE), jnp.float32)
    _, block_outputs = lax.scan(one_block, start_state, pieces)
    return block_outputs.reshape(row_count, HEADS, HEAD_DIM)


def mixer_rows(projected, conv_kernel, conv_shift, gate_scale, step_bias, decay_log, skip_scale):
    row_count = projected.shape[0]
    split_end = 2 * INNER + 2 * STATE
    gate_part = projected[:, :INNER]
    conv_in = projected[:, INNER:split_end]
    step_raw = projected[:, split_end:]
    padded = jnp.concatenate(
        [jnp.zeros((CONV - 1, conv_in.shape[1]), jnp.float32), conv_in], axis=0
    )
    conv_total = jnp.zeros_like(conv_in) + conv_shift
    for offset in range(CONV):
        conv_total = conv_total + conv_kernel[offset] * padded[offset : offset + row_count]
    activated = jax.nn.silu(conv_total)
    x_heads = activated[:, :INNER].reshape(row_count, HEADS, HEAD_DIM)
    b_mat = activated[:, INNER : INNER + STATE]
    c_mat = activated[:, INNER + STATE :]
    step_size = jax.nn.softplus(step_raw + step_bias)
    log_decay = step_size * -jnp.exp(decay_log)
    mixed = ssd_blocks(x_heads, b_mat, c_mat, step_size, log_decay)
    mixed = mixed + skip_scale[None, :, None] * x_heads
    gated_rows = mixed.reshape(row_count, INNER) * jax.nn.silu(gate_part)
    return rms_rows(gated_rows, gate_scale)


def layer_forward(inputs_f, live_rows, weights, head_params):
    in_matrix, out_matrix, conv_kernel, conv_shift, norm_scale, gate_scale = weights
    step_bias, decay_log, skip_scale = head_params
    normed = rms_rows(inputs_f, norm_scale.astype(jnp.float32)).astype(jnp.bfloat16)
    projected = jnp.dot(normed, in_matrix, preferred_element_type=jnp.float32)
    gated_rows = mixer_rows(
        projected,
        conv_kernel.astype(jnp.float32),
        conv_shift.astype(jnp.float32),
        gate_scale.astype(jnp.float32),
        step_bias,
        decay_log,
        skip_scale,
    )
    branch = jnp.dot(
        gated_rows.astype(jnp.bfloat16), out_matrix, preferred_element_type=jnp.float32
    )
    return (inputs_f + live_rows * branch, normed, projected)


def layer_backward(inputs_f, projected, incoming, live_rows, weights, head_params):
    in_matrix, out_matrix, conv_kernel, conv_shift, norm_scale, gate_scale = weights
    step_bias, decay_log, skip_scale = head_params
    norm_f = norm_scale.astype(jnp.float32)
    gated_rows, mixer_back = jax.vjp(
        mixer_rows,
        projected,
        conv_kernel.astype(jnp.float32),
        conv_shift.astype(jnp.float32),
        gate_scale.astype(jnp.float32),
        step_bias,
        decay_log,
        skip_scale,
    )
    gated_low = gated_rows.astype(jnp.bfloat16)
    branch_grad = (live_rows * incoming).astype(jnp.bfloat16)
    grad_gated = lax.dot_general(
        branch_grad, out_matrix, (((1,), (1,)), ((), ())), preferred_element_type=jnp.float32
    )
    grad_proj, grad_kernel, grad_shift, grad_gate, grad_step, grad_decay, grad_skip = mixer_back(
        grad_gated
    )
    proj_low = grad_proj.astype(jnp.bfloat16)
    grad_normed = lax.dot_general(
        proj_low, in_matrix, (((1,), (1,)), ((), ())), preferred_element_type=jnp.float32
    )
    _, norm_back = jax.vjp(rms_rows, inputs_f, norm_f)
    grad_rows, grad_norm = norm_back(grad_normed)
    return (
        incoming + grad_rows,
        (proj_low, gated_low, branch_grad),
        (grad_kernel, grad_shift, grad_norm, grad_gate),
        (grad_step, grad_decay, grad_skip),
    )


def matrix_terms(normed, proj_low, gated_low, branch_grad):
    grad_in = lax.dot_general(
        normed, proj_low, (((0,), (0,)), ((), ())), preferred_element_type=jnp.float32
    )
    grad_out = lax.dot_general(
        gated_low, branch_grad, (((0,), (0,)), ((), ())), preferred_element_type=jnp.float32
    )
    return (grad_in, grad_out)


def store_slot(buffer, value, slot_index, active):
    previous = lax.dynamic_index_in_dim(buffer, slot_index, 0, keepdims=False)
    return lax.dynamic_update_index_in_dim(
        buffer, jnp.where(active, value, previous), slot_index, 0
    )


def body(
    block_input,
    cotangent,
    lengths,
    in_weight,
    out_weight,
    conv_weight,
    conv_bias,
    norm_gain,
    gate_gain,
    dt_bias,
    a_log,
    skip_d,
):
    section_index = lax.axis_index("section")
    head_params = (dt_bias[0], a_log[0], skip_d[0])
    shards = (in_weight[0], out_weight[0], conv_weight[0], conv_bias[0], norm_gain[0], gate_gain[0])
    weights = (
        lax.all_gather(shards[0], "fsdp", axis=0, tiled=True),
        lax.all_gather(shards[1], "fsdp", axis=0, tiled=True),
        lax.all_gather(shards[2], "fsdp", axis=1, tiled=True),
        lax.all_gather(shards[3], "fsdp", axis=0, tiled=True),
        lax.all_gather(shards[4], "fsdp", axis=0, tiled=True),
        lax.all_gather(shards[5], "fsdp", axis=0, tiled=True),
    )
    micro_count = block_input.shape[0]
    row_count = block_input.shape[1]
    model_width = block_input.shape[2]
    proj_cols = weights[0].shape[1]
    inner_cols = weights[1].shape[0]
    positions = jnp.arange(row_count, dtype=jnp.int32)
    kept_input = jnp.zeros((micro_count, row_count, model_width), jnp.bfloat16)
    kept_normed = jnp.zeros((micro_count, row_count, model_width), jnp.bfloat16)
    kept_proj = jnp.zeros((micro_count, row_count, proj_cols), jnp.float32)
    outputs = jnp.zeros((micro_count, row_count, model_width), jnp.bfloat16)
    arriving = jnp.zeros((row_count, model_width), jnp.bfloat16)
    for moment in range(micro_count + 1):
        position = moment - section_index
        active = (position >= 0) & (position < micro_count)
        slot_index = jnp.clip(position, 0, micro_count - 1)
        own_rows = lax.dynamic_index_in_dim(block_input, slot_index, 0, keepdims=False)
        entering = jnp.where(section_index == 0, own_rows, arriving)
        live_rows = (positions < lengths[slot_index, 0]).astype(jnp.float32)[:, None]

        def compute_slot(operand):
            return layer_forward(operand.astype(jnp.float32), live_rows, weights, head_params)

        def vacant_slot(operand):
            return (
                jnp.zeros((row_count, model_width), jnp.float32),
                jnp.zeros((row_count, model_width), jnp.bfloat16),
                jnp.zeros((row_count, proj_cols), jnp.float32),
            )

        result, normed, projected = lax.cond(active, compute_slot, vacant_slot, entering)
        result_low = result.astype(jnp.bfloat16)
        kept_input = store_slot(kept_input, entering, slot_index, active)
        kept_normed = store_slot(kept_normed, normed, slot_index, active)
        kept_proj = store_slot(kept_proj, projected, slot_index, active)
        outputs = store_slot(outputs, result_low, slot_index, active)
        if moment < micro_count:
            arriving = from_behind(result_low, "section", 1)
    weights = (
        lax.all_gather(shards[0], "fsdp", axis=0, tiled=True),
        lax.all_gather(shards[1], "fsdp", axis=0, tiled=True),
        lax.all_gather(shards[2], "fsdp", axis=1, tiled=True),
        lax.all_gather(shards[3], "fsdp", axis=0, tiled=True),
        lax.all_gather(shards[4], "fsdp", axis=0, tiled=True),
        lax.all_gather(shards[5], "fsdp", axis=0, tiled=True),
    )
    small_totals = tuple((jnp.zeros(matrix.shape, jnp.float32) for matrix in weights[2:]))
    head_totals = tuple((jnp.zeros_like(param_arr) for param_arr in head_params))
    kept_dproj = jnp.zeros((micro_count, row_count, proj_cols), jnp.bfloat16)
    kept_gated = jnp.zeros((micro_count, row_count, inner_cols), jnp.bfloat16)
    kept_branch = jnp.zeros((micro_count, row_count, model_width), jnp.bfloat16)
    input_grads = jnp.zeros((micro_count, row_count, model_width), jnp.bfloat16)
    returning = jnp.zeros((row_count, model_width), jnp.bfloat16)
    for moment in range(micro_count + 1):
        position = micro_count - 1 - moment + (1 - section_index)
        active = (position >= 0) & (position < micro_count)
        slot_index = jnp.clip(position, 0, micro_count - 1)
        own_rows = lax.dynamic_index_in_dim(cotangent, slot_index, 0, keepdims=False)
        incoming = jnp.where(section_index == 1, own_rows, returning)
        live_rows = (positions < lengths[slot_index, 0]).astype(jnp.float32)[:, None]
        operands = (
            incoming,
            lax.dynamic_index_in_dim(kept_input, slot_index, 0, keepdims=False),
            lax.dynamic_index_in_dim(kept_proj, slot_index, 0, keepdims=False),
        )

        def compute_back(operand):
            grad_in_rows, input_rows, proj_rows = operand
            return layer_backward(
                input_rows.astype(jnp.float32),
                proj_rows,
                grad_in_rows.astype(jnp.float32),
                live_rows,
                weights,
                head_params,
            )

        def vacant_back(operand):
            return (
                jnp.zeros((row_count, model_width), jnp.float32),
                (
                    jnp.zeros((row_count, proj_cols), jnp.bfloat16),
                    jnp.zeros((row_count, inner_cols), jnp.bfloat16),
                    jnp.zeros((row_count, model_width), jnp.bfloat16),
                ),
                tuple((jnp.zeros(matrix.shape, jnp.float32) for matrix in weights[2:])),
                tuple((jnp.zeros_like(param_arr) for param_arr in head_params)),
            )

        grad_rows, row_pieces, small_terms, head_terms = lax.cond(
            active, compute_back, vacant_back, operands
        )
        kept_dproj = store_slot(kept_dproj, row_pieces[0], slot_index, active)
        kept_gated = store_slot(kept_gated, row_pieces[1], slot_index, active)
        kept_branch = store_slot(kept_branch, row_pieces[2], slot_index, active)
        small_totals = jax.tree.map(jnp.add, small_totals, tuple(small_terms))
        head_totals = jax.tree.map(jnp.add, head_totals, head_terms)
        grad_low = grad_rows.astype(jnp.bfloat16)
        input_grads = store_slot(input_grads, grad_low, slot_index, active)
        if moment < micro_count:
            returning = from_behind(grad_low, "section", -1)
    all_rows = micro_count * row_count
    grad_in, grad_out = matrix_terms(
        kept_normed.reshape(all_rows, model_width),
        kept_dproj.reshape(all_rows, proj_cols),
        kept_gated.reshape(all_rows, inner_cols),
        kept_branch.reshape(all_rows, model_width),
    )
    grad_totals = (grad_in, grad_out) + small_totals
    owned = (
        lax.psum_scatter(grad_totals[0], "fsdp", scatter_dimension=0, tiled=True),
        lax.psum_scatter(grad_totals[1], "fsdp", scatter_dimension=0, tiled=True),
        lax.psum_scatter(grad_totals[2], "fsdp", scatter_dimension=1, tiled=True),
        lax.psum_scatter(grad_totals[3], "fsdp", scatter_dimension=0, tiled=True),
        lax.psum_scatter(grad_totals[4], "fsdp", scatter_dimension=0, tiled=True),
        lax.psum_scatter(grad_totals[5], "fsdp", scatter_dimension=0, tiled=True),
    )
    head_sums = lax.psum(head_totals, "fsdp")
    return (
        outputs[None],
        input_grads[None],
        owned[0][None],
        owned[1][None],
        owned[2][None],
        owned[3][None],
        owned[4][None],
        owned[5][None],
        head_sums[0][None],
        head_sums[1][None],
        head_sums[2][None],
    )


def solution(mesh):
    in_specs = (
        P(None, "fsdp", None),
        P(None, "fsdp", None),
        P(None, "fsdp"),
        P("section", "fsdp", None),
        P("section", "fsdp", None),
        P("section", None, "fsdp"),
        P("section", "fsdp"),
        P("section", "fsdp"),
        P("section", "fsdp"),
        P("section", None),
        P("section", None),
        P("section", None),
    )
    out_specs = (
        P("section", None, "fsdp", None),
        P("section", None, "fsdp", None),
        P("section", "fsdp", None),
        P("section", "fsdp", None),
        P("section", None, "fsdp"),
        P("section", "fsdp"),
        P("section", "fsdp"),
        P("section", "fsdp"),
        P("section", None),
        P("section", None),
        P("section", None),
    )
    return jax.shard_map(body, mesh=mesh, in_specs=in_specs, out_specs=out_specs, check_vma=False)
```

profile of v0, /device:TPU:8, one launch (start us, length us, event | category | flops | bytes accessed | tf_op | source)
XLA Modules:
  0.0 1832.6 jit_solution(8733698535329881367)
XLA Ops:
  14.3 33.7 %all-gather.3 = bf16[1,4,3328]{1,0,2:T(2,128)(2,1)S(1)} all-gather(bf16[1,4,208]{1,0,2:T(2,128)(2,1)S(1)} %copy.400), channel_id=5, replica_groups=mesh['section'=2,'fsdp'=16] {'fsdp'}, dimensions={2}, use_global_device_ids=true | all-gather | bytes 28288 | tf_op jit(solution)/shard_map/all_gather | solution.py:180
  51.0 53.4 %all-reduce.58 = (bf16[1536]{0:T(1024)(128)(2,1)S(1)}, bf16[3328]{0:T(1024)(128)(2,1)S(1)}, bf16[3072]{0:T(1024)(128)(2,1)S(1)}) all-reduce(bf16[1536]{0:T(1024)(128)(2,1)S(1)} %dynamic-update-slice, bf16[3328]{0:T(1024)(128)(2,1)S(1)} %dynamic-update-slice.1, ...), channel_id=2, replica_groups=mesh['section'=2,'fsdp'=16] {'fsdp'}, use_global_device_ids=true, to_apply=%add.51 | all-reduce | flops 7936 | bytes 31744 | tf_op jit(solution)/shard_map/all_gather | solution.py:182
  109.6 95.4 %all-gather.9.cloned.1.call-done = bf16[1,1536,6448]{2,1,0:T(8,128)(2,1)} async-done(((bf16[1,96,6448]{2,1,0:T(8,128)(2,1)}), bf16[1,1536,6448]{2,1,0:T(8,128)(2,1)}) %all-gather.9.cloned.1.call-update) | async-done | bytes 19808272 | tf_op jit(solution)/shard_map/all_gather | solution.py:178
  206.1 70.2 %conditional.6 = (bf16[256,1536]{1,0:T(8,128)(2,1)}, bf16[256,1536]{1,0:T(8,128)(2,1)}, f32[256,6448]{1,0:T(8,128)}) conditional(s32[]{:T(128)} %convert_element_type.296, () %tuple.167, (pred[]{:T(512)}, bf16[1,256,1536]{2,1,0:T(8,128)(2,1)}, bf16[256,1536]{1,0:T(8,128)(2,1)S(1)}, bf16[1536]{0:T(1024)(128)(2,1)S(1)}, bf16[1536,6448]{1,0:T(8,128)(2,1)}, ...), branch_computations={%region_0.1_spmd, %region_1.6_spmd} | conditional | flops 11254827008 | bytes 142545664 | solution.py:214
  209.3 14.1 fusion.377
  238.8 17.5 bitcast_add_fusion.1
  296.7 70.8 %conditional.7 = (bf16[256,1536]{1,0:T(8,128)(2,1)}, bf16[256,1536]{1,0:T(8,128)(2,1)}, f32[256,6448]{1,0:T(8,128)}) conditional(s32[]{:T(128)} %convert_element_type.298, () %tuple.169, (bf16[256,1536]{1,0:T(8,128)(2,1)S(1)}, bf16[1536]{0:T(1024)(128)(2,1)S(1)}, bf16[1536,6448]{1,0:T(8,128)(2,1)}, f32[256,1]{0,1:T(1,128)S(1)}, ...), branch_computations={%region_6.7_spmd, %region_7.12_spmd} | conditional | flops 11254433792 | bytes 144118560 | solution.py:214
  297.3 14.9 fusion.378
  330.0 17.7 bitcast_add_fusion.3
  389.0 14.5 conditional.8
  410.8 16.7 conditional.9
  436.0 276.6 %collective-permute-done.2 = bf16[256,1536]{1,0:T(8,128)(2,1)} collective-permute-done((bf16[256,1536]{1,0:T(8,128)(2,1)}, bf16[256,1536]{1,0:T(8,128)(2,1)}, u32[]{:S(2)}, u32[]{:S(2)}) %collective-permute-start.2) | collective-permute-done | bytes 786464 | tf_op jit(solution)/shard_map/ppermute | solution.py:21
  712.5 222.6 %conditional.10 = (bf16[256,6448]{1,0:T(8,128)(2,1)}, bf16[256,3072]{1,0:T(8,128)(2,1)}, bf16[256,1536]{1,0:T(8,128)(2,1)}, f32[4,3328]{1,0:T(4,128)}, f32[3328]...) conditional(s32[]{:T(128)} %convert_element_type.298, ...), branch_computations={%region_45.47_spmd, %region_46.73_spmd} | conditional | flops 20038688768 | bytes 543754304 | solution.py:273
  751.0 18.3 %bitcast_add_fusion.13 = f32[256,48,64]{0,2,1:T(8,128)} fusion(f32[256,48,64]{0,2,1:T(8,128)S(1)} %fusion.244, f32[256,48,64]{0,2,1:T(8,128)S(1)} %bitcast.636, f32[48,256]{1,0:T(8,128)S(1)} %copy-done.157, f32[256,256]{1,0:T(8,128)} %fusion.259, f32[48,256]{1,0:T(8,128)S(1)} %copy-done.160, pred[256,256]{1,0:T(8,128)(4,1)S(1)} %iota_compare_fusion.4, ...), kind=kOutput, calls=%fused_computation.390 | convolution fusion | flops 2433220608 | bytes 9912320 | tf_op jit(solution)/shard_map/cond/branch_1_fun/jvp()/while/body/eval_jaxpr/hts,shp->thp/dot_general | solution.py:49
  806.1 22.5 %fusion.205 = (f32[48,256]{1,0:T(8,128)}, f32[48,256]{1,0:T(8,128)}, f32[48,256]{1,0:T(8,128)}, f32[256,256]{1,0:T(8,128)}) fusion(f32[48,256]{1,0:T(8,128)} %copy.367, f32[256,256]{1,0:T(8,128)} %fusion.259, f32[48,256]{1,0:T(8,128)} %copy.365, pred[256,256]{1,0:T(8,128)(4,1)} %copy-done.153, f32[48,64,256]{2,1,0:T(8,128)} %bitcast.654, ...), kind=kOutput, calls=%fused_computation.357 | convolution fusion | flops 2463002624 | bytes 7127040 | tf_op jit(solution)/shard_map/cond/branch_1_fun/transpose(jvp())/while/body/eval_jaxpr/hts,shp->thp/dot_general | solution.py:49
  852.3 14.2 bitcast_add_fusion.12
  955.0 221.3 %conditional.11 = (bf16[256,6448]{1,0:T(8,128)(2,1)}, bf16[256,3072]{1,0:T(8,128)(2,1)}, bf16[256,1536]{1,0:T(8,128)(2,1)}, f32[4,3328]{1,0:T(4,128)}, f32[3328]...) conditional(s32[]{:T(128)} %convert_element_type.296, ...), branch_computations={%region_72.74_spmd, %region_73.100_spmd} | conditional | flops 20038688768 | bytes 543829696 | solution.py:273
  992.9 18.1 bitcast_add_fusion.19
  1047.9 22.1 %fusion.282 = (f32[48,256]{1,0:T(8,128)}, f32[48,256]{1,0:T(8,128)}, f32[48,256]{1,0:T(8,128)}, f32[256,256]{1,0:T(8,128)}) fusion(f32[48,256]{1,0:T(8,128)} %copy.386, f32[256,256]{1,0:T(8,128)} %fusion.336, f32[48,256]{1,0:T(8,128)} %copy.384, pred[256,256]{1,0:T(8,128)(4,1)} %copy-done.154, f32[48,64,256]{2,1,0:T(8,128)} %bitcast.657, ...), kind=kOutput, calls=%fused_computation.506 | convolution fusion | flops 2463002624 | bytes 7127040 | tf_op jit(solution)/shard_map/cond/branch_1_fun/transpose(jvp())/while/body/eval_jaxpr/hts,shp->thp/dot_general | solution.py:49
  1093.9 14.2 bitcast_add_fusion.18
  1249.4 27.3 %convolution_bitcast_fusion.3 = f32[1536,6448]{1,0:T(8,128)} fusion(bf16[2,256,1536]{2,1,0:T(8,128)(2,1)} %bitcast_dynamic-update-slice_fusion.6, bf16[2,256,6448]{1,2,0:T(8,128)(2,1)} %constant_dynamic-update-slice_fusion.3), kind=kOutput, calls=%fused_computation.643 | convolution fusion | flops 10141827072 | bytes 47792128 | tf_op jit(solution)/shard_map/dot_general | solution.py:144
  1288.8 54.3 %all-reduce.57 = (f32[3328]{0:T(1024)S(1)}, f32[1536]{0:T(1024)S(1)}, f32[3072]{0:T(1024)S(1)}, f32[1,48]{1,0:T(1,128)}, f32[1,48]{1,0:T(1,128)}, /*index=5*/f32[1,48]{1,0:T(1,128)}) all-reduce(f32[3328]{0:T(1024)S(1)} %add_add_fusion.7, f32[1536]{0:T(1024)S(1)} %add_add_fusion.9, ...), channel_id=11, replica_groups=mesh['section'=2,'fsdp'=16] {'fsdp'}, use_global_device_ids=true, to_apply=%region_102.104.clone | all-reduce | flops 8080 | bytes 64640
  1348.0 87.4 %reduce-scatter.8.cloned.1.call-done = f32[192,1536]{1,0:T(8,128)} async-done(((f32[3072,1536]{1,0:T(8,128)}), f32[192,1536]{1,0:T(8,128)}) %reduce-scatter.8.cloned.1.call-update) | async-done | bytes 1179664 | tf_op jit(solution)/shard_map/reduce_scatter | solution.py:295
  1435.5 390.4 %reduce-scatter.6.cloned.1.call-done = f32[96,6448]{1,0:T(8,128)} async-done(((f32[1536,6448]{1,0:T(8,128)}), f32[96,6448]{1,0:T(8,128)}) %reduce-scatter.6.cloned.1.call-update) | async-done | bytes 2476048 | tf_op jit(solution)/shard_map/reduce_scatter | solution.py:294
  (668 shorter events, 602.5 us)
Async XLA Ops:
  7.2 43.0 %copy-start.188 = (bf16[1,96]{1,0:T(2,128)(2,1)S(1)}, bf16[1,96]{1,0:T(2,128)(2,1)}, u32[]{:S(2)}) copy-start(bf16[1,96]{1,0:T(2,128)(2,1)} %param.32) | copy-start | bytes 580
  7.2 43.3 %copy-start.174 = (s32[2,1]{0,1:T(1,128)S(1)}, s32[2,1]{0,1:T(1,128)}, u32[]{:S(2)}) copy-start(s32[2,1]{0,1:T(1,128)} %param.27) | copy-start | bytes 28
  7.2 102.5 %all-gather.11.cloned.1.call-start = ((), (), s32[]{:S(2)}) async-start(), calls=%async_computation.6 | async-start | bytes 10027008 | tf_op jit(solution)/shard_map/all_gather | solution.py:179
  7.9 99.7 %copy-start.72 = (bf16[2,256,1536]{2,1,0:T(8,128)(2,1)S(1)}, bf16[2,256,1536]{2,1,0:T(8,128)(2,1)}, u32[]{:S(2)}) copy-start(bf16[2,256,1536]{2,1,0:T(8,128)(2,1)} %param.25) | copy-start | bytes 4718596
  7.9 197.1 %all-gather.9.cloned.1.call-start = ((), (), s32[]{:S(2)}) async-start(), calls=%async_computation.5 | async-start | bytes 21307392 | tf_op jit(solution)/shard_map/all_gather | solution.py:178
  8.7 1337.6 %reduce-scatter.10.cloned.1.call-start = ((), (), s32[]{:S(2)}) async-start(), calls=%async_computation.7 | async-start | bytes 1810432
  49.7 361.1 %copy-start.83 = (bf16[1,4,3328]{2,1,0:T(4,128)(2,1)}, bf16[1,4,3328]{2,1,0:T(4,128)(2,1)S(1)}, u32[]{:S(2)}) copy-start(bf16[1,4,3328]{2,1,0:T(4,128)(2,1)S(1)} %copy.401) | copy-start | bytes 79876
  104.4 306.4 %copy-start.107 = (bf16[1536]{0:T(1024)(128)(2,1)}, bf16[1536]{0:T(1024)(128)(2,1)S(1)}, u32[]{:S(2)}) copy-start(bf16[1536]{0:T(1024)(128)(2,1)S(1)} %get-tuple-element.2047) | copy-start | bytes 9220
  105.1 100.1 %copy-start.175 = (f32[256,1]{0,1:T(1,128)}, f32[256,1]{0,1:T(1,128)S(1)}, u32[]{:S(2)}) copy-start(f32[256,1]{0,1:T(1,128)S(1)} %compare_convert_fusion.2) | copy-start | bytes 3076
  107.5 97.7 %copy-start.136 = (f32[1,48]{1,0:T(1,128)S(1)}, f32[1,48]{1,0:T(1,128)}, u32[]{:S(2)}) copy-start(f32[1,48]{1,0:T(1,128)} %param.34) | copy-start | bytes 580
  107.5 97.7 %copy-start.163 = (f32[1,48]{1,0:T(1,128)S(1)}, f32[1,48]{1,0:T(1,128)}, u32[]{:S(2)}) copy-start(f32[1,48]{1,0:T(1,128)} %param.36) | copy-start | bytes 580
  107.5 97.7 %copy-start.189 = (f32[1,48]{1,0:T(1,128)S(1)}, f32[1,48]{1,0:T(1,128)}, u32[]{:S(2)}) copy-start(f32[1,48]{1,0:T(1,128)} %param.35) | copy-start | bytes 580
  276.4 19.1 %collective-permute-start = (bf16[256,1536]{1,0:T(8,128)(2,1)}, bf16[256,1536]{1,0:T(8,128)(2,1)S(1)}, u32[]{:S(2)}, u32[]{:S(2)}) collective-permute-start(bf16[256,1536]{1,0:T(8,128)(2,1)} %get-tuple-element.1850), channel_id=1, source_target_pairs={{0,16},{1,17},{2,18},{3,19},{4,20},{5,21},{6,22},{7,23},{8,24},{9,... | collective-permute-start | bytes 2359304 | tf_op jit(solution)/shard_map/ppermute | solution.py:21
  367.5 21.1 %collective-permute-start.1 = (bf16[256,1536]{1,0:T(8,128)(2,1)}, bf16[256,1536]{1,0:T(8,128)(2,1)S(1)}, u32[]{:S(2)}, u32[]{:S(2)}) collective-permute-start(bf16[256,1536]{1,0:T(8,128)(2,1)} %get-tuple-element.1851), channel_id=1, source_target_pairs={{0,16},{1,17},{2,18},{3,19},{4,20},{5,21},{6,22},{7,23},{8,24},{9,... | collective-permute-start | bytes 2359304 | tf_op jit(solution)/shard_map/ppermute | solution.py:21
  427.5 285.0 %collective-permute-start.2 = (bf16[256,1536]{1,0:T(8,128)(2,1)}, bf16[256,1536]{1,0:T(8,128)(2,1)}, u32[]{:S(2)}, u32[]{:S(2)}) collective-permute-start(bf16[256,1536]{1,0:T(8,128)(2,1)} %get-tuple-element.1856), channel_id=1, source_target_pairs={{16,0},{17,1},{18,2},{19,3},{20,4},{21,5},{22,6},{23,7},{24,8},{25... | collective-permute-start | bytes 2359304 | tf_op jit(solution)/shard_map/ppermute | solution.py:21
  433.5 279.0 %copy-start.84 = (bf16[1,4,3328]{2,1,0:T(4,128)(2,1)S(1)}, bf16[1,4,3328]{2,1,0:T(4,128)(2,1)}, u32[]{:S(2)}) copy-start(bf16[1,4,3328]{2,1,0:T(4,128)(2,1)} %copy-done.83) | copy-start | bytes 79876
  433.5 279.0 %copy-start.191 = (f32[1,48]{1,0:T(1,128)S(1)}, f32[1,48]{1,0:T(1,128)}, u32[]{:S(2)}) copy-start(f32[1,48]{1,0:T(1,128)} %param.35) | copy-start | bytes 580
  739.6 29.7 %copy-start.70 = (f32[48,2,128]{0,2,1:T(8,128)}, f32[48,2,128]{0,2,1:T(8,128)S(1)}, u32[]{:S(2)}) copy-start(f32[48,2,128]{0,2,1:T(8,128)S(1)} %copy.363) | copy-start | bytes 147460 | tf_op jit(solution)/shard_map/cond
  935.1 19.9 %collective-permute-start.3 = (bf16[256,1536]{1,0:T(8,128)(2,1)}, bf16[256,1536]{1,0:T(8,128)(2,1)}, u32[]{:S(2)}, u32[]{:S(2)}) collective-permute-start(bf16[256,1536]{1,0:T(8,128)(2,1)} %get-tuple-element.1857), channel_id=1, source_target_pairs={{16,0},{17,1},{18,2},{19,3},{20,4},{21,5},{22,6},{23,7},{24,8},{25... | collective-permute-start | bytes 2359304 | tf_op jit(solution)/shard_map/ppermute | solution.py:21
  982.2 28.9 %copy-start.71 = (f32[48,2,128]{0,2,1:T(8,128)}, f32[48,2,128]{0,2,1:T(8,128)S(1)}, u32[]{:S(2)}) copy-start(f32[48,2,128]{0,2,1:T(8,128)S(1)} %copy.382) | copy-start | bytes 147460 | tf_op jit(solution)/shard_map/cond
  982.2 28.9 %copy-start.173 = (f32[48]{0:T(128)}, f32[48]{0:T(128)S(1)}, u32[]{:S(2)}) copy-start(f32[48]{0:T(128)S(1)} %slice_bitcast_fusion.2) | copy-start | bytes 580 | tf_op jit(solution)/shard_map/cond
  1179.1 256.4 %reduce-scatter.8.cloned.1.call-start = ((), (), s32[]{:S(2)}) async-start(), calls=%async_computation.4 | async-start | bytes 20054016 | tf_op jit(solution)/shard_map/reduce_scatter | solution.py:295
  1197.8 628.0 %reduce-scatter.6.cloned.1.call-start = ((), (), s32[]{:S(2)}) async-start(), calls=%async_computation.3 | async-start | bytes 42614784 | tf_op jit(solution)/shard_map/reduce_scatter | solution.py:294
  1346.3 479.5 %copy-start.81 = (bf16[1,2,256,1536]{3,2,1,0:T(8,128)(2,1)}, bf16[1,2,256,1536]{3,2,1,0:T(8,128)(2,1)S(1)}, u32[]{:S(2)}) copy-start(bf16[1,2,256,1536]{3,2,1,0:T(8,128)(2,1)S(1)} %bitcast_dynamic-update-slice_fusion.9) | copy-start | bytes 4718596
  (144 other events, 1049.3 us)
Sparse Core Ops, SparseCore 0:
  10.3 89.4 all-gather.10
  101.4 103.6 all-gather.8
  1179.2 59.0 reduce-scatter.9
  1242.8 192.6 reduce-scatter.7
  1440.2 385.5 reduce-scatter.5
where the time goes:
time: 1840 us; the launch traced here: 1830 us
  waiting for transfers between devices  862 us (47%)
  matrix products  325 us (18%)
  local copies, waits for them, and re-layouts  236 us (13%)
  other arithmetic  222 us (12%)
  blocking collectives  141 us (8%)
  loops' own time  19.4 us (1%)
  between operations  18.5 us (1%)
    reduce_scatter x1, waiting for transfers between devices, body(): lax.psum_scatter(grad_totals[0], 'fsdp', scatter_dimension=0, tiled=True)  390 us
    ppermute x4, waiting for transfers between devices, from_behind(): lax.ppermute(value, axis, [(source, source + steps) for source in range(f...  287 us
    dot_general x8, matrix products, one_block(): jnp.einsum('hts,shp->thp', mixing, x_block, precision=exact_mode)  145 us
    all_gather x1, waiting for transfers between devices, body(): lax.all_gather(shards[0], 'fsdp', axis=0, tiled=True)  95.4 us
    reduce_scatter x1, waiting for transfers between devices, body(): lax.psum_scatter(grad_totals[1], 'fsdp', scatter_dimension=0, tiled=True)  87.4 us
    unnamed x1, blocking collectives  54.3 us
    all_gather x1, blocking collectives, body(): lax.all_gather(shards[4], 'fsdp', axis=0, tiled=True)  53.4 us
  transfers between devices with their start and end apart: 9, of which 7 were waited for; matrix products, arithmetic and copies ran while one was open for 9% of the time, Pallas kernels for 0%

commit v1 on v0

v1 whole, which is shorter than its diff:
```python
import jax
import jax.numpy as jnp
from jax import lax
from jax.experimental import pallas as pl
from jax.experimental.pallas import tpu as pltpu
from jax.sharding import PartitionSpec as P

HEAD_DIM = 64
STATE = 128
CONV = 4
EPS = 1e-05
LOG2E = 1.4426950408889634
HALF = 128
WIDE = 512
GROUP = WIDE // HEAD_DIM
TINY = 1e-30
NEG = -1e30
VMEM = 56 * 1024 * 1024
F32 = jnp.float32
BF16 = jnp.bfloat16
EXACT = lax.Precision.HIGHEST


def nt_dot(a, b):
    return lax.dot_general(a, b, (((1,), (1,)), ((), ())), preferred_element_type=F32)


def nn_dot(a, b):
    return jnp.dot(a, b, preferred_element_type=F32)


def sigmoid(v):
    return 0.5 * jnp.tanh(0.5 * v) + 0.5


def conv_rows(values, taps, bias):
    rows = lax.broadcasted_iota(jnp.int32, values.shape, 0)
    total = bias + taps[CONV - 1 : CONV, :] * values
    for back in range(1, CONV):
        moved = jnp.where(rows >= back, pltpu.roll(values, back, 0), 0.0)
        total = total + taps[CONV - 1 - back : CONV - back, :] * moved
    return total


def softplus(v):
    return jnp.maximum(v, 0.0) + jnp.log1p(jnp.exp(-jnp.abs(v)))


def step_terms(step_raw, head_ref):
    rows = step_raw.shape[0]
    step = jnp.maximum(softplus(step_raw + head_ref[0:1, :]), TINY)
    rate = -jnp.exp(head_ref[1:2, :])
    at = lax.broadcasted_iota(jnp.int32, (rows, rows), 0)
    of = lax.broadcasted_iota(jnp.int32, (rows, rows), 1)
    lower = (at >= of).astype(F32)
    sums = jnp.dot(lower, step * rate, precision=EXACT, preferred_element_type=F32) * LOG2E
    return step, rate, sums, sums - jnp.log2(step)


def spread(target, values, groups):
    for g in range(groups):
        target[g] = pltpu.roll(values, (HALF - g * GROUP) % HALF, 1) if g else values


def forward_kernel(
    u_ref, wz_ref, wx_ref, wr_ref, norm_ref, chan_ref, chanr_ref, head_ref, *rest
):
    (nb_ref, gb_ref, z_ref, v_ref, c_ref, y_ref, vr_ref, cr_ref, w_scr, sq_scr, s_scr, col_scr, row_scr) = rest[-13:]
    step_at = pl.program_id(0)
    groups = pl.num_programs(0)
    rows = u_ref.shape[0]

    @pl.when(step_at == 0)
    def _():
        u = u_ref[...].astype(F32)
        scale = lax.rsqrt(jnp.mean(u * u, axis=1, keepdims=True) + EPS)
        nb_ref[0] = (u * scale * norm_ref[...]).astype(BF16)
        raw = nn_dot(nb_ref[0], wr_ref[...])
        vr_ref[0] = raw
        pre = conv_rows(raw[:, : 2 * STATE], chanr_ref[0:4, :], chanr_ref[4:5, :])
        cr_ref[0] = pre
        act = pre * sigmoid(pre)
        s_scr[...] = lax.dot_general(
            act[:, STATE:], act[:, :STATE], (((1,), (1,)), ((), ())), precision=EXACT, preferred_element_type=F32
        )
        _, _, sums, shifted = step_terms(raw[:, 2 * STATE : 3 * STATE], head_ref)
        spread(col_scr, sums, w_scr.shape[0])
        row_scr[...] = shifted.T
        sq_scr[...] = jnp.zeros_like(sq_scr)

    nb = nb_ref[0]
    z = nn_dot(nb, wz_ref[...])
    z_ref[0] = z
    v = nn_dot(nb, wx_ref[...])
    v_ref[0] = v
    c = conv_rows(v, chan_ref[0:4, :], chan_ref[4:5, :])
    c_ref[0] = c
    x = c * sigmoid(c)
    x_low = x.astype(BF16)
    cols = col_scr[step_at]
    rws = row_scr[pl.ds(pl.multiple_of(step_at * GROUP, GROUP), GROUP), :]
    lane = lax.broadcasted_iota(jnp.int32, (HALF, HALF), 1)
    causal = lax.broadcasted_iota(jnp.int32, (HALF, HALF), 0) >= lane
    first = lane < HEAD_DIM
    parts = []
    for pair in range(GROUP // 2):
        here = slice(pair * HALF, (pair + 1) * HALF)
        pieces = []
        for tb in range(rows // HALF):
            t_here = slice(tb * HALF, (tb + 1) * HALF)
            both = []
            for h in (2 * pair, 2 * pair + 1):
                col = cols[t_here, h : h + 1]
                mix = []
                for sb in range(tb + 1):
                    s_here = slice(sb * HALF, (sb + 1) * HALF)
                    gap = col - rws[h : h + 1, s_here]
                    if sb == tb:
                        gap = jnp.where(causal, gap, NEG)
                    mix.append((jnp.exp2(gap) * s_scr[t_here, s_here]).astype(BF16))
                mix = jnp.concatenate(mix, axis=1) if len(mix) > 1 else mix[0]
                both.append(nn_dot(mix, x_low[: (tb + 1) * HALF, here]))
            pieces.append(jnp.where(first, both[0], both[1]))
        parts.append(jnp.concatenate(pieces, axis=0))
    y = jnp.concatenate(parts, axis=1) + chan_ref[6:7, :] * x
    y_ref[0] = y
    w = y * (z * sigmoid(z))
    w_scr[step_at] = w
    sq_scr[...] += jnp.sum(w * w, axis=1, keepdims=True)

    @pl.when(step_at == groups - 1)
    def _():
        inner = w_scr.shape[0] * WIDE
        scale = lax.rsqrt(sq_scr[...] * (1.0 / inner) + EPS)
        for g in range(w_scr.shape[0]):
            here = slice(g * WIDE, (g + 1) * WIDE)
            gb_ref[0, :, here] = (w_scr[g] * scale * gain_of(norm_ref, rest[0], g)).astype(BF16)


def gain_of(_, gain_ref, g):
    return gain_ref[:, g * WIDE : (g + 1) * WIDE]


def forward_slot(place, kept, u, w_in, norm_gain, chan, chan_r, heads, gate_gain, slots):
    rows, width = u.shape
    inner = chan.shape[1]
    groups = inner // WIDE
    tail = w_in.shape[1] - 2 * inner
    shapes = [
        ((rows, width), BF16),
        ((rows, inner), BF16),
        ((rows, inner), F32),
        ((rows, inner), F32),
        ((rows, inner), F32),
        ((rows, inner), F32),
        ((rows, tail), F32),
        ((rows, 2 * STATE), F32),
    ]
    wide_out = lambda: pl.BlockSpec((1, rows, WIDE), lambda i: (place, 0, i))
    whole = lambda a, b: pl.BlockSpec((a, b), lambda i: (0, 0))
    whole_out = lambda b: pl.BlockSpec((1, rows, b), lambda i: (place, 0, 0))
    in_specs = [
        whole(rows, width),
        pl.BlockSpec((width, WIDE), lambda i: (0, i)),
        pl.BlockSpec((width, WIDE), lambda i: (0, groups + i)),
        pl.BlockSpec((width, tail), lambda i: (0, 2 * inner // tail)),
        whole(1, width),
        pl.BlockSpec((8, WIDE), lambda i: (0, i)),
        whole(8, 2 * STATE),
        whole(8, HALF),
        whole(1, inner),
    ]
    args = [u, w_in, w_in, w_in, norm_gain, chan, chan_r, heads, gate_gain]
    aliases = {}
    if kept is not None:
        for k, arr in enumerate(kept):
            aliases[len(args)] = k
            args.append(arr)
            in_specs.append(pl.BlockSpec(memory_space=pl.ANY))
    out_specs = [whole_out(width), whole_out(inner)] + [wide_out() for _ in range(4)] + [whole_out(tail), whole_out(2 * STATE)]
    return pl.pallas_call(
        forward_kernel,
        grid=(groups,),
        in_specs=in_specs,
        out_specs=out_specs,
        out_shape=[jax.ShapeDtypeStruct((slots,) + s, d) for s, d in shapes],
        scratch_shapes=[
            pltpu.VMEM((groups, rows, WIDE), F32),
            pltpu.VMEM((rows, 1), F32),
            pltpu.VMEM((rows, rows), F32),
            pltpu.VMEM((groups, rows, HALF), F32),
            pltpu.VMEM((HALF, rows), F32),
        ],
        input_output_aliases=aliases,
        compiler_params=pltpu.CompilerParams(vmem_limit_bytes=VMEM),
        name="forward_slot",
    )(*args)


def backward_kernel(
    at_ref,
    g_ref,
    u_ref,
    wo_ref,
    wz_ref,
    wx_ref,
    wr_ref,
    z_ref,
    v_ref,
    c_ref,
    y_ref,
    vr_ref,
    cr_ref,
    norm_ref,
    chan_ref,
    chanr_ref,
    head_ref,
    *rest,
):
    (
        du_ref, dz_ref, dv_ref, dr_ref, cg_ref, cgr_ref, ng_ref, hg_ref,
        dob_scr, dgb_scr, sq_scr, we_scr, st_scr, ds_scr, bcol_scr, trow_scr, colr_scr, rowr_scr, step_scr, act_scr, dn_scr,
    ) = rest[-21:]
    groups = pl.num_programs(0) // 2
    at = pl.program_id(0)
    rows, width = g_ref.shape
    inner = dgb_scr.shape[0] * WIDE

    @pl.when(at == 0)
    def _():
        live = lax.broadcasted_iota(jnp.int32, (rows, 1), 0) < at_ref[1]
        dob_scr[...] = jnp.where(live, g_ref[...].astype(F32), 0.0).astype(BF16)
        sq_scr[...] = jnp.zeros_like(sq_scr)
        we_scr[...] = jnp.zeros_like(we_scr)
        ds_scr[...] = jnp.zeros_like(ds_scr)
        dn_scr[...] = jnp.zeros_like(dn_scr)
        rowr_scr[...] = jnp.zeros_like(rowr_scr)
        pre = cr_ref[0]
        act = pre * sigmoid(pre)
        act_scr[...] = act
        st_scr[...] = lax.dot_general(
            act[:, :STATE], act[:, STATE:], (((1,), (1,)), ((), ())), precision=EXACT, preferred_element_type=F32
        )
        step, rate, sums, shifted = step_terms(vr_ref[0, :, 2 * STATE : 3 * STATE], head_ref)
        step_scr[...] = step
        spread(bcol_scr, shifted, dgb_scr.shape[0])
        trow_scr[...] = sums.T

    @pl.when(at < groups)
    def _():
        dgb = nt_dot(dob_scr[...], wo_ref[...])
        dgb_scr[at] = dgb
        z = z_ref[0]
        w = y_ref[0] * (z * sigmoid(z))
        sq_scr[...] += jnp.sum(w * w, axis=1, keepdims=True)
        we_scr[...] += jnp.sum(w * (dgb * chan_ref[5:6, :]), axis=1, keepdims=True)

    @pl.when(at >= groups)
    def _():
        j = at - groups
        q = lax.rsqrt(sq_scr[...] * (1.0 / inner) + EPS)
        pull = q * q * q * (we_scr[...] * (1.0 / inner))
        dgb = dgb_scr[j]
        z = z_ref[0]
        y = y_ref[0]
        sz = sigmoid(z)
        silu_z = z * sz
        w = y * silu_z
        dw = q * (dgb * chan_ref[5:6, :]) - w * pull
        cg_ref[5:6, :] = jnp.sum(w * q * dgb, axis=0, keepdims=True)
        dy = dw * silu_z
        dz = (dw * y * (sz * (1.0 + z * (1.0 - sz)))).astype(BF16)
        dz_ref[0] = dz
        dn = nt_dot(dz, wz_ref[...])

        c = c_ref[0]
        sc = sigmoid(c)
        x = c * sc
        x_low = x.astype(BF16)
        dy_low = dy.astype(BF16)
        cg_ref[6:7, :] = jnp.sum(dy * x, axis=0, keepdims=True)
        cg_ref[7:8, :] = jnp.zeros((1, WIDE), F32)
        cols = bcol_scr[j]
        head_rows = pl.ds(pl.multiple_of(j * GROUP, GROUP), GROUP)
        rws = trow_scr[head_rows, :]
        lane = lax.broadcasted_iota(jnp.int32, (HALF, HALF), 1)
        causal = lane >= lax.broadcasted_iota(jnp.int32, (HALF, HALF), 0)
        first = lane < HEAD_DIM
        lane_row = lax.broadcasted_iota(jnp.int32, (1, HALF), 1)
        sub = lax.broadcasted_iota(jnp.int32, (GROUP, HALF), 0)
        blocks = rows // HALF
        col_sums = [jnp.zeros((HALF, HALF), F32) for _ in range(blocks)]
        row_sums = [jnp.zeros((GROUP, HALF), F32) for _ in range(blocks)]
        parts = []
        for pair in range(GROUP // 2):
            here = slice(pair * HALF, (pair + 1) * HALF)
            pieces = []
            row_part = [[None] * blocks, [None] * blocks]
            for sb in range(blocks):
                s_here = slice(sb * HALF, (sb + 1) * HALF)
                x_here = x_low[s_here, here]
                split = (
                    jnp.where(first, x_here, jnp.zeros_like(x_here)),
                    jnp.where(first, jnp.zeros_like(x_here), x_here),
                )
                mixes = [[], []]
                lane_sum = [None, None]
                for tb in range(sb, blocks):
                    t_here = slice(tb * HALF, (tb + 1) * HALF)
                    dy_here = dy_low[t_here, here]
                    contact = st_scr[s_here, t_here]
                    touched = None
                    for k in range(2):
                        h = 2 * pair + k
                        gap = rws[h : h + 1, t_here] - cols[s_here, h : h + 1]
                        if sb == tb:
                            gap = jnp.where(causal, gap, NEG)
                        decay = jnp.exp2(gap)
                        mix = decay * contact
                        meet = nt_dot(split[k], dy_here)
                        through = decay * meet
                        pairs = through * contact
                        touched = through if touched is None else touched + through
                        mixes[k].append(mix.astype(BF16))
                        lane_sum[k] = pairs if lane_sum[k] is None else lane_sum[k] + pairs
                        down = jnp.sum(pairs, axis=0, keepdims=True)
                        row_part[k][tb] = down if row_part[k][tb] is None else row_part[k][tb] + down
                    ds_scr[s_here, t_here] += touched
                out = []
                for k in range(2):
                    h = 2 * pair + k
                    mix = jnp.concatenate(mixes[k], axis=1) if len(mixes[k]) > 1 else mixes[k][0]
                    out.append(nn_dot(mix, dy_low[sb * HALF :, here]))
                    total = jnp.sum(lane_sum[k], axis=1, keepdims=True)
                    col_sums[sb] = jnp.where(lane_row == h, total, col_sums[sb])
                pieces.append(jnp.where(first, out[0], out[1]))
            for k in range(2):
                for tb in range(blocks):
                    row_sums[tb] = jnp.where(sub == 2 * pair + k, row_part[k][tb], row_sums[tb])
            parts.append(jnp.concatenate(pieces, axis=0))
        colr_scr[j] = jnp.concatenate(col_sums, axis=0)
        rowr_scr[head_rows, :] = jnp.concatenate(row_sums, axis=1)
        dx = jnp.concatenate(parts, axis=1) + chan_ref[6:7, :] * dy
        dc = dx * (sc * (1.0 + c * (1.0 - sc)))
        dv = conv_back(dc, v_ref[0], chan_ref, cg_ref).astype(BF16)
        dv_ref[0] = dv
        dn_scr[...] += dn + nt_dot(dv, wx_ref[...])

    @pl.when(at == 2 * groups - 1)
    def _():
        act = act_scr[...]
        ds = ds_scr[...].astype(BF16)
        act_low = act.astype(BF16)
        d_b = nn_dot(ds, act_low[:, STATE:])
        d_c = lax.dot_general(ds, act_low[:, :STATE], (((0,), (0,)), ((), ())), preferred_element_type=F32)
        pre = cr_ref[0]
        sp = sigmoid(pre)
        d_pre = jnp.concatenate([d_b, d_c], axis=1) * (sp * (1.0 + pre * (1.0 - sp)))
        d_raw = conv_back(d_pre, vr_ref[0, :, : 2 * STATE], chanr_ref, cgr_ref)
        cgr_ref[5:8, :] = jnp.zeros((3, 2 * STATE), F32)
        col_total = colr_scr[0]
        for g in range(1, colr_scr.shape[0]):
            col_total = col_total + pltpu.roll(colr_scr[g], g * GROUP, 1)
        d_sums = rowr_scr[...].T - col_total
        at_row = lax.broadcasted_iota(jnp.int32, (rows, rows), 0)
        of_row = lax.broadcasted_iota(jnp.int32, (rows, rows), 1)
        upper = (of_row >= at_row).astype(F32)
        d_log = jnp.dot(upper, d_sums, precision=EXACT, preferred_element_type=F32)
        step = step_scr[...]
        rate = -jnp.exp(head_ref[1:2, :])
        d_step = col_total / step + rate * d_log
        raw_step = vr_ref[0, :, 2 * STATE : 3 * STATE] + head_ref[0:1, :]
        lanes = lax.broadcasted_iota(jnp.int32, (rows, HALF), 1)
        used = lanes < inner // HEAD_DIM
        d_raw_step = jnp.where(used, d_step * jax.nn.sigmoid(raw_step), 0.0)
        hg_ref[0:1, :] = jnp.sum(d_raw_step, axis=0, keepdims=True)
        hg_ref[1:2, :] = jnp.sum(jnp.where(used, d_log * step * rate, 0.0), axis=0, keepdims=True)
        hg_ref[2:8, :] = jnp.zeros((6, HALF), F32)
        dr = jnp.concatenate([d_raw, d_raw_step], axis=1).astype(BF16)
        dr_ref[0] = dr
        dn = dn_scr[...] + nt_dot(dr, wr_ref[...])
        u = u_ref[...].astype(F32)
        p = lax.rsqrt(jnp.mean(u * u, axis=1, keepdims=True) + EPS)
        e = dn * norm_ref[...]
        du = g_ref[...].astype(F32) + p * e - u * (p * p * p * jnp.mean(u * e, axis=1, keepdims=True))
        du_ref[...] = du.astype(BF16)
        ng_ref[0:1, :] = jnp.sum(u * p * dn, axis=0, keepdims=True)
        ng_ref[1:8, :] = jnp.zeros((7, width), F32)


def conv_back(dc, values, taps_ref, grad_ref):
    rows = lax.broadcasted_iota(jnp.int32, dc.shape, 0)
    count = dc.shape[0]
    grad_ref[4:5, :] = jnp.sum(dc, axis=0, keepdims=True)
    grad_ref[CONV - 1 : CONV, :] = jnp.sum(dc * values, axis=0, keepdims=True)
    total = taps_ref[CONV - 1 : CONV, :] * dc
    for ahead in range(1, CONV):
        moved = jnp.where(rows < count - ahead, pltpu.roll(dc, count - ahead, 0), 0.0)
        tap = CONV - 1 - ahead
        grad_ref[tap : tap + 1, :] = jnp.sum(moved * values, axis=0, keepdims=True)
        total = total + taps_ref[tap : tap + 1, :] * moved
    return total


def backward_slot(numbers, kept, grads, g, u, w_out, w_in, norm_gain, chan, chan_r, heads, slots):
    rows, width = g.shape
    inner = chan.shape[1]
    groups = inner // WIDE
    tail = w_in.shape[1] - 2 * inner
    z, v, c, y, v_r, c_r = kept
    early = lambda i: jnp.minimum(i, groups - 1)
    late = lambda i: jnp.maximum(i - groups, 0)
    cycle = lambda i: lax.rem(i, groups)
    whole = lambda a, b: pl.BlockSpec((a, b), lambda i, n: (0, 0))
    kept_whole = lambda b: pl.BlockSpec((1, rows, b), lambda i, n: (n[0], 0, 0))
    in_specs = [
        whole(rows, width),
        whole(rows, width),
        pl.BlockSpec((WIDE, width), lambda i, n: (early(i), 0)),
        pl.BlockSpec((width, WIDE), lambda i, n: (0, late(i))),
        pl.BlockSpec((width, WIDE), lambda i, n: (0, groups + late(i))),
        pl.BlockSpec((width, tail), lambda i, n: (0, 2 * inner // tail)),
        pl.BlockSpec((1, rows, WIDE), lambda i, n: (n[0], 0, cycle(i))),
        pl.BlockSpec((1, rows, WIDE), lambda i, n: (n[0], 0, late(i))),
        pl.BlockSpec((1, rows, WIDE), lambda i, n: (n[0], 0, late(i))),
        pl.BlockSpec((1, rows, WIDE), lambda i, n: (n[0], 0, cycle(i))),
        kept_whole(tail),
        kept_whole(2 * STATE),
        whole(1, width),
        pl.BlockSpec((8, WIDE), lambda i, n: (0, cycle(i))),
        whole(8, 2 * STATE),
        whole(8, HALF),
    ]
    args = [g, u, w_out, w_in, w_in, w_in, z, v, c, y, v_r, c_r, norm_gain, chan, chan_r, heads]
    aliases = {}
    if grads is not None:
        for k, arr in enumerate(grads):
            aliases[len(args) + 1] = k + 1
            args.append(arr)
            in_specs.append(pl.BlockSpec(memory_space=pl.ANY))
    out_shape = [
        jax.ShapeDtypeStruct((rows, width), BF16),
        jax.ShapeDtypeStruct((slots, rows, inner), BF16),
        jax.ShapeDtypeStruct((slots, rows, inner), BF16),
        jax.ShapeDtypeStruct((slots, rows, tail), BF16),
        jax.ShapeDtypeStruct((8, inner), F32),
        jax.ShapeDtypeStruct((8, 2 * STATE), F32),
        jax.ShapeDtypeStruct((8, width), F32),
        jax.ShapeDtypeStruct((8, HALF), F32),
    ]
    out_specs = [
        whole(rows, width),
        pl.BlockSpec((1, rows, WIDE), lambda i, n: (n[2], 0, late(i))),
        pl.BlockSpec((1, rows, WIDE), lambda i, n: (n[2], 0, late(i))),
        pl.BlockSpec((1, rows, tail), lambda i, n: (n[2], 0, 0)),
        pl.BlockSpec((8, WIDE), lambda i, n: (0, late(i))),
        whole(8, 2 * STATE),
        whole(8, width),
        whole(8, HALF),
    ]
    return pl.pallas_call(
        backward_kernel,
        grid_spec=pltpu.PrefetchScalarGridSpec(
            num_scalar_prefetch=1,
            grid=(2 * groups,),
            in_specs=in_specs,
            out_specs=out_specs,
            scratch_shapes=[
                pltpu.VMEM((rows, width), BF16),
                pltpu.VMEM((groups, rows, WIDE), F32),
                pltpu.VMEM((rows, 1), F32),
                pltpu.VMEM((rows, 1), F32),
                pltpu.VMEM((rows, rows), F32),
                pltpu.VMEM((rows, rows), F32),
                pltpu.VMEM((groups, rows, HALF), F32),
                pltpu.VMEM((HALF, rows), F32),
                pltpu.VMEM((groups, rows, HALF), F32),
                pltpu.VMEM((HALF, rows), F32),
                pltpu.VMEM((rows, HALF), F32),
                pltpu.VMEM((rows, 2 * STATE), F32),
                pltpu.VMEM((rows, width), F32),
            ],
        ),
        out_shape=out_shape,
        input_output_aliases=aliases,
        compiler_params=pltpu.CompilerParams(vmem_limit_bytes=VMEM),
        name="backward_slot",
    )(numbers, *args)


def pick(values, index, axis):
    return lax.dynamic_index_in_dim(values, index, axis, keepdims=False)


def swap(values, axis, bit):
    return lax.ppermute(values, axis, [(a, a ^ bit) for a in range(lax.axis_size(axis))])


def line_sum(blocks, axis, scale):
    count = lax.axis_size(axis)
    length = count // scale
    here = lax.axis_index(axis) // scale
    up = down = None
    for step in range(1, length):
        send_up = pick(blocks, jnp.clip(length - step + here, 0, length - 1), 0)
        send_down = pick(blocks, jnp.clip(here - (length - step), 0, length - 1), 0)
        if step > 1:
            send_up = (send_up.astype(F32) + up.astype(F32)).astype(BF16)
            send_down = (send_down.astype(F32) + down.astype(F32)).astype(BF16)
        up = lax.ppermute(send_up, axis, [(a, a + scale) for a in range(count - scale) if a // scale <= step - 1])
        down = lax.ppermute(
            send_down, axis, [(a, a - scale) for a in range(scale, count) if a // scale >= length - step]
        )
    own = pick(blocks, here, 0).astype(F32)
    return own if up is None else own + up.astype(F32) + down.astype(F32)


def tn_dot(a, b):
    return lax.dot_general(a, b, (((0,), (0,)), ((), ())), preferred_element_type=F32)


def by_partner(values, axis):
    count = lax.axis_size(axis)
    rows, total = values.shape
    split = values.reshape(rows, count // 4, 4, total // count)
    mine = lax.axis_index(axis) % 4
    return [pick(split, mine ^ delta, 2).reshape(rows, total // 4) for delta in range(4)]


def owned_sum(left, right, axis):
    count = lax.axis_size(axis)
    near = swap(tn_dot(jnp.concatenate([left[1], left[3]], axis=1), right).astype(BF16), axis, 1)
    half = near.shape[0] // 2
    far = swap((tn_dot(left[2], right) + near[half:].astype(F32)).astype(BF16), axis, 2)
    total = (tn_dot(left[0], right) + near[:half].astype(F32) + far.astype(F32)).astype(BF16)
    return line_sum(total.reshape(count // 4, -1, total.shape[1]), axis, 4)


def small_sums(scattered, common, axis):
    count = lax.axis_size(axis)
    place = lax.axis_index(axis)
    common = jnp.pad(common, (0, scattered.shape[1] - common.shape[0]))[None]
    bit = 1
    while bit < count:
        mine = (place // bit) % 2
        split = scattered.reshape(-1, 2, scattered.shape[1])
        sent = jnp.concatenate([pick(split, 1 - mine, 1), common], axis=0)
        came = swap(sent, axis, bit)
        scattered = pick(split, mine, 1) + came[:-1]
        common = common + came[-1:]
        bit *= 2
    return scattered[0], common[0]


def body(
    block_input,
    cotangent,
    lengths,
    in_weight,
    out_weight,
    conv_weight,
    conv_bias,
    norm_gain,
    gate_gain,
    dt_bias,
    a_log,
    skip_d,
):
    axis = "fsdp"
    count = lax.axis_size(axis)
    section = lax.axis_index("section")
    micro, rows, width = block_input.shape
    depth, proj_cols = in_weight.shape[1:]
    inner = gate_gain.shape[1] * count
    channels = conv_bias.shape[1] * count
    heads = dt_bias.shape[1]
    cols = -(-proj_cols // HALF) * HALF
    small = [a.reshape(-1) for a in (conv_weight[0], conv_bias[0], norm_gain[0], gate_gain[0])]
    sizes = [a.shape[0] for a in small]
    small_cols = -(-sum(sizes) // depth)
    packed = jnp.pad(jnp.concatenate(small), (0, small_cols * depth - sum(sizes))).reshape(depth, small_cols)
    packed = jnp.concatenate(
        [in_weight[0], packed, jnp.zeros((depth, cols - proj_cols - small_cols), BF16)], axis=1
    )
    w_in = lax.all_gather(packed, axis, axis=0, tiled=True)
    w_out = lax.all_gather(out_weight[0], axis, axis=0, tiled=True)
    flat = w_in[:, proj_cols : proj_cols + small_cols].reshape(count, depth * small_cols).astype(F32)
    cuts = [0]
    for size in sizes:
        cuts.append(cuts[-1] + size)
    taps = flat[:, cuts[0] : cuts[1]].reshape(count, CONV, -1).transpose(1, 0, 2).reshape(CONV, channels)
    bias = flat[:, cuts[1] : cuts[2]].reshape(1, channels)
    norm = flat[:, cuts[2] : cuts[3]].reshape(1, width)
    gate = flat[:, cuts[3] : cuts[4]].reshape(1, inner)
    skip = jnp.repeat(skip_d[0], HEAD_DIM)[None]
    chan = jnp.concatenate([taps[:, :inner], bias[:, :inner], gate, skip, jnp.zeros((1, inner), F32)], axis=0)
    chan_r = jnp.concatenate([taps[:, inner:], bias[:, inner:], jnp.zeros((3, channels - inner), F32)], axis=0)
    head_rows = jnp.pad(jnp.stack([dt_bias[0], a_log[0]]), ((0, 6), (0, HALF - heads)))
    places = jnp.arange(rows, dtype=jnp.int32)
    live = [(places < lengths[m, 0])[:, None] for m in range(micro)]

    kept = None

    def run_forward(kept, place, u):
        return forward_slot(place, kept, u, w_in, norm, chan, chan_r, head_rows, gate, 2 * micro)

    def finish(place, u, alive):
        branch = nn_dot(kept[1][place], w_out)
        return (u.astype(F32) + jnp.where(alive, branch, 0.0)).astype(BF16)

    for m in range(micro):
        kept = run_forward(kept, m, block_input[m])
    first = [finish(m, block_input[m], live[m]) for m in range(micro)]
    arrived = [lax.ppermute(h, "section", [(0, 1)]) for h in first]
    for m in range(micro):
        kept = run_forward(kept, micro + m, arrived[m])
    second = [finish(micro + m, arrived[m], live[m]) for m in range(micro)]
    outputs = jnp.stack([jnp.where(section == 0, a, b) for a, b in zip(first, second)])
    entered = [jnp.where(section == 0, block_input[m], arrived[m]) for m in range(micro)]

    is_last = section == 1
    returning = jnp.zeros((rows, width), BF16)
    grads = None
    gradients, incomings, small_terms = [], [], []
    for moment in range(micro + 1):
        position = micro - 1 - moment + (1 - section)
        active = (position >= 0) & (position < micro)
        slot = jnp.clip(position, 0, micro - 1)
        own = cotangent[micro - 1 - moment] if moment < micro else jnp.zeros((rows, width), BF16)
        incoming = jnp.where(is_last, own, returning)
        numbers = jnp.stack(
            [section * micro + slot, lengths[slot, 0], jnp.where(active, position, micro)]
        ).astype(jnp.int32)
        before, after = min(micro - 1, micro - moment), max(0, micro - 1 - moment)
        u = jnp.where(is_last, entered[after], entered[before])
        du, *rest = backward_slot(
            numbers, kept[2:], grads, incoming, u, w_out, w_in, norm, chan, chan_r, head_rows, micro + 1
        )
        grads, terms = rest[:3], rest[3:]
        gradients.append(du)
        incomings.append(incoming)
        small_terms.append(terms)
        if moment < micro:
            returning = lax.ppermute(du, "section", [(1, 0)])
    input_grads = jnp.stack(
        [jnp.where(is_last, gradients[micro - 1 - m], gradients[micro - m]) for m in range(micro)]
    )
    branch = [
        jnp.where(live[m], jnp.where(is_last, incomings[micro - 1 - m], incomings[micro - m]), jnp.zeros((), BF16))
        for m in range(micro)
    ]
    all_rows = micro * rows
    mine = lambda a: lax.dynamic_slice_in_dim(a, section * micro, micro, 0).reshape(all_rows, -1)
    left_out = by_partner(mine(kept[1]), axis)
    left_in = by_partner(mine(kept[0]), axis)
    out_grad = owned_sum(left_out, jnp.concatenate(branch, axis=0), axis)
    steady = lambda a: a[:micro].reshape(all_rows, -1)
    grad_z = owned_sum(left_in, steady(grads[0]), axis)
    grad_x = owned_sum(left_in, jnp.concatenate([steady(grads[1]), steady(grads[2])], axis=1), axis)
    in_grad = jnp.concatenate([grad_z, grad_x[:, : proj_cols - inner]], axis=1)

    chan_g, chan_rg, norm_g, head_g = [sum(t[k] for t in small_terms) for k in range(4)]
    taps_g = jnp.concatenate([chan_g[:CONV], chan_rg[:CONV]], axis=1)
    bias_g = jnp.concatenate([chan_g[CONV], chan_rg[CONV]])
    pieces = [
        taps_g.reshape(CONV, count, -1).transpose(1, 0, 2).reshape(count, -1),
        bias_g.reshape(count, -1),
        norm_g[0].reshape(count, -1),
        chan_g[5].reshape(count, -1),
    ]
    skip_g = chan_g[6].reshape(heads, HEAD_DIM).sum(axis=1)
    own_small, head_small = small_sums(
        jnp.concatenate(pieces, axis=1), jnp.concatenate([head_g[0, :heads], head_g[1, :heads], skip_g]), axis
    )
    parts = [own_small[a:b] for a, b in zip(cuts[:-1], cuts[1:])]
    return (
        outputs[None],
        input_grads[None],
        in_grad[None],
        out_grad[None],
        parts[0].reshape(1, CONV, -1),
        parts[1][None],
        parts[2][None],
        parts[3][None],
        head_small[None, :heads],
        head_small[None, heads : 2 * heads],
        head_small[None, 2 * heads : 3 * heads],
    )


def solution(mesh):
    in_specs = (
        P(None, "fsdp", None),
        P(None, "fsdp", None),
        P(None, "fsdp"),
        P("section", "fsdp", None),
        P("section", "fsdp", None),
        P("section", None, "fsdp"),
        P("section", "fsdp"),
        P("section", "fsdp"),
        P("section", "fsdp"),
        P("section", None),
        P("section", None),
        P("section", None),
    )
    out_specs = (
        P("section", None, "fsdp", None),
        P("section", None, "fsdp", None),
        P("section", "fsdp", None),
        P("section", "fsdp", None),
        P("section", None, "fsdp"),
        P("section", "fsdp"),
        P("section", "fsdp"),
        P("section", "fsdp"),
        P("section", None),
        P("section", None),
        P("section", None),
    )
    return jax.shard_map(body, mesh=mesh, in_specs=in_specs, out_specs=out_specs, check_vma=False)
```

time: 1840 us -> 803 us (0.44)
  waiting for transfers between devices: 862 us -> 371 us
  matrix products: 325 us -> 69.8 us
  Pallas kernels: 0 us -> 184 us
  other arithmetic: 222 us -> 42.7 us
  local copies, waits for them, and re-layouts: 236 us -> 59.6 us
  blocking collectives: 141 us -> 0 us
  starting transfers between devices: 8.24 us -> 50.4 us
  loops' own time: 19.4 us -> 0 us
    reduce_scatter x2 -> x0, waiting for transfers between devices: 478 us -> none  [the longest x1 390 us: body(): lax.psum_scatter(grad_totals[0], 'fsdp', scatter_dimension=0, tiled=True)]
    dot_general x36 -> x13, matrix products: 325 us -> 69.8 us  [the longest x9 44.1 us: tn_dot(): lax.dot_general(a, b, (((0,), (0,)), ((), ())), preferred_element_type=F32)]
    pallas_call x0 -> x7, Pallas kernels: none -> 184 us  [the longest x3 103 us: backward_slot(): pl.pallas_call(backward_kernel, grid_spec=pltpu.PrefetchScalarGridSpec(nu...]
    all_gather x2 -> x0, blocking collectives: 87.1 us -> none  [the longest x1 53.4 us: body(): lax.all_gather(shards[4], 'fsdp', axis=0, tiled=True)]
    reduce_sum x18 -> x1, other arithmetic: 70.8 us -> 0.85 us  [body(): skip_g = chan_g[6].reshape(heads, HEAD_DIM).sum(axis=1)]
    ppermute x4 -> x32, waiting for transfers between devices: 287 us -> 232 us  [the longest x10 127 us: swap(): lax.ppermute(values, axis, [(a, a ^ bit) for a in range(lax.axis_size(axi...]
    unnamed x1 -> x0, blocking collectives: 54.3 us -> none
    all_gather x2, waiting for transfers between devices: 95.4 us -> 138 us  [the longest x1 101 us: body(): w_in = lax.all_gather(packed, axis, axis=0, tiled=True)]
  transfers between devices with their start and end apart: 9 -> 34, of which waited for: 7 -> 17; matrix products, arithmetic and copies ran while one was open for 9% -> 17% of each run, Pallas kernels for 0% -> 5%
where the time goes in v1:
time: 803 us; the launch traced here: 793 us
  waiting for transfers between devices  371 us (46%)
  Pallas kernels  184 us (23%)
  matrix products  69.8 us (9%)
  local copies, waits for them, and re-layouts  59.6 us (7%)
  starting transfers between devices  50.4 us (6%)
  other arithmetic  42.7 us (5%)
  between operations  15.6 us (2%)
    ppermute x10, waiting for transfers between devices, swap(): lax.ppermute(values, axis, [(a, a ^ bit) for a in range(lax.axis_size(axi...  127 us
    pallas_call x3, Pallas kernels, backward_slot(): pl.pallas_call(backward_kernel, grid_spec=pltpu.PrefetchScalarGridSpec(nu...  103 us
    all_gather x1, waiting for transfers between devices, body(): w_in = lax.all_gather(packed, axis, axis=0, tiled=True)  101 us
    pallas_call x4, Pallas kernels, forward_slot(): pl.pallas_call(forward_kernel, grid=(groups,), in_specs=in_specs, out_spe...  81.1 us
    dot_general x9, matrix products, tn_dot(): lax.dot_general(a, b, (((0,), (0,)), ((), ())), preferred_element_type=F32)  44.1 us
    ppermute x9, waiting for transfers between devices, line_sum(): lax.ppermute(send_up, axis, [(a, a + scale) for a in range(count - scale)...  43.5 us
    all_gather x1, waiting for transfers between devices, body(): w_out = lax.all_gather(out_weight[0], axis, axis=0, tiled=True)  37.6 us
    ppermute x9, waiting for transfers between devices, line_sum(): lax.ppermute(send_down, axis, [(a, a - scale) for a in range(scale, count...  25.9 us
  transfers between devices with their start and end apart: 34, of which 17 were waited for; matrix products, arithmetic and copies ran while one was open for 17% of the time, Pallas kernels for 5%

profile of v1, /device:TPU:8, one launch (start us, length us, event | category | flops | bytes accessed | tf_op | source)
XLA Modules:
  0.0 793.2 jit_solution(11493778411123146693)
XLA Ops:
  18.8 100.8 %all-gather.4.cloned.1.call-done.wz_ref.wx_ref.wr_ref = bf16[1536,6528]{1,0:T(8,128)(2,1)} async-done(((bf16[96,6528]{1,0:T(8,128)(2,1)}), bf16[1536,6528]{1,0:T(8,128)(2,1)}) %all-gather.4.cloned.1.call-update) | async-done | bytes 20054032 | tf_op jit(solution)/shard_map/all_gather | solution.py:585
  123.9 20.1 %forward_slot.4 = (bf16[4,256,1536]{2,1,0:T(8,128)(2,1)}, bf16[4,256,3072]{2,1,0:T(8,128)(2,1)}, f32[4,256,3072]{2,1,0:T(8,128)}, f32[4,256,3072]{2,1,0:T(8,128)...) custom-call(bf16[256,1536]{1,0:T(8,128)(2,1)} %get-tuple-element.151.u_re, ...), custom_call_target="tpu_custom_call" | custom-call | tf_op jit(solution)/shard_map/forward_slot/pallas_call | solution.py:181
  144.0 20.8 %forward_slot.5 = (bf16[4,256,1536]{2,1,0:T(8,128)(2,1)}, bf16[4,256,3072]{2,1,0:T(8,128)(2,1)}, f32[4,256,3072]{2,1,0:T(8,128)}, f32[4,256,3072]{2,1,0:T(8,128)...) custom-call(bf16[256,1536]{1,0:T(8,128)(2,1)} %get-tuple-element.152, ...), custom_call_target="tpu_custom_call", output_to_operand_aliasing={{0}: (9, {}), {1}: (10, {}), {2}: (11, {}), {3}: (12, {}), ... | custom-call | tf_op jit(solution)/shard_map/forward_slot/pallas_call | solution.py:181
  164.8 37.6 %all-gather.6.cloned.1.call-done = bf16[1,3072,1536]{2,1,0:T(8,128)(2,1)} async-done(((bf16[1,192,1536]{2,1,0:T(8,128)(2,1)}), bf16[1,3072,1536]{2,1,0:T(8,128)(2,1)}) %all-gather.6.cloned.1.call-update) | async-done | bytes 9437200 | tf_op jit(solution)/shard_map/all_gather | solution.py:586
  202.4 6.9 fusion.2
  223.4 7.3 collective-permute-done.1.u_ref
  230.7 16.2 %collective-permute-done.u_ref = bf16[256,1536]{1,0:T(8,128)(2,1)S(1)} collective-permute-done((bf16[256,1536]{1,0:T(8,128)(2,1)S(1)}, bf16[256,1536]{1,0:T(8,128)(2,1)S(1)}, u32[]{:S(2)}, u32[]{:S(2)}) %collective-permute-start) | collective-permute-done | bytes 786464 | tf_op jit(solution)/shard_map/ppermute | solution.py:614
  248.6 20.1 %forward_slot.6 = (bf16[4,256,1536]{2,1,0:T(8,128)(2,1)}, bf16[4,256,3072]{2,1,0:T(8,128)(2,1)}, f32[4,256,3072]{2,1,0:T(8,128)}, f32[4,256,3072]{2,1,0:T(8,128)...) custom-call(bf16[256,1536]{1,0:T(8,128)(2,1)} %copy-done.12, ...), custom_call_target="tpu_custom_call", output_to_operand_aliasing={{0}: (9, {}), {1}: (10, {}), {2}: (11, {}), {3}: (12, {}), ... | custom-call | tf_op jit(solution)/shard_map/forward_slot/pallas_call | solution.py:181
  268.7 20.1 %forward_slot.7 = (bf16[4,256,1536]{2,1,0:T(8,128)(2,1)}, bf16[4,256,3072]{2,1,0:T(8,128)(2,1)}, f32[4,256,3072]{2,1,0:T(8,128)}, f32[4,256,3072]{2,1,0:T(8,128)...) custom-call(bf16[256,1536]{1,0:T(8,128)(2,1)} %copy-done.14, ...), custom_call_target="tpu_custom_call", output_to_operand_aliasing={{0}: (9, {}), {1}: (10, {}), {2}: (11, {}), {3}: (12, {}), ... | custom-call | tf_op jit(solution)/shard_map/forward_slot/pallas_call | solution.py:181
  288.8 34.2 %backward_slot.3 = (bf16[256,1536]{1,0:T(8,128)(2,1)}, bf16[3,256,3072]{2,1,0:T(8,128)(2,1)}, bf16[3,256,3072]{2,1,0:T(8,128)(2,1)}, bf16[3,256,384]{2,1,0:T(8,1...) custom-call(s32[3]{0:T(128)} %pad_add_fusion.1.at_ref, ...), custom_call_target="tpu_custom_call" | custom-call | tf_op jit(solution)/shard_map/backward_slot/pallas_call | solution.py:461
  335.9 6.1 reshape_reshape.7
  348.3 7.4 fusion.36
  358.1 34.2 %backward_slot.4 = (bf16[256,1536]{1,0:T(8,128)(2,1)}, bf16[3,256,3072]{2,1,0:T(8,128)(2,1)}, bf16[3,256,3072]{2,1,0:T(8,128)(2,1)}, bf16[3,256,384]{2,1,0:T(8,1...) custom-call(s32[3]{0:T(128)} %pad_add_fusion.at_ref, ...), custom_call_target="tpu_custom_call", output_to_operand_aliasing={{1}: (17, {}), {2}: (18, {}), {3}: (19, {})} | custom-call | tf_op jit(solution)/shard_map/backward_slot/pallas_call | solution.py:461
  393.8 7.4 fusion.34
  401.2 12.3 %collective-permute-done.3 = bf16[256,1536]{1,0:T(8,128)(2,1)S(1)} collective-permute-done((bf16[256,1536]{1,0:T(8,128)(2,1)}, bf16[256,1536]{1,0:T(8,128)(2,1)S(1)}, u32[]{:S(2)}, u32[]{:S(2)}) %collective-permute-start.3) | collective-permute-done | bytes 786464 | tf_op jit(solution)/shard_map/ppermute | solution.py:644
  414.6 34.5 %backward_slot.5 = (bf16[256,1536]{1,0:T(8,128)(2,1)}, bf16[3,256,3072]{2,1,0:T(8,128)(2,1)}, bf16[3,256,3072]{2,1,0:T(8,128)(2,1)}, bf16[3,256,384]{2,1,0:T(8,1...) custom-call(s32[3]{0:T(128)} %pad_add_fusion.2.at_ref, ...), custom_call_target="tpu_custom_call", output_to_operand_aliasing={{1}: (17, {}), {2}: (18, {}), {3}: (19, {})} | custom-call | tf_op jit(solution)/shard_map/backward_slot/pallas_call | solution.py:461
  541.2 35.5 %collective-permute-done.21 = bf16[768,1536]{1,0:T(8,128)(2,1)S(1)} collective-permute-done((bf16[768,1536]{1,0:T(8,128)(2,1)}, bf16[768,1536]{1,0:T(8,128)(2,1)S(1)}, u32[]{:S(2)}, u32[]{:S(2)}) %collective-permute-start.21) | collective-permute-done | bytes 2359328 | tf_op jit(solution)/shard_map/ppermute | solution.py:496
  581.0 46.4 %collective-permute-done.5 = bf16[384,3072]{1,0:T(8,128)(2,1)} collective-permute-done((bf16[384,3072]{1,0:T(8,128)(2,1)}, bf16[384,3072]{1,0:T(8,128)(2,1)}, u32[]{:S(2)}, u32[]{:S(2)}) %collective-permute-start.5) | collective-permute-done | bytes 2359328 | tf_op jit(solution)/shard_map/ppermute | solution.py:496
  637.9 44.7 %collective-permute-done.13 = bf16[384,3456]{1,0:T(8,128)(2,1)S(1)} collective-permute-done((bf16[384,3456]{1,0:T(8,128)(2,1)}, bf16[384,3456]{1,0:T(8,128)(2,1)S(1)}, u32[]{:S(2)}, u32[]{:S(2)}) %collective-permute-start.13) | collective-permute-done | bytes 2654240 | tf_op jit(solution)/shard_map/ppermute | solution.py:496
  691.3 14.0 %collective-permute-done.14 = bf16[96,3456]{1,0:T(8,128)(2,1)S(1)} collective-permute-done((bf16[96,3456]{1,0:T(8,128)(2,1)S(1)}, bf16[96,3456]{1,0:T(8,128)(2,1)S(1)}, u32[]{:S(2)}, u32[]{:S(2)}) %collective-permute-start.14) | collective-permute-done | bytes 663584 | tf_op jit(solution)/shard_map/ppermute | solution.py:510
  707.3 10.5 %collective-permute-done.7 = bf16[96,3072]{1,0:T(8,128)(2,1)S(1)} collective-permute-done((bf16[96,3072]{1,0:T(8,128)(2,1)S(1)}, bf16[96,3072]{1,0:T(8,128)(2,1)S(1)}, u32[]{:S(2)}, u32[]{:S(2)}) %collective-permute-start.7) | collective-permute-done | bytes 589856 | tf_op jit(solution)/shard_map/ppermute | solution.py:510
  737.8 17.1 %collective-permute-done.24 = bf16[192,1536]{1,0:T(8,128)(2,1)S(1)} collective-permute-done((bf16[192,1536]{1,0:T(8,128)(2,1)S(1)}, bf16[192,1536]{1,0:T(8,128)(2,1)S(1)}, u32[]{:S(2)}, u32[]{:S(2)}) %collective-permute-start.24) | collective-permute-done | bytes 589856 | tf_op jit(solution)/shard_map/ppermute | solution.py:510
  764.7 10.5 %collective-permute-done.11 = bf16[96,3072]{1,0:T(8,128)(2,1)S(1)} collective-permute-done((bf16[96,3072]{1,0:T(8,128)(2,1)S(1)}, bf16[96,3072]{1,0:T(8,128)(2,1)S(1)}, u32[]{:S(2)}, u32[]{:S(2)}) %collective-permute-start.11) | collective-permute-done | bytes 589856 | tf_op jit(solution)/shard_map/ppermute | solution.py:511
  775.4 8.8 %collective-permute-done.19 = bf16[96,3456]{1,0:T(8,128)(2,1)S(1)} collective-permute-done((bf16[96,3456]{1,0:T(8,128)(2,1)S(1)}, bf16[96,3456]{1,0:T(8,128)(2,1)S(1)}, u32[]{:S(2)}, u32[]{:S(2)}) %collective-permute-start.19) | collective-permute-done | bytes 663584 | tf_op jit(solution)/shard_map/ppermute | solution.py:511
  (309 shorter events, 204.2 us)
Async XLA Ops:
  7.2 112.3 %all-gather.4.cloned.1.call-start = ((), (), s32[]{:S(2)}) async-start(), calls=%async_computation | async-start | bytes 21307392 | tf_op jit(solution)/shard_map/all_gather | solution.py:585
  13.7 188.7 %all-gather.6.cloned.1.call-start = ((), (), s32[]{:S(2)}) async-start(), calls=%async_computation.1 | async-start | bytes 10027008 | tf_op jit(solution)/shard_map/all_gather | solution.py:586
  217.4 29.5 %collective-permute-start = (bf16[256,1536]{1,0:T(8,128)(2,1)S(1)}, bf16[256,1536]{1,0:T(8,128)(2,1)S(1)}, u32[]{:S(2)}, u32[]{:S(2)}) collective-permute-start(bf16[256,1536]{1,0:T(8,128)(2,1)S(1)} %fusion.3), channel_id=1, source_target_pairs={{0,16},{1,17},{2,18},{3,19},{4,20},{5,21},{6,22},{7,23},{8,24},{9,... | collective-permute-start | bytes 2359304 | tf_op jit(solution)/shard_map/ppermute | solution.py:614
  323.0 32.7 %collective-permute-start.2 = (bf16[256,1536]{1,0:T(8,128)(2,1)}, bf16[256,1536]{1,0:T(8,128)(2,1)}, u32[]{:S(2)}, u32[]{:S(2)}) collective-permute-start(bf16[256,1536]{1,0:T(8,128)(2,1)} %get-tuple-element.98), channel_id=1, source_target_pairs={{16,0},{17,1},{18,2},{19,3},{20,4},{21,5},{22,6},{23,7},{24,8},{25... | collective-permute-start | bytes 2359304 | tf_op jit(solution)/shard_map/ppermute | solution.py:644
  467.0 50.4 %collective-permute-start.20 = (bf16[1536,1536]{1,0:T(8,128)(2,1)}, bf16[1536,1536]{1,0:T(8,128)(2,1)}, u32[]{:S(2)}, u32[]{:S(2)}) collective-permute-start(bf16[1536,1536]{1,0:T(8,128)(2,1)} %convolution_convert_fusion), channel_id=1, source_target_pairs={{0,1},{1,0},{2,3},{3,2},{4,5},{5,4},{6,7},{7,6},{8,9},{9,8},{10,11... | collective-permute-start | bytes 14155784 | tf_op jit(solution)/shard_map/ppermute | solution.py:496
  505.4 28.3 %collective-permute-start.12 = (bf16[768,3456]{1,0:T(8,128)(2,1)}, bf16[768,3456]{1,0:T(8,128)(2,1)}, u32[]{:S(2)}, u32[]{:S(2)}) collective-permute-start(bf16[768,3456]{1,0:T(8,128)(2,1)} %convolution_convert_fusion.1), channel_id=1, source_target_pairs={{0,1},{1,0},{2,3},{3,2},{4,5},{5,4},{6,7},{7,6},{8,9},{9,8},{10,11... | collective-permute-start | bytes 15925256 | tf_op jit(solution)/shard_map/ppermute | solution.py:496
  522.3 54.4 %collective-permute-start.21 = (bf16[768,1536]{1,0:T(8,128)(2,1)}, bf16[768,1536]{1,0:T(8,128)(2,1)S(1)}, u32[]{:S(2)}, u32[]{:S(2)}) collective-permute-start(bf16[768,1536]{1,0:T(8,128)(2,1)} %add_convert_fusion.3), channel_id=1, source_target_pairs={{0,2},{1,3},{2,0},{3,1},{4,6},{5,7},{6,4},{7,5},{8,10},{9,11},{10,... | collective-permute-start | bytes 7077896 | tf_op jit(solution)/shard_map/ppermute | solution.py:496
  530.0 97.4 %collective-permute-start.5 = (bf16[384,3072]{1,0:T(8,128)(2,1)}, bf16[384,3072]{1,0:T(8,128)(2,1)}, u32[]{:S(2)}, u32[]{:S(2)}) collective-permute-start(bf16[384,3072]{1,0:T(8,128)(2,1)} %add_convert_fusion.5), channel_id=1, source_target_pairs={{0,2},{1,3},{2,0},{3,1},{4,6},{5,7},{6,4},{7,5},{8,10},{9,11},{10,... | collective-permute-start | bytes 7077896 | tf_op jit(solution)/shard_map/ppermute | solution.py:496
  539.8 142.8 %collective-permute-start.13 = (bf16[384,3456]{1,0:T(8,128)(2,1)}, bf16[384,3456]{1,0:T(8,128)(2,1)S(1)}, u32[]{:S(2)}, u32[]{:S(2)}) collective-permute-start(bf16[384,3456]{1,0:T(8,128)(2,1)} %add_convert_fusion.1), channel_id=1, source_target_pairs={{0,2},{1,3},{2,0},{3,1},{4,6},{5,7},{6,4},{7,5},{8,10},{9,11},{10,... | collective-permute-start | bytes 7962632 | tf_op jit(solution)/shard_map/ppermute | solution.py:496
  579.4 54.3 %collective-permute-start.22 = (bf16[192,1536]{1,0:T(8,128)(2,1)S(1)}, bf16[192,1536]{1,0:T(8,128)(2,1)S(1)}, u32[]{:S(2)}, u32[]{:S(2)}) collective-permute-start(bf16[192,1536]{1,0:T(8,128)(2,1)S(1)} %get-tuple-element.141), channel_id=1, source_target_pairs={{0,4},{1,5},{2,6},{3,7},{16,20},{17,21},{18,22},{19,23}} | collective-permute-start | bytes 1769480 | tf_op jit(solution)/shard_map/ppermute | solution.py:510
  631.0 55.8 %collective-permute-start.6 = (bf16[96,3072]{1,0:T(8,128)(2,1)S(1)}, bf16[96,3072]{1,0:T(8,128)(2,1)S(1)}, u32[]{:S(2)}, u32[]{:S(2)}) collective-permute-start(bf16[96,3072]{1,0:T(8,128)(2,1)S(1)} %get-tuple-element.145), channel_id=1, source_target_pairs={{0,4},{1,5},{2,6},{3,7},{16,20},{17,21},{18,22},{19,23}} | collective-permute-start | bytes 1769480 | tf_op jit(solution)/shard_map/ppermute | solution.py:510
  632.3 75.0 %collective-permute-start.9 = (bf16[96,3072]{1,0:T(8,128)(2,1)S(1)}, bf16[96,3072]{1,0:T(8,128)(2,1)S(1)}, u32[]{:S(2)}, u32[]{:S(2)}) collective-permute-start(bf16[96,3072]{1,0:T(8,128)(2,1)S(1)} %get-tuple-element.146), channel_id=1, source_target_pairs={{12,8},{13,9},{14,10},{15,11},{28,24},{29,25},{30,26},{31,27}} | collective-permute-start | bytes 1769480 | tf_op jit(solution)/shard_map/ppermute | solution.py:511
  633.0 55.9 %collective-permute-start.25 = (bf16[192,1536]{1,0:T(8,128)(2,1)S(1)}, bf16[192,1536]{1,0:T(8,128)(2,1)S(1)}, u32[]{:S(2)}, u32[]{:S(2)}) collective-permute-start(bf16[192,1536]{1,0:T(8,128)(2,1)S(1)} %get-tuple-element.142), channel_id=1, source_target_pairs={{12,8},{13,9},{14,10},{15,11},{28,24},{29,25},{30,26},{31,27}} | collective-permute-start | bytes 1769480 | tf_op jit(solution)/shard_map/ppermute | solution.py:511
  633.9 55.7 %collective-permute-start.23 = (bf16[192,1536]{1,0:T(8,128)(2,1)S(1)}, bf16[192,1536]{1,0:T(8,128)(2,1)S(1)}, u32[]{:S(2)}, u32[]{:S(2)}) collective-permute-start(bf16[192,1536]{1,0:T(8,128)(2,1)S(1)} %fusion.22), channel_id=1, source_target_pairs={{0,4},{1,5},{2,6},{3,7},{4,8},{5,9},{6,10},{7,11},{16,20},{17,21},... | collective-permute-start | bytes 1769480 | tf_op jit(solution)/shard_map/ppermute | solution.py:510
  687.0 30.9 %collective-permute-start.7 = (bf16[96,3072]{1,0:T(8,128)(2,1)S(1)}, bf16[96,3072]{1,0:T(8,128)(2,1)S(1)}, u32[]{:S(2)}, u32[]{:S(2)}) collective-permute-start(bf16[96,3072]{1,0:T(8,128)(2,1)S(1)} %fusion.28), channel_id=1, source_target_pairs={{0,4},{1,5},{2,6},{3,7},{4,8},{5,9},{6,10},{7,11},{16,20},{17,21},... | collective-permute-start | bytes 1769480 | tf_op jit(solution)/shard_map/ppermute | solution.py:510
  688.9 37.3 %collective-permute-start.17 = (bf16[96,3456]{1,0:T(8,128)(2,1)S(1)}, bf16[96,3456]{1,0:T(8,128)(2,1)S(1)}, u32[]{:S(2)}, u32[]{:S(2)}) collective-permute-start(bf16[96,3456]{1,0:T(8,128)(2,1)S(1)} %get-tuple-element.137), channel_id=1, source_target_pairs={{12,8},{13,9},{14,10},{15,11},{28,24},{29,25},{30,26},{31,27}} | collective-permute-start | bytes 1990664 | tf_op jit(solution)/shard_map/ppermute | solution.py:511
  690.0 34.2 %collective-permute-start.26 = (bf16[192,1536]{1,0:T(8,128)(2,1)S(1)}, bf16[192,1536]{1,0:T(8,128)(2,1)S(1)}, u32[]{:S(2)}, u32[]{:S(2)}) collective-permute-start(bf16[192,1536]{1,0:T(8,128)(2,1)S(1)} %get-tuple-element.140), channel_id=1, source_target_pairs={{8,4},{9,5},{10,6},{11,7},{12,8},{13,9},{14,10},{15,11},{24,20},{2... | collective-permute-start | bytes 1769480 | tf_op jit(solution)/shard_map/ppermute | solution.py:511
  705.4 26.7 %collective-permute-start.15 = (bf16[96,3456]{1,0:T(8,128)(2,1)S(1)}, bf16[96,3456]{1,0:T(8,128)(2,1)S(1)}, u32[]{:S(2)}, u32[]{:S(2)}) collective-permute-start(bf16[96,3456]{1,0:T(8,128)(2,1)S(1)} %fusion.17), channel_id=1, source_target_pairs={{0,4},{1,5},{2,6},{3,7},{4,8},{5,9},{6,10},{7,11},{16,20},{17,21},... | collective-permute-start | bytes 1990664 | tf_op jit(solution)/shard_map/ppermute | solution.py:510
  719.6 45.1 %collective-permute-start.8 = (bf16[96,3072]{1,0:T(8,128)(2,1)S(1)}, bf16[96,3072]{1,0:T(8,128)(2,1)S(1)}, u32[]{:S(2)}, u32[]{:S(2)}) collective-permute-start(bf16[96,3072]{1,0:T(8,128)(2,1)S(1)} %get-tuple-element.143), channel_id=1, source_target_pairs={{0,4},{1,5},{2,6},{3,7},{4,8},{5,9},{6,10},{7,11},{8,12},{9,13},{1... | collective-permute-start | bytes 1769480 | tf_op jit(solution)/shard_map/ppermute | solution.py:510
  724.2 30.7 %collective-permute-start.24 = (bf16[192,1536]{1,0:T(8,128)(2,1)S(1)}, bf16[192,1536]{1,0:T(8,128)(2,1)S(1)}, u32[]{:S(2)}, u32[]{:S(2)}) collective-permute-start(bf16[192,1536]{1,0:T(8,128)(2,1)S(1)} %get-tuple-element.139), channel_id=1, source_target_pairs={{0,4},{1,5},{2,6},{3,7},{4,8},{5,9},{6,10},{7,11},{8,12},{9,13},{1... | collective-permute-start | bytes 1769480 | tf_op jit(solution)/shard_map/ppermute | solution.py:510
  726.3 30.6 %collective-permute-start.27 = (bf16[192,1536]{1,0:T(8,128)(2,1)S(1)}, bf16[192,1536]{1,0:T(8,128)(2,1)S(1)}, u32[]{:S(2)}, u32[]{:S(2)}) collective-permute-start(bf16[192,1536]{1,0:T(8,128)(2,1)S(1)} %fusion.21), channel_id=1, source_target_pairs={{4,0},{5,1},{6,2},{7,3},{8,4},{9,5},{10,6},{11,7},{12,8},{13,9},{1... | collective-permute-start | bytes 1769480 | tf_op jit(solution)/shard_map/ppermute | solution.py:511
  732.5 30.1 %collective-permute-start.18 = (bf16[96,3456]{1,0:T(8,128)(2,1)S(1)}, bf16[96,3456]{1,0:T(8,128)(2,1)S(1)}, u32[]{:S(2)}, u32[]{:S(2)}) collective-permute-start(bf16[96,3456]{1,0:T(8,128)(2,1)S(1)} %get-tuple-element.135), channel_id=1, source_target_pairs={{8,4},{9,5},{10,6},{11,7},{12,8},{13,9},{14,10},{15,11},{24,20},{2... | collective-permute-start | bytes 1990664 | tf_op jit(solution)/shard_map/ppermute | solution.py:511
  735.9 39.3 %collective-permute-start.11 = (bf16[96,3072]{1,0:T(8,128)(2,1)S(1)}, bf16[96,3072]{1,0:T(8,128)(2,1)S(1)}, u32[]{:S(2)}, u32[]{:S(2)}) collective-permute-start(bf16[96,3072]{1,0:T(8,128)(2,1)S(1)} %fusion.27), channel_id=1, source_target_pairs={{4,0},{5,1},{6,2},{7,3},{8,4},{9,5},{10,6},{11,7},{12,8},{13,9},{1... | collective-permute-start | bytes 1769480 | tf_op jit(solution)/shard_map/ppermute | solution.py:511
  762.8 21.5 %collective-permute-start.19 = (bf16[96,3456]{1,0:T(8,128)(2,1)S(1)}, bf16[96,3456]{1,0:T(8,128)(2,1)S(1)}, u32[]{:S(2)}, u32[]{:S(2)}) collective-permute-start(bf16[96,3456]{1,0:T(8,128)(2,1)S(1)} %fusion.16), channel_id=1, source_target_pairs={{4,0},{5,1},{6,2},{7,3},{8,4},{9,5},{10,6},{11,7},{12,8},{13,9},{1... | collective-permute-start | bytes 1990664 | tf_op jit(solution)/shard_map/ppermute | solution.py:511
  (69 other events, 1555.9 us)
Sparse Core Ops, SparseCore 0:
  13.8 105.6 all-gather.3
  121.8 80.5 all-gather.5

commit v2 on v1

v2 whole, which is shorter than its diff:
```python
import functools

import jax
import jax.numpy as jnp
from jax import lax
from jax.experimental import pallas as pl
from jax.experimental.pallas import tpu as pltpu
from jax.sharding import PartitionSpec as P

HEAD_DIM = 64
STATE = 128
CONV = 4
EPS = 1e-05
LOG2E = 1.4426950408889634
HALF = 128
WIDE = 512
GROUP = WIDE // HEAD_DIM
TINY = 1e-30
NEG = -1e30
VMEM = 56 * 1024 * 1024
F32 = jnp.float32
BF16 = jnp.bfloat16
EXACT = lax.Precision.HIGHEST


def nt_dot(a, b):
    return lax.dot_general(a, b, (((1,), (1,)), ((), ())), preferred_element_type=F32)


def nn_dot(a, b):
    return jnp.dot(a, b, preferred_element_type=F32)


def sigmoid(v):
    return 0.5 * jnp.tanh(0.5 * v) + 0.5


def conv_rows(values, taps, bias):
    rows = lax.broadcasted_iota(jnp.int32, values.shape, 0)
    total = bias + taps[CONV - 1 : CONV, :] * values
    for back in range(1, CONV):
        moved = jnp.where(rows >= back, pltpu.roll(values, back, 0), 0.0)
        total = total + taps[CONV - 1 - back : CONV - back, :] * moved
    return total


def softplus(v):
    return jnp.maximum(v, 0.0) + jnp.log1p(jnp.exp(-jnp.abs(v)))


def step_terms(step_raw, head_ref):
    rows = step_raw.shape[0]
    step = jnp.maximum(softplus(step_raw + head_ref[0:1, :]), TINY)
    rate = -jnp.exp(head_ref[1:2, :])
    at = lax.broadcasted_iota(jnp.int32, (rows, rows), 0)
    of = lax.broadcasted_iota(jnp.int32, (rows, rows), 1)
    lower = (at >= of).astype(F32)
    sums = jnp.dot(lower, step * rate, precision=EXACT, preferred_element_type=F32) * LOG2E
    return step, rate, sums, sums - jnp.log2(step)


def spread(target, values, groups):
    for g in range(groups):
        target[g] = pltpu.roll(values, (HALF - g * GROUP) % HALF, 1) if g else values


def fold(block):
    return block[:, 0].reshape(-1, block.shape[-1])


def forward_kernel(
    at_ref, u_ref, ublk_ref, wo_ref, wz_ref, wx_ref, wb_ref, wc_ref, wt_ref, norm_ref, chan_ref, chanr_ref, head_ref, gate_ref, *rest
):
    (nb_ref, gb_ref, z_ref, v_ref, c_ref, y_ref, vr_ref, cr_ref, h_ref, w_scr, sq_scr, s_scr, col_scr, row_scr) = rest[-14:]
    step_at = pl.program_id(0)
    groups = w_scr.shape[0]
    rows = u_ref.shape[0]

    @pl.when(step_at == 0)
    def _():
        u = u_ref[...].astype(F32)
        scale = lax.rsqrt(jnp.mean(u * u, axis=1, keepdims=True) + EPS)
        nb_ref[0] = (u * scale * norm_ref[...]).astype(BF16)
        nb = nb_ref[0]
        raw = jnp.concatenate([nn_dot(nb, fold(wb_ref[...])), nn_dot(nb, fold(wc_ref[...]))], axis=1)
        steps = nn_dot(nb, fold(wt_ref[...]))
        vr_ref[0, :, : 2 * STATE] = raw
        vr_ref[0, :, 2 * STATE :] = steps
        pre = conv_rows(raw, chanr_ref[0:4, :], chanr_ref[4:5, :])
        cr_ref[0] = pre
        act = pre * sigmoid(pre)
        s_scr[...] = lax.dot_general(
            act[:, STATE:], act[:, :STATE], (((1,), (1,)), ((), ())), precision=EXACT, preferred_element_type=F32
        )
        _, _, sums, shifted = step_terms(steps, head_ref)
        spread(col_scr, sums, groups)
        row_scr[...] = shifted.T
        sq_scr[...] = jnp.zeros_like(sq_scr)

    @pl.when(step_at < groups)
    def _():
        nb = nb_ref[0]
        z = nn_dot(nb, fold(wz_ref[...]))
        z_ref[0] = z
        v = nn_dot(nb, fold(wx_ref[...]))
        v_ref[0] = v
        c = conv_rows(v, chan_ref[0:4, :], chan_ref[4:5, :])
        c_ref[0] = c
        x = c * sigmoid(c)
        x_low = x.astype(BF16)
        cols = col_scr[step_at]
        rws = row_scr[pl.ds(pl.multiple_of(step_at * GROUP, GROUP), GROUP), :]
        lane = lax.broadcasted_iota(jnp.int32, (HALF, HALF), 1)
        causal = lax.broadcasted_iota(jnp.int32, (HALF, HALF), 0) >= lane
        first = lane < HEAD_DIM
        parts = []
        for pair in range(GROUP // 2):
            here = slice(pair * HALF, (pair + 1) * HALF)
            pieces = []
            for tb in range(rows // HALF):
                t_here = slice(tb * HALF, (tb + 1) * HALF)
                both = []
                for h in (2 * pair, 2 * pair + 1):
                    col = cols[t_here, h : h + 1]
                    mix = []
                    for sb in range(tb + 1):
                        s_here = slice(sb * HALF, (sb + 1) * HALF)
                        gap = col - rws[h : h + 1, s_here]
                        if sb == tb:
                            gap = jnp.where(causal, gap, NEG)
                        mix.append((jnp.exp2(gap) * s_scr[t_here, s_here]).astype(BF16))
                    mix = jnp.concatenate(mix, axis=1) if len(mix) > 1 else mix[0]
                    both.append(nn_dot(mix, x_low[: (tb + 1) * HALF, here]))
                pieces.append(jnp.where(first, both[0], both[1]))
            parts.append(jnp.concatenate(pieces, axis=0))
        y = jnp.concatenate(parts, axis=1) + chan_ref[6:7, :] * x
        y_ref[0] = y
        w = y * (z * sigmoid(z))
        w_scr[step_at] = w
        sq_scr[...] += jnp.sum(w * w, axis=1, keepdims=True)

    @pl.when(step_at == groups - 1)
    def _():
        scale = lax.rsqrt(sq_scr[...] * (1.0 / (groups * WIDE)) + EPS)
        for g in range(groups):
            here = slice(g * WIDE, (g + 1) * WIDE)
            gb_ref[0, :, here] = (w_scr[g] * scale * gate_ref[:, here]).astype(BF16)

    @pl.when(step_at >= groups)
    def _():
        live = lax.broadcasted_iota(jnp.int32, (rows, 1), 0) < at_ref[0]
        branch = jnp.where(live, nn_dot(gb_ref[0], wo_ref[...]), 0.0)
        h_ref[...] = (ublk_ref[...].astype(F32) + branch).astype(BF16)


def in_specs_of(view, groups, late):
    parts, _, depth, _ = view.shape
    width = parts * depth
    start = width // WIDE
    small = (width + groups * WIDE) // HALF
    tall = lambda half, cols, at: pl.BlockSpec((parts, 1, depth, cols), lambda i, n: (0, half, 0, at(i)))
    return [
        tall(0, WIDE, lambda i: start + late(i)),
        tall(1, WIDE, lambda i: start + late(i)),
        tall(0, HALF, lambda i: small),
        tall(1, HALF, lambda i: small),
        tall(0, HALF, lambda i: small + 1),
    ]


def forward_slot(place, length, kept, u, w_all, view, norm_gain, chan, chan_r, heads, gate_gain, slots):
    rows, width = u.shape
    inner = chan.shape[1]
    groups = inner // WIDE
    shapes = [
        ((rows, width), BF16),
        ((rows, inner), BF16),
        ((rows, inner), F32),
        ((rows, inner), F32),
        ((rows, inner), F32),
        ((rows, inner), F32),
        ((rows, 3 * STATE), F32),
        ((rows, 2 * STATE), F32),
    ]
    early = lambda i: jnp.minimum(i, groups - 1)
    late = lambda i: jnp.maximum(i - groups, 0)
    wide_out = lambda: pl.BlockSpec((1, rows, WIDE), lambda i, n: (place, 0, early(i)))
    whole = lambda a, b: pl.BlockSpec((a, b), lambda i, n: (0, 0))
    whole_out = lambda b: pl.BlockSpec((1, rows, b), lambda i, n: (place, 0, 0))
    in_specs = [
        whole(rows, width),
        pl.BlockSpec((rows, WIDE), lambda i, n: (0, late(i))),
        pl.BlockSpec((inner, WIDE), lambda i, n: (0, late(i))),
        *in_specs_of(view, groups, early),
        whole(1, width),
        pl.BlockSpec((8, WIDE), lambda i, n: (0, early(i))),
        whole(8, 2 * STATE),
        whole(8, HALF),
        whole(1, inner),
    ]
    args = [u, u, w_all] + [view] * 5 + [norm_gain, chan, chan_r, heads, gate_gain]
    aliases = {}
    if kept is not None:
        for k, arr in enumerate(kept):
            aliases[len(args) + 1] = k
            args.append(arr)
            in_specs.append(pl.BlockSpec(memory_space=pl.ANY))
    out_specs = [whole_out(width), whole_out(inner)] + [wide_out() for _ in range(4)]
    out_specs += [whole_out(3 * STATE), whole_out(2 * STATE), pl.BlockSpec((rows, WIDE), lambda i, n: (0, late(i)))]
    out_shape = [jax.ShapeDtypeStruct((slots,) + s, d) for s, d in shapes]
    *kept, h = pl.pallas_call(
        forward_kernel,
        grid_spec=pltpu.PrefetchScalarGridSpec(
            num_scalar_prefetch=1,
            grid=(groups + width // WIDE,),
            in_specs=in_specs,
            out_specs=out_specs,
            scratch_shapes=[
                pltpu.VMEM((groups, rows, WIDE), F32),
                pltpu.VMEM((rows, 1), F32),
                pltpu.VMEM((rows, rows), F32),
                pltpu.VMEM((groups, rows, HALF), F32),
                pltpu.VMEM((HALF, rows), F32),
            ],
        ),
        out_shape=out_shape + [jax.ShapeDtypeStruct((rows, width), BF16)],
        input_output_aliases=aliases,
        compiler_params=pltpu.CompilerParams(vmem_limit_bytes=VMEM),
        cost_estimate=pl.CostEstimate(flops=22 * 10**9, bytes_accessed=60 * 10**6, transcendentals=0),
        name="forward_slot",
    )(length, *args)
    return kept, h


def backward_kernel(
    at_ref,
    g_ref,
    u_ref,
    wo_ref,
    wz_ref,
    wx_ref,
    wb_ref,
    wc_ref,
    wt_ref,
    z_ref,
    v_ref,
    c_ref,
    y_ref,
    vr_ref,
    cr_ref,
    norm_ref,
    chan_ref,
    chanr_ref,
    head_ref,
    past_ref,
    *rest,
):
    (
        du_ref, dz_ref, dv_ref, sum_ref,
        dob_scr, dgb_scr, sq_scr, we_scr, st_scr, ds_scr, bcol_scr, trow_scr, colr_scr, rowr_scr, step_scr, act_scr, dn_scr,
    ) = rest[-17:]
    groups = pl.num_programs(0) // 2
    at = pl.program_id(0)
    rows, width = g_ref.shape
    inner = dgb_scr.shape[0] * WIDE

    @pl.when(at == 0)
    def _():
        live = lax.broadcasted_iota(jnp.int32, (rows, 1), 0) < at_ref[1]
        dob_scr[...] = jnp.where(live, g_ref[...].astype(F32), 0.0).astype(BF16)
        sq_scr[...] = jnp.zeros_like(sq_scr)
        we_scr[...] = jnp.zeros_like(we_scr)
        ds_scr[...] = jnp.zeros_like(ds_scr)
        dn_scr[...] = jnp.zeros_like(dn_scr)
        rowr_scr[...] = jnp.zeros_like(rowr_scr)
        pre = cr_ref[0]
        act = pre * sigmoid(pre)
        act_scr[...] = act
        st_scr[...] = lax.dot_general(
            act[:, :STATE], act[:, STATE:], (((1,), (1,)), ((), ())), precision=EXACT, preferred_element_type=F32
        )
        step, rate, sums, shifted = step_terms(vr_ref[0, :, 2 * STATE : 3 * STATE], head_ref)
        step_scr[...] = step
        spread(bcol_scr, shifted, dgb_scr.shape[0])
        trow_scr[...] = sums.T

    @pl.when(at < groups)
    def _():
        dgb = nt_dot(dob_scr[...], wo_ref[...])
        dgb_scr[at] = dgb
        z = z_ref[0]
        w = y_ref[0] * (z * sigmoid(z))
        sq_scr[...] += jnp.sum(w * w, axis=1, keepdims=True)
        we_scr[...] += jnp.sum(w * (dgb * chan_ref[5:6, :]), axis=1, keepdims=True)

    @pl.when(at >= groups)
    def _():
        j = at - groups
        q = lax.rsqrt(sq_scr[...] * (1.0 / inner) + EPS)
        pull = q * q * q * (we_scr[...] * (1.0 / inner))
        dgb = dgb_scr[j]
        z = z_ref[0]
        y = y_ref[0]
        sz = sigmoid(z)
        silu_z = z * sz
        w = y * silu_z
        dw = q * (dgb * chan_ref[5:6, :]) - w * pull
        wide = pl.ds(pl.multiple_of(j * WIDE, WIDE), WIDE)
        sum_ref[5:6, wide] = past_ref[5:6, wide] + jnp.sum(w * q * dgb, axis=0, keepdims=True)
        dy = dw * silu_z
        dz = (dw * y * (sz * (1.0 + z * (1.0 - sz)))).astype(BF16)
        dz_ref[0] = dz
        dn = nt_dot(dz, fold(wz_ref[...]))

        c = c_ref[0]
        sc = sigmoid(c)
        x = c * sc
        x_low = x.astype(BF16)
        dy_low = dy.astype(BF16)
        sum_ref[6:7, wide] = past_ref[6:7, wide] + jnp.sum(dy * x, axis=0, keepdims=True)
        cols = bcol_scr[j]
        head_rows = pl.ds(pl.multiple_of(j * GROUP, GROUP), GROUP)
        rws = trow_scr[head_rows, :]
        lane = lax.broadcasted_iota(jnp.int32, (HALF, HALF), 1)
        causal = lane >= lax.broadcasted_iota(jnp.int32, (HALF, HALF), 0)
        first = lane < HEAD_DIM
        lane_row = lax.broadcasted_iota(jnp.int32, (1, HALF), 1)
        sub = lax.broadcasted_iota(jnp.int32, (GROUP, HALF), 0)
        blocks = rows // HALF
        col_sums = [jnp.zeros((HALF, HALF), F32) for _ in range(blocks)]
        row_sums = [jnp.zeros((GROUP, HALF), F32) for _ in range(blocks)]
        parts = []
        for pair in range(GROUP // 2):
            here = slice(pair * HALF, (pair + 1) * HALF)
            pieces = []
            row_part = [[None] * blocks, [None] * blocks]
            for sb in range(blocks):
                s_here = slice(sb * HALF, (sb + 1) * HALF)
                x_here = x_low[s_here, here]
                split = (
                    jnp.where(first, x_here, jnp.zeros_like(x_here)),
                    jnp.where(first, jnp.zeros_like(x_here), x_here),
                )
                mixes = [[], []]
                lane_sum = [None, None]
                for tb in range(sb, blocks):
                    t_here = slice(tb * HALF, (tb + 1) * HALF)
                    dy_here = dy_low[t_here, here]
                    contact = st_scr[s_here, t_here]
                    touched = None
                    for k in range(2):
                        h = 2 * pair + k
                        gap = rws[h : h + 1, t_here] - cols[s_here, h : h + 1]
                        if sb == tb:
                            gap = jnp.where(causal, gap, NEG)
                        decay = jnp.exp2(gap)
                        mix = decay * contact
                        meet = nt_dot(split[k], dy_here)
                        through = decay * meet
                        pairs = through * contact
                        touched = through if touched is None else touched + through
                        mixes[k].append(mix.astype(BF16))
                        lane_sum[k] = pairs if lane_sum[k] is None else lane_sum[k] + pairs
                        down = jnp.sum(pairs, axis=0, keepdims=True)
                        row_part[k][tb] = down if row_part[k][tb] is None else row_part[k][tb] + down
                    ds_scr[s_here, t_here] += touched
                out = []
                for k in range(2):
                    h = 2 * pair + k
                    mix = jnp.concatenate(mixes[k], axis=1) if len(mixes[k]) > 1 else mixes[k][0]
                    out.append(nn_dot(mix, dy_low[sb * HALF :, here]))
                    total = jnp.sum(lane_sum[k], axis=1, keepdims=True)
                    col_sums[sb] = jnp.where(lane_row == h, total, col_sums[sb])
                pieces.append(jnp.where(first, out[0], out[1]))
            for k in range(2):
                for tb in range(blocks):
                    row_sums[tb] = jnp.where(sub == 2 * pair + k, row_part[k][tb], row_sums[tb])
            parts.append(jnp.concatenate(pieces, axis=0))
        colr_scr[j] = jnp.concatenate(col_sums, axis=0)
        rowr_scr[head_rows, :] = jnp.concatenate(row_sums, axis=1)
        dx = jnp.concatenate(parts, axis=1) + chan_ref[6:7, :] * dy
        dc = dx * (sc * (1.0 + c * (1.0 - sc)))
        dv = conv_back(dc, v_ref[0], chan_ref, past_ref, sum_ref, wide).astype(BF16)
        dv_ref[0, :, wide] = dv
        dn_scr[...] += dn + nt_dot(dv, fold(wx_ref[...]))

    @pl.when(at == 2 * groups - 1)
    def _():
        act = act_scr[...]
        ds = ds_scr[...].astype(BF16)
        act_low = act.astype(BF16)
        d_b = nn_dot(ds, act_low[:, STATE:])
        d_c = lax.dot_general(ds, act_low[:, :STATE], (((0,), (0,)), ((), ())), preferred_element_type=F32)
        pre = cr_ref[0]
        sp = sigmoid(pre)
        d_pre = jnp.concatenate([d_b, d_c], axis=1) * (sp * (1.0 + pre * (1.0 - sp)))
        narrow = slice(inner, inner + 2 * STATE)
        d_raw = conv_back(d_pre, vr_ref[0, :, : 2 * STATE], chanr_ref, past_ref, sum_ref, narrow)
        sum_ref[5:7, narrow] = jnp.zeros((2, 2 * STATE), F32)
        col_total = colr_scr[0]
        for g in range(1, colr_scr.shape[0]):
            col_total = col_total + pltpu.roll(colr_scr[g], g * GROUP, 1)
        d_sums = rowr_scr[...].T - col_total
        at_row = lax.broadcasted_iota(jnp.int32, (rows, rows), 0)
        of_row = lax.broadcasted_iota(jnp.int32, (rows, rows), 1)
        upper = (of_row >= at_row).astype(F32)
        d_log = jnp.dot(upper, d_sums, precision=EXACT, preferred_element_type=F32)
        step = step_scr[...]
        rate = -jnp.exp(head_ref[1:2, :])
        d_step = col_total / step + rate * d_log
        raw_step = vr_ref[0, :, 2 * STATE : 3 * STATE] + head_ref[0:1, :]
        lanes = lax.broadcasted_iota(jnp.int32, (rows, HALF), 1)
        used = lanes < inner // HEAD_DIM
        d_raw_step = jnp.where(used, d_step * jax.nn.sigmoid(raw_step), 0.0)
        last = past_ref[7:8, :]
        sum_ref[7:8, width : width + HALF] = last[:, width : width + HALF] + jnp.sum(d_raw_step, axis=0, keepdims=True)
        sum_ref[7:8, width + HALF : width + 2 * HALF] = last[:, width + HALF : width + 2 * HALF] + jnp.sum(
            jnp.where(used, d_log * step * rate, 0.0), axis=0, keepdims=True
        )
        sum_ref[7:8, width + 2 * HALF :] = jnp.zeros((1, inner - width), F32)
        dr = jnp.concatenate([d_raw, d_raw_step], axis=1).astype(BF16)
        dv_ref[0, :, inner:] = dr
        dn = dn_scr[...] + nt_dot(dr[:, :STATE], fold(wb_ref[...]))
        dn = dn + nt_dot(dr[:, STATE : 2 * STATE], fold(wc_ref[...])) + nt_dot(dr[:, 2 * STATE :], fold(wt_ref[...]))
        u = u_ref[...].astype(F32)
        p = lax.rsqrt(jnp.mean(u * u, axis=1, keepdims=True) + EPS)
        e = dn * norm_ref[...]
        du = g_ref[...].astype(F32) + p * e - u * (p * p * p * jnp.mean(u * e, axis=1, keepdims=True))
        du_ref[...] = du.astype(BF16)
        sum_ref[7:8, :width] = last[:, :width] + jnp.sum(u * p * dn, axis=0, keepdims=True)


def conv_back(dc, values, taps_ref, past_ref, sum_ref, here):
    rows = lax.broadcasted_iota(jnp.int32, dc.shape, 0)
    count = dc.shape[0]
    sum_ref[4:5, here] = past_ref[4:5, here] + jnp.sum(dc, axis=0, keepdims=True)
    total = 0.0
    for ahead in range(CONV):
        moved = jnp.where(rows < count - ahead, pltpu.roll(dc, count - ahead, 0), 0.0) if ahead else dc
        tap = CONV - 1 - ahead
        sum_ref[tap : tap + 1, here] = past_ref[tap : tap + 1, here] + jnp.sum(moved * values, axis=0, keepdims=True)
        total = total + taps_ref[tap : tap + 1, :] * moved
    return total


def backward_slot(numbers, kept, grads, past, g, u, w_all, view, norm_gain, chan, chan_r, heads, slots):
    rows, width = g.shape
    inner = chan.shape[1]
    groups = inner // WIDE
    tail = 3 * STATE
    z, v, c, y, v_r, c_r = kept
    early = lambda i: jnp.minimum(i, groups - 1)
    late = lambda i: jnp.maximum(i - groups, 0)
    cycle = lambda i: lax.rem(i, groups)
    whole = lambda a, b: pl.BlockSpec((a, b), lambda i, n: (0, 0))
    kept_whole = lambda b: pl.BlockSpec((1, rows, b), lambda i, n: (n[0], 0, 0))
    in_specs = [
        whole(rows, width),
        whole(rows, width),
        pl.BlockSpec((WIDE, width), lambda i, n: (early(i), 0)),
        *in_specs_of(view, groups, late),
        pl.BlockSpec((1, rows, WIDE), lambda i, n: (n[0], 0, cycle(i))),
        pl.BlockSpec((1, rows, WIDE), lambda i, n: (n[0], 0, late(i))),
        pl.BlockSpec((1, rows, WIDE), lambda i, n: (n[0], 0, late(i))),
        pl.BlockSpec((1, rows, WIDE), lambda i, n: (n[0], 0, cycle(i))),
        kept_whole(tail),
        kept_whole(2 * STATE),
        whole(1, width),
        pl.BlockSpec((8, WIDE), lambda i, n: (0, cycle(i))),
        whole(8, 2 * STATE),
        whole(8, HALF),
        whole(8, inner + 2 * STATE),
    ]
    args = [g, u, w_all] + [view] * 5 + [z, v, c, y, v_r, c_r, norm_gain, chan, chan_r, heads, past]
    aliases = {}
    if grads is not None:
        for k, arr in enumerate(grads):
            aliases[len(args) + 1] = k + 1
            args.append(arr)
            in_specs.append(pl.BlockSpec(memory_space=pl.ANY))
    out_shape = [
        jax.ShapeDtypeStruct((rows, width), BF16),
        jax.ShapeDtypeStruct((slots, rows, inner), BF16),
        jax.ShapeDtypeStruct((slots, rows, inner + tail), BF16),
        jax.ShapeDtypeStruct((8, inner + 2 * STATE), F32),
    ]
    out_specs = [
        whole(rows, width),
        pl.BlockSpec((1, rows, WIDE), lambda i, n: (n[2], 0, late(i))),
        pl.BlockSpec((1, rows, inner + tail), lambda i, n: (n[2], 0, 0)),
        whole(8, inner + 2 * STATE),
    ]
    return pl.pallas_call(
        backward_kernel,
        grid_spec=pltpu.PrefetchScalarGridSpec(
            num_scalar_prefetch=1,
            grid=(2 * groups,),
            in_specs=in_specs,
            out_specs=out_specs,
            scratch_shapes=[
                pltpu.VMEM((rows, width), BF16),
                pltpu.VMEM((groups, rows, WIDE), F32),
                pltpu.VMEM((rows, 1), F32),
                pltpu.VMEM((rows, 1), F32),
                pltpu.VMEM((rows, rows), F32),
                pltpu.VMEM((rows, rows), F32),
                pltpu.VMEM((groups, rows, HALF), F32),
                pltpu.VMEM((HALF, rows), F32),
                pltpu.VMEM((groups, rows, HALF), F32),
                pltpu.VMEM((HALF, rows), F32),
                pltpu.VMEM((rows, HALF), F32),
                pltpu.VMEM((rows, 2 * STATE), F32),
                pltpu.VMEM((rows, width), F32),
            ],
        ),
        out_shape=out_shape,
        input_output_aliases=aliases,
        compiler_params=pltpu.CompilerParams(vmem_limit_bytes=VMEM),
        cost_estimate=pl.CostEstimate(flops=10**9, bytes_accessed=10**6, transcendentals=0),
        name="backward_slot",
    )(numbers, *args)


def pack_kernel(inner, in_ref, out_ref, packed_ref):
    depth, width = in_ref.shape[0], out_ref.shape[1]
    mid, end = 2 * inner + 2 * STATE, in_ref.shape[1]
    packed_ref[:, :width] = out_ref[...]
    tail = width + inner
    for half in range(2):
        rows = slice(half * depth, (half + 1) * depth)
        packed_ref[rows, width:tail] = in_ref[:, half * inner : (half + 1) * inner]
        packed_ref[rows, tail : tail + STATE] = in_ref[:, mid - 2 * STATE + half * STATE : mid - STATE + half * STATE]
        packed_ref[rows, tail + STATE :] = jnp.zeros((depth, STATE), BF16)
    packed_ref[:depth, tail + STATE : tail + STATE + end - mid] = in_ref[:, mid:]


def pack(in_shard, out_shard, inner):
    depth, width = in_shard.shape[0], out_shard.shape[1]
    return pl.pallas_call(
        functools.partial(pack_kernel, inner),
        out_shape=jax.ShapeDtypeStruct((2 * depth, width + inner + 2 * STATE), BF16),
        name="pack",
    )(in_shard, out_shard)


def order_kernel(at_ref, a_ref, own_ref, other_ref, turn_scr):
    turn_scr[...] = a_ref[0].astype(F32).T.reshape(turn_scr.shape)
    for part in range(2):
        for line in range(own_ref.shape[2]):
            own_ref[part, 0, line] = turn_scr[4 * line + at_ref[1 + 2 * part]].astype(BF16)
            other_ref[part, 0, line] = turn_scr[4 * line + at_ref[2 + 2 * part]].astype(BF16)


def by_owner(numbers, values, micro, count):
    _, rows, total = values.shape
    depth = total // count
    line = count // 4
    out = pl.BlockSpec((2, 1, line, depth, rows), lambda i, n: (0, i, 0, 0, 0))
    made = jax.ShapeDtypeStruct((2, micro, line, depth, rows), BF16)
    own, other = pl.pallas_call(
        order_kernel,
        grid_spec=pltpu.PrefetchScalarGridSpec(
            num_scalar_prefetch=1,
            grid=(micro,),
            in_specs=[pl.BlockSpec((1, rows, total), lambda i, n: (n[0] + i, 0, 0))],
            out_specs=[out, out],
            scratch_shapes=[pltpu.VMEM((count, depth, rows), F32)],
        ),
        out_shape=[made, made],
        compiler_params=pltpu.CompilerParams(vmem_limit_bytes=VMEM),
        cost_estimate=pl.CostEstimate(flops=3 * 10**9, bytes_accessed=2 * 10**6, transcendentals=0),
        name="by_owner",
    )(numbers, values)
    flat = (2, micro, line * depth, rows)
    return own.reshape(flat), other.reshape(flat)


def outer_kernel(own_ref, sib_ref, right_ref, first_ref, later_ref, keep_ref, send_ref):
    micro = own_ref.shape[1]
    for part, out_ref in ((0, keep_ref), (1, send_ref)):
        total = None
        for m in range(micro):
            term = nn_dot(own_ref[part, m], right_ref[m])
            term = term + nn_dot(sib_ref[part, m], first_ref[...] if m == 0 else later_ref[m - 1])
            total = term if total is None else total + term
        out_ref[...] = total.astype(BF16)


def outer_sum(own, sib, right, first, later, start, stop, block):
    _, micro, high, rows = own.shape
    low, steps = start // block, (stop - start) // block
    full = pl.BlockSpec(own.shape, lambda i: (0, 0, 0, 0))
    out = pl.BlockSpec((high, block), lambda i: (0, i))
    made = jax.ShapeDtypeStruct((high, stop - start), BF16)
    return pl.pallas_call(
        outer_kernel,
        grid=(steps,),
        in_specs=[
            full,
            full,
            pl.BlockSpec((micro, rows, block), lambda i: (0, 0, low + i)),
            pl.BlockSpec((rows, block), lambda i: (0, low + i)),
            pl.BlockSpec((micro - 1, rows, block), lambda i: (0, 0, low + i)),
        ],
        out_specs=[out, out],
        out_shape=[made, made],
        compiler_params=pltpu.CompilerParams(vmem_limit_bytes=VMEM),
        cost_estimate=pl.CostEstimate(flops=10**9, bytes_accessed=10**6, transcendentals=0),
        name="outer_sum",
    )(own, sib, right, first, later)


def pick(values, index, axis):
    return lax.dynamic_index_in_dim(values, index, axis, keepdims=False)


def swap(values, axis, bit):
    return lax.ppermute(values, axis, [(a, a ^ bit) for a in range(lax.axis_size(axis))])


def all_rows_of(row, axis):
    count = lax.axis_size(axis)
    place = lax.axis_index(axis)
    table = jnp.where(jnp.arange(count, dtype=jnp.int32)[:, None] == place, row[None], jnp.zeros((), row.dtype))
    bit = 1
    while bit < count:
        table = table + swap(table, axis, bit)
        bit *= 2
    return table


def owned_sums(chunks, axis):
    count = lax.axis_size(axis)
    length = count // 4
    results, token = [], None
    for keep, far, eager in chunks:
        if token is not None:
            far, _ = lax.optimization_barrier((far, token))
        terms = [a.reshape(length, -1, a.shape[1]) for a in (keep, far)]
        bit = 1
        while bit < length:
            mine = (lax.axis_index(axis) // (4 * bit)) % 2
            half = lambda a, which: pick(a.reshape((-1, 2) + a.shape[1:]), which, 1)
            sent = sum(half(a, 1 - mine).astype(F32) for a in terms).astype(BF16)
            came = swap(sent, axis, 4 * bit)
            terms = [half(a, mine) for a in terms] + [came]
            if bit == 1 or not eager:
                token = sent
            bit *= 2
        results.append(sum(a[0].astype(F32) for a in terms))
    return results


def all_sum(values, axis):
    bit = 1
    while bit < lax.axis_size(axis):
        values = values + swap(values, axis, bit)
        bit *= 2
    return values


def body(
    block_input,
    cotangent,
    lengths,
    in_weight,
    out_weight,
    conv_weight,
    conv_bias,
    norm_gain,
    gate_gain,
    dt_bias,
    a_log,
    skip_d,
):
    axis = "fsdp"
    count = lax.axis_size(axis)
    section = lax.axis_index("section")
    micro, rows, width = block_input.shape
    depth, proj_cols = in_weight.shape[1:]
    inner = gate_gain.shape[1] * count
    channels = conv_bias.shape[1] * count
    heads = dt_bias.shape[1]
    small = [a.reshape(-1) for a in (conv_weight[0], conv_bias[0], norm_gain[0], gate_gain[0])]
    sizes = [a.shape[0] for a in small]
    w_all = lax.all_gather(pack(in_weight[0], out_weight[0], inner), axis, axis=0, tiled=True)
    view = w_all.reshape(count, 2, depth, -1)
    if depth % 16:
        view = view.transpose(1, 0, 2, 3).reshape(1, 2, width, -1)
    flat = all_rows_of(jnp.concatenate(small), axis).astype(F32)
    cuts = [0]
    for size in sizes:
        cuts.append(cuts[-1] + size)
    taps = flat[:, cuts[0] : cuts[1]].reshape(count, CONV, -1).transpose(1, 0, 2).reshape(CONV, channels)
    bias = flat[:, cuts[1] : cuts[2]].reshape(1, channels)
    norm = flat[:, cuts[2] : cuts[3]].reshape(1, width)
    gate = flat[:, cuts[3] : cuts[4]].reshape(1, inner)
    skip = jnp.repeat(skip_d[0], HEAD_DIM)[None]
    chan = jnp.concatenate([taps[:, :inner], bias[:, :inner], gate, skip, jnp.zeros((1, inner), F32)], axis=0)
    chan_r = jnp.concatenate([taps[:, inner:], bias[:, inner:], jnp.zeros((3, channels - inner), F32)], axis=0)
    head_rows = jnp.pad(jnp.stack([dt_bias[0], a_log[0]]), ((0, 6), (0, HALF - heads)))
    places = jnp.arange(rows, dtype=jnp.int32)
    live = [(places < lengths[m, 0])[:, None] for m in range(micro)]

    kept = None

    def run_forward(kept, place, m, u):
        return forward_slot(
            place, lengths[m], kept, u, w_all, view, norm, chan, chan_r, head_rows, gate, 2 * micro
        )

    first, second = [], []
    for m in range(micro):
        kept, h = run_forward(kept, m, m, block_input[m])
        first.append(h)
    arrived = [lax.ppermute(h, "section", [(0, 1)]) for h in first]
    for m in range(micro):
        kept, h = run_forward(kept, micro + m, m, arrived[m])
        second.append(h)
    outputs = jnp.stack([jnp.where(section == 0, a, b) for a, b in zip(first, second)])
    arrived, second = lax.optimization_barrier((arrived, second))
    entered = [jnp.where(section == 0, block_input[m], arrived[m]) for m in range(micro)]

    is_last = section == 1
    returning = jnp.zeros((rows, width), BF16)
    grads = None
    gradients, branch = [], [None] * micro
    sums = jnp.zeros((8, inner + 2 * STATE), F32)
    mine = (lax.axis_index(axis) % 4).astype(jnp.int32)
    owners = jnp.stack([section * micro, mine, mine ^ 1, mine ^ 2, mine ^ 3]).astype(jnp.int32)
    for moment in range(micro + 1):
        position = micro - 1 - moment + (1 - section)
        active = (position >= 0) & (position < micro)
        slot = jnp.clip(position, 0, micro - 1)
        own = cotangent[micro - 1 - moment] if moment < micro else jnp.zeros((rows, width), BF16)
        incoming = jnp.where(is_last, own, returning)
        if moment > 0:
            m = micro - moment
            branch[m] = jnp.where(live[m], jnp.where(is_last, cotangent[m], returning), jnp.zeros((), BF16))
        if moment == micro:
            branch_sib = swap(branch[0], axis, 1)
            out_pairs = []
            for a, b in ((0, width - WIDE), (width - WIDE, width)):
                out_pairs.append(outer_sum(out_own, out_sib, jnp.stack(branch), branch_sib, branch_later, a, b, WIDE))
                branch_sib, out_pairs = lax.optimization_barrier((branch_sib, out_pairs))
            incoming, out_pairs = lax.optimization_barrier((incoming, out_pairs))
            out_fars = [swap(send, axis, 2) for _, send in out_pairs]
        numbers = jnp.stack(
            [section * micro + slot, lengths[slot, 0], jnp.where(active, position, micro)]
        ).astype(jnp.int32)
        before, after = min(micro - 1, micro - moment), max(0, micro - 1 - moment)
        u = jnp.where(is_last, entered[after], entered[before])
        du, *grads, sums = backward_slot(
            numbers, kept[2:], grads, sums, incoming, u, w_all, view, norm, chan, chan_r, head_rows, micro + 1
        )
        gradients.append(du)
        if moment < micro:
            returning = lax.ppermute(du, "section", [(1, 0)])
        if moment == micro - 1:
            nb, gb, _ = lax.optimization_barrier((kept[0], kept[1], du))
            out_own, out_other = by_owner(owners, gb, micro, count)
            in_own, in_other = by_owner(owners, nb, micro, count)
            ready = (out_other, in_other, jnp.stack(branch[1:]), grads[0][1:micro], grads[1][1:micro])
            returning, ready, out_own, in_own = lax.optimization_barrier((returning, ready, out_own, in_own))
            out_sib, in_sib, branch_later, z_later, v_later = (swap(a, axis, 1) for a in ready)
    input_grads = jnp.stack(
        [jnp.where(is_last, gradients[micro - 1 - m], gradients[micro - m]) for m in range(micro)]
    )
    firsts, out_fars[0] = lax.optimization_barrier(([a[0] for a in grads], out_fars[0]))
    z_first, v_first = (swap(a, axis, 1) for a in firsts)
    cut, end = 5 * 384, inner + 3 * STATE
    keeps, sends = zip(
        outer_sum(in_own, in_sib, grads[0], z_first, z_later, 0, inner, WIDE),
        outer_sum(in_own, in_sib, grads[1], v_first, v_later, 0, cut, 640),
        outer_sum(in_own, in_sib, grads[1], v_first, v_later, cut, end, 384),
    )
    sums, _ = lax.optimization_barrier((sums, sends[-1]))
    fars = out_fars + [swap(a, axis, 2) for a in sends]
    keeps = [keep for keep, _ in out_pairs] + list(keeps)
    parts = owned_sums(list(zip(keeps, fars, [False, False, True, True, True])), axis)
    out_grad, in_parts = jnp.concatenate(parts[:2], axis=1), parts[2:]
    in_grad = jnp.concatenate(in_parts, axis=1)[:, :proj_cols]

    sums = all_sum(sums, axis)
    place = lax.axis_index(axis)
    cut_out = lambda row, size: lax.dynamic_slice(sums, (row, place * size), (1, size))
    taps_g = lax.dynamic_slice(sums, (0, place * (channels // count)), (CONV, channels // count))
    skip_g = sums[6, :inner].reshape(heads, HEAD_DIM).sum(axis=1)
    return (
        outputs[None],
        input_grads[None],
        in_grad[None],
        out_grad[None],
        taps_g[None],
        cut_out(4, channels // count),
        cut_out(7, width // count),
        cut_out(5, inner // count),
        sums[7:8, width : width + heads],
        sums[7:8, width + HALF : width + HALF + heads],
        skip_g[None],
    )


def solution(mesh):
    in_specs = (
        P(None, "fsdp", None),
        P(None, "fsdp", None),
        P(None, "fsdp"),
        P("section", "fsdp", None),
        P("section", "fsdp", None),
        P("section", None, "fsdp"),
        P("section", "fsdp"),
        P("section", "fsdp"),
        P("section", "fsdp"),
        P("section", None),
        P("section", None),
        P("section", None),
    )
    out_specs = (
        P("section", None, "fsdp", None),
        P("section", None, "fsdp", None),
        P("section", "fsdp", None),
        P("section", "fsdp", None),
        P("section", None, "fsdp"),
        P("section", "fsdp"),
        P("section", "fsdp"),
        P("section", "fsdp"),
        P("section", None),
        P("section", None),
        P("section", None),
    )
    return jax.shard_map(body, mesh=mesh, in_specs=in_specs, out_specs=out_specs, check_vma=False)
```

time: 803 us -> 703 us (0.88)
  Pallas kernels: 184 us -> 256 us
  matrix products: 69.8 us -> 0 us
  waiting for transfers between devices: 371 us -> 304 us
  local copies, waits for them, and re-layouts: 59.6 us -> 31.4 us
  starting transfers between devices: 50.4 us -> 38.6 us
    pallas_call x4 -> x12, Pallas kernels: 81.1 us -> 152 us  [the longest x4 106 us: forward_slot(): pl.pallas_call(forward_kernel, grid_spec=pltpu.PrefetchScalarGridSpec(num...]
    dot_general x13 -> x0, matrix products: 69.8 us -> none  [the longest x9 44.1 us: tn_dot(): lax.dot_general(a, b, (((0,), (0,)), ((), ())), preferred_element_type=F32)]
    ppermute x18 -> x0, waiting for transfers between devices: 69.4 us -> none  [the longest x9 43.5 us: line_sum(): lax.ppermute(send_up, axis, [(a, a + scale) for a in range(count - scale)...]
    ppermute x18 -> x0, starting transfers between devices: 34.1 us -> none  [the longest x9 20.3 us: line_sum(): lax.ppermute(send_up, axis, [(a, a + scale) for a in range(count - scale)...]
    ppermute x2, waiting for transfers between devices: 23.5 us -> 0.01 us  [body(): arrived = [lax.ppermute(h, 'section', [(0, 1)]) for h in first]]
    ppermute x10 -> x31, starting transfers between devices: 8.14 us -> 30.7 us  [swap(): lax.ppermute(values, axis, [(a, a ^ bit) for a in range(lax.axis_size(axi...]
    ppermute x10 -> x31, waiting for transfers between devices: 127 us -> 149 us  [swap(): lax.ppermute(values, axis, [(a, a ^ bit) for a in range(lax.axis_size(axi...]
    dynamic_slice x9 -> x3, local copies, waits for them, and re-layouts: 16.6 us -> 2.56 us  [body(): lax.dynamic_slice(sums, (row, place * size), (1, size))]
  transfers between devices with their start and end apart: 34 -> 36, of which waited for: 17 -> 17; matrix products, arithmetic and copies ran while one was open for 17% -> 9% of each run, Pallas kernels for 5% -> 19%
where the time goes in v2:
time: 703 us; the launch traced here: 690 us
  waiting for transfers between devices  304 us (43%)
  Pallas kernels  256 us (36%)
  other arithmetic  43.6 us (6%)
  starting transfers between devices  38.6 us (5%)
  local copies, waits for them, and re-layouts  31.4 us (4%)
  between operations  15.1 us (2%)
    ppermute x31, waiting for transfers between devices, swap(): lax.ppermute(values, axis, [(a, a ^ bit) for a in range(lax.axis_size(axi...  149 us
    all_gather x1, waiting for transfers between devices, body(): lax.all_gather(pack(in_weight[0], out_weight[0], inner), axis, axis=0, ti...  132 us
    pallas_call x4, Pallas kernels, forward_slot(): pl.pallas_call(forward_kernel, grid_spec=pltpu.PrefetchScalarGridSpec(num...  106 us
    pallas_call x3, Pallas kernels, backward_slot(): pl.pallas_call(backward_kernel, grid_spec=pltpu.PrefetchScalarGridSpec(nu...  104 us
    pallas_call x5, Pallas kernels, outer_sum(): pl.pallas_call(outer_kernel, grid=(steps,), in_specs=[full, full, pl.Bloc...  35.4 us
    ppermute x31, starting transfers between devices, swap(): lax.ppermute(values, axis, [(a, a ^ bit) for a in range(lax.axis_size(axi...  30.7 us
    ppermute x2, waiting for transfers between devices, body(): returning = lax.ppermute(du, 'section', [(1, 0)])  23.4 us
    convert_element_type x10, other arithmetic, owned_sums(): sent = sum((half(a, 1 - mine).astype(F32) for a in terms)).astype(BF16)  16.7 us
  transfers between devices with their start and end apart: 36, of which 17 were waited for; matrix products, arithmetic and copies ran while one was open for 9% of the time, Pallas kernels for 19%

profile of v2, /device:TPU:8, one launch (start us, length us, event | category | flops | bytes accessed | tf_op | source)
XLA Modules:
  0.0 689.6 jit_solution(1234121364579878807)
XLA Ops:
  19.4 4.3 collective-permute-done.2
  32.5 131.6 %all-gather.2.cloned.1.call-done.wo_ref = bf16[3072,4864]{1,0:T(8,128)(2,1)} async-done(((bf16[192,4864]{1,0:T(8,128)(2,1)}), bf16[3072,4864]{1,0:T(8,128)(2,1)}) %all-gather.2.cloned.1.call-update) | async-done | bytes 29884432 | tf_op jit(solution)/shard_map/all_gather | solution.py:686
  164.2 26.4 %forward_slot.4 = (bf16[4,256,1536]{2,1,0:T(8,128)(2,1)}, bf16[4,256,3072]{2,1,0:T(8,128)(2,1)}, f32[4,256,3072]{2,1,0:T(8,128)}, f32[4,256,3072]{2,1,0:T(8,128)...) custom-call(s32[1]{0:T(128)} %bitcast.at_ref, ...), custom_call_target="tpu_custom_call" | custom-call | flops 22000001024 | bytes 60000000 | tf_op jit(solution)/shard_map/forward_slot/pallas_call | solution.py:211
  194.0 26.4 %forward_slot.5 = (bf16[4,256,1536]{2,1,0:T(8,128)(2,1)}, bf16[4,256,3072]{2,1,0:T(8,128)(2,1)}, f32[4,256,3072]{2,1,0:T(8,128)}, f32[4,256,3072]{2,1,0:T(8,128)...) custom-call(s32[1]{0:T(128)} %bitcast.8.at_ref, ...), custom_call_target="tpu_custom_call", output_to_operand_aliasing={{0}: (14, {}), {1}: (15, {}), {2}: (16, {}), {3}: (17, {}),... | custom-call | flops 22000001024 | bytes 60000000 | tf_op jit(solution)/shard_map/forward_slot/pallas_call | solution.py:211
  223.1 26.4 %forward_slot.6 = (bf16[4,256,1536]{2,1,0:T(8,128)(2,1)}, bf16[4,256,3072]{2,1,0:T(8,128)(2,1)}, f32[4,256,3072]{2,1,0:T(8,128)}, f32[4,256,3072]{2,1,0:T(8,128)...) custom-call(s32[1]{0:T(128)} %bitcast.at_ref, ...), custom_call_target="tpu_custom_call", output_to_operand_aliasing={{0}: (14, {}), {1}: (15, {}), {2}: (16, {}), {3}: (17, {}),... | custom-call | flops 22000001024 | bytes 60000000 | tf_op jit(solution)/shard_map/forward_slot/pallas_call | solution.py:211
  250.4 26.7 %forward_slot.7 = (bf16[4,256,1536]{2,1,0:T(8,128)(2,1)}, bf16[4,256,3072]{2,1,0:T(8,128)(2,1)}, f32[4,256,3072]{2,1,0:T(8,128)}, f32[4,256,3072]{2,1,0:T(8,128)...) custom-call(s32[1]{0:T(128)} %bitcast.8.at_ref, ...), custom_call_target="tpu_custom_call", output_to_operand_aliasing={{0}: (14, {}), {1}: (15, {}), {2}: (16, {}), {3}: (17, {}),... | custom-call | flops 22000001024 | bytes 60000000 | tf_op jit(solution)/shard_map/forward_slot/pallas_call | solution.py:211
  279.3 34.9 %backward_slot.3 = (bf16[256,1536]{1,0:T(8,128)(2,1)}, bf16[3,256,3072]{2,1,0:T(8,128)(2,1)}, bf16[3,256,3456]{2,1,0:T(8,128)(2,1)}, f32[8,3328]{1,0:T(8,128)}) custom-call(s32[3]{0:T(128)} %get-tuple-element.217.at_ref, bf16[256,1536]{1,0:T(8,128)(2,1)} %bitcast_select_fusion.1.g_ref, bf16[256,1536]{1,0:T(8,128)(2,1)} %get-tuple-element.201.u_ref, ...), custom_call_target="tpu_custom_call" | custom-call | flops 1000000000 | bytes 1000000 | tf_op jit(solution)/shard_map/backward_slot/pallas_call | solution.py:493
  317.5 18.3 %collective-permute-done.6 = bf16[256,1536]{1,0:T(8,128)(2,1)S(1)} collective-permute-done((bf16[256,1536]{1,0:T(8,128)(2,1)}, bf16[256,1536]{1,0:T(8,128)(2,1)S(1)}, u32[]{:S(2)}, u32[]{:S(2)}) %collective-permute-start.6) | collective-permute-done | bytes 786464 | tf_op jit(solution)/shard_map/ppermute | solution.py:758
  336.9 34.6 %backward_slot.4 = (bf16[256,1536]{1,0:T(8,128)(2,1)}, bf16[3,256,3072]{2,1,0:T(8,128)(2,1)}, bf16[3,256,3456]{2,1,0:T(8,128)(2,1)}, f32[8,3328]{1,0:T(8,128)}) custom-call(s32[3]{0:T(128)} %pad_add_fusion.at_ref, bf16[256,1536]{1,0:T(8,128)(2,1)} %get-tuple-element.203.g_ref, ...), custom_call_target="tpu_custom_call", output_to_operand_aliasing={{1}: (20, {}), {2}: (21, {})} | custom-call | flops 1000000000 | bytes 1000000 | tf_op jit(solution)/shard_map/backward_slot/pallas_call | solution.py:493
  378.9 4.7 by_owner.2
  387.1 5.0 collective-permute-done.7
  402.1 6.9 outer_sum.5
  409.0 5.0 outer_sum.6
  415.1 34.6 %backward_slot.5 = (bf16[256,1536]{1,0:T(8,128)(2,1)}, bf16[3,256,3072]{2,1,0:T(8,128)(2,1)}, bf16[3,256,3456]{2,1,0:T(8,128)(2,1)}, f32[8,3328]{1,0:T(8,128)}) custom-call(s32[3]{0:T(128)} %get-tuple-element.218.at_ref, bf16[256,1536]{1,0:T(8,128)(2,1)} %get-tuple-element.171.g_ref, ...), custom_call_target="tpu_custom_call", output_to_operand_aliasing={{1}: (20, {}), {2}: (21, {})} | custom-call | flops 1000000000 | bytes 1000000 | tf_op jit(solution)/shard_map/backward_slot/pallas_call | solution.py:493
  462.2 9.6 %outer_sum.7 = (bf16[384,3072]{1,0:T(8,128)(2,1)}, bf16[384,3072]{1,0:T(8,128)(2,1)}) custom-call(bf16[2,2,384,256]{3,2,1,0:T(8,128)(2,1)} %bitcast.193, bf16[2,2,384,256]{3,2,1,0:T(8,128)(2,1)} %copy-done, bf16[3,256,3072]{2,1,0:T(8,128)(2,1)} %get-tuple-element.176.right_ref, bf16[256,3072]{1,0:T(8,128)(2,1)} %collective-permute-done.13.first_ref, ...), custom_call_target="tpu_custom_call" | custom-call | flops 1000000000 | bytes 1000000 | tf_op jit(solution)/shard_map/outer_sum/pallas_call | solution.py:595
  474.5 7.0 %collective-permute-done.17 = bf16[2,192,1024]{2,1,0:T(8,128)(2,1)} collective-permute-done((bf16[2,192,1024]{2,1,0:T(8,128)(2,1)}, bf16[2,192,1024]{2,1,0:T(8,128)(2,1)}, u32[]{:S(2)}, u32[]{:S(2)}) %collective-permute-start.17) | collective-permute-done | bytes 786464 | tf_op jit(solution)/shard_map/ppermute | solution.py:618
  491.0 7.3 %outer_sum.8 = (bf16[384,1920]{1,0:T(8,128)(2,1)}, bf16[384,1920]{1,0:T(8,128)(2,1)}) custom-call(bf16[2,2,384,256]{3,2,1,0:T(8,128)(2,1)} %bitcast.194, bf16[2,2,384,256]{3,2,1,0:T(8,128)(2,1)} %copy-done, bf16[3,256,3456]{2,1,0:T(8,128)(2,1)} %get-tuple-element.177.right_ref, bf16[256,3456]{1,0:T(8,128)(2,1)} %copy-done.2, bf16[1,256,3456]{2,1,0:T(8,128)(2,1)} %copy-done.1), custom_call_target="tpu_custom_call" | custom-call | flops 1000000000 | bytes 1000000 | tf_op jit(solution)/shard_map/outer_sum/pallas_call | solution.py:595
  500.6 6.7 outer_sum.9
  512.9 52.9 %collective-permute-done.32 = f32[8,3328]{1,0:T(8,128)S(1)} collective-permute-done((f32[8,3328]{1,0:T(8,128)S(1)}, f32[8,3328]{1,0:T(8,128)S(1)}, u32[]{:S(2)}, u32[]{:S(2)}) %collective-permute-start.32) | collective-permute-done | bytes 106528 | tf_op jit(solution)/shard_map/ppermute | solution.py:618
  582.2 8.3 %collective-permute-done.26 = bf16[384,1536]{1,0:T(8,128)(2,1)S(1)} collective-permute-done((bf16[384,1536]{1,0:T(8,128)(2,1)S(1)}, bf16[384,1536]{1,0:T(8,128)(2,1)S(1)}, u32[]{:S(2)}, u32[]{:S(2)}) %collective-permute-start.26) | collective-permute-done | bytes 1179680 | tf_op jit(solution)/shard_map/ppermute | solution.py:618
  600.8 22.7 %collective-permute-done.27 = bf16[2,96,1536]{2,1,0:T(8,128)(2,1)} collective-permute-done((bf16[2,96,1536]{2,1,0:T(8,128)(2,1)}, bf16[2,96,1536]{2,1,0:T(8,128)(2,1)}, u32[]{:S(2)}, u32[]{:S(2)}) %collective-permute-start.27) | collective-permute-done | bytes 589856 | tf_op jit(solution)/shard_map/ppermute | solution.py:618
  628.4 9.9 %collective-permute-done.24 = bf16[2,96,1920]{2,1,0:T(8,128)(2,1)} collective-permute-done((bf16[2,96,1920]{2,1,0:T(8,128)(2,1)}, bf16[2,96,1920]{2,1,0:T(8,128)(2,1)}, u32[]{:S(2)}, u32[]{:S(2)}) %collective-permute-start.24) | collective-permute-done | bytes 737312 | tf_op jit(solution)/shard_map/ppermute | solution.py:618
  646.3 20.4 %collective-permute-done.25 = bf16[1,96,1920]{2,1,0:T(8,128)(2,1)S(1)} collective-permute-done((bf16[1,96,1920]{2,1,0:T(8,128)(2,1)S(1)}, bf16[1,96,1920]{2,1,0:T(8,128)(2,1)S(1)}, u32[]{:S(2)}, u32[]{:S(2)}) %collective-permute-start.25) | collective-permute-done | bytes 368672 | tf_op jit(solution)/shard_map/ppermute | solution.py:618
  668.0 11.2 %collective-permute-done.20 = bf16[1,96,3072]{2,1,0:T(8,128)(2,1)S(1)} collective-permute-done((bf16[1,96,3072]{2,1,0:T(8,128)(2,1)S(1)}, bf16[1,96,3072]{2,1,0:T(8,128)(2,1)S(1)}, u32[]{:S(2)}, u32[]{:S(2)}) %collective-permute-start.20) | collective-permute-done | bytes 589856 | tf_op jit(solution)/shard_map/ppermute | solution.py:618
  (223 shorter events, 132.7 us)
Async XLA Ops:
  7.2 157.0 %all-gather.2.cloned.1.call-start = ((), (), s32[]{:S(2)}) async-start(), calls=%async_computation | async-start | bytes 31752192 | tf_op jit(solution)/shard_map/all_gather | solution.py:686
  190.6 31.7 %collective-permute-start.4 = (bf16[256,1536]{1,0:T(8,128)(2,1)}, bf16[256,1536]{1,0:T(8,128)(2,1)S(1)}, u32[]{:S(2)}, u32[]{:S(2)}) collective-permute-start(bf16[256,1536]{1,0:T(8,128)(2,1)} %get-tuple-element.105), channel_id=1, source_target_pairs={{0,16},{1,17},{2,18},{3,19},{4,20},{5,21},{6,22},{7,23},{8,24},{9,... | collective-permute-start | bytes 2359304 | tf_op jit(solution)/shard_map/ppermute | solution.py:716
  220.4 29.1 %collective-permute-start.5 = (bf16[256,1536]{1,0:T(8,128)(2,1)}, bf16[256,1536]{1,0:T(8,128)(2,1)S(1)}, u32[]{:S(2)}, u32[]{:S(2)}) collective-permute-start(bf16[256,1536]{1,0:T(8,128)(2,1)} %get-tuple-element.123), channel_id=1, source_target_pairs={{0,16},{1,17},{2,18},{3,19},{4,20},{5,21},{6,22},{7,23},{8,24},{9,... | collective-permute-start | bytes 2359304 | tf_op jit(solution)/shard_map/ppermute | solution.py:716
  314.3 21.5 %collective-permute-start.6 = (bf16[256,1536]{1,0:T(8,128)(2,1)}, bf16[256,1536]{1,0:T(8,128)(2,1)S(1)}, u32[]{:S(2)}, u32[]{:S(2)}) collective-permute-start(bf16[256,1536]{1,0:T(8,128)(2,1)} %get-tuple-element.140), channel_id=1, source_target_pairs={{16,0},{17,1},{18,2},{19,3},{20,4},{21,5},{22,6},{23,7},{24,8},{25... | collective-permute-start | bytes 2359304 | tf_op jit(solution)/shard_map/ppermute | solution.py:758
  371.5 20.7 %collective-permute-start.7 = (bf16[256,1536]{1,0:T(8,128)(2,1)}, bf16[256,1536]{1,0:T(8,128)(2,1)S(1)}, u32[]{:S(2)}, u32[]{:S(2)}) collective-permute-start(bf16[256,1536]{1,0:T(8,128)(2,1)} %get-tuple-element.145), channel_id=1, source_target_pairs={{16,0},{17,1},{18,2},{19,3},{20,4},{21,5},{22,6},{23,7},{24,8},{25... | collective-permute-start | bytes 2359304 | tf_op jit(solution)/shard_map/ppermute | solution.py:758
  394.3 67.3 %collective-permute-start.14 = (bf16[1,256,3072]{2,1,0:T(8,128)(2,1)}, bf16[1,256,3072]{2,1,0:T(8,128)(2,1)}, u32[]{:S(2)}, u32[]{:S(2)}) collective-permute-start(bf16[1,256,3072]{2,1,0:T(8,128)(2,1)} %slice.88), channel_id=1, source_target_pairs={{0,1},{1,0},{2,3},{3,2},{4,5},{5,4},{6,7},{7,6},{8,9},{9,8},{10,11... | collective-permute-start | bytes 4718600 | tf_op jit(solution)/shard_map/ppermute | solution.py:618
  414.0 41.3 %collective-permute-start.12 = (bf16[768,1024]{1,0:T(8,128)(2,1)S(1)}, bf16[768,1024]{1,0:T(8,128)(2,1)}, u32[]{:S(2)}, u32[]{:S(2)}) collective-permute-start(bf16[768,1024]{1,0:T(8,128)(2,1)S(1)} %copy-done.36), channel_id=1, source_target_pairs={{0,2},{1,3},{2,0},{3,1},{4,6},{5,7},{6,4},{7,5},{8,10},{9,11},{10,... | collective-permute-start | bytes 4718600 | tf_op jit(solution)/shard_map/ppermute | solution.py:618
  456.7 31.8 %collective-permute-start.22 = (bf16[1,256,3456]{2,1,0:T(8,128)(2,1)S(1)}, bf16[1,256,3456]{2,1,0:T(8,128)(2,1)S(1)}, u32[]{:S(2)}, u32[]{:S(2)}) collective-permute-start(bf16[1,256,3456]{2,1,0:T(8,128)(2,1)S(1)} %copy-done.14), channel_id=1, source_target_pairs={{0,1},{1,0},{2,3},{3,2},{4,5},{5,4},{6,7},{7,6},{8,9},{9,8},{10,11... | collective-permute-start | bytes 5308424 | tf_op jit(solution)/shard_map/ppermute | solution.py:618
  456.7 31.8 %collective-permute-start.21 = (bf16[256,3456]{1,0:T(8,128)(2,1)}, bf16[256,3456]{1,0:T(8,128)(2,1)S(1)}, u32[]{:S(2)}, u32[]{:S(2)}) collective-permute-start(bf16[256,3456]{1,0:T(8,128)(2,1)} %slice_bitcast_fusion), channel_id=1, source_target_pairs={{0,1},{1,0},{2,3},{3,2},{4,5},{5,4},{6,7},{7,6},{8,9},{9,8},{10,11... | collective-permute-start | bytes 5308424 | tf_op jit(solution)/shard_map/ppermute | solution.py:618
  460.8 24.2 %collective-permute-start.16 = (bf16[768,512]{1,0:T(8,128)(2,1)}, bf16[768,512]{1,0:T(8,128)(2,1)}, u32[]{:S(2)}, u32[]{:S(2)}) collective-permute-start(bf16[768,512]{1,0:T(8,128)(2,1)} %get-tuple-element.184), channel_id=1, source_target_pairs={{0,2},{1,3},{2,0},{3,1},{4,6},{5,7},{6,4},{7,5},{8,10},{9,11},{10,... | collective-permute-start | bytes 2359304 | tf_op jit(solution)/shard_map/ppermute | solution.py:618
  461.7 19.8 %collective-permute-start.17 = (bf16[2,192,1024]{2,1,0:T(8,128)(2,1)}, bf16[2,192,1024]{2,1,0:T(8,128)(2,1)}, u32[]{:S(2)}, u32[]{:S(2)}) collective-permute-start(bf16[2,192,1024]{2,1,0:T(8,128)(2,1)} %fusion.3), channel_id=1, source_target_pairs={{0,4},{1,5},{2,6},{3,7},{4,0},{5,1},{6,2},{7,3},{8,12},{9,13},{10,... | collective-permute-start | bytes 2359304 | tf_op jit(solution)/shard_map/ppermute | solution.py:618
  471.9 104.6 %collective-permute-start.15 = (bf16[384,3072]{1,0:T(8,128)(2,1)}, bf16[384,3072]{1,0:T(8,128)(2,1)}, u32[]{:S(2)}, u32[]{:S(2)}) collective-permute-start(bf16[384,3072]{1,0:T(8,128)(2,1)} %get-tuple-element.182), channel_id=1, source_target_pairs={{0,2},{1,3},{2,0},{3,1},{4,6},{5,7},{6,4},{7,5},{8,10},{9,11},{10,... | collective-permute-start | bytes 7077896 | tf_op jit(solution)/shard_map/ppermute | solution.py:618
  483.7 26.5 %collective-permute-start.29 = (bf16[1,192,1024]{2,1,0:T(8,128)(2,1)}, bf16[1,192,1024]{2,1,0:T(8,128)(2,1)S(1)}, u32[]{:S(2)}, u32[]{:S(2)}) collective-permute-start(bf16[1,192,1024]{2,1,0:T(8,128)(2,1)} %fusion.4), channel_id=1, source_target_pairs={{0,8},{1,9},{2,10},{3,11},{4,12},{5,13},{6,14},{7,15},{8,0},{9,1},... | collective-permute-start | bytes 1179656 | tf_op jit(solution)/shard_map/ppermute | solution.py:618
  486.8 20.6 %collective-permute-start.18 = (bf16[2,192,512]{2,1,0:T(8,128)(2,1)}, bf16[2,192,512]{2,1,0:T(8,128)(2,1)}, u32[]{:S(2)}, u32[]{:S(2)}) collective-permute-start(bf16[2,192,512]{2,1,0:T(8,128)(2,1)} %fusion.12), channel_id=1, source_target_pairs={{0,4},{1,5},{2,6},{3,7},{4,0},{5,1},{6,2},{7,3},{8,12},{9,13},{10,... | collective-permute-start | bytes 1179656 | tf_op jit(solution)/shard_map/ppermute | solution.py:618
  498.2 82.7 %collective-permute-start.23 = (bf16[384,1920]{1,0:T(8,128)(2,1)}, bf16[384,1920]{1,0:T(8,128)(2,1)S(1)}, u32[]{:S(2)}, u32[]{:S(2)}) collective-permute-start(bf16[384,1920]{1,0:T(8,128)(2,1)} %get-tuple-element.192), channel_id=1, source_target_pairs={{0,2},{1,3},{2,0},{3,1},{4,6},{5,7},{6,4},{7,5},{8,10},{9,11},{10,... | collective-permute-start | bytes 4423688 | tf_op jit(solution)/shard_map/ppermute | solution.py:618
  508.7 57.8 %collective-permute-start.30 = (bf16[1,192,512]{2,1,0:T(8,128)(2,1)S(1)}, bf16[1,192,512]{2,1,0:T(8,128)(2,1)S(1)}, u32[]{:S(2)}, u32[]{:S(2)}) collective-permute-start(bf16[1,192,512]{2,1,0:T(8,128)(2,1)S(1)} %fusion.13), channel_id=1, source_target_pairs={{0,8},{1,9},{2,10},{3,11},{4,12},{5,13},{6,14},{7,15},{8,0},{9,1},... | collective-permute-start | bytes 589832 | tf_op jit(solution)/shard_map/ppermute | solution.py:618
  509.3 56.6 %collective-permute-start.32 = (f32[8,3328]{1,0:T(8,128)S(1)}, f32[8,3328]{1,0:T(8,128)S(1)}, u32[]{:S(2)}, u32[]{:S(2)}) collective-permute-start(f32[8,3328]{1,0:T(8,128)S(1)} %add.453), channel_id=1, source_target_pairs={{0,2},{1,3},{2,0},{3,1},{4,6},{5,7},{6,4},{7,5},{8,10},{9,11},{10,... | collective-permute-start | bytes 319496 | tf_op jit(solution)/shard_map/ppermute | solution.py:618
  511.7 78.8 %collective-permute-start.26 = (bf16[384,1536]{1,0:T(8,128)(2,1)S(1)}, bf16[384,1536]{1,0:T(8,128)(2,1)S(1)}, u32[]{:S(2)}, u32[]{:S(2)}) collective-permute-start(bf16[384,1536]{1,0:T(8,128)(2,1)S(1)} %copy-done.37), channel_id=1, source_target_pairs={{0,2},{1,3},{2,0},{3,1},{4,6},{5,7},{6,4},{7,5},{8,10},{9,11},{10,... | collective-permute-start | bytes 3538952 | tf_op jit(solution)/shard_map/ppermute | solution.py:618
  579.4 64.2 %collective-permute-start.19 = (bf16[2,96,3072]{2,1,0:T(8,128)(2,1)}, bf16[2,96,3072]{2,1,0:T(8,128)(2,1)}, u32[]{:S(2)}, u32[]{:S(2)}) collective-permute-start(bf16[2,96,3072]{2,1,0:T(8,128)(2,1)} %fusion.1), channel_id=1, source_target_pairs={{0,4},{1,5},{2,6},{3,7},{4,0},{5,1},{6,2},{7,3},{8,12},{9,13},{10,... | collective-permute-start | bytes 3538952 | tf_op jit(solution)/shard_map/ppermute | solution.py:618
  591.6 31.9 %collective-permute-start.27 = (bf16[2,96,1536]{2,1,0:T(8,128)(2,1)}, bf16[2,96,1536]{2,1,0:T(8,128)(2,1)}, u32[]{:S(2)}, u32[]{:S(2)}) collective-permute-start(bf16[2,96,1536]{2,1,0:T(8,128)(2,1)} %fusion.10), channel_id=1, source_target_pairs={{0,4},{1,5},{2,6},{3,7},{4,0},{5,1},{6,2},{7,3},{8,12},{9,13},{10,... | collective-permute-start | bytes 1769480 | tf_op jit(solution)/shard_map/ppermute | solution.py:618
  592.8 45.6 %collective-permute-start.24 = (bf16[2,96,1920]{2,1,0:T(8,128)(2,1)}, bf16[2,96,1920]{2,1,0:T(8,128)(2,1)}, u32[]{:S(2)}, u32[]{:S(2)}) collective-permute-start(bf16[2,96,1920]{2,1,0:T(8,128)(2,1)} %fusion.8), channel_id=1, source_target_pairs={{0,4},{1,5},{2,6},{3,7},{4,0},{5,1},{6,2},{7,3},{8,12},{9,13},{10,... | collective-permute-start | bytes 2211848 | tf_op jit(solution)/shard_map/ppermute | solution.py:618
  624.6 20.4 %collective-permute-start.28 = (bf16[1,96,1536]{2,1,0:T(8,128)(2,1)S(1)}, bf16[1,96,1536]{2,1,0:T(8,128)(2,1)S(1)}, u32[]{:S(2)}, u32[]{:S(2)}) collective-permute-start(bf16[1,96,1536]{2,1,0:T(8,128)(2,1)S(1)} %fusion.11), channel_id=1, source_target_pairs={{0,8},{1,9},{2,10},{3,11},{4,12},{5,13},{6,14},{7,15},{8,0},{9,1},... | collective-permute-start | bytes 884744 | tf_op jit(solution)/shard_map/ppermute | solution.py:618
  639.7 26.9 %collective-permute-start.25 = (bf16[1,96,1920]{2,1,0:T(8,128)(2,1)S(1)}, bf16[1,96,1920]{2,1,0:T(8,128)(2,1)S(1)}, u32[]{:S(2)}, u32[]{:S(2)}) collective-permute-start(bf16[1,96,1920]{2,1,0:T(8,128)(2,1)S(1)} %fusion.9), channel_id=1, source_target_pairs={{0,8},{1,9},{2,10},{3,11},{4,12},{5,13},{6,14},{7,15},{8,0},{9,1},... | collective-permute-start | bytes 1105928 | tf_op jit(solution)/shard_map/ppermute | solution.py:618
  645.0 34.2 %collective-permute-start.20 = (bf16[1,96,3072]{2,1,0:T(8,128)(2,1)S(1)}, bf16[1,96,3072]{2,1,0:T(8,128)(2,1)S(1)}, u32[]{:S(2)}, u32[]{:S(2)}) collective-permute-start(bf16[1,96,3072]{2,1,0:T(8,128)(2,1)S(1)} %fusion.2), channel_id=1, source_target_pairs={{0,8},{1,9},{2,10},{3,11},{4,12},{5,13},{6,14},{7,15},{8,0},{9,1},... | collective-permute-start | bytes 1769480 | tf_op jit(solution)/shard_map/ppermute | solution.py:618
  (50 other events, 444.4 us)
Sparse Core Ops, SparseCore 0:
  10.2 153.8 all-gather.1

commit v3 on v2

v3 whole, which is shorter than its diff:
```python
import functools

import jax
import jax.numpy as jnp
from jax import lax
from jax.experimental import pallas as pl
from jax.experimental.pallas import tpu as pltpu
from jax.sharding import PartitionSpec as P

HEAD_DIM = 64
STATE = 128
CONV = 4
EPS = 1e-05
LOG2E = 1.4426950408889634
HALF = 128
WIDE = 512
GROUP = WIDE // HEAD_DIM
TINY = 1e-30
NEG = -1e30
VMEM = 60 * 1024 * 1024
F32 = jnp.float32
BF16 = jnp.bfloat16
EXACT = lax.Precision.HIGHEST


def nt_dot(a, b):
    return lax.dot_general(a, b, (((1,), (1,)), ((), ())), preferred_element_type=F32)


def nn_dot(a, b):
    return jnp.dot(a, b, preferred_element_type=F32)


def sigmoid(v):
    return 0.5 * jnp.tanh(0.5 * v) + 0.5


def conv_rows(values, taps, bias):
    rows = lax.broadcasted_iota(jnp.int32, values.shape, 0)
    total = bias + taps[CONV - 1 : CONV, :] * values
    for back in range(1, CONV):
        moved = jnp.where(rows >= back, pltpu.roll(values, back, 0), 0.0)
        total = total + taps[CONV - 1 - back : CONV - back, :] * moved
    return total


def softplus(v):
    return jnp.maximum(v, 0.0) + jnp.log1p(jnp.exp(-jnp.abs(v)))


def step_terms(step_raw, head_ref):
    rows = step_raw.shape[0]
    step = jnp.maximum(softplus(step_raw + head_ref[0:1, :]), TINY)
    rate = -jnp.exp(head_ref[1:2, :])
    at = lax.broadcasted_iota(jnp.int32, (rows, rows), 0)
    of = lax.broadcasted_iota(jnp.int32, (rows, rows), 1)
    lower = (at >= of).astype(F32)
    sums = jnp.dot(lower, step * rate, precision=EXACT, preferred_element_type=F32) * LOG2E
    return step, rate, sums, sums - jnp.log2(step)


def spread(target, values, groups):
    for g in range(groups):
        target[g] = pltpu.roll(values, (HALF - g * GROUP) % HALF, 1) if g else values


def fold(block):
    return block.reshape(-1, block.shape[-1])


def lanes(index):
    return pl.ds(pl.multiple_of(index * WIDE, WIDE), WIDE)


def in_copies(view_ref, wz_scr, wx_scr, wr_scr, sem, base):
    parts, _, depth, _ = view_ref.shape
    width, groups = parts * depth, wz_scr.shape[0]
    tail = width + groups * WIDE

    def of_group(j):
        here = pl.ds(pl.multiple_of(width + j * WIDE, WIDE), WIDE)
        return [
            pltpu.make_async_copy(view_ref.at[:, 0, :, here], wz_scr.at[j], sem.at[base + j]),
            pltpu.make_async_copy(view_ref.at[:, 1, :, here], wx_scr.at[j], sem.at[base + groups + j]),
        ]

    def of_rest():
        return [
            pltpu.make_async_copy(view_ref.at[:, half, :, pl.ds(at, HALF)], wr_scr.at[k], sem.at[base + 2 * groups + k])
            for k, (half, at) in enumerate(((0, tail), (1, tail), (0, tail + HALF)))
        ]

    return of_group, of_rest


def start_all(copies):
    for copy in copies:
        copy.start()


def wait_all(copies):
    for copy in copies:
        copy.wait()


def forward_kernel(place, at_ref, u_hbm, w_hbm, view_hbm, norm_ref, chan_ref, chanr_ref, head_ref, gate_ref, *rest):
    (
        nb_hbm, gb_hbm, z_hbm, v_hbm, y_hbm, vr_hbm, cr_hbm, h_hbm,
        u_scr, wz_scr, wx_scr, wr_scr, wo_scr, nb_scr, gb_scr, z_scr, v_scr, y_scr, vr_scr, cr_scr, h_scr,
        w_scr, sq_scr, s_scr, col_scr, row_scr, sem, out_sem,
    ) = rest[-28:]
    groups, rows, _ = w_scr.shape
    of_group, of_rest = in_copies(view_hbm, wz_scr, wx_scr, wr_scr, sem, 1)
    spare = 2 * groups + 4
    u_copy = pltpu.make_async_copy(u_hbm, u_scr, sem.at[0])

    def of_out(k):
        return pltpu.make_async_copy(w_hbm.at[:, lanes(k)], wo_scr.at[k], sem.at[spare + k])

    def kept_copies(j):
        return [
            pltpu.make_async_copy(scr.at[j], hbm.at[place, :, lanes(j)], out_sem.at[k * groups + j])
            for k, (scr, hbm) in enumerate(((z_scr, z_hbm), (v_scr, v_hbm), (y_scr, y_hbm)))
        ]

    last = 3 * groups
    whole_copies = [
        pltpu.make_async_copy(scr, hbm.at[place], out_sem.at[last + k])
        for k, (scr, hbm) in enumerate(((nb_scr, nb_hbm), (gb_scr, gb_hbm), (vr_scr, vr_hbm), (cr_scr, cr_hbm)))
    ]
    h_copy = pltpu.make_async_copy(h_scr, h_hbm, out_sem.at[last + 4])

    @pl.when(at_ref[1] == 1)
    def _():
        u_copy.start()
        start_all(of_rest())
        for j in range(groups):
            start_all(of_group(j))
        for k in range(wo_scr.shape[0]):
            of_out(k).start()

        u_copy.wait()
        u = u_scr[...].astype(F32)
        scale = lax.rsqrt(jnp.mean(u * u, axis=1, keepdims=True) + EPS)
        nb_scr[...] = (u * scale * norm_ref[...]).astype(BF16)
        nb = nb_scr[...]
        wait_all(of_rest())
        raw = jnp.concatenate([nn_dot(nb, fold(wr_scr[0])), nn_dot(nb, fold(wr_scr[1]))], axis=1)
        steps = nn_dot(nb, fold(wr_scr[2]))
        vr_scr[:, : 2 * STATE] = raw
        vr_scr[:, 2 * STATE :] = steps
        pre = conv_rows(raw, chanr_ref[0:4, :], chanr_ref[4:5, :])
        cr_scr[...] = pre
        act = pre * sigmoid(pre)
        s_scr[...] = lax.dot_general(
            act[:, STATE:], act[:, :STATE], (((1,), (1,)), ((), ())), precision=EXACT, preferred_element_type=F32
        )
        _, _, sums, shifted = step_terms(steps, head_ref)
        spread(col_scr, sums, groups)
        row_scr[...] = shifted.T
        sq_scr[...] = jnp.zeros_like(sq_scr)

        def group(j, carry):
            wait_all(of_group(j))
            nb = nb_scr[...]
            z = nn_dot(nb, fold(wz_scr[j]))
            z_scr[j] = z
            v = nn_dot(nb, fold(wx_scr[j]))
            v_scr[j] = v
            taps = chan_ref[:, lanes(j)]
            c = conv_rows(v, taps[0:4, :], taps[4:5, :])
            x = c * sigmoid(c)
            x_low = x.astype(BF16)
            cols = col_scr[j]
            rws = row_scr[pl.ds(pl.multiple_of(j * GROUP, GROUP), GROUP), :]
            lane = lax.broadcasted_iota(jnp.int32, (HALF, HALF), 1)
            causal = lax.broadcasted_iota(jnp.int32, (HALF, HALF), 0) >= lane
            first = lane < HEAD_DIM
            parts = []
            for pair in range(GROUP // 2):
                here = slice(pair * HALF, (pair + 1) * HALF)
                pieces = []
                for tb in range(rows // HALF):
                    t_here = slice(tb * HALF, (tb + 1) * HALF)
                    both = []
                    for h in (2 * pair, 2 * pair + 1):
                        col = cols[t_here, h : h + 1]
                        mix = []
                        for sb in range(tb + 1):
                            s_here = slice(sb * HALF, (sb + 1) * HALF)
                            gap = col - rws[h : h + 1, s_here]
                            if sb == tb:
                                gap = jnp.where(causal, gap, NEG)
                            mix.append((jnp.exp2(gap) * s_scr[t_here, s_here]).astype(BF16))
                        mix = jnp.concatenate(mix, axis=1) if len(mix) > 1 else mix[0]
                        both.append(nn_dot(mix, x_low[: (tb + 1) * HALF, here]))
                    pieces.append(jnp.where(first, both[0], both[1]))
                parts.append(jnp.concatenate(pieces, axis=0))
            y = jnp.concatenate(parts, axis=1) + taps[6:7, :] * x
            y_scr[j] = y
            w = y * (z * sigmoid(z))
            w_scr[j] = w
            sq_scr[...] += jnp.sum(w * w, axis=1, keepdims=True)
            start_all(kept_copies(j))
            return carry

        lax.fori_loop(0, groups, group, 0)
        scale = lax.rsqrt(sq_scr[...] * (1.0 / (groups * WIDE)) + EPS)
        for g in range(groups):
            here = slice(g * WIDE, (g + 1) * WIDE)
            gb_scr[:, here] = (w_scr[g] * scale * gate_ref[:, here]).astype(BF16)
        start_all(whole_copies)
        live = lax.broadcasted_iota(jnp.int32, (rows, 1), 0) < at_ref[0]
        for k in range(wo_scr.shape[0]):
            here = slice(k * WIDE, (k + 1) * WIDE)
            of_out(k).wait()
            branch = jnp.where(live, nn_dot(gb_scr[...], wo_scr[k]), 0.0)
            h_scr[:, here] = (u_scr[:, here].astype(F32) + branch).astype(BF16)
        h_copy.start()
        for j in range(groups):
            wait_all(kept_copies(j))
        wait_all(whole_copies)
        h_copy.wait()


def forward_slot(place, numbers, kept, u, w_all, view, norm_gain, chan, chan_r, heads, gate_gain, slots):
    rows, width = u.shape
    inner = chan.shape[1]
    groups = inner // WIDE
    parts, _, depth, _ = view.shape
    shapes = [((rows, width), BF16), ((rows, inner), BF16)] + [((rows, inner), F32)] * 3
    shapes += [((rows, 3 * STATE), F32), ((rows, 2 * STATE), F32)]
    far = pl.BlockSpec(memory_space=pl.ANY)
    near = pl.BlockSpec(memory_space=pltpu.VMEM)
    args = [numbers, u, w_all, view, norm_gain, chan, chan_r, heads, gate_gain]
    in_specs = [pl.BlockSpec(memory_space=pltpu.SMEM), far, far, far] + [near] * 5
    aliases = {}
    if kept is not None:
        for k, arr in enumerate(kept):
            aliases[len(args)] = k
            args.append(arr)
            in_specs.append(far)
    out_shape = [jax.ShapeDtypeStruct((slots,) + s, d) for s, d in shapes]
    tall = pltpu.VMEM((groups, parts, depth, WIDE), BF16)
    wide = pltpu.VMEM((groups, rows, WIDE), F32)
    *kept, h = pl.pallas_call(
        functools.partial(forward_kernel, place),
        in_specs=in_specs,
        out_specs=[far] * 8,
        out_shape=out_shape + [jax.ShapeDtypeStruct((rows, width), BF16)],
        scratch_shapes=[
            pltpu.VMEM((rows, width), BF16),
            tall,
            tall,
            pltpu.VMEM((3, parts, depth, HALF), BF16),
            pltpu.VMEM((width // WIDE, inner, WIDE), BF16),
            pltpu.VMEM((rows, width), BF16),
            pltpu.VMEM((rows, inner), BF16),
            wide,
            wide,
            wide,
            pltpu.VMEM((rows, 3 * STATE), F32),
            pltpu.VMEM((rows, 2 * STATE), F32),
            pltpu.VMEM((rows, width), BF16),
            wide,
            pltpu.VMEM((rows, 1), F32),
            pltpu.VMEM((rows, rows), F32),
            pltpu.VMEM((groups, rows, HALF), F32),
            pltpu.VMEM((HALF, rows), F32),
            pltpu.SemaphoreType.DMA((2 * groups + 4 + width // WIDE,)),
            pltpu.SemaphoreType.DMA((3 * groups + 5,)),
        ],
        input_output_aliases=aliases,
        compiler_params=pltpu.CompilerParams(vmem_limit_bytes=VMEM),
        cost_estimate=pl.CostEstimate(flops=22 * 10**9, bytes_accessed=60 * 10**6, transcendentals=0),
        name="forward_slot",
    )(*args)
    return kept, h


def backward_kernel(
    place, at_ref, g_hbm, u_hbm, w_hbm, view_hbm, z_hbm, v_hbm, y_hbm, vr_hbm, cr_hbm,
    norm_ref, chan_ref, chanr_ref, head_ref, past_ref, *rest
):
    (
        du_hbm, dz_hbm, dv_hbm, sum_ref,
        g_scr, u_scr, wo_scr, wz_scr, wx_scr, wr_scr, z_scr, v_scr, y_scr, vr_scr, cr_scr, dz_scr, dv_scr,
        dob_scr, dgb_scr, sq_scr, we_scr, st_scr, ds_scr, bcol_scr, trow_scr, colr_scr, rowr_scr, step_scr, act_scr, dn_scr,
        sem, out_sem,
    ) = rest[-32:]
    groups, rows, _ = dgb_scr.shape
    width = g_scr.shape[1]
    inner = groups * WIDE
    of_group, of_rest = in_copies(view_hbm, wz_scr, wx_scr, wr_scr, sem, 4)
    base = 2 * groups + 7
    g_copy = pltpu.make_async_copy(g_hbm, g_scr, sem.at[0])
    u_copy = pltpu.make_async_copy(u_hbm, u_scr, sem.at[1])
    vr_copy = pltpu.make_async_copy(vr_hbm.at[place], vr_scr, sem.at[2])
    cr_copy = pltpu.make_async_copy(cr_hbm.at[place], cr_scr, sem.at[3])

    def early(j):
        tall = pl.ds(pl.multiple_of(j * WIDE, WIDE), WIDE)
        return [
            pltpu.make_async_copy(w_hbm.at[tall, pl.ds(0, width)], wo_scr.at[j], sem.at[base + j]),
            pltpu.make_async_copy(z_hbm.at[place, :, lanes(j)], z_scr.at[j], sem.at[base + groups + j]),
            pltpu.make_async_copy(y_hbm.at[place, :, lanes(j)], y_scr.at[j], sem.at[base + 2 * groups + j]),
        ]

    def late(j):
        return of_group(j) + [
            pltpu.make_async_copy(v_hbm.at[place, :, lanes(j)], v_scr.at[j], sem.at[base + 3 * groups + j]),
        ]

    def dz_copy(j):
        return pltpu.make_async_copy(dz_scr.at[j], dz_hbm.at[:, lanes(j)], out_sem.at[j])

    dv_copy = pltpu.make_async_copy(dv_scr, dv_hbm, out_sem.at[groups])
    du_copy = pltpu.make_async_copy(dob_scr, du_hbm, out_sem.at[groups + 1])

    @pl.when(at_ref[1] != 1)
    def _():
        sum_ref[...] = past_ref[...]

    @pl.when(at_ref[1] == 1)
    def _():
        start_all([g_copy, vr_copy, cr_copy])
        for j in range(groups):
            start_all(early(j))
        for j in range(groups):
            start_all(late(j))
        start_all(of_rest() + [u_copy])

        sq_scr[...] = jnp.zeros_like(sq_scr)
        we_scr[...] = jnp.zeros_like(we_scr)
        ds_scr[...] = jnp.zeros_like(ds_scr)
        dn_scr[...] = jnp.zeros_like(dn_scr)
        rowr_scr[...] = jnp.zeros_like(rowr_scr)
        g_copy.wait()
        live = lax.broadcasted_iota(jnp.int32, (rows, 1), 0) < at_ref[0]
        dob_scr[...] = jnp.where(live, g_scr[...].astype(F32), 0.0).astype(BF16)
        cr_copy.wait()
        pre = cr_scr[...]
        act = pre * sigmoid(pre)
        act_scr[...] = act
        st_scr[...] = lax.dot_general(
            act[:, :STATE], act[:, STATE:], (((1,), (1,)), ((), ())), precision=EXACT, preferred_element_type=F32
        )
        vr_copy.wait()
        step, rate, sums, shifted = step_terms(vr_scr[:, 2 * STATE : 3 * STATE], head_ref)
        step_scr[...] = step
        spread(bcol_scr, shifted, groups)
        trow_scr[...] = sums.T

        def first_pass(j, carry):
            wait_all(early(j))
            dgb = nt_dot(dob_scr[...], wo_scr[j])
            dgb_scr[j] = dgb
            z = z_scr[j]
            w = y_scr[j] * (z * sigmoid(z))
            sq_scr[...] += jnp.sum(w * w, axis=1, keepdims=True)
            we_scr[...] += jnp.sum(w * (dgb * chan_ref[5:6, lanes(j)]), axis=1, keepdims=True)
            return carry

        lax.fori_loop(0, groups, first_pass, 0)

        def second_pass(j, carry):
            wait_all(late(j))
            wide = lanes(j)
            taps = chan_ref[:, wide]
            q = lax.rsqrt(sq_scr[...] * (1.0 / inner) + EPS)
            pull = q * q * q * (we_scr[...] * (1.0 / inner))
            dgb = dgb_scr[j]
            z = z_scr[j]
            y = y_scr[j]
            sz = sigmoid(z)
            silu_z = z * sz
            w = y * silu_z
            dw = q * (dgb * taps[5:6, :]) - w * pull
            sum_ref[5:6, wide] = past_ref[5:6, wide] + jnp.sum(w * q * dgb, axis=0, keepdims=True)
            dy = dw * silu_z
            dz = (dw * y * (sz * (1.0 + z * (1.0 - sz)))).astype(BF16)
            dz_scr[j] = dz
            dz_copy(j).start()
            dn = nt_dot(dz, fold(wz_scr[j]))

            c = conv_rows(v_scr[j], taps[0:4, :], taps[4:5, :])
            sc = sigmoid(c)
            x = c * sc
            x_low = x.astype(BF16)
            dy_low = dy.astype(BF16)
            sum_ref[6:7, wide] = past_ref[6:7, wide] + jnp.sum(dy * x, axis=0, keepdims=True)
            cols = bcol_scr[j]
            head_rows = pl.ds(pl.multiple_of(j * GROUP, GROUP), GROUP)
            rws = trow_scr[head_rows, :]
            lane = lax.broadcasted_iota(jnp.int32, (HALF, HALF), 1)
            causal = lane >= lax.broadcasted_iota(jnp.int32, (HALF, HALF), 0)
            first = lane < HEAD_DIM
            lane_row = lax.broadcasted_iota(jnp.int32, (1, HALF), 1)
            sub = lax.broadcasted_iota(jnp.int32, (GROUP, HALF), 0)
            blocks = rows // HALF
            col_sums = [jnp.zeros((HALF, HALF), F32) for _ in range(blocks)]
            row_sums = [jnp.zeros((GROUP, HALF), F32) for _ in range(blocks)]
            parts = []
            for pair in range(GROUP // 2):
                here = slice(pair * HALF, (pair + 1) * HALF)
                pieces = []
                row_part = [[None] * blocks, [None] * blocks]
                for sb in range(blocks):
                    s_here = slice(sb * HALF, (sb + 1) * HALF)
                    x_here = x_low[s_here, here]
                    split = (
                        jnp.where(first, x_here, jnp.zeros_like(x_here)),
                        jnp.where(first, jnp.zeros_like(x_here), x_here),
                    )
                    mixes = [[], []]
                    lane_sum = [None, None]
                    for tb in range(sb, blocks):
                        t_here = slice(tb * HALF, (tb + 1) * HALF)
                        dy_here = dy_low[t_here, here]
                        contact = st_scr[s_here, t_here]
                        touched = None
                        for k in range(2):
                            h = 2 * pair + k
                            gap = rws[h : h + 1, t_here] - cols[s_here, h : h + 1]
                            if sb == tb:
                                gap = jnp.where(causal, gap, NEG)
                            decay = jnp.exp2(gap)
                            mix = decay * contact
                            meet = nt_dot(split[k], dy_here)
                            through = decay * meet
                            pairs = through * contact
                            touched = through if touched is None else touched + through
                            mixes[k].append(mix.astype(BF16))
                            lane_sum[k] = pairs if lane_sum[k] is None else lane_sum[k] + pairs
                            down = jnp.sum(pairs, axis=0, keepdims=True)
                            row_part[k][tb] = down if row_part[k][tb] is None else row_part[k][tb] + down
                        ds_scr[s_here, t_here] += touched
                    out = []
                    for k in range(2):
                        h = 2 * pair + k
                        mix = jnp.concatenate(mixes[k], axis=1) if len(mixes[k]) > 1 else mixes[k][0]
                        out.append(nn_dot(mix, dy_low[sb * HALF :, here]))
                        total = jnp.sum(lane_sum[k], axis=1, keepdims=True)
                        col_sums[sb] = jnp.where(lane_row == h, total, col_sums[sb])
                    pieces.append(jnp.where(first, out[0], out[1]))
                for k in range(2):
                    for tb in range(blocks):
                        row_sums[tb] = jnp.where(sub == 2 * pair + k, row_part[k][tb], row_sums[tb])
                parts.append(jnp.concatenate(pieces, axis=0))
            colr_scr[j] = jnp.concatenate(col_sums, axis=0)
            rowr_scr[head_rows, :] = jnp.concatenate(row_sums, axis=1)
            dx = jnp.concatenate(parts, axis=1) + taps[6:7, :] * dy
            dc = dx * (sc * (1.0 + c * (1.0 - sc)))
            dv = conv_back(dc, v_scr[j], taps, past_ref, sum_ref, wide).astype(BF16)
            dv_scr[:, wide] = dv
            dn_scr[...] += dn + nt_dot(dv, fold(wx_scr[j]))
            return carry

        lax.fori_loop(0, groups, second_pass, 0)
        act = act_scr[...]
        ds = ds_scr[...].astype(BF16)
        act_low = act.astype(BF16)
        d_b = nn_dot(ds, act_low[:, STATE:])
        d_c = lax.dot_general(ds, act_low[:, :STATE], (((0,), (0,)), ((), ())), preferred_element_type=F32)
        pre = cr_scr[...]
        sp = sigmoid(pre)
        d_pre = jnp.concatenate([d_b, d_c], axis=1) * (sp * (1.0 + pre * (1.0 - sp)))
        narrow = slice(inner, inner + 2 * STATE)
        d_raw = conv_back(d_pre, vr_scr[:, : 2 * STATE], chanr_ref[...], past_ref, sum_ref, narrow)
        sum_ref[5:7, narrow] = jnp.zeros((2, 2 * STATE), F32)
        col_total = colr_scr[0]
        for g in range(1, groups):
            col_total = col_total + pltpu.roll(colr_scr[g], g * GROUP, 1)
        d_sums = rowr_scr[...].T - col_total
        at_row = lax.broadcasted_iota(jnp.int32, (rows, rows), 0)
        of_row = lax.broadcasted_iota(jnp.int32, (rows, rows), 1)
        upper = (of_row >= at_row).astype(F32)
        d_log = jnp.dot(upper, d_sums, precision=EXACT, preferred_element_type=F32)
        step = step_scr[...]
        rate = -jnp.exp(head_ref[1:2, :])
        d_step = col_total / step + rate * d_log
        raw_step = vr_scr[:, 2 * STATE : 3 * STATE] + head_ref[0:1, :]
        used = lax.broadcasted_iota(jnp.int32, (rows, HALF), 1) < inner // HEAD_DIM
        d_raw_step = jnp.where(used, d_step * jax.nn.sigmoid(raw_step), 0.0)
        last = past_ref[7:8, :]
        sum_ref[7:8, width : width + HALF] = last[:, width : width + HALF] + jnp.sum(d_raw_step, axis=0, keepdims=True)
        sum_ref[7:8, width + HALF : width + 2 * HALF] = last[:, width + HALF : width + 2 * HALF] + jnp.sum(
            jnp.where(used, d_log * step * rate, 0.0), axis=0, keepdims=True
        )
        sum_ref[7:8, width + 2 * HALF :] = jnp.zeros((1, inner - width), F32)
        dr = jnp.concatenate([d_raw, d_raw_step], axis=1).astype(BF16)
        dv_scr[:, inner:] = dr
        dv_copy.start()
        wait_all(of_rest())
        dn = dn_scr[...]
        for k in range(3):
            dn = dn + nt_dot(dr[:, k * STATE : (k + 1) * STATE], fold(wr_scr[k]))
        u_copy.wait()
        u = u_scr[...].astype(F32)
        p = lax.rsqrt(jnp.mean(u * u, axis=1, keepdims=True) + EPS)
        e = dn * norm_ref[...]
        du = g_scr[...].astype(F32) + p * e - u * (p * p * p * jnp.mean(u * e, axis=1, keepdims=True))
        dob_scr[...] = du.astype(BF16)
        du_copy.start()
        sum_ref[7:8, :width] = last[:, :width] + jnp.sum(u * p * dn, axis=0, keepdims=True)
        for j in range(groups):
            dz_copy(j).wait()
        dv_copy.wait()
        du_copy.wait()


def conv_back(dc, values, taps, past_ref, sum_ref, here):
    rows = lax.broadcasted_iota(jnp.int32, dc.shape, 0)
    count = dc.shape[0]
    sum_ref[4:5, here] = past_ref[4:5, here] + jnp.sum(dc, axis=0, keepdims=True)
    total = 0.0
    for ahead in range(CONV):
        moved = jnp.where(rows < count - ahead, pltpu.roll(dc, count - ahead, 0), 0.0) if ahead else dc
        tap = CONV - 1 - ahead
        sum_ref[tap : tap + 1, here] = past_ref[tap : tap + 1, here] + jnp.sum(moved * values, axis=0, keepdims=True)
        total = total + taps[tap : tap + 1, :] * moved
    return total


def backward_slot(place, numbers, kept, grads, past, g, u, w_all, view, norm_gain, chan, chan_r, heads):
    rows, width = g.shape
    inner = chan.shape[1]
    groups = inner // WIDE
    parts, _, depth, _ = view.shape
    far = pl.BlockSpec(memory_space=pl.ANY)
    near = pl.BlockSpec(memory_space=pltpu.VMEM)
    args = [numbers, g, u, w_all, view, *kept, norm_gain, chan, chan_r, heads, past]
    in_specs = [pl.BlockSpec(memory_space=pltpu.SMEM)] + [far] * 9 + [near] * 5
    aliases = {}
    if grads is not None:
        for k, arr in enumerate(grads):
            aliases[len(args)] = k + 1
            args.append(arr)
            in_specs.append(far)
    tall = pltpu.VMEM((groups, parts, depth, WIDE), BF16)
    wide = pltpu.VMEM((groups, rows, WIDE), F32)
    slot = pltpu.VMEM((rows, width), BF16)
    return pl.pallas_call(
        functools.partial(backward_kernel, place),
        in_specs=in_specs,
        out_specs=[far, far, far, near],
        out_shape=[
            jax.ShapeDtypeStruct((rows, width), BF16),
            jax.ShapeDtypeStruct((rows, inner), BF16),
            jax.ShapeDtypeStruct((rows, inner + 3 * STATE), BF16),
            jax.ShapeDtypeStruct((8, inner + 2 * STATE), F32),
        ],
        scratch_shapes=[
            slot,
            slot,
            pltpu.VMEM((groups, WIDE, width), BF16),
            tall,
            tall,
            pltpu.VMEM((3, parts, depth, HALF), BF16),
            wide,
            wide,
            wide,
            pltpu.VMEM((rows, 3 * STATE), F32),
            pltpu.VMEM((rows, 2 * STATE), F32),
            pltpu.VMEM((groups, rows, WIDE), BF16),
            pltpu.VMEM((rows, inner + 3 * STATE), BF16),
            slot,
            wide,
            pltpu.VMEM((rows, 1), F32),
            pltpu.VMEM((rows, 1), F32),
            pltpu.VMEM((rows, rows), F32),
            pltpu.VMEM((rows, rows), F32),
            pltpu.VMEM((groups, rows, HALF), F32),
            pltpu.VMEM((HALF, rows), F32),
            pltpu.VMEM((groups, rows, HALF), F32),
            pltpu.VMEM((HALF, rows), F32),
            pltpu.VMEM((rows, HALF), F32),
            pltpu.VMEM((rows, 2 * STATE), F32),
            pltpu.VMEM((rows, width), F32),
            pltpu.SemaphoreType.DMA((6 * groups + 7,)),
            pltpu.SemaphoreType.DMA((groups + 2,)),
        ],
        input_output_aliases=aliases,
        compiler_params=pltpu.CompilerParams(vmem_limit_bytes=VMEM),
        cost_estimate=pl.CostEstimate(flops=10**9, bytes_accessed=10**6, transcendentals=0),
        name="backward_slot",
    )(*args)


def pack_kernel(inner, in_ref, out_ref, packed_ref):
    depth, width = in_ref.shape[0], out_ref.shape[1]
    mid, end = 2 * inner + 2 * STATE, in_ref.shape[1]
    packed_ref[:, :width] = out_ref[...]
    tail = width + inner
    for half in range(2):
        rows = slice(half * depth, (half + 1) * depth)
        packed_ref[rows, width:tail] = in_ref[:, half * inner : (half + 1) * inner]
        packed_ref[rows, tail : tail + STATE] = in_ref[:, mid - 2 * STATE + half * STATE : mid - STATE + half * STATE]
        packed_ref[rows, tail + STATE :] = jnp.zeros((depth, STATE), BF16)
    packed_ref[:depth, tail + STATE : tail + STATE + end - mid] = in_ref[:, mid:]


def pack(in_shard, out_shard, inner):
    depth, width = in_shard.shape[0], out_shard.shape[1]
    return pl.pallas_call(
        functools.partial(pack_kernel, inner),
        out_shape=jax.ShapeDtypeStruct((2 * depth, width + inner + 2 * STATE), BF16),
        name="pack",
    )(in_shard, out_shard)


def order_kernel(at_ref, a_ref, own_ref, other_ref, turn_scr):
    turn_scr[...] = a_ref[0].astype(F32).T.reshape(turn_scr.shape)
    for part in range(2):
        for line in range(own_ref.shape[2]):
            own_ref[part, 0, line] = turn_scr[4 * line + at_ref[1 + 2 * part]].astype(BF16)
            other_ref[part, 0, line] = turn_scr[4 * line + at_ref[2 + 2 * part]].astype(BF16)


def by_owner(numbers, values, micro, count):
    _, rows, total = values.shape
    depth = total // count
    line = count // 4
    out = pl.BlockSpec((2, 1, line, depth, rows), lambda i, n: (0, i, 0, 0, 0))
    made = jax.ShapeDtypeStruct((2, micro, line, depth, rows), BF16)
    own, other = pl.pallas_call(
        order_kernel,
        grid_spec=pltpu.PrefetchScalarGridSpec(
            num_scalar_prefetch=1,
            grid=(micro,),
            in_specs=[pl.BlockSpec((1, rows, total), lambda i, n: (n[0] + i, 0, 0))],
            out_specs=[out, out],
            scratch_shapes=[pltpu.VMEM((count, depth, rows), F32)],
        ),
        out_shape=[made, made],
        compiler_params=pltpu.CompilerParams(vmem_limit_bytes=VMEM),
        cost_estimate=pl.CostEstimate(flops=3 * 10**9, bytes_accessed=2 * 10**6, transcendentals=0),
        name="by_owner",
    )(numbers, values)
    flat = (2, micro, line * depth, rows)
    return own.reshape(flat), other.reshape(flat)


def outer_kernel(own_ref, sib_ref, *rest):
    rights, outs = rest[:-2], rest[-2:]
    micro = own_ref.shape[1]
    right = jnp.concatenate([ref[...] for ref in rights], axis=0)
    for part, out_ref in enumerate(outs):
        left = jnp.concatenate([ref[part, m] for ref in (own_ref, sib_ref) for m in range(micro)], axis=1)
        out_ref[...] = nn_dot(left, right).astype(BF16)


def outer_sum(own, sib, rights, start, stop, block):
    _, micro, high, rows = own.shape
    low, steps = start // block, (stop - start) // block
    full = pl.BlockSpec(own.shape, lambda i: (0, 0, 0, 0))
    out = pl.BlockSpec((high, block), lambda i: (0, i))
    made = jax.ShapeDtypeStruct((high, stop - start), BF16)
    return pl.pallas_call(
        outer_kernel,
        grid=(steps,),
        in_specs=[full, full] + [pl.BlockSpec((rows, block), lambda i: (0, low + i)) for _ in rights],
        out_specs=[out, out],
        out_shape=[made, made],
        compiler_params=pltpu.CompilerParams(vmem_limit_bytes=VMEM),
        cost_estimate=pl.CostEstimate(flops=10**9, bytes_accessed=10**6, transcendentals=0),
        name="outer_sum",
    )(own, sib, *rights)


def pick(values, index, axis):
    return lax.dynamic_index_in_dim(values, index, axis, keepdims=False)


def swap(values, axis, bit):
    return lax.ppermute(values, axis, [(a, a ^ bit) for a in range(lax.axis_size(axis))])


def all_rows_of(row, axis):
    count = lax.axis_size(axis)
    place = lax.axis_index(axis)
    table = jnp.where(jnp.arange(count, dtype=jnp.int32)[:, None] == place, row[None], jnp.zeros((), row.dtype))
    bit = 1
    while bit < count:
        table = table + swap(table, axis, bit)
        bit *= 2
    return table


def owned_sums(chunks, axis, rider):
    count = lax.axis_size(axis)
    length = count // 4
    results, token = [], None
    rider_far = swap(rider, axis, 2)
    for k, (keep, far) in enumerate(chunks):
        rides = k == len(chunks) - 1
        if token is not None:
            far, _ = lax.optimization_barrier((far, token))
        if rides:
            far, rider_far = lax.optimization_barrier((far, rider_far))
            rider = rider + rider_far
        terms = [a.reshape(length, -1, a.shape[1]) for a in (keep, far)]
        bit = 1
        while bit < length:
            mine = (lax.axis_index(axis) // (4 * bit)) % 2
            half = lambda a, which: pick(a.reshape((-1, 2) + a.shape[1:]), which, 1)
            sent = sum(half(a, 1 - mine).astype(F32) for a in terms).astype(BF16)
            if rides:
                sent, rider = lax.optimization_barrier((sent, rider))
            came = swap(sent, axis, 4 * bit)
            if rides:
                rider = rider + swap(rider, axis, 4 * bit)
            terms = [half(a, mine) for a in terms] + [came]
            token = came if k == 0 else sent
            bit *= 2
        results.append(sum(a[0].astype(F32) for a in terms))
    return results, rider


def body(
    block_input,
    cotangent,
    lengths,
    in_weight,
    out_weight,
    conv_weight,
    conv_bias,
    norm_gain,
    gate_gain,
    dt_bias,
    a_log,
    skip_d,
):
    axis = "fsdp"
    count = lax.axis_size(axis)
    section = lax.axis_index("section")
    micro, rows, width = block_input.shape
    depth, proj_cols = in_weight.shape[1:]
    inner = gate_gain.shape[1] * count
    channels = conv_bias.shape[1] * count
    heads = dt_bias.shape[1]
    small = [a.reshape(-1) for a in (conv_weight[0], conv_bias[0], norm_gain[0], gate_gain[0])]
    sizes = [a.shape[0] for a in small]
    w_all = lax.all_gather(pack(in_weight[0], out_weight[0], inner), axis, axis=0, tiled=True)
    view = w_all.reshape(count, 2, depth, -1)
    if depth % 16:
        view = view.transpose(1, 0, 2, 3).reshape(1, 2, width, -1)
    flat = all_rows_of(jnp.concatenate(small), axis).astype(F32)
    cuts = [0]
    for size in sizes:
        cuts.append(cuts[-1] + size)
    taps = flat[:, cuts[0] : cuts[1]].reshape(count, CONV, -1).transpose(1, 0, 2).reshape(CONV, channels)
    bias = flat[:, cuts[1] : cuts[2]].reshape(1, channels)
    norm = flat[:, cuts[2] : cuts[3]].reshape(1, width)
    gate = flat[:, cuts[3] : cuts[4]].reshape(1, inner)
    skip = jnp.repeat(skip_d[0], HEAD_DIM)[None]
    chan = jnp.concatenate([taps[:, :inner], bias[:, :inner], gate, skip, jnp.zeros((1, inner), F32)], axis=0)
    chan_r = jnp.concatenate([taps[:, inner:], bias[:, inner:], jnp.zeros((3, channels - inner), F32)], axis=0)
    head_rows = jnp.pad(jnp.stack([dt_bias[0], a_log[0]]), ((0, 6), (0, HALF - heads)))
    places = jnp.arange(rows, dtype=jnp.int32)
    live = [(places < lengths[m, 0])[:, None] for m in range(micro)]

    def numbers(m, stage):
        return jnp.stack([lengths[m, 0], (section == stage).astype(jnp.int32)])

    kept = None
    first, second = [], []
    for m in range(micro):
        kept, h = forward_slot(
            m, numbers(m, 0), kept, block_input[m], w_all, view, norm, chan, chan_r, head_rows, gate, 2 * micro
        )
        first.append(h)
    arrived = [lax.ppermute(h, "section", [(0, 1)]) for h in first]
    for m in range(micro):
        kept, h = forward_slot(
            micro + m, numbers(m, 1), kept, arrived[m], w_all, view, norm, chan, chan_r, head_rows, gate, 2 * micro
        )
        second.append(h)
    outputs = jnp.stack([jnp.where(section == 0, a, b) for a, b in zip(first, second)])

    def run_backward(place, m, stage, grads, sums, g, u):
        return backward_slot(
            place, numbers(m, stage), kept[2:], grads, sums, g, u, w_all, view, norm, chan, chan_r, head_rows
        )

    is_last = section == 1
    sums = jnp.zeros((8, inner + 2 * STATE), F32)
    grads, late_grads, early_grads, returned = [None] * micro, [None] * micro, [None] * micro, [None] * micro
    for m in reversed(range(micro)):
        late_grads[m], *grads[m], sums = run_backward(micro + m, m, 1, None, sums, cotangent[m], arrived[m])
        returned[m] = lax.ppermute(late_grads[m], "section", [(1, 0)])

    mine = (lax.axis_index(axis) % 4).astype(jnp.int32)
    owners = jnp.stack([section * micro, mine, mine ^ 1, mine ^ 2, mine ^ 3]).astype(jnp.int32)
    nb, gb, _ = lax.optimization_barrier((kept[0], kept[1], late_grads[0]))
    out_own, out_other = by_owner(owners, gb, micro, count)
    in_own, in_other = by_owner(owners, nb, micro, count)
    out_sib, in_sib = swap(out_other, axis, 1), swap(in_other, axis, 1)
    returned[-1], out_own, in_own = lax.optimization_barrier((returned[-1], out_own, in_own))

    branch, branch_sib, z_sib, v_sib = [None] * micro, [None] * micro, [None] * micro, [None] * micro

    def take_branch(m):
        branch[m] = jnp.where(live[m], jnp.where(is_last, cotangent[m], returned[m]), jnp.zeros((), BF16))
        branch_sib[m] = swap(branch[m], axis, 1)

    for m in reversed(range(1, micro)):
        take_branch(m)
        early_grads[m], *grads[m], sums = run_backward(m, m, 0, grads[m], sums, returned[m], block_input[m])
        z_sib[m], v_sib[m] = (swap(a, axis, 1) for a in grads[m])
    returned[0], early_grads[-1] = lax.optimization_barrier((returned[0], early_grads[-1]))
    take_branch(0)
    out_keep, out_send = outer_sum(out_own, out_sib, branch + branch_sib, 0, width, WIDE)
    returned[0], out_send = lax.optimization_barrier((returned[0], out_send))
    out_far = swap(out_send, axis, 2)
    early_grads[0], *grads[0], sums = run_backward(0, 0, 0, grads[0], sums, returned[0], block_input[0])
    z_sib[0], v_sib[0] = (swap(a, axis, 1) for a in grads[0])
    input_grads = jnp.stack([jnp.where(is_last, a, b) for a, b in zip(late_grads, early_grads)])

    z_rows = [a for a, _ in grads] + z_sib
    v_rows = [a for _, a in grads] + v_sib
    cut, end = 5 * 384, inner + 3 * STATE
    pairs = [
        outer_sum(in_own, in_sib, z_rows, 0, inner, 2 * WIDE),
        outer_sum(in_own, in_sib, v_rows, 0, cut, 640),
        outer_sum(in_own, in_sib, v_rows, cut, end, 384),
    ]
    pairs[0], out_far = lax.optimization_barrier((pairs[0], out_far))
    sums, _ = lax.optimization_barrier((sums, pairs[-1][1]))
    sums = sums + swap(sums, axis, 1)
    chunks = [(out_keep, out_far)] + [(keep, swap(send, axis, 2)) for keep, send in pairs]
    parts, sums = owned_sums(chunks, axis, sums)
    out_grad, in_grad = parts[0], jnp.concatenate(parts[1:], axis=1)[:, :proj_cols]

    place = lax.axis_index(axis)
    cut_out = lambda row, size: lax.dynamic_slice(sums, (row, place * size), (1, size))
    taps_g = lax.dynamic_slice(sums, (0, place * (channels // count)), (CONV, channels // count))
    skip_g = sums[6, :inner].reshape(heads, HEAD_DIM).sum(axis=1)
    return (
        outputs[None],
        input_grads[None],
        in_grad[None],
        out_grad[None],
        taps_g[None],
        cut_out(4, channels // count),
        cut_out(7, width // count),
        cut_out(5, inner // count),
        sums[7:8, width : width + heads],
        sums[7:8, width + HALF : width + HALF + heads],
        skip_g[None],
    )


def solution(mesh):
    in_specs = (
        P(None, "fsdp", None),
        P(None, "fsdp", None),
        P(None, "fsdp"),
        P("section", "fsdp", None),
        P("section", "fsdp", None),
        P("section", None, "fsdp"),
        P("section", "fsdp"),
        P("section", "fsdp"),
        P("section", "fsdp"),
        P("section", None),
        P("section", None),
        P("section", None),
    )
    out_specs = (
        P("section", None, "fsdp", None),
        P("section", None, "fsdp", None),
        P("section", "fsdp", None),
        P("section", "fsdp", None),
        P("section", None, "fsdp"),
        P("section", "fsdp"),
        P("section", "fsdp"),
        P("section", "fsdp"),
        P("section", None),
        P("section", None),
        P("section", None),
    )
    return jax.shard_map(body, mesh=mesh, in_specs=in_specs, out_specs=out_specs, check_vma=False)
```

time: 703 us -> 595 us (0.85)
  Pallas kernels: 256 us -> 153 us
  waiting for transfers between devices: 304 us -> 330 us
  local copies, waits for them, and re-layouts: 31.4 us -> 16.6 us
  other arithmetic: 43.6 us -> 34.8 us
    pallas_call x12, Pallas kernels: 245 us -> 142 us  [the longest x4 68.1 us: backward_slot(): pl.pallas_call(functools.partial(backward_kernel, place), in_specs=in_spe...]
    ppermute x2, waiting for transfers between devices: 23.4 us -> 53.6 us  [body(): returned[m] = lax.ppermute(late_grads[m], 'section', [(1, 0)])]
    ppermute x31 -> x28, waiting for transfers between devices: 149 us -> 131 us  [swap(): lax.ppermute(values, axis, [(a, a ^ bit) for a in range(lax.axis_size(axi...]
    ppermute x2, waiting for transfers between devices: 0.01 us -> 15.6 us  [body(): arrived = [lax.ppermute(h, 'section', [(0, 1)]) for h in first]]
    convert_element_type x10 -> x8, other arithmetic: 16.7 us -> 11.8 us  [owned_sums(): sent = sum((half(a, 1 - mine).astype(F32) for a in terms)).astype(BF16)]
    ppermute x31 -> x28, starting transfers between devices: 30.7 us -> 29.5 us  [swap(): lax.ppermute(values, axis, [(a, a ^ bit) for a in range(lax.axis_size(axi...]
  transfers between devices with their start and end apart: 36 -> 33, of which waited for: 17 -> 21; matrix products, arithmetic and copies ran while one was open for 9% -> 7% of each run, Pallas kernels for 19% -> 20%
where the time goes in v3:
time: 595 us; the launch traced here: 584 us
  waiting for transfers between devices  330 us (55%)
  Pallas kernels  153 us (26%)
  starting transfers between devices  34.8 us (6%)
  other arithmetic  34.8 us (6%)
  local copies, waits for them, and re-layouts  16.6 us (3%)
  between operations  15.1 us (3%)
    ppermute x28, waiting for transfers between devices, swap(): lax.ppermute(values, axis, [(a, a ^ bit) for a in range(lax.axis_size(axi...  131 us
    all_gather x1, waiting for transfers between devices, body(): lax.all_gather(pack(in_weight[0], out_weight[0], inner), axis, axis=0, ti...  130 us
    pallas_call x4, Pallas kernels, backward_slot(): pl.pallas_call(functools.partial(backward_kernel, place), in_specs=in_spe...  68.1 us
    ppermute x2, waiting for transfers between devices, body(): returned[m] = lax.ppermute(late_grads[m], 'section', [(1, 0)])  53.6 us
    pallas_call x4, Pallas kernels, forward_slot(): pl.pallas_call(functools.partial(forward_kernel, place), in_specs=in_spec...  42.7 us
    pallas_call x4, Pallas kernels, outer_sum(): pl.pallas_call(outer_kernel, grid=(steps,), in_specs=[full, full] + [pl.B...  31.3 us
    ppermute x28, starting transfers between devices, swap(): lax.ppermute(values, axis, [(a, a ^ bit) for a in range(lax.axis_size(axi...  29.5 us
    ppermute x2, waiting for transfers between devices, body(): arrived = [lax.ppermute(h, 'section', [(0, 1)]) for h in first]  15.6 us
  transfers between devices with their start and end apart: 33, of which 21 were waited for; matrix products, arithmetic and copies ran while one was open for 7% of the time, Pallas kernels for 20%

profile of v3, /device:TPU:8, one launch (start us, length us, event | category | flops | bytes accessed | tf_op | source)
XLA Modules:
  0.0 584.4 jit_solution(5688962561207058716)
XLA Ops:
  33.7 130.4 %all-gather.2.cloned.1.call-done.w_hbm = bf16[3072,4864]{1,0:T(8,128)(2,1)} async-done(((bf16[192,4864]{1,0:T(8,128)(2,1)}), bf16[3072,4864]{1,0:T(8,128)(2,1)}) %all-gather.2.cloned.1.call-update) | async-done | bytes 29884432 | tf_op jit(solution)/shard_map/all_gather | solution.py:744
  164.2 19.7 %forward_slot.4 = (bf16[4,256,1536]{2,1,0:T(8,128)(2,1)}, bf16[4,256,3072]{2,1,0:T(8,128)(2,1)}, f32[4,256,3072]{2,1,0:T(8,128)}, f32[4,256,3072]{2,1,0:T(8,128)...) custom-call(s32[2]{0:T(128)} %pad_add_fusion.1.at_ref, ...), custom_call_target="tpu_custom_call" | custom-call | flops 22000001024 | bytes 60000000 | tf_op jit(solution)/shard_map/forward_slot/pallas_call | solution.py:246
  185.3 20.0 %forward_slot.5 = (bf16[4,256,1536]{2,1,0:T(8,128)(2,1)}, bf16[4,256,3072]{2,1,0:T(8,128)(2,1)}, f32[4,256,3072]{2,1,0:T(8,128)}, f32[4,256,3072]{2,1,0:T(8,128)...) custom-call(s32[2]{0:T(128)} %pad_add_fusion.at_ref, ...), custom_call_target="tpu_custom_call", output_to_operand_aliasing={{0}: (9, {}), {1}: (10, {}), {2}: (11, {}), {3}: (12, {}), ... | custom-call | flops 22000001024 | bytes 60000000 | tf_op jit(solution)/shard_map/forward_slot/pallas_call | solution.py:246
  208.8 15.6 %collective-permute-done.5.u_hbm = bf16[256,1536]{1,0:T(8,128)(2,1)S(1)} collective-permute-done((bf16[256,1536]{1,0:T(8,128)(2,1)}, bf16[256,1536]{1,0:T(8,128)(2,1)S(1)}, u32[]{:S(2)}, u32[]{:S(2)}) %collective-permute-start.5) | collective-permute-done | bytes 786464 | tf_op jit(solution)/shard_map/ppermute | solution.py:773
  237.2 4.6 by_owner.2
  245.2 53.2 %collective-permute-done.7.g_hbm = bf16[256,1536]{1,0:T(8,128)(2,1)S(1)} collective-permute-done((bf16[256,1536]{1,0:T(8,128)(2,1)}, bf16[256,1536]{1,0:T(8,128)(2,1)S(1)}, u32[]{:S(2)}, u32[]{:S(2)}) %collective-permute-start.7) | collective-permute-done | bytes 786464 | tf_op jit(solution)/shard_map/ppermute | solution.py:791
  299.3 31.4 %backward_slot.6 = (bf16[256,1536]{1,0:T(8,128)(2,1)}, bf16[256,3072]{1,0:T(8,128)(2,1)}, bf16[256,3456]{1,0:T(8,128)(2,1)}, f32[8,3328]{1,0:T(8,128)}) custom-call(s32[2]{0:T(128)} %pad_add_fusion.at_ref, bf16[256,1536]{1,0:T(8,128)(2,1)} %copy-done.10, bf16[256,1536]{1,0:T(8,128)(2,1)} %get-tuple-element.180.u_hbm, ...), custom_call_target="tpu_custom_call", output_to_operand_aliasing={{1}: (15, {}), {2}: (16, {})} | custom-call | flops 1000000000 | bytes 1000000 | tf_op jit(solution)/shard_map/backward_slot/pallas_call | solution.py:543
  337.1 8.8 %outer_sum.4 = (bf16[768,1536]{1,0:T(8,128)(2,1)}, bf16[768,1536]{1,0:T(8,128)(2,1)}) custom-call(bf16[2,2,768,256]{3,2,1,0:T(8,128)(2,1)} %bitcast.129, bf16[2,2,768,256]{3,2,1,0:T(8,128)(2,1)} %collective-permute-done.8.sib_ref, bf16[256,1536]{1,0:T(8,128)(2,1)} %copy-done.12, bf16[256,1536]{1,0:T(8,128)(2,1)} %copy-done.11, bf16[256,1536]{1,0:T(8,128)(2,1)} %copy-done.24, ...), custom_call_target="tpu_custom_call" | custom-call | flops 1000000000 | bytes 1000000 | tf_op jit(solution)/shard_map/outer_sum/pallas_call | solution.py:659
  347.1 31.7 %backward_slot.7 = (bf16[256,1536]{1,0:T(8,128)(2,1)}, bf16[256,3072]{1,0:T(8,128)(2,1)}, bf16[256,3456]{1,0:T(8,128)(2,1)}, f32[8,3328]{1,0:T(8,128)}) custom-call(s32[2]{0:T(128)} %pad_add_fusion.1.at_ref, bf16[256,1536]{1,0:T(8,128)(2,1)} %copy-done.9, ...), custom_call_target="tpu_custom_call", output_to_operand_aliasing={{1}: (15, {}), {2}: (16, {})} | custom-call | flops 1000000000 | bytes 1000000 | tf_op jit(solution)/shard_map/backward_slot/pallas_call | solution.py:543
  379.4 3.9 collective-permute-done.11.sib_ref
  384.2 8.6 %outer_sum.5 = (bf16[384,3072]{1,0:T(8,128)(2,1)}, bf16[384,3072]{1,0:T(8,128)(2,1)}) custom-call(bf16[2,2,384,256]{3,2,1,0:T(8,128)(2,1)} %bitcast.120, bf16[2,2,384,256]{3,2,1,0:T(8,128)(2,1)} %copy-done.3, bf16[256,3072]{1,0:T(8,128)(2,1)} %get-tuple-element.149.rest_0_, bf16[256,3072]{1,0:T(8,128)(2,1)} %get-tuple-element.150.rest_1_, ...), custom_call_target="tpu_custom_call" | custom-call | flops 1000000000 | bytes 1000000 | tf_op jit(solution)/shard_map/outer_sum/pallas_call | solution.py:659
  392.8 6.7 %collective-permute-done.14 = bf16[768,1536]{1,0:T(8,128)(2,1)} collective-permute-done((bf16[768,1536]{1,0:T(8,128)(2,1)}, bf16[768,1536]{1,0:T(8,128)(2,1)}, u32[]{:S(2)}, u32[]{:S(2)}) %collective-permute-start.14) | collective-permute-done | bytes 2359328 | tf_op jit(solution)/shard_map/ppermute | solution.py:676
  406.0 24.9 %collective-permute-done.16 = bf16[2,192,1536]{2,1,0:T(8,128)(2,1)} collective-permute-done((bf16[2,192,1536]{2,1,0:T(8,128)(2,1)}, bf16[2,192,1536]{2,1,0:T(8,128)(2,1)}, u32[]{:S(2)}, u32[]{:S(2)}) %collective-permute-start.16) | collective-permute-done | bytes 1179680 | tf_op jit(solution)/shard_map/ppermute | solution.py:676
  435.8 22.1 %collective-permute-done.17 = bf16[1,192,1536]{2,1,0:T(8,128)(2,1)S(1)} collective-permute-done((bf16[1,192,1536]{2,1,0:T(8,128)(2,1)S(1)}, bf16[1,192,1536]{2,1,0:T(8,128)(2,1)S(1)}, u32[]{:S(2)}, u32[]{:S(2)}) %collective-permute-start.17) | collective-permute-done | bytes 589856 | tf_op jit(solution)/shard_map/ppermute | solution.py:676
  464.2 6.9 %outer_sum.6 = (bf16[384,1920]{1,0:T(8,128)(2,1)}, bf16[384,1920]{1,0:T(8,128)(2,1)}) custom-call(bf16[2,2,384,256]{3,2,1,0:T(8,128)(2,1)} %bitcast.121, bf16[2,2,384,256]{3,2,1,0:T(8,128)(2,1)} %copy-done.3, bf16[256,3456]{1,0:T(8,128)(2,1)} %get-tuple-element.159.rest_0_, bf16[256,3456]{1,0:T(8,128)(2,1)} %get-tuple-element.160.rest_1_, ...), custom_call_target="tpu_custom_call" | custom-call | flops 1000000000 | bytes 1000000 | tf_op jit(solution)/shard_map/outer_sum/pallas_call | solution.py:659
  473.4 7.0 %outer_sum.7 = (bf16[384,1536]{1,0:T(8,128)(2,1)}, bf16[384,1536]{1,0:T(8,128)(2,1)}) custom-call(bf16[2,2,384,256]{3,2,1,0:T(8,128)(2,1)} %bitcast.122, bf16[2,2,384,256]{3,2,1,0:T(8,128)(2,1)} %copy-done.3, bf16[256,3456]{1,0:T(8,128)(2,1)} %get-tuple-element.159.rest_0_, bf16[256,3456]{1,0:T(8,128)(2,1)} %get-tuple-element.160.rest_1_, ...), custom_call_target="tpu_custom_call" | custom-call | flops 1000000000 | bytes 1000000 | tf_op jit(solution)/shard_map/outer_sum/pallas_call | solution.py:659
  481.6 6.8 %collective-permute-done.18 = bf16[2,96,3072]{2,1,0:T(8,128)(2,1)} collective-permute-done((bf16[2,96,3072]{2,1,0:T(8,128)(2,1)}, bf16[2,96,3072]{2,1,0:T(8,128)(2,1)}, u32[]{:S(2)}, u32[]{:S(2)}) %collective-permute-start.18) | collective-permute-done | bytes 1179680 | tf_op jit(solution)/shard_map/ppermute | solution.py:676
  489.9 16.8 %collective-permute-done.22 = bf16[384,1920]{1,0:T(8,128)(2,1)} collective-permute-done((bf16[384,1920]{1,0:T(8,128)(2,1)}, bf16[384,1920]{1,0:T(8,128)(2,1)}, u32[]{:S(2)}, u32[]{:S(2)}) %collective-permute-start.22) | collective-permute-done | bytes 1474592 | tf_op jit(solution)/shard_map/ppermute | solution.py:676
  515.9 16.9 %collective-permute-done.23 = bf16[2,96,1920]{2,1,0:T(8,128)(2,1)S(1)} collective-permute-done((bf16[2,96,1920]{2,1,0:T(8,128)(2,1)S(1)}, bf16[2,96,1920]{2,1,0:T(8,128)(2,1)S(1)}, u32[]{:S(2)}, u32[]{:S(2)}) %collective-permute-start.23) | collective-permute-done | bytes 737312 | tf_op jit(solution)/shard_map/ppermute | solution.py:676
  533.9 4.0 collective-permute-start.24
  541.8 7.5 %collective-permute-done.29 = f32[8,3328]{1,0:T(8,128)S(1)} collective-permute-done((f32[8,3328]{1,0:T(8,128)S(1)}, f32[8,3328]{1,0:T(8,128)S(1)}, u32[]{:S(2)}, u32[]{:S(2)}) %collective-permute-start.29) | collective-permute-done | bytes 106528 | tf_op jit(solution)/shard_map/ppermute | solution.py:676
  549.3 8.9 %collective-permute-done.28 = bf16[2,96,1536]{2,1,0:T(8,128)(2,1)S(1)} collective-permute-done((bf16[2,96,1536]{2,1,0:T(8,128)(2,1)S(1)}, bf16[2,96,1536]{2,1,0:T(8,128)(2,1)S(1)}, u32[]{:S(2)}, u32[]{:S(2)}) %collective-permute-start.28) | collective-permute-done | bytes 589856 | tf_op jit(solution)/shard_map/ppermute | solution.py:676
  558.3 3.9 collective-permute-start.31
  563.5 6.4 %collective-permute-done.31 = f32[8,3328]{1,0:T(8,128)S(1)} collective-permute-done((f32[8,3328]{1,0:T(8,128)S(1)}, f32[8,3328]{1,0:T(8,128)S(1)}, u32[]{:S(2)}, u32[]{:S(2)}) %collective-permute-start.31) | collective-permute-done | bytes 106528 | tf_op jit(solution)/shard_map/ppermute | solution.py:676
  (209 shorter events, 102.5 us)
Async XLA Ops:
  7.2 157.0 %all-gather.2.cloned.1.call-start = ((), (), s32[]{:S(2)}) async-start(), calls=%async_computation | async-start | bytes 31752192 | tf_op jit(solution)/shard_map/all_gather | solution.py:744
  183.9 22.7 %collective-permute-start.4 = (bf16[256,1536]{1,0:T(8,128)(2,1)}, bf16[256,1536]{1,0:T(8,128)(2,1)S(1)}, u32[]{:S(2)}, u32[]{:S(2)}) collective-permute-start(bf16[256,1536]{1,0:T(8,128)(2,1)} %get-tuple-element.93), channel_id=1, source_target_pairs={{0,16},{1,17},{2,18},{3,19},{4,20},{5,21},{6,22},{7,23},{8,24},{9,... | collective-permute-start | bytes 2359304 | tf_op jit(solution)/shard_map/ppermute | solution.py:773
  205.2 19.1 %collective-permute-start.5 = (bf16[256,1536]{1,0:T(8,128)(2,1)}, bf16[256,1536]{1,0:T(8,128)(2,1)S(1)}, u32[]{:S(2)}, u32[]{:S(2)}) collective-permute-start(bf16[256,1536]{1,0:T(8,128)(2,1)} %get-tuple-element.109), channel_id=1, source_target_pairs={{0,16},{1,17},{2,18},{3,19},{4,20},{5,21},{6,22},{7,23},{8,24},{9,... | collective-permute-start | bytes 2359304 | tf_op jit(solution)/shard_map/ppermute | solution.py:773
  229.7 68.8 %collective-permute-start.7 = (bf16[256,1536]{1,0:T(8,128)(2,1)}, bf16[256,1536]{1,0:T(8,128)(2,1)S(1)}, u32[]{:S(2)}, u32[]{:S(2)}) collective-permute-start(bf16[256,1536]{1,0:T(8,128)(2,1)} %get-tuple-element.125), channel_id=1, source_target_pairs={{16,0},{17,1},{18,2},{19,3},{20,4},{21,5},{22,6},{23,7},{24,8},{25... | collective-permute-start | bytes 2359304 | tf_op jit(solution)/shard_map/ppermute | solution.py:791
  234.0 97.1 %collective-permute-start.6 = (bf16[256,1536]{1,0:T(8,128)(2,1)}, bf16[256,1536]{1,0:T(8,128)(2,1)S(1)}, u32[]{:S(2)}, u32[]{:S(2)}) collective-permute-start(bf16[256,1536]{1,0:T(8,128)(2,1)} %get-tuple-element.124), channel_id=1, source_target_pairs={{16,0},{17,1},{18,2},{19,3},{20,4},{21,5},{22,6},{23,7},{24,8},{25... | collective-permute-start | bytes 2359304 | tf_op jit(solution)/shard_map/ppermute | solution.py:791
  241.8 95.3 %collective-permute-start.8 = (bf16[2,2,768,256]{3,2,1,0:T(8,128)(2,1)}, bf16[2,2,768,256]{3,2,1,0:T(8,128)(2,1)}, u32[]{:S(2)}, u32[]{:S(2)}) collective-permute-start(bf16[2,2,768,256]{3,2,1,0:T(8,128)(2,1)} %bitcast.145), channel_id=1, source_target_pairs={{0,1},{1,0},{2,3},{3,2},{4,5},{5,4},{6,7},{7,6},{8,9},{9,8},{10,11... | collective-permute-start | bytes 4718600 | tf_op jit(solution)/shard_map/ppermute | solution.py:676
  345.9 53.6 %collective-permute-start.14 = (bf16[768,1536]{1,0:T(8,128)(2,1)}, bf16[768,1536]{1,0:T(8,128)(2,1)}, u32[]{:S(2)}, u32[]{:S(2)}) collective-permute-start(bf16[768,1536]{1,0:T(8,128)(2,1)} %get-tuple-element.153), channel_id=1, source_target_pairs={{0,2},{1,3},{2,0},{3,1},{4,6},{5,7},{6,4},{7,5},{8,10},{9,11},{10,... | collective-permute-start | bytes 7077896 | tf_op jit(solution)/shard_map/ppermute | solution.py:676
  347.1 36.3 %collective-permute-start.13 = (bf16[256,3072]{1,0:T(8,128)(2,1)S(1)}, bf16[256,3072]{1,0:T(8,128)(2,1)}, u32[]{:S(2)}, u32[]{:S(2)}) collective-permute-start(bf16[256,3072]{1,0:T(8,128)(2,1)S(1)} %copy-done.6), channel_id=1, source_target_pairs={{0,1},{1,0},{2,3},{3,2},{4,5},{5,4},{6,7},{7,6},{8,9},{9,8},{10,11... | collective-permute-start | bytes 4718600 | tf_op jit(solution)/shard_map/ppermute | solution.py:676
  399.5 58.4 %collective-permute-start.15 = (bf16[384,3072]{1,0:T(8,128)(2,1)}, bf16[384,3072]{1,0:T(8,128)(2,1)}, u32[]{:S(2)}, u32[]{:S(2)}) collective-permute-start(bf16[384,3072]{1,0:T(8,128)(2,1)} %get-tuple-element.155), channel_id=1, source_target_pairs={{0,2},{1,3},{2,0},{3,1},{4,6},{5,7},{6,4},{7,5},{8,10},{9,11},{10,... | collective-permute-start | bytes 7077896 | tf_op jit(solution)/shard_map/ppermute | solution.py:676
  403.7 27.2 %collective-permute-start.16 = (bf16[2,192,1536]{2,1,0:T(8,128)(2,1)}, bf16[2,192,1536]{2,1,0:T(8,128)(2,1)}, u32[]{:S(2)}, u32[]{:S(2)}) collective-permute-start(bf16[2,192,1536]{2,1,0:T(8,128)(2,1)} %fusion.1), channel_id=1, source_target_pairs={{0,4},{1,5},{2,6},{3,7},{4,0},{5,1},{6,2},{7,3},{8,12},{9,13},{10,... | collective-permute-start | bytes 3538952 | tf_op jit(solution)/shard_map/ppermute | solution.py:676
  404.3 58.7 %collective-permute-start.21 = (bf16[256,3456]{1,0:T(8,128)(2,1)S(1)}, bf16[256,3456]{1,0:T(8,128)(2,1)S(1)}, u32[]{:S(2)}, u32[]{:S(2)}) collective-permute-start(bf16[256,3456]{1,0:T(8,128)(2,1)S(1)} %copy-done.1), channel_id=1, source_target_pairs={{0,1},{1,0},{2,3},{3,2},{4,5},{5,4},{6,7},{7,6},{8,9},{9,8},{10,11... | collective-permute-start | bytes 5308424 | tf_op jit(solution)/shard_map/ppermute | solution.py:676
  404.3 59.9 %collective-permute-start.20 = (bf16[256,3456]{1,0:T(8,128)(2,1)S(1)}, bf16[256,3456]{1,0:T(8,128)(2,1)}, u32[]{:S(2)}, u32[]{:S(2)}) collective-permute-start(bf16[256,3456]{1,0:T(8,128)(2,1)S(1)} %copy-done), channel_id=1, source_target_pairs={{0,1},{1,0},{2,3},{3,2},{4,5},{5,4},{6,7},{7,6},{8,9},{9,8},{10,11... | collective-permute-start | bytes 5308424 | tf_op jit(solution)/shard_map/ppermute | solution.py:676
  432.6 25.4 %collective-permute-start.17 = (bf16[1,192,1536]{2,1,0:T(8,128)(2,1)S(1)}, bf16[1,192,1536]{2,1,0:T(8,128)(2,1)S(1)}, u32[]{:S(2)}, u32[]{:S(2)}) collective-permute-start(bf16[1,192,1536]{2,1,0:T(8,128)(2,1)S(1)} %fusion.5), channel_id=1, source_target_pairs={{0,8},{1,9},{2,10},{3,11},{4,12},{5,13},{6,14},{7,15},{8,0},{9,1},... | collective-permute-start | bytes 1769480 | tf_op jit(solution)/shard_map/ppermute | solution.py:676
  460.9 27.6 %collective-permute-start.18 = (bf16[2,96,3072]{2,1,0:T(8,128)(2,1)}, bf16[2,96,3072]{2,1,0:T(8,128)(2,1)}, u32[]{:S(2)}, u32[]{:S(2)}) collective-permute-start(bf16[2,96,3072]{2,1,0:T(8,128)(2,1)} %fusion.2), channel_id=1, source_target_pairs={{0,4},{1,5},{2,6},{3,7},{4,0},{5,1},{6,2},{7,3},{8,12},{9,13},{10,... | collective-permute-start | bytes 3538952 | tf_op jit(solution)/shard_map/ppermute | solution.py:676
  471.1 35.6 %collective-permute-start.22 = (bf16[384,1920]{1,0:T(8,128)(2,1)}, bf16[384,1920]{1,0:T(8,128)(2,1)}, u32[]{:S(2)}, u32[]{:S(2)}) collective-permute-start(bf16[384,1920]{1,0:T(8,128)(2,1)} %get-tuple-element.162), channel_id=1, source_target_pairs={{0,2},{1,3},{2,0},{3,1},{4,6},{5,7},{6,4},{7,5},{8,10},{9,11},{10,... | collective-permute-start | bytes 4423688 | tf_op jit(solution)/shard_map/ppermute | solution.py:676
  480.4 57.5 %collective-permute-start.25 = (bf16[384,1536]{1,0:T(8,128)(2,1)}, bf16[384,1536]{1,0:T(8,128)(2,1)S(1)}, u32[]{:S(2)}, u32[]{:S(2)}) collective-permute-start(bf16[384,1536]{1,0:T(8,128)(2,1)} %get-tuple-element.165), channel_id=1, source_target_pairs={{0,2},{1,3},{2,0},{3,1},{4,6},{5,7},{6,4},{7,5},{8,10},{9,11},{10,... | collective-permute-start | bytes 3538952 | tf_op jit(solution)/shard_map/ppermute | solution.py:676
  481.6 27.8 %collective-permute-start.26 = (f32[8,3328]{1,0:T(8,128)S(1)}, f32[8,3328]{1,0:T(8,128)S(1)}, u32[]{:S(2)}, u32[]{:S(2)}) collective-permute-start(f32[8,3328]{1,0:T(8,128)S(1)} %copy-done.29), channel_id=1, source_target_pairs={{0,1},{1,0},{2,3},{3,2},{4,5},{5,4},{6,7},{7,6},{8,9},{9,8},{10,11... | collective-permute-start | bytes 319496 | tf_op jit(solution)/shard_map/ppermute | solution.py:676
  508.0 24.7 %collective-permute-start.23 = (bf16[2,96,1920]{2,1,0:T(8,128)(2,1)S(1)}, bf16[2,96,1920]{2,1,0:T(8,128)(2,1)S(1)}, u32[]{:S(2)}, u32[]{:S(2)}) collective-permute-start(bf16[2,96,1920]{2,1,0:T(8,128)(2,1)S(1)} %fusion.6), channel_id=1, source_target_pairs={{0,4},{1,5},{2,6},{3,7},{4,0},{5,1},{6,2},{7,3},{8,12},{9,13},{10,... | collective-permute-start | bytes 2211848 | tf_op jit(solution)/shard_map/ppermute | solution.py:676
  509.4 28.5 %collective-permute-start.27 = (f32[8,3328]{1,0:T(8,128)S(1)}, f32[8,3328]{1,0:T(8,128)S(1)}, u32[]{:S(2)}, u32[]{:S(2)}) collective-permute-start(f32[8,3328]{1,0:T(8,128)S(1)} %add.356), channel_id=1, source_target_pairs={{0,2},{1,3},{2,0},{3,1},{4,6},{5,7},{6,4},{7,5},{8,10},{9,11},{10,... | collective-permute-start | bytes 319496 | tf_op jit(solution)/shard_map/ppermute | solution.py:676
  510.4 29.9 %collective-permute-start.19 = (bf16[1,96,3072]{2,1,0:T(8,128)(2,1)S(1)}, bf16[1,96,3072]{2,1,0:T(8,128)(2,1)S(1)}, u32[]{:S(2)}, u32[]{:S(2)}) collective-permute-start(bf16[1,96,3072]{2,1,0:T(8,128)(2,1)S(1)} %fusion.4), channel_id=1, source_target_pairs={{0,8},{1,9},{2,10},{3,11},{4,12},{5,13},{6,14},{7,15},{8,0},{9,1},... | collective-permute-start | bytes 1769480 | tf_op jit(solution)/shard_map/ppermute | solution.py:676
  533.9 28.3 %collective-permute-start.24 = (bf16[1,96,1920]{2,1,0:T(8,128)(2,1)S(1)}, bf16[1,96,1920]{2,1,0:T(8,128)(2,1)S(1)}, u32[]{:S(2)}, u32[]{:S(2)}) collective-permute-start(bf16[1,96,1920]{2,1,0:T(8,128)(2,1)S(1)} %fusion.7), channel_id=1, source_target_pairs={{0,8},{1,9},{2,10},{3,11},{4,12},{5,13},{6,14},{7,15},{8,0},{9,1},... | collective-permute-start | bytes 1105928 | tf_op jit(solution)/shard_map/ppermute | solution.py:676
  538.1 11.1 %collective-permute-start.29 = (f32[8,3328]{1,0:T(8,128)S(1)}, f32[8,3328]{1,0:T(8,128)S(1)}, u32[]{:S(2)}, u32[]{:S(2)}) collective-permute-start(f32[8,3328]{1,0:T(8,128)S(1)} %add.360), channel_id=1, source_target_pairs={{0,4},{1,5},{2,6},{3,7},{4,0},{5,1},{6,2},{7,3},{8,12},{9,13},{10,... | collective-permute-start | bytes 319496 | tf_op jit(solution)/shard_map/ppermute | solution.py:676
  538.2 19.9 %collective-permute-start.28 = (bf16[2,96,1536]{2,1,0:T(8,128)(2,1)S(1)}, bf16[2,96,1536]{2,1,0:T(8,128)(2,1)S(1)}, u32[]{:S(2)}, u32[]{:S(2)}) collective-permute-start(bf16[2,96,1536]{2,1,0:T(8,128)(2,1)S(1)} %fusion.8), channel_id=1, source_target_pairs={{0,4},{1,5},{2,6},{3,7},{4,0},{5,1},{6,2},{7,3},{8,12},{9,13},{10,... | collective-permute-start | bytes 1769480 | tf_op jit(solution)/shard_map/ppermute | solution.py:676
  558.3 11.6 %collective-permute-start.31 = (f32[8,3328]{1,0:T(8,128)S(1)}, f32[8,3328]{1,0:T(8,128)S(1)}, u32[]{:S(2)}, u32[]{:S(2)}) collective-permute-start(f32[8,3328]{1,0:T(8,128)S(1)} %add.365), channel_id=1, source_target_pairs={{0,8},{1,9},{2,10},{3,11},{4,12},{5,13},{6,14},{7,15},{8,0},{9,1},... | collective-permute-start | bytes 319496 | tf_op jit(solution)/shard_map/ppermute | solution.py:676
  (48 other events, 494.8 us)
Sparse Core Ops, SparseCore 0:
  10.2 153.8 all-gather.1

commit v4 on v3

--- a/solution.py
+++ b/solution.py
@@ -16,6 +16,8 @@
 WIDE = 512
 GROUP = WIDE // HEAD_DIM
 TINY = 1e-30
+SUB = 8
+CHUNK = 64
 NEG = -1e30
 VMEM = 60 * 1024 * 1024
 F32 = jnp.float32
@@ -35,13 +37,35 @@
     return 0.5 * jnp.tanh(0.5 * v) + 0.5
 
 
+def down(values, steps):
+    count = values.shape[0]
+    moved = pltpu.roll(values, steps % count, 0)
+    rows = lax.broadcasted_iota(jnp.int32, (SUB, values.shape[1]), 0)
+    if steps > 0:
+        return jnp.concatenate([jnp.where(rows >= steps, moved[:SUB], 0.0), moved[SUB:]], axis=0)
+    return jnp.concatenate([moved[:-SUB], jnp.where(rows < SUB + steps, moved[-SUB:], 0.0)], axis=0)
+
+
 def conv_rows(values, taps, bias):
-    rows = lax.broadcasted_iota(jnp.int32, values.shape, 0)
     total = bias + taps[CONV - 1 : CONV, :] * values
     for back in range(1, CONV):
-        moved = jnp.where(rows >= back, pltpu.roll(values, back, 0), 0.0)
-        total = total + taps[CONV - 1 - back : CONV - back, :] * moved
+        total = total + taps[CONV - 1 - back : CONV - back, :] * down(values, back)
     return total
+
+
+def fewer(block):
+    total = block[:SUB]
+    for at in range(SUB, block.shape[0], SUB):
+        total = total + block[at : at + SUB]
+    return total
+
+
+def piece_of(scr, j, piece, pieces):
+    _, parts, depth, _ = scr.shape
+    if parts % pieces == 0:
+        return fold(scr[j, piece * (parts // pieces) : (piece + 1) * (parts // pieces)])
+    size = parts * depth // pieces
+    return fold(scr[j])[piece * size : (piece + 1) * size]
 
 
 def softplus(v):
@@ -206,6 +230,7 @@
 
         lax.fori_loop(0, groups, group, 0)
         scale = lax.rsqrt(sq_scr[...] * (1.0 / (groups * WIDE)) + EPS)
+        vr_scr[:, 3 * STATE - 1 :] = scale
         for g in range(groups):
             here = slice(g * WIDE, (g + 1) * WIDE)
             gb_scr[:, here] = (w_scr[g] * scale * gate_ref[:, here]).astype(BF16)
@@ -279,15 +304,15 @@
 
 
 def backward_kernel(
-    place, at_ref, g_hbm, u_hbm, w_hbm, view_hbm, z_hbm, v_hbm, y_hbm, vr_hbm, cr_hbm,
+    place, at_ref, g_hbm, u_hbm, w_hbm, view_hbm, gb_hbm, z_hbm, v_hbm, y_hbm, vr_hbm, cr_hbm,
     norm_ref, chan_ref, chanr_ref, head_ref, past_ref, *rest
 ):
     (
         du_hbm, dz_hbm, dv_hbm, sum_ref,
-        g_scr, u_scr, wo_scr, wz_scr, wx_scr, wr_scr, z_scr, v_scr, y_scr, vr_scr, cr_scr, dz_scr, dv_scr,
-        dob_scr, dgb_scr, sq_scr, we_scr, st_scr, ds_scr, bcol_scr, trow_scr, colr_scr, rowr_scr, step_scr, act_scr, dn_scr,
+        g_scr, u_scr, wo_scr, wz_scr, wx_scr, wr_scr, gb_scr, z_scr, v_scr, y_scr, vr_scr, cr_scr, dz_scr, dv_scr,
+        dob_scr, dgb_scr, dzp_scr, dvp_scr, c_scr, dy_scr, slope_scr, xl_scr, dyl_scr, q_scr, pull_scr, we_scr, st_scr, ds_scr, bcol_scr, trow_scr, colr_scr, rowr_scr, step_scr, act_scr, dn_scr,
         sem, out_sem,
-    ) = rest[-32:]
+    ) = rest[-41:]
     groups, rows, _ = dgb_scr.shape
     width = g_scr.shape[1]
     inner = groups * WIDE
@@ -302,12 +327,13 @@
         tall = pl.ds(pl.multiple_of(j * WIDE, WIDE), WIDE)
         return [
             pltpu.make_async_copy(w_hbm.at[tall, pl.ds(0, width)], wo_scr.at[j], sem.at[base + j]),
+            pltpu.make_async_copy(gb_hbm.at[place, :, lanes(j)], gb_scr.at[j], sem.at[base + 4 * groups + j]),
+        ]
+
+    def late(j):
+        return of_group(j) + [
             pltpu.make_async_copy(z_hbm.at[place, :, lanes(j)], z_scr.at[j], sem.at[base + groups + j]),
             pltpu.make_async_copy(y_hbm.at[place, :, lanes(j)], y_scr.at[j], sem.at[base + 2 * groups + j]),
-        ]
-
-    def late(j):
-        return of_group(j) + [
             pltpu.make_async_copy(v_hbm.at[place, :, lanes(j)], v_scr.at[j], sem.at[base + 3 * groups + j]),
         ]
 
@@ -330,7 +356,6 @@
             start_all(late(j))
         start_all(of_rest() + [u_copy])
 
-        sq_scr[...] = jnp.zeros_like(sq_scr)
         we_scr[...] = jnp.zeros_like(we_scr)
         ds_scr[...] = jnp.zeros_like(ds_scr)
         dn_scr[...] = jnp.zeros_like(dn_scr)
@@ -353,42 +378,23 @@
 
         def first_pass(j, carry):
             wait_all(early(j))
-            dgb = nt_dot(dob_scr[...], wo_scr[j])
-            dgb_scr[j] = dgb
-            z = z_scr[j]
-            w = y_scr[j] * (z * sigmoid(z))
-            sq_scr[...] += jnp.sum(w * w, axis=1, keepdims=True)
-            we_scr[...] += jnp.sum(w * (dgb * chan_ref[5:6, lanes(j)]), axis=1, keepdims=True)
+            for half in range(2):
+                wide = slice(half * 2 * HALF, (half + 1) * 2 * HALF)
+                dgb = nt_dot(dob_scr[...], wo_scr[j, wide, :])
+                dgb_scr[j, :, wide] = dgb
+                for at in range(0, rows, CHUNK):
+                    at = slice(at, at + CHUNK)
+                    product = dgb[at] * gb_scr[j, at, wide].astype(F32)
+                    we_scr[at, :] += product[:, :HALF] + product[:, HALF:]
             return carry
 
         lax.fori_loop(0, groups, first_pass, 0)
 
         def second_pass(j, carry):
             wait_all(late(j))
-            wide = lanes(j)
-            taps = chan_ref[:, wide]
-            q = lax.rsqrt(sq_scr[...] * (1.0 / inner) + EPS)
-            pull = q * q * q * (we_scr[...] * (1.0 / inner))
-            dgb = dgb_scr[j]
-            z = z_scr[j]
-            y = y_scr[j]
-            sz = sigmoid(z)
-            silu_z = z * sz
-            w = y * silu_z
-            dw = q * (dgb * taps[5:6, :]) - w * pull
-            sum_ref[5:6, wide] = past_ref[5:6, wide] + jnp.sum(w * q * dgb, axis=0, keepdims=True)
-            dy = dw * silu_z
-            dz = (dw * y * (sz * (1.0 + z * (1.0 - sz)))).astype(BF16)
-            dz_scr[j] = dz
-            dz_copy(j).start()
-            dn = nt_dot(dz, fold(wz_scr[j]))
-
-            c = conv_rows(v_scr[j], taps[0:4, :], taps[4:5, :])
-            sc = sigmoid(c)
-            x = c * sc
-            x_low = x.astype(BF16)
-            dy_low = dy.astype(BF16)
-            sum_ref[6:7, wide] = past_ref[6:7, wide] + jnp.sum(dy * x, axis=0, keepdims=True)
+            taps = chan_ref[:, lanes(j)]
+            past = past_ref[:, lanes(j)]
+            before = jnp.maximum(j - 1, 0)
             cols = bcol_scr[j]
             head_rows = pl.ds(pl.multiple_of(j * GROUP, GROUP), GROUP)
             rws = trow_scr[head_rows, :]
@@ -398,25 +404,56 @@
             lane_row = lax.broadcasted_iota(jnp.int32, (1, HALF), 1)
             sub = lax.broadcasted_iota(jnp.int32, (GROUP, HALF), 0)
             blocks = rows // HALF
+            pairs = GROUP // 2
             col_sums = [jnp.zeros((HALF, HALF), F32) for _ in range(blocks)]
             row_sums = [jnp.zeros((GROUP, HALF), F32) for _ in range(blocks)]
-            parts = []
-            for pair in range(GROUP // 2):
+            for pair in range(pairs):
                 here = slice(pair * HALF, (pair + 1) * HALF)
+                col = pl.ds(pl.multiple_of(j * WIDE + pair * HALF, HALF), HALF)
+                share = slice(pair * (width // pairs), (pair + 1) * (width // pairs))
+                dn_scr[:, share] += nt_dot(dzp_scr[...], piece_of(wz_scr, before, pair, pairs)) + nt_dot(
+                    dvp_scr[...], piece_of(wx_scr, before, pair, pairs)
+                )
+                c_scr[...] = conv_rows(v_scr[j, :, here], taps[0:4, here], taps[4:5, here])
+                gate_sum = jnp.zeros((SUB, HALF), F32)
+                skip_sum = jnp.zeros((SUB, HALF), F32)
+                for at in range(0, rows, CHUNK):
+                    at = slice(at, at + CHUNK)
+                    q = q_scr[at, :]
+                    dgb = dgb_scr[j, at, here]
+                    z = z_scr[j, at, here]
+                    y = y_scr[j, at, here]
+                    sz = sigmoid(z)
+                    silu_z = z * sz
+                    w = y * silu_z
+                    scaled = q * dgb
+                    dw = scaled * taps[5:6, here] - w * pull_scr[at, :]
+                    gate_sum = gate_sum + fewer(w * scaled)
+                    dy = dw * silu_z
+                    dy_scr[at, :] = dy
+                    dyl_scr[at, :] = dy.astype(BF16)
+                    dz_scr[j, at, here] = (dw * y * (sz + silu_z * (1.0 - sz))).astype(BF16)
+                    c = c_scr[at, :]
+                    sc = sigmoid(c)
+                    x = c * sc
+                    xl_scr[at, :] = x.astype(BF16)
+                    slope_scr[at, :] = sc + x * (1.0 - sc)
+                    skip_sum = skip_sum + fewer(dy * x)
+                sum_ref[5:6, col] = past[5:6, here] + jnp.sum(gate_sum, axis=0, keepdims=True)
+                sum_ref[6:7, col] = past[6:7, here] + jnp.sum(skip_sum, axis=0, keepdims=True)
+
                 pieces = []
                 row_part = [[None] * blocks, [None] * blocks]
                 for sb in range(blocks):
                     s_here = slice(sb * HALF, (sb + 1) * HALF)
-                    x_here = x_low[s_here, here]
-                    split = (
-                        jnp.where(first, x_here, jnp.zeros_like(x_here)),
-                        jnp.where(first, jnp.zeros_like(x_here), x_here),
-                    )
+                    x_here = xl_scr[s_here, :]
+                    none = jnp.zeros_like(x_here)
+                    split = jnp.concatenate([jnp.where(first, x_here, none), jnp.where(first, none, x_here)], axis=0)
+                    meets = nt_dot(split, dyl_scr[sb * HALF :, :])
                     mixes = [[], []]
                     lane_sum = [None, None]
                     for tb in range(sb, blocks):
                         t_here = slice(tb * HALF, (tb + 1) * HALF)
-                        dy_here = dy_low[t_here, here]
                         contact = st_scr[s_here, t_here]
                         touched = None
                         for k in range(2):
@@ -425,38 +462,48 @@
                             if sb == tb:
                                 gap = jnp.where(causal, gap, NEG)
                             decay = jnp.exp2(gap)
-                            mix = decay * contact
-                            meet = nt_dot(split[k], dy_here)
+                            meet = meets[k * HALF : (k + 1) * HALF, (tb - sb) * HALF : (tb - sb + 1) * HALF]
                             through = decay * meet
-                            pairs = through * contact
+                            both = through * contact
                             touched = through if touched is None else touched + through
-                            mixes[k].append(mix.astype(BF16))
-                            lane_sum[k] = pairs if lane_sum[k] is None else lane_sum[k] + pairs
-                            down = jnp.sum(pairs, axis=0, keepdims=True)
-                            row_part[k][tb] = down if row_part[k][tb] is None else row_part[k][tb] + down
+                            mixes[k].append((decay * contact).astype(BF16))
+                            lane_sum[k] = both if lane_sum[k] is None else lane_sum[k] + both
+                            falling = fewer(both)
+                            row_part[k][tb] = falling if row_part[k][tb] is None else row_part[k][tb] + falling
                         ds_scr[s_here, t_here] += touched
-                    out = []
+                    mix = jnp.concatenate([jnp.concatenate(m, axis=1) if len(m) > 1 else m[0] for m in mixes], axis=0)
+                    out = nn_dot(mix, dyl_scr[sb * HALF :, :])
                     for k in range(2):
-                        h = 2 * pair + k
-                        mix = jnp.concatenate(mixes[k], axis=1) if len(mixes[k]) > 1 else mixes[k][0]
-                        out.append(nn_dot(mix, dy_low[sb * HALF :, here]))
                         total = jnp.sum(lane_sum[k], axis=1, keepdims=True)
-                        col_sums[sb] = jnp.where(lane_row == h, total, col_sums[sb])
-                    pieces.append(jnp.where(first, out[0], out[1]))
+                        col_sums[sb] = jnp.where(lane_row == 2 * pair + k, total, col_sums[sb])
+                    pieces.append(jnp.where(first, out[:HALF], out[HALF:]))
                 for k in range(2):
                     for tb in range(blocks):
-                        row_sums[tb] = jnp.where(sub == 2 * pair + k, row_part[k][tb], row_sums[tb])
-                parts.append(jnp.concatenate(pieces, axis=0))
+                        total = jnp.sum(row_part[k][tb], axis=0, keepdims=True)
+                        row_sums[tb] = jnp.where(sub == 2 * pair + k, total, row_sums[tb])
+                dx = jnp.concatenate(pieces, axis=0)
+                dc = (dx + taps[6:7, here] * dy_scr[...]) * slope_scr[...]
+                dv, tap_sums = conv_back(dc, v_scr[j, :, here], taps[:, here])
+                dv_scr[:, col] = dv.astype(BF16)
+                for row, one in enumerate(tap_sums):
+                    sum_ref[row : row + 1, col] = past[row : row + 1, here] + one
             colr_scr[j] = jnp.concatenate(col_sums, axis=0)
             rowr_scr[head_rows, :] = jnp.concatenate(row_sums, axis=1)
-            dx = jnp.concatenate(parts, axis=1) + taps[6:7, :] * dy
-            dc = dx * (sc * (1.0 + c * (1.0 - sc)))
-            dv = conv_back(dc, v_scr[j], taps, past_ref, sum_ref, wide).astype(BF16)
-            dv_scr[:, wide] = dv
-            dn_scr[...] += dn + nt_dot(dv, fold(wx_scr[j]))
+            dzp_scr[...] = dz_scr[j]
+            dvp_scr[...] = dv_scr[:, lanes(j)]
+            dz_copy(j).start()
             return carry
 
+        for at in range(0, rows, CHUNK):
+            at = slice(at, at + CHUNK)
+            q = vr_scr[at, 3 * STATE - 1 :]
+            pull = q * q * (jnp.sum(we_scr[at, :], axis=1, keepdims=True) * (1.0 / inner))
+            q_scr[at, :] = jnp.broadcast_to(q, (CHUNK, HALF))
+            pull_scr[at, :] = jnp.broadcast_to(pull, (CHUNK, HALF))
+        dzp_scr[...] = jnp.zeros_like(dzp_scr)
+        dvp_scr[...] = jnp.zeros_like(dvp_scr)
         lax.fori_loop(0, groups, second_pass, 0)
+        dn_scr[...] += nt_dot(dzp_scr[...], fold(wz_scr[groups - 1])) + nt_dot(dvp_scr[...], fold(wx_scr[groups - 1]))
         act = act_scr[...]
         ds = ds_scr[...].astype(BF16)
         act_low = act.astype(BF16)
@@ -466,7 +513,9 @@
         sp = sigmoid(pre)
         d_pre = jnp.concatenate([d_b, d_c], axis=1) * (sp * (1.0 + pre * (1.0 - sp)))
         narrow = slice(inner, inner + 2 * STATE)
-        d_raw = conv_back(d_pre, vr_scr[:, : 2 * STATE], chanr_ref[...], past_ref, sum_ref, narrow)
+        d_raw, tap_sums = conv_back(d_pre, vr_scr[:, : 2 * STATE], chanr_ref[...])
+        for row, one in enumerate(tap_sums):
+            sum_ref[row : row + 1, narrow] = past_ref[row : row + 1, narrow] + one
         sum_ref[5:7, narrow] = jnp.zeros((2, 2 * STATE), F32)
         col_total = colr_scr[0]
         for g in range(1, groups):
@@ -492,34 +541,35 @@
         dv_scr[:, inner:] = dr
         dv_copy.start()
         wait_all(of_rest())
-        dn = dn_scr[...]
         for k in range(3):
-            dn = dn + nt_dot(dr[:, k * STATE : (k + 1) * STATE], fold(wr_scr[k]))
+            dn_scr[...] += nt_dot(dr[:, k * STATE : (k + 1) * STATE], fold(wr_scr[k]))
         u_copy.wait()
-        u = u_scr[...].astype(F32)
-        p = lax.rsqrt(jnp.mean(u * u, axis=1, keepdims=True) + EPS)
-        e = dn * norm_ref[...]
-        du = g_scr[...].astype(F32) + p * e - u * (p * p * p * jnp.mean(u * e, axis=1, keepdims=True))
-        dob_scr[...] = du.astype(BF16)
+        norm_sum = jnp.zeros((SUB, width), F32)
+        for at in range(0, rows, 16):
+            at = slice(at, at + 16)
+            u = u_scr[at, :].astype(F32)
+            dn = dn_scr[at, :]
+            p = lax.rsqrt(jnp.mean(u * u, axis=1, keepdims=True) + EPS)
+            e = dn * norm_ref[...]
+            du = g_scr[at, :].astype(F32) + p * e - u * (p * p * p * jnp.mean(u * e, axis=1, keepdims=True))
+            dob_scr[at, :] = du.astype(BF16)
+            norm_sum = norm_sum + fewer(u * p * dn)
         du_copy.start()
-        sum_ref[7:8, :width] = last[:, :width] + jnp.sum(u * p * dn, axis=0, keepdims=True)
+        sum_ref[7:8, :width] = last[:, :width] + jnp.sum(norm_sum, axis=0, keepdims=True)
         for j in range(groups):
             dz_copy(j).wait()
         dv_copy.wait()
         du_copy.wait()
 
 
-def conv_back(dc, values, taps, past_ref, sum_ref, here):
-    rows = lax.broadcasted_iota(jnp.int32, dc.shape, 0)
-    count = dc.shape[0]
-    sum_ref[4:5, here] = past_ref[4:5, here] + jnp.sum(dc, axis=0, keepdims=True)
-    total = 0.0
+def conv_back(dc, values, taps):
+    total, sums = 0.0, [None] * CONV
     for ahead in range(CONV):
-        moved = jnp.where(rows < count - ahead, pltpu.roll(dc, count - ahead, 0), 0.0) if ahead else dc
+        moved = down(dc, -ahead) if ahead else dc
         tap = CONV - 1 - ahead
-        sum_ref[tap : tap + 1, here] = past_ref[tap : tap + 1, here] + jnp.sum(moved * values, axis=0, keepdims=True)
         total = total + taps[tap : tap + 1, :] * moved
-    return total
+        sums[tap] = jnp.sum(fewer(moved * values), axis=0, keepdims=True)
+    return total, sums + [jnp.sum(fewer(dc), axis=0, keepdims=True)]
 
 
 def backward_slot(place, numbers, kept, grads, past, g, u, w_all, view, norm_gain, chan, chan_r, heads):
@@ -530,7 +580,7 @@
     far = pl.BlockSpec(memory_space=pl.ANY)
     near = pl.BlockSpec(memory_space=pltpu.VMEM)
     args = [numbers, g, u, w_all, view, *kept, norm_gain, chan, chan_r, heads, past]
-    in_specs = [pl.BlockSpec(memory_space=pltpu.SMEM)] + [far] * 9 + [near] * 5
+    in_specs = [pl.BlockSpec(memory_space=pltpu.SMEM)] + [far] * 10 + [near] * 5
     aliases = {}
     if grads is not None:
         for k, arr in enumerate(grads):
@@ -557,6 +607,7 @@
             tall,
             tall,
             pltpu.VMEM((3, parts, depth, HALF), BF16),
+            pltpu.VMEM((groups, rows, WIDE), BF16),
             wide,
             wide,
             wide,
@@ -566,8 +617,16 @@
             pltpu.VMEM((rows, inner + 3 * STATE), BF16),
             slot,
             wide,
-            pltpu.VMEM((rows, 1), F32),
-            pltpu.VMEM((rows, 1), F32),
+            pltpu.VMEM((rows, WIDE), BF16),
+            pltpu.VMEM((rows, WIDE), BF16),
+            pltpu.VMEM((rows, HALF), F32),
+            pltpu.VMEM((rows, HALF), F32),
+            pltpu.VMEM((rows, HALF), F32),
+            pltpu.VMEM((rows, HALF), BF16),
+            pltpu.VMEM((rows, HALF), BF16),
+            pltpu.VMEM((rows, HALF), F32),
+            pltpu.VMEM((rows, HALF), F32),
+            pltpu.VMEM((rows, HALF), F32),
             pltpu.VMEM((rows, rows), F32),
             pltpu.VMEM((rows, rows), F32),
             pltpu.VMEM((groups, rows, HALF), F32),
@@ -577,7 +636,7 @@
             pltpu.VMEM((rows, HALF), F32),
             pltpu.VMEM((rows, 2 * STATE), F32),
             pltpu.VMEM((rows, width), F32),
-            pltpu.SemaphoreType.DMA((6 * groups + 7,)),
+            pltpu.SemaphoreType.DMA((7 * groups + 7,)),
             pltpu.SemaphoreType.DMA((groups + 2,)),
         ],
         input_output_aliases=aliases,
@@ -687,7 +746,7 @@
     return table
 
 
-def owned_sums(chunks, axis, rider):
+def owned_sums(chunks, axis, rider, ahead):
     count = lax.axis_size(axis)
     length = count // 4
     results, token = [], None
@@ -699,6 +758,8 @@
         if rides:
             far, rider_far = lax.optimization_barrier((far, rider_far))
             rider = rider + rider_far
+        if k == 0:
+            far, _ = lax.optimization_barrier((far, ahead[0]))
         terms = [a.reshape(length, -1, a.shape[1]) for a in (keep, far)]
         bit = 1
         while bit < length:
@@ -707,6 +768,8 @@
             sent = sum(half(a, 1 - mine).astype(F32) for a in terms).astype(BF16)
             if rides:
                 sent, rider = lax.optimization_barrier((sent, rider))
+            if k == 0 and bit > 1:
+                sent, _ = lax.optimization_barrier((sent, ahead[1:]))
             came = swap(sent, axis, 4 * bit)
             if rides:
                 rider = rider + swap(rider, axis, 4 * bit)
@@ -780,7 +843,7 @@
 
     def run_backward(place, m, stage, grads, sums, g, u):
         return backward_slot(
-            place, numbers(m, stage), kept[2:], grads, sums, g, u, w_all, view, norm, chan, chan_r, head_rows
+            place, numbers(m, stage), kept[1:], grads, sums, g, u, w_all, view, norm, chan, chan_r, head_rows
         )
 
     is_last = section == 1
@@ -819,17 +882,17 @@
 
     z_rows = [a for a, _ in grads] + z_sib
     v_rows = [a for _, a in grads] + v_sib
-    cut, end = 5 * 384, inner + 3 * STATE
+    cut, block, end = 5 * 384, 384, inner + 3 * STATE
     pairs = [
         outer_sum(in_own, in_sib, z_rows, 0, inner, 2 * WIDE),
         outer_sum(in_own, in_sib, v_rows, 0, cut, 640),
-        outer_sum(in_own, in_sib, v_rows, cut, end, 384),
     ]
+    pairs += [outer_sum(in_own, in_sib, v_rows, a, a + 2 * block, block) for a in range(cut, end, 2 * block)]
     pairs[0], out_far = lax.optimization_barrier((pairs[0], out_far))
     sums, _ = lax.optimization_barrier((sums, pairs[-1][1]))
     sums = sums + swap(sums, axis, 1)
     chunks = [(out_keep, out_far)] + [(keep, swap(send, axis, 2)) for keep, send in pairs]
-    parts, sums = owned_sums(chunks, axis, sums)
+    parts, sums = owned_sums(chunks, axis, sums, [send for _, send in pairs[1:]])
     out_grad, in_grad = parts[0], jnp.concatenate(parts[1:], axis=1)[:, :proj_cols]
 
     place = lax.axis_index(axis)

time: 595 us -> 585 us (0.983)
  other arithmetic: 34.8 us -> 27.7 us
    ppermute x28 -> x31, waiting for transfers between devices: 131 us -> 128 us  [swap(): lax.ppermute(values, axis, [(a, a ^ bit) for a in range(lax.axis_size(axi...]
    pallas_call x4 -> x5, Pallas kernels: 31.3 us -> 33.4 us  [outer_sum(): pl.pallas_call(outer_kernel, grid=(steps,), in_specs=[full, full] + [pl.B...]
    ppermute x28 -> x31, starting transfers between devices: 29.5 us -> 30.5 us  [swap(): lax.ppermute(values, axis, [(a, a ^ bit) for a in range(lax.axis_size(axi...]
  transfers between devices with their start and end apart: 33 -> 36, of which waited for: 21 -> 21; matrix products, arithmetic and copies ran while one was open for 7% -> 6% of each run, Pallas kernels for 20% -> 22%
where the time goes in v4:
time: 585 us; the launch traced here: 575 us
  waiting for transfers between devices  326 us (56%)
  Pallas kernels  152 us (26%)
  starting transfers between devices  35.8 us (6%)
  other arithmetic  27.7 us (5%)
  local copies, waits for them, and re-layouts  18.4 us (3%)
  between operations  15.2 us (3%)
    all_gather x1, waiting for transfers between devices, body(): lax.all_gather(pack(in_weight[0], out_weight[0], inner), axis, axis=0, ti...  130 us
    ppermute x31, waiting for transfers between devices, swap(): lax.ppermute(values, axis, [(a, a ^ bit) for a in range(lax.axis_size(axi...  128 us
    pallas_call x4, Pallas kernels, backward_slot(): pl.pallas_call(functools.partial(backward_kernel, place), in_specs=in_spe...  64.7 us
    ppermute x2, waiting for transfers between devices, body(): returned[m] = lax.ppermute(late_grads[m], 'section', [(1, 0)])  51.6 us
    pallas_call x4, Pallas kernels, forward_slot(): pl.pallas_call(functools.partial(forward_kernel, place), in_specs=in_spec...  42.8 us
    pallas_call x5, Pallas kernels, outer_sum(): pl.pallas_call(outer_kernel, grid=(steps,), in_specs=[full, full] + [pl.B...  33.4 us
    ppermute x31, starting transfers between devices, swap(): lax.ppermute(values, axis, [(a, a ^ bit) for a in range(lax.axis_size(axi...  30.5 us
    ppermute x2, waiting for transfers between devices, body(): arrived = [lax.ppermute(h, 'section', [(0, 1)]) for h in first]  15.6 us
  transfers between devices with their start and end apart: 36, of which 21 were waited for; matrix products, arithmetic and copies ran while one was open for 6% of the time, Pallas kernels for 22%

profile of v4, /device:TPU:8, one launch (start us, length us, event | category | flops | bytes accessed | tf_op | source)
XLA Modules:
  0.0 574.9 jit_solution(7196548114241405798)
XLA Ops:
  21.6 3.4 collective-permute-done.2
  33.8 130.4 %all-gather.2.cloned.1.call-done.w_hbm = bf16[3072,4864]{1,0:T(8,128)(2,1)} async-done(((bf16[192,4864]{1,0:T(8,128)(2,1)}), bf16[3072,4864]{1,0:T(8,128)(2,1)}) %all-gather.2.cloned.1.call-update) | async-done | bytes 29884432 | tf_op jit(solution)/shard_map/all_gather | solution.py:807
  164.2 19.8 %forward_slot.4 = (bf16[4,256,1536]{2,1,0:T(8,128)(2,1)}, bf16[4,256,3072]{2,1,0:T(8,128)(2,1)}, f32[4,256,3072]{2,1,0:T(8,128)}, f32[4,256,3072]{2,1,0:T(8,128)...) custom-call(s32[2]{0:T(128)} %pad_add_fusion.1.at_ref, ...), custom_call_target="tpu_custom_call" | custom-call | flops 22000001024 | bytes 60000000 | tf_op jit(solution)/shard_map/forward_slot/pallas_call | solution.py:271
  185.3 20.0 %forward_slot.5 = (bf16[4,256,1536]{2,1,0:T(8,128)(2,1)}, bf16[4,256,3072]{2,1,0:T(8,128)(2,1)}, f32[4,256,3072]{2,1,0:T(8,128)}, f32[4,256,3072]{2,1,0:T(8,128)...) custom-call(s32[2]{0:T(128)} %pad_add_fusion.at_ref, ...), custom_call_target="tpu_custom_call", output_to_operand_aliasing={{0}: (9, {}), {1}: (10, {}), {2}: (11, {}), {3}: (12, {}), ... | custom-call | flops 22000001024 | bytes 60000000 | tf_op jit(solution)/shard_map/forward_slot/pallas_call | solution.py:271
  208.9 15.6 %collective-permute-done.5.u_hbm = bf16[256,1536]{1,0:T(8,128)(2,1)S(1)} collective-permute-done((bf16[256,1536]{1,0:T(8,128)(2,1)}, bf16[256,1536]{1,0:T(8,128)(2,1)S(1)}, u32[]{:S(2)}, u32[]{:S(2)}) %collective-permute-start.5) | collective-permute-done | bytes 786464 | tf_op jit(solution)/shard_map/ppermute | solution.py:836
  237.4 4.6 by_owner.2
  242.0 3.5 by_owner.3
  245.5 51.4 %collective-permute-done.7.g_hbm = bf16[256,1536]{1,0:T(8,128)(2,1)S(1)} collective-permute-done((bf16[256,1536]{1,0:T(8,128)(2,1)}, bf16[256,1536]{1,0:T(8,128)(2,1)S(1)}, u32[]{:S(2)}, u32[]{:S(2)}) %collective-permute-start.7) | collective-permute-done | bytes 786464 | tf_op jit(solution)/shard_map/ppermute | solution.py:854
  297.8 29.7 %backward_slot.6 = (bf16[256,1536]{1,0:T(8,128)(2,1)}, bf16[256,3072]{1,0:T(8,128)(2,1)}, bf16[256,3456]{1,0:T(8,128)(2,1)}, f32[8,3328]{1,0:T(8,128)}) custom-call(s32[2]{0:T(128)} %pad_add_fusion.at_ref, bf16[256,1536]{1,0:T(8,128)(2,1)} %copy-done.7, bf16[256,1536]{1,0:T(8,128)(2,1)} %get-tuple-element.190.u_hbm, ...), custom_call_target="tpu_custom_call", output_to_operand_aliasing={{1}: (16, {}), {2}: (17, {})} | custom-call | flops 1000000000 | bytes 1000000 | tf_op jit(solution)/shard_map/backward_slot/pallas_call | solution.py:593
  335.0 8.7 %outer_sum.5 = (bf16[768,1536]{1,0:T(8,128)(2,1)}, bf16[768,1536]{1,0:T(8,128)(2,1)}) custom-call(bf16[2,2,768,256]{3,2,1,0:T(8,128)(2,1)} %bitcast.146, bf16[2,2,768,256]{3,2,1,0:T(8,128)(2,1)} %collective-permute-done.8.sib_ref, bf16[256,1536]{1,0:T(8,128)(2,1)} %copy-done.9, bf16[256,1536]{1,0:T(8,128)(2,1)} %copy-done.8, bf16[256,1536]{1,0:T(8,128)(2,1)} %copy-done.23, ...), custom_call_target="tpu_custom_call" | custom-call | flops 1000000000 | bytes 1000000 | tf_op jit(solution)/shard_map/outer_sum/pallas_call | solution.py:718
  344.8 29.9 %backward_slot.7 = (bf16[256,1536]{1,0:T(8,128)(2,1)}, bf16[256,3072]{1,0:T(8,128)(2,1)}, bf16[256,3456]{1,0:T(8,128)(2,1)}, f32[8,3328]{1,0:T(8,128)}) custom-call(s32[2]{0:T(128)} %pad_add_fusion.1.at_ref, bf16[256,1536]{1,0:T(8,128)(2,1)} %copy-done.6, ...), custom_call_target="tpu_custom_call", output_to_operand_aliasing={{1}: (16, {}), {2}: (17, {})} | custom-call | flops 1000000000 | bytes 1000000 | tf_op jit(solution)/shard_map/backward_slot/pallas_call | solution.py:593
  375.8 5.4 collective-permute-done.13.rest_3_
  383.4 8.6 %outer_sum.6 = (bf16[384,3072]{1,0:T(8,128)(2,1)}, bf16[384,3072]{1,0:T(8,128)(2,1)}) custom-call(bf16[2,2,384,256]{3,2,1,0:T(8,128)(2,1)} %bitcast.136, bf16[2,2,384,256]{3,2,1,0:T(8,128)(2,1)} %collective-permute-done.11.sib_ref, bf16[256,3072]{1,0:T(8,128)(2,1)} %get-tuple-element.154.rest_0_, bf16[256,3072]{1,0:T(8,128)(2,1)} %get-tuple-element.155.rest_1_, ...), custom_call_target="tpu_custom_call" | custom-call | flops 1000000000 | bytes 1000000 | tf_op jit(solution)/shard_map/outer_sum/pallas_call | solution.py:718
  393.4 6.8 %outer_sum.7 = (bf16[384,1920]{1,0:T(8,128)(2,1)}, bf16[384,1920]{1,0:T(8,128)(2,1)}) custom-call(bf16[2,2,384,256]{3,2,1,0:T(8,128)(2,1)} %bitcast.137, bf16[2,2,384,256]{3,2,1,0:T(8,128)(2,1)} %collective-permute-done.11.sib_ref, bf16[256,3456]{1,0:T(8,128)(2,1)} %get-tuple-element.163.rest_0_, bf16[256,3456]{1,0:T(8,128)(2,1)} %get-tuple-element.164.rest_1_, ...), custom_call_target="tpu_custom_call" | custom-call | flops 1000000000 | bytes 1000000 | tf_op jit(solution)/shard_map/outer_sum/pallas_call | solution.py:718
  404.6 4.6 outer_sum.9
  409.1 4.7 outer_sum.8
  413.9 17.7 %collective-permute-done.18 = bf16[2,192,1536]{2,1,0:T(8,128)(2,1)S(1)} collective-permute-done((bf16[2,192,1536]{2,1,0:T(8,128)(2,1)}, bf16[2,192,1536]{2,1,0:T(8,128)(2,1)S(1)}, u32[]{:S(2)}, u32[]{:S(2)}) %collective-permute-start.18) | collective-permute-done | bytes 1179680 | tf_op jit(solution)/shard_map/ppermute | solution.py:735
  435.5 24.4 %collective-permute-done.19 = bf16[1,192,1536]{2,1,0:T(8,128)(2,1)S(1)} collective-permute-done((bf16[1,192,1536]{2,1,0:T(8,128)(2,1)S(1)}, bf16[1,192,1536]{2,1,0:T(8,128)(2,1)S(1)}, u32[]{:S(2)}, u32[]{:S(2)}) %collective-permute-start.19) | collective-permute-done | bytes 589856 | tf_op jit(solution)/shard_map/ppermute | solution.py:735
  466.7 22.3 %collective-permute-done.20 = bf16[2,96,3072]{2,1,0:T(8,128)(2,1)S(1)} collective-permute-done((bf16[2,96,3072]{2,1,0:T(8,128)(2,1)S(1)}, bf16[2,96,3072]{2,1,0:T(8,128)(2,1)S(1)}, u32[]{:S(2)}, u32[]{:S(2)}) %collective-permute-start.20) | collective-permute-done | bytes 1179680 | tf_op jit(solution)/shard_map/ppermute | solution.py:735
  500.0 19.0 %collective-permute-done.23 = bf16[2,96,1920]{2,1,0:T(8,128)(2,1)S(1)} collective-permute-done((bf16[2,96,1920]{2,1,0:T(8,128)(2,1)S(1)}, bf16[2,96,1920]{2,1,0:T(8,128)(2,1)S(1)}, u32[]{:S(2)}, u32[]{:S(2)}) %collective-permute-start.23) | collective-permute-done | bytes 737312 | tf_op jit(solution)/shard_map/ppermute | solution.py:735
  521.9 8.7 %collective-permute-done.21 = bf16[1,96,3072]{2,1,0:T(8,128)(2,1)S(1)} collective-permute-done((bf16[1,96,3072]{2,1,0:T(8,128)(2,1)S(1)}, bf16[1,96,3072]{2,1,0:T(8,128)(2,1)S(1)}, u32[]{:S(2)}, u32[]{:S(2)}) %collective-permute-start.21) | collective-permute-done | bytes 589856 | tf_op jit(solution)/shard_map/ppermute | solution.py:735
  540.3 5.6 collective-permute-done.32
  545.9 4.0 collective-permute-done.31
  553.7 6.7 %collective-permute-done.34 = f32[8,3328]{1,0:T(8,128)S(1)} collective-permute-done((f32[8,3328]{1,0:T(8,128)S(1)}, f32[8,3328]{1,0:T(8,128)S(1)}, u32[]{:S(2)}, u32[]{:S(2)}) %collective-permute-start.34) | collective-permute-done | bytes 106528 | tf_op jit(solution)/shard_map/ppermute | solution.py:735
  (223 shorter events, 104.2 us)
Async XLA Ops:
  7.2 157.0 %all-gather.2.cloned.1.call-start = ((), (), s32[]{:S(2)}) async-start(), calls=%async_computation | async-start | bytes 31752192 | tf_op jit(solution)/shard_map/all_gather | solution.py:807
  184.0 22.7 %collective-permute-start.4 = (bf16[256,1536]{1,0:T(8,128)(2,1)}, bf16[256,1536]{1,0:T(8,128)(2,1)S(1)}, u32[]{:S(2)}, u32[]{:S(2)}) collective-permute-start(bf16[256,1536]{1,0:T(8,128)(2,1)} %get-tuple-element.98), channel_id=1, source_target_pairs={{0,16},{1,17},{2,18},{3,19},{4,20},{5,21},{6,22},{7,23},{8,24},{9,... | collective-permute-start | bytes 2359304 | tf_op jit(solution)/shard_map/ppermute | solution.py:836
  205.3 19.1 %collective-permute-start.5 = (bf16[256,1536]{1,0:T(8,128)(2,1)}, bf16[256,1536]{1,0:T(8,128)(2,1)S(1)}, u32[]{:S(2)}, u32[]{:S(2)}) collective-permute-start(bf16[256,1536]{1,0:T(8,128)(2,1)} %get-tuple-element.114), channel_id=1, source_target_pairs={{0,16},{1,17},{2,18},{3,19},{4,20},{5,21},{6,22},{7,23},{8,24},{9,... | collective-permute-start | bytes 2359304 | tf_op jit(solution)/shard_map/ppermute | solution.py:836
  229.9 67.0 %collective-permute-start.7 = (bf16[256,1536]{1,0:T(8,128)(2,1)}, bf16[256,1536]{1,0:T(8,128)(2,1)S(1)}, u32[]{:S(2)}, u32[]{:S(2)}) collective-permute-start(bf16[256,1536]{1,0:T(8,128)(2,1)} %get-tuple-element.131), channel_id=1, source_target_pairs={{16,0},{17,1},{18,2},{19,3},{20,4},{21,5},{22,6},{23,7},{24,8},{25... | collective-permute-start | bytes 2359304 | tf_op jit(solution)/shard_map/ppermute | solution.py:854
  234.2 93.6 %collective-permute-start.6 = (bf16[256,1536]{1,0:T(8,128)(2,1)}, bf16[256,1536]{1,0:T(8,128)(2,1)S(1)}, u32[]{:S(2)}, u32[]{:S(2)}) collective-permute-start(bf16[256,1536]{1,0:T(8,128)(2,1)} %get-tuple-element.130), channel_id=1, source_target_pairs={{16,0},{17,1},{18,2},{19,3},{20,4},{21,5},{22,6},{23,7},{24,8},{25... | collective-permute-start | bytes 2359304 | tf_op jit(solution)/shard_map/ppermute | solution.py:854
  242.0 92.9 %collective-permute-start.8 = (bf16[2,2,768,256]{3,2,1,0:T(8,128)(2,1)}, bf16[2,2,768,256]{3,2,1,0:T(8,128)(2,1)}, u32[]{:S(2)}, u32[]{:S(2)}) collective-permute-start(bf16[2,2,768,256]{3,2,1,0:T(8,128)(2,1)} %bitcast.171), channel_id=1, source_target_pairs={{0,1},{1,0},{2,3},{3,2},{4,5},{5,4},{6,7},{7,6},{8,9},{9,8},{10,11... | collective-permute-start | bytes 4718600 | tf_op jit(solution)/shard_map/ppermute | solution.py:735
  330.0 45.3 %collective-permute-start.11 = (bf16[2,2,384,256]{3,2,1,0:T(8,128)(2,1)}, bf16[2,2,384,256]{3,2,1,0:T(8,128)(2,1)}, u32[]{:S(2)}, u32[]{:S(2)}) collective-permute-start(bf16[2,2,384,256]{3,2,1,0:T(8,128)(2,1)} %bitcast.30), channel_id=1, source_target_pairs={{0,1},{1,0},{2,3},{3,2},{4,5},{5,4},{6,7},{7,6},{8,9},{9,8},{10,11... | collective-permute-start | bytes 2359304 | tf_op jit(solution)/shard_map/ppermute | solution.py:735
  343.7 56.5 %collective-permute-start.14 = (bf16[768,1536]{1,0:T(8,128)(2,1)}, bf16[768,1536]{1,0:T(8,128)(2,1)}, u32[]{:S(2)}, u32[]{:S(2)}) collective-permute-start(bf16[768,1536]{1,0:T(8,128)(2,1)} %get-tuple-element.158), channel_id=1, source_target_pairs={{0,2},{1,3},{2,0},{3,1},{4,6},{5,7},{6,4},{7,5},{8,10},{9,11},{10,... | collective-permute-start | bytes 7077896 | tf_op jit(solution)/shard_map/ppermute | solution.py:735
  344.8 47.3 %collective-permute-start.17 = (bf16[256,3456]{1,0:T(8,128)(2,1)S(1)}, bf16[256,3456]{1,0:T(8,128)(2,1)S(1)}, u32[]{:S(2)}, u32[]{:S(2)}) collective-permute-start(bf16[256,3456]{1,0:T(8,128)(2,1)S(1)} %copy-done), channel_id=1, source_target_pairs={{0,1},{1,0},{2,3},{3,2},{4,5},{5,4},{6,7},{7,6},{8,9},{9,8},{10,11... | collective-permute-start | bytes 5308424 | tf_op jit(solution)/shard_map/ppermute | solution.py:735
  374.7 17.4 %collective-permute-start.16 = (bf16[256,3456]{1,0:T(8,128)(2,1)}, bf16[256,3456]{1,0:T(8,128)(2,1)}, u32[]{:S(2)}, u32[]{:S(2)}) collective-permute-start(bf16[256,3456]{1,0:T(8,128)(2,1)} %get-tuple-element.163.rest_0_), channel_id=1, source_target_pairs={{0,1},{1,0},{2,3},{3,2},{4,5},{5,4},{6,7},{7,6},{8,9},{9,8},{10,11... | collective-permute-start | bytes 5308424 | tf_op jit(solution)/shard_map/ppermute | solution.py:735
  403.1 28.5 %collective-permute-start.18 = (bf16[2,192,1536]{2,1,0:T(8,128)(2,1)}, bf16[2,192,1536]{2,1,0:T(8,128)(2,1)S(1)}, u32[]{:S(2)}, u32[]{:S(2)}) collective-permute-start(bf16[2,192,1536]{2,1,0:T(8,128)(2,1)} %fusion.1), channel_id=1, source_target_pairs={{0,4},{1,5},{2,6},{3,7},{4,0},{5,1},{6,2},{7,3},{8,12},{9,13},{10,... | collective-permute-start | bytes 3538952 | tf_op jit(solution)/shard_map/ppermute | solution.py:735
  403.7 56.2 %collective-permute-start.15 = (bf16[384,3072]{1,0:T(8,128)(2,1)}, bf16[384,3072]{1,0:T(8,128)(2,1)}, u32[]{:S(2)}, u32[]{:S(2)}) collective-permute-start(bf16[384,3072]{1,0:T(8,128)(2,1)} %get-tuple-element.160), channel_id=1, source_target_pairs={{0,2},{1,3},{2,0},{3,1},{4,6},{5,7},{6,4},{7,5},{8,10},{9,11},{10,... | collective-permute-start | bytes 7077896 | tf_op jit(solution)/shard_map/ppermute | solution.py:735
  433.0 26.9 %collective-permute-start.19 = (bf16[1,192,1536]{2,1,0:T(8,128)(2,1)S(1)}, bf16[1,192,1536]{2,1,0:T(8,128)(2,1)S(1)}, u32[]{:S(2)}, u32[]{:S(2)}) collective-permute-start(bf16[1,192,1536]{2,1,0:T(8,128)(2,1)S(1)} %fusion.5), channel_id=1, source_target_pairs={{0,8},{1,9},{2,10},{3,11},{4,12},{5,13},{6,14},{7,15},{8,0},{9,1},... | collective-permute-start | bytes 1769480 | tf_op jit(solution)/shard_map/ppermute | solution.py:735
  435.1 55.2 %collective-permute-start.22 = (bf16[384,1920]{1,0:T(8,128)(2,1)S(1)}, bf16[384,1920]{1,0:T(8,128)(2,1)S(1)}, u32[]{:S(2)}, u32[]{:S(2)}) collective-permute-start(bf16[384,1920]{1,0:T(8,128)(2,1)S(1)} %copy-done.38), channel_id=1, source_target_pairs={{0,2},{1,3},{2,0},{3,1},{4,6},{5,7},{6,4},{7,5},{8,10},{9,11},{10,... | collective-permute-start | bytes 4423688 | tf_op jit(solution)/shard_map/ppermute | solution.py:735
  461.6 27.4 %collective-permute-start.20 = (bf16[2,96,3072]{2,1,0:T(8,128)(2,1)S(1)}, bf16[2,96,3072]{2,1,0:T(8,128)(2,1)S(1)}, u32[]{:S(2)}, u32[]{:S(2)}) collective-permute-start(bf16[2,96,3072]{2,1,0:T(8,128)(2,1)S(1)} %fusion.2), channel_id=1, source_target_pairs={{0,4},{1,5},{2,6},{3,7},{4,0},{5,1},{6,2},{7,3},{8,12},{9,13},{10,... | collective-permute-start | bytes 3538952 | tf_op jit(solution)/shard_map/ppermute | solution.py:735
  466.6 29.1 %collective-permute-start.29 = (f32[8,3328]{1,0:T(8,128)S(1)}, f32[8,3328]{1,0:T(8,128)S(1)}, u32[]{:S(2)}, u32[]{:S(2)}) collective-permute-start(f32[8,3328]{1,0:T(8,128)S(1)} %copy-done.29), channel_id=1, source_target_pairs={{0,1},{1,0},{2,3},{3,2},{4,5},{5,4},{6,7},{7,6},{8,9},{9,8},{10,11... | collective-permute-start | bytes 319496 | tf_op jit(solution)/shard_map/ppermute | solution.py:735
  490.5 28.5 %collective-permute-start.23 = (bf16[2,96,1920]{2,1,0:T(8,128)(2,1)S(1)}, bf16[2,96,1920]{2,1,0:T(8,128)(2,1)S(1)}, u32[]{:S(2)}, u32[]{:S(2)}) collective-permute-start(bf16[2,96,1920]{2,1,0:T(8,128)(2,1)S(1)} %fusion.6), channel_id=1, source_target_pairs={{0,4},{1,5},{2,6},{3,7},{4,0},{5,1},{6,2},{7,3},{8,12},{9,13},{10,... | collective-permute-start | bytes 2211848 | tf_op jit(solution)/shard_map/ppermute | solution.py:735
  493.6 28.1 %collective-permute-start.25 = (bf16[384,768]{1,0:T(8,128)(2,1)S(1)}, bf16[384,768]{1,0:T(8,128)(2,1)S(1)}, u32[]{:S(2)}, u32[]{:S(2)}) collective-permute-start(bf16[384,768]{1,0:T(8,128)(2,1)S(1)} %copy-done.40), channel_id=1, source_target_pairs={{0,2},{1,3},{2,0},{3,1},{4,6},{5,7},{6,4},{7,5},{8,10},{9,11},{10,... | collective-permute-start | bytes 1769480 | tf_op jit(solution)/shard_map/ppermute | solution.py:735
  494.5 42.5 %collective-permute-start.28 = (bf16[384,768]{1,0:T(8,128)(2,1)S(1)}, bf16[384,768]{1,0:T(8,128)(2,1)S(1)}, u32[]{:S(2)}, u32[]{:S(2)}) collective-permute-start(bf16[384,768]{1,0:T(8,128)(2,1)S(1)} %copy-done.39), channel_id=1, source_target_pairs={{0,2},{1,3},{2,0},{3,1},{4,6},{5,7},{6,4},{7,5},{8,10},{9,11},{10,... | collective-permute-start | bytes 1769480 | tf_op jit(solution)/shard_map/ppermute | solution.py:735
  495.7 41.3 %collective-permute-start.30 = (f32[8,3328]{1,0:T(8,128)S(1)}, f32[8,3328]{1,0:T(8,128)S(1)}, u32[]{:S(2)}, u32[]{:S(2)}) collective-permute-start(f32[8,3328]{1,0:T(8,128)S(1)} %add.427), channel_id=1, source_target_pairs={{0,2},{1,3},{2,0},{3,1},{4,6},{5,7},{6,4},{7,5},{8,10},{9,11},{10,... | collective-permute-start | bytes 319496 | tf_op jit(solution)/shard_map/ppermute | solution.py:735
  496.6 34.0 %collective-permute-start.21 = (bf16[1,96,3072]{2,1,0:T(8,128)(2,1)S(1)}, bf16[1,96,3072]{2,1,0:T(8,128)(2,1)S(1)}, u32[]{:S(2)}, u32[]{:S(2)}) collective-permute-start(bf16[1,96,3072]{2,1,0:T(8,128)(2,1)S(1)} %fusion.4), channel_id=1, source_target_pairs={{0,8},{1,9},{2,10},{3,11},{4,12},{5,13},{6,14},{7,15},{8,0},{9,1},... | collective-permute-start | bytes 1769480 | tf_op jit(solution)/shard_map/ppermute | solution.py:735
  519.2 20.9 %collective-permute-start.24 = (bf16[1,96,1920]{2,1,0:T(8,128)(2,1)S(1)}, bf16[1,96,1920]{2,1,0:T(8,128)(2,1)S(1)}, u32[]{:S(2)}, u32[]{:S(2)}) collective-permute-start(bf16[1,96,1920]{2,1,0:T(8,128)(2,1)S(1)} %fusion.7), channel_id=1, source_target_pairs={{0,8},{1,9},{2,10},{3,11},{4,12},{5,13},{6,14},{7,15},{8,0},{9,1},... | collective-permute-start | bytes 1105928 | tf_op jit(solution)/shard_map/ppermute | solution.py:735
  521.8 12.5 %collective-permute-start.26 = (bf16[2,96,768]{2,1,0:T(8,128)(2,1)S(1)}, bf16[2,96,768]{2,1,0:T(8,128)(2,1)S(1)}, u32[]{:S(2)}, u32[]{:S(2)}) collective-permute-start(bf16[2,96,768]{2,1,0:T(8,128)(2,1)S(1)} %fusion.8), channel_id=1, source_target_pairs={{0,4},{1,5},{2,6},{3,7},{4,0},{5,1},{6,2},{7,3},{8,12},{9,13},{10,... | collective-permute-start | bytes 884744 | tf_op jit(solution)/shard_map/ppermute | solution.py:735
  534.4 18.4 %collective-permute-start.27 = (bf16[1,96,768]{2,1,0:T(8,128)(2,1)S(1)}, bf16[1,96,768]{2,1,0:T(8,128)(2,1)S(1)}, u32[]{:S(2)}, u32[]{:S(2)}) collective-permute-start(bf16[1,96,768]{2,1,0:T(8,128)(2,1)S(1)} %fusion.11), channel_id=1, source_target_pairs={{0,8},{1,9},{2,10},{3,11},{4,12},{5,13},{6,14},{7,15},{8,0},{9,1},... | collective-permute-start | bytes 442376 | tf_op jit(solution)/shard_map/ppermute | solution.py:735
  (53 other events, 492.2 us)
Sparse Core Ops, SparseCore 0:
  10.2 153.8 all-gather.1

commit v5 on v4

--- a/solution.py
+++ b/solution.py
@@ -670,19 +670,19 @@
 
 def order_kernel(at_ref, a_ref, own_ref, other_ref, turn_scr):
     turn_scr[...] = a_ref[0].astype(F32).T.reshape(turn_scr.shape)
-    for part in range(2):
-        for line in range(own_ref.shape[2]):
-            own_ref[part, 0, line] = turn_scr[4 * line + at_ref[1 + 2 * part]].astype(BF16)
-            other_ref[part, 0, line] = turn_scr[4 * line + at_ref[2 + 2 * part]].astype(BF16)
-
-
-def by_owner(numbers, values, micro, count):
+    spots = own_ref.shape[1]
+    for spot in range(spots):
+        own_ref[0, spot] = turn_scr[at_ref[1 + spot]].astype(BF16)
+        other_ref[0, spot] = turn_scr[at_ref[1 + spots + spot]].astype(BF16)
+
+
+def by_owner(table, values, micro):
     _, rows, total = values.shape
+    count = table.shape[0] - 1
     depth = total // count
-    line = count // 4
-    out = pl.BlockSpec((2, 1, line, depth, rows), lambda i, n: (0, i, 0, 0, 0))
-    made = jax.ShapeDtypeStruct((2, micro, line, depth, rows), BF16)
-    own, other = pl.pallas_call(
+    out = pl.BlockSpec((1, count // 2, depth, rows), lambda i, n: (i, 0, 0, 0))
+    made = jax.ShapeDtypeStruct((micro, count // 2, depth, rows), BF16)
+    parts = pl.pallas_call(
         order_kernel,
         grid_spec=pltpu.PrefetchScalarGridSpec(
             num_scalar_prefetch=1,
@@ -695,40 +695,48 @@
         compiler_params=pltpu.CompilerParams(vmem_limit_bytes=VMEM),
         cost_estimate=pl.CostEstimate(flops=3 * 10**9, bytes_accessed=2 * 10**6, transcendentals=0),
         name="by_owner",
-    )(numbers, values)
-    flat = (2, micro, line * depth, rows)
-    return own.reshape(flat), other.reshape(flat)
-
-
-def outer_kernel(own_ref, sib_ref, *rest):
+    )(table, values)
+    return [a.reshape(micro, total // 2, rows) for a in parts]
+
+
+def outer_kernel(with_extra, own_ref, sib_ref, *rest):
     rights, outs = rest[:-2], rest[-2:]
-    micro = own_ref.shape[1]
+    micro, high = own_ref.shape[0], outs[0].shape[0]
+    if with_extra:
+        extra_ref, rights = rights[-1], rights[:-1]
     right = jnp.concatenate([ref[...] for ref in rights], axis=0)
     for part, out_ref in enumerate(outs):
-        left = jnp.concatenate([ref[part, m] for ref in (own_ref, sib_ref) for m in range(micro)], axis=1)
-        out_ref[...] = nn_dot(left, right).astype(BF16)
-
-
-def outer_sum(own, sib, rights, start, stop, block):
-    _, micro, high, rows = own.shape
+        rows = slice(part * high, (part + 1) * high)
+        left = jnp.concatenate([ref[m, rows] for ref in (own_ref, sib_ref) for m in range(micro)], axis=1)
+        total = nn_dot(left, right)
+        out_ref[...] = total.astype(BF16)
+        if with_extra:
+            extra = extra_ref[rows, :]
+
+            @pl.when(pl.program_id(0) == pl.num_programs(0) - 1)
+            def _():
+                out_ref[:, -HALF:] = (total[:, -HALF:] + extra).astype(BF16)
+
+
+def outer_sum(own, sib, rights, start, stop, block, extra=None):
+    _, total, rows = own.shape
     low, steps = start // block, (stop - start) // block
-    full = pl.BlockSpec(own.shape, lambda i: (0, 0, 0, 0))
-    out = pl.BlockSpec((high, block), lambda i: (0, i))
-    made = jax.ShapeDtypeStruct((high, stop - start), BF16)
+    full = pl.BlockSpec(own.shape, lambda i: (0, 0, 0))
+    out = pl.BlockSpec((total // 2, block), lambda i: (0, i))
+    made = jax.ShapeDtypeStruct((total // 2, stop - start), BF16)
+    more = [] if extra is None else [extra]
     return pl.pallas_call(
-        outer_kernel,
+        functools.partial(outer_kernel, extra is not None),
         grid=(steps,),
-        in_specs=[full, full] + [pl.BlockSpec((rows, block), lambda i: (0, low + i)) for _ in rights],
+        in_specs=[full, full]
+        + [pl.BlockSpec((rows, block), lambda i: (0, low + i)) for _ in rights]
+        + [pl.BlockSpec(a.shape, lambda i: (0, 0)) for a in more],
         out_specs=[out, out],
         out_shape=[made, made],
         compiler_params=pltpu.CompilerParams(vmem_limit_bytes=VMEM),
         cost_estimate=pl.CostEstimate(flops=10**9, bytes_accessed=10**6, transcendentals=0),
         name="outer_sum",
-    )(own, sib, *rights)
-
-
-def pick(values, index, axis):
-    return lax.dynamic_index_in_dim(values, index, axis, keepdims=False)
+    )(own, sib, *rights, *more)
 
 
 def swap(values, axis, bit):
@@ -746,38 +754,22 @@
     return table
 
 
-def owned_sums(chunks, axis, rider, ahead):
-    count = lax.axis_size(axis)
-    length = count // 4
-    results, token = [], None
-    rider_far = swap(rider, axis, 2)
-    for k, (keep, far) in enumerate(chunks):
-        rides = k == len(chunks) - 1
-        if token is not None:
-            far, _ = lax.optimization_barrier((far, token))
-        if rides:
-            far, rider_far = lax.optimization_barrier((far, rider_far))
-            rider = rider + rider_far
-        if k == 0:
-            far, _ = lax.optimization_barrier((far, ahead[0]))
-        terms = [a.reshape(length, -1, a.shape[1]) for a in (keep, far)]
-        bit = 1
-        while bit < length:
-            mine = (lax.axis_index(axis) // (4 * bit)) % 2
-            half = lambda a, which: pick(a.reshape((-1, 2) + a.shape[1:]), which, 1)
-            sent = sum(half(a, 1 - mine).astype(F32) for a in terms).astype(BF16)
-            if rides:
-                sent, rider = lax.optimization_barrier((sent, rider))
-            if k == 0 and bit > 1:
-                sent, _ = lax.optimization_barrier((sent, ahead[1:]))
-            came = swap(sent, axis, 4 * bit)
-            if rides:
-                rider = rider + swap(rider, axis, 4 * bit)
-            terms = [half(a, mine) for a in terms] + [came]
-            token = came if k == 0 else sent
-            bit *= 2
-        results.append(sum(a[0].astype(F32) for a in terms))
-    return results, rider
+def held(value, *after):
+    return lax.optimization_barrier((value, after))[0]
+
+
+def total_of(terms):
+    return sum(a.astype(F32) for a in terms)
+
+
+def exchange(terms, axis, bit):
+    half = terms[0].shape[0] // 2
+    sent = total_of([a[half:] for a in terms]).astype(BF16)
+    return [a[:half] for a in terms] + [swap(sent, axis, bit)], sent
+
+
+def spots_of(order):
+    return [sum(bit for k, bit in enumerate(order) if p >> (len(order) - 1 - k) & 1) for p in range(2 ** len(order))]
 
 
 def body(
@@ -853,11 +845,17 @@
         late_grads[m], *grads[m], sums = run_backward(micro + m, m, 1, None, sums, cotangent[m], arrived[m])
         returned[m] = lax.ppermute(late_grads[m], "section", [(1, 0)])
 
-    mine = (lax.axis_index(axis) % 4).astype(jnp.int32)
-    owners = jnp.stack([section * micro, mine, mine ^ 1, mine ^ 2, mine ^ 3]).astype(jnp.int32)
+    place = lax.axis_index(axis).astype(jnp.int32)
+    line = [4 << k for k in range(count.bit_length() - 3)]
+    in_order, out_order = [2] + line, line + [2]
+
+    def table_of(order):
+        spots = jnp.array(spots_of(order), jnp.int32)
+        return jnp.concatenate([(section * micro)[None].astype(jnp.int32), place ^ spots, place ^ 1 ^ spots])
+
     nb, gb, _ = lax.optimization_barrier((kept[0], kept[1], late_grads[0]))
-    out_own, out_other = by_owner(owners, gb, micro, count)
-    in_own, in_other = by_owner(owners, nb, micro, count)
+    out_own, out_other = by_owner(table_of(out_order), gb, micro)
+    in_own, in_other = by_owner(table_of(in_order), nb, micro)
     out_sib, in_sib = swap(out_other, axis, 1), swap(in_other, axis, 1)
     returned[-1], out_own, in_own = lax.optimization_barrier((returned[-1], out_own, in_own))
 
@@ -873,9 +871,10 @@
         z_sib[m], v_sib[m] = (swap(a, axis, 1) for a in grads[m])
     returned[0], early_grads[-1] = lax.optimization_barrier((returned[0], early_grads[-1]))
     take_branch(0)
+
     out_keep, out_send = outer_sum(out_own, out_sib, branch + branch_sib, 0, width, WIDE)
-    returned[0], out_send = lax.optimization_barrier((returned[0], out_send))
-    out_far = swap(out_send, axis, 2)
+    returned[0] = held(returned[0], out_send)
+    out_terms = [out_keep, swap(out_send, axis, out_order[0])]
     early_grads[0], *grads[0], sums = run_backward(0, 0, 0, grads[0], sums, returned[0], block_input[0])
     z_sib[0], v_sib[0] = (swap(a, axis, 1) for a in grads[0])
     input_grads = jnp.stack([jnp.where(is_last, a, b) for a, b in zip(late_grads, early_grads)])
@@ -883,34 +882,80 @@
     z_rows = [a for a, _ in grads] + z_sib
     v_rows = [a for _, a in grads] + v_sib
     cut, block, end = 5 * 384, 384, inner + 3 * STATE
+    z_keep, z_send = outer_sum(in_own, in_sib, z_rows, 0, inner, 2 * WIDE)
+    (z_keep, z_send), out_terms[-1] = lax.optimization_barrier(((z_keep, z_send), out_terms[-1]))
+    token = z_send
+    for bit in out_order[1:-1]:
+        out_terms, token = exchange(out_terms, axis, bit)
+    sums, v_rows[0] = held((sums, v_rows[0]), token)
+    sums = sums + swap(sums, axis, 1)
+    per_owner = lambda rows: rows.reshape(-1, count, rows.shape[1] // count).transpose(1, 0, 2).reshape(count, -1)
+    skip_g = sums[6, :inner].reshape(heads, HEAD_DIM).sum(axis=1)
+    shared = jnp.concatenate([sums[7, width : width + heads], sums[7, width + HALF : width + HALF + heads], skip_g])
+    listed = jnp.concatenate(
+        [
+            per_owner(sums[:CONV]),
+            per_owner(sums[CONV : CONV + 1]),
+            per_owner(sums[7:8, :width]),
+            per_owner(sums[5:6, :inner]),
+            jnp.broadcast_to(shared, (count, shared.shape[0])),
+        ],
+        axis=1,
+    )
+    listed_cols = -(-listed.shape[1] // depth)
+    listed = jnp.pad(listed, ((0, 0), (0, listed_cols * depth - listed.shape[1]))).reshape(count, depth, listed_cols)
+    listed = jnp.take(listed, place ^ jnp.array(spots_of(in_order), jnp.int32), axis=0).reshape(width // 2, listed_cols)
+    at_lane = (proj_cols - inner) % HALF
+    extra = jnp.pad(listed, ((0, 0), (at_lane, HALF - at_lane - listed_cols)))
+    mid = end - 2 * block
     pairs = [
-        outer_sum(in_own, in_sib, z_rows, 0, inner, 2 * WIDE),
+        (z_keep, z_send),
         outer_sum(in_own, in_sib, v_rows, 0, cut, 640),
+        outer_sum(in_own, in_sib, v_rows, mid, end, block, extra),
+        outer_sum(in_own, in_sib, [held(v_rows[0], out_terms[-1])] + v_rows[1:], cut, mid, block),
     ]
-    pairs += [outer_sum(in_own, in_sib, v_rows, a, a + 2 * block, block) for a in range(cut, end, 2 * block)]
-    pairs[0], out_far = lax.optimization_barrier((pairs[0], out_far))
-    sums, _ = lax.optimization_barrier((sums, pairs[-1][1]))
-    sums = sums + swap(sums, axis, 1)
-    chunks = [(out_keep, out_far)] + [(keep, swap(send, axis, 2)) for keep, send in pairs]
-    parts, sums = owned_sums(chunks, axis, sums, [send for _, send in pairs[1:]])
-    out_grad, in_grad = parts[0], jnp.concatenate(parts[1:], axis=1)[:, :proj_cols]
-
-    place = lax.axis_index(axis)
-    cut_out = lambda row, size: lax.dynamic_slice(sums, (row, place * size), (1, size))
-    taps_g = lax.dynamic_slice(sums, (0, place * (channels // count)), (CONV, channels // count))
-    skip_g = sums[6, :inner].reshape(heads, HEAD_DIM).sum(axis=1)
+    sends = [send for _, send in pairs]
+    chunks = [[keep, swap(send, axis, 2)] for keep, send in pairs]
+    token, out_came = sends[:-1], out_terms[-1]
+    last = len(chunks) - 1
+
+    def first_step(k, token):
+        chunks[k][-1] = held(chunks[k][-1], token)
+        chunks[k], token = exchange(chunks[k], axis, line[0])
+        return token
+
+    def other_steps(k, token):
+        for bit in line[1:]:
+            chunks[k][-1] = held(chunks[k][-1], token)
+            chunks[k], token = exchange(chunks[k], axis, bit)
+        return token
+
+    token = first_step(0, token)
+    for k in range(1, last):
+        token = first_step(k, token)
+        token = other_steps(k - 1, (token, out_came) if k == 1 else token)
+    token = first_step(last, token)
+    out_terms[-1] = held(out_terms[-1], token)
+    out_terms, _ = exchange(out_terms, axis, 2)
+    token = other_steps(last - 1, token)
+    token = other_steps(last, token)
+    out_grad = total_of(out_terms)
+    in_parts = [total_of(terms) for terms in chunks]
+    tail = in_parts[2]
+    own_cols = proj_cols - inner - mid
+    in_grad = jnp.concatenate([in_parts[0], in_parts[1], in_parts[3], tail[:, :own_cols]], axis=1)
+    own_list = tail[:, own_cols : own_cols + listed_cols].reshape(-1)
+    cuts = [0]
+    for size in sizes + [heads] * 3:
+        cuts.append(cuts[-1] + size)
+    lists = [own_list[a:b] for a, b in zip(cuts[:-1], cuts[1:])]
     return (
         outputs[None],
         input_grads[None],
         in_grad[None],
         out_grad[None],
-        taps_g[None],
-        cut_out(4, channels // count),
-        cut_out(7, width // count),
-        cut_out(5, inner // count),
-        sums[7:8, width : width + heads],
-        sums[7:8, width + HALF : width + HALF + heads],
-        skip_g[None],
+        lists[0].reshape(1, CONV, -1),
+        *[one[None] for one in lists[1:]],
     )
 
 

time: 585 us -> 572 us (0.978)
  waiting for transfers between devices: 326 us -> 295 us
  other arithmetic: 27.7 us -> 45.2 us
    ppermute x31 -> x28, waiting for transfers between devices: 128 us -> 101 us  [swap(): lax.ppermute(values, axis, [(a, a ^ bit) for a in range(lax.axis_size(axi...]
    convert_element_type x10, other arithmetic: 8.55 us -> 15.5 us  [exchange(): sent = total_of([a[half:] for a in terms]).astype(BF16)]
    ppermute x31 -> x28, starting transfers between devices: 30.5 us -> 26.6 us  [swap(): lax.ppermute(values, axis, [(a, a ^ bit) for a in range(lax.axis_size(axi...]
  transfers between devices with their start and end apart: 36 -> 33, of which waited for: 21 -> 18; matrix products, arithmetic and copies ran while one was open for 6% -> 10% of each run, Pallas kernels for 22% -> 21%
where the time goes in v5:
time: 572 us; the launch traced here: 562 us
  waiting for transfers between devices  295 us (52%)
  Pallas kernels  153 us (27%)
  other arithmetic  45.2 us (8%)
  starting transfers between devices  31.9 us (6%)
  local copies, waits for them, and re-layouts  21.9 us (4%)
  between operations  15.2 us (3%)
    all_gather x1, waiting for transfers between devices, body(): lax.all_gather(pack(in_weight[0], out_weight[0], inner), axis, axis=0, ti...  127 us
    ppermute x28, waiting for transfers between devices, swap(): lax.ppermute(values, axis, [(a, a ^ bit) for a in range(lax.axis_size(axi...  101 us
    pallas_call x4, Pallas kernels, backward_slot(): pl.pallas_call(functools.partial(backward_kernel, place), in_specs=in_spe...  64.9 us
    ppermute x2, waiting for transfers between devices, body(): returned[m] = lax.ppermute(late_grads[m], 'section', [(1, 0)])  51.9 us
    pallas_call x4, Pallas kernels, forward_slot(): pl.pallas_call(functools.partial(forward_kernel, place), in_specs=in_spec...  42.8 us
    pallas_call x5, Pallas kernels, outer_sum(): pl.pallas_call(functools.partial(outer_kernel, extra is not None), grid=(...  34.2 us
    ppermute x28, starting transfers between devices, swap(): lax.ppermute(values, axis, [(a, a ^ bit) for a in range(lax.axis_size(axi...  26.6 us
    ppermute x2, waiting for transfers between devices, body(): arrived = [lax.ppermute(h, 'section', [(0, 1)]) for h in first]  15.6 us
  transfers between devices with their start and end apart: 33, of which 18 were waited for; matrix products, arithmetic and copies ran while one was open for 10% of the time, Pallas kernels for 21%

profile of v5, /device:TPU:8, one launch (start us, length us, event | category | flops | bytes accessed | tf_op | source)
XLA Modules:
  0.0 562.0 jit_solution(5588504828566318552)
XLA Ops:
  24.6 2.9 collective-permute-done.2
  27.5 3.8 collective-permute-start.3
  37.1 127.1 %all-gather.2.cloned.1.call-done.w_hbm = bf16[3072,4864]{1,0:T(8,128)(2,1)} async-done(((bf16[192,4864]{1,0:T(8,128)(2,1)}), bf16[3072,4864]{1,0:T(8,128)(2,1)}) %all-gather.2.cloned.1.call-update) | async-done | bytes 29884432 | tf_op jit(solution)/shard_map/all_gather | solution.py:799
  164.2 19.8 %forward_slot.4 = (bf16[4,256,1536]{2,1,0:T(8,128)(2,1)}, bf16[4,256,3072]{2,1,0:T(8,128)(2,1)}, f32[4,256,3072]{2,1,0:T(8,128)}, f32[4,256,3072]{2,1,0:T(8,128)...) custom-call(s32[2]{0:T(128)} %pad_add_fusion.3.at_ref, ...), custom_call_target="tpu_custom_call" | custom-call | flops 22000001024 | bytes 60000000 | tf_op jit(solution)/shard_map/forward_slot/pallas_call | solution.py:271
  185.4 20.0 %forward_slot.5 = (bf16[4,256,1536]{2,1,0:T(8,128)(2,1)}, bf16[4,256,3072]{2,1,0:T(8,128)(2,1)}, f32[4,256,3072]{2,1,0:T(8,128)}, f32[4,256,3072]{2,1,0:T(8,128)...) custom-call(s32[2]{0:T(128)} %pad_add_fusion.2.at_ref, ...), custom_call_target="tpu_custom_call", output_to_operand_aliasing={{0}: (9, {}), {1}: (10, {}), {2}: (11, {}), {3}: (12, {}), ... | custom-call | flops 22000001024 | bytes 60000000 | tf_op jit(solution)/shard_map/forward_slot/pallas_call | solution.py:271
  209.0 15.6 %collective-permute-done.5.u_hbm = bf16[256,1536]{1,0:T(8,128)(2,1)S(1)} collective-permute-done((bf16[256,1536]{1,0:T(8,128)(2,1)}, bf16[256,1536]{1,0:T(8,128)(2,1)S(1)}, u32[]{:S(2)}, u32[]{:S(2)}) %collective-permute-start.5) | collective-permute-done | bytes 786464 | tf_op jit(solution)/shard_map/ppermute | solution.py:828
  231.2 3.0 backward_slot.5
  237.4 4.4 by_owner.2
  241.9 3.5 by_owner.3
  245.4 51.6 %collective-permute-done.7.g_hbm = bf16[256,1536]{1,0:T(8,128)(2,1)S(1)} collective-permute-done((bf16[256,1536]{1,0:T(8,128)(2,1)}, bf16[256,1536]{1,0:T(8,128)(2,1)S(1)}, u32[]{:S(2)}, u32[]{:S(2)}) %collective-permute-start.7) | collective-permute-done | bytes 786464 | tf_op jit(solution)/shard_map/ppermute | solution.py:846
  297.9 29.7 %backward_slot.6 = (bf16[256,1536]{1,0:T(8,128)(2,1)}, bf16[256,3072]{1,0:T(8,128)(2,1)}, bf16[256,3456]{1,0:T(8,128)(2,1)}, f32[8,3328]{1,0:T(8,128)}) custom-call(s32[2]{0:T(128)} %pad_add_fusion.2.at_ref, bf16[256,1536]{1,0:T(8,128)(2,1)} %copy-done.7, ...), custom_call_target="tpu_custom_call", output_to_operand_aliasing={{1}: (16, {}), {2}: (17, {})} | custom-call | flops 1000000000 | bytes 1000000 | tf_op jit(solution)/shard_map/backward_slot/pallas_call | solution.py:593
  334.0 8.7 %outer_sum.5 = (bf16[768,1536]{1,0:T(8,128)(2,1)}, bf16[768,1536]{1,0:T(8,128)(2,1)}) custom-call(bf16[2,1536,256]{2,1,0:T(8,128)(2,1)} %bitcast.69, bf16[2,1536,256]{2,1,0:T(8,128)(2,1)} %collective-permute-done.8.sib_ref, bf16[256,1536]{1,0:T(8,128)(2,1)} %copy-done.10, bf16[256,1536]{1,0:T(8,128)(2,1)} %copy-done.9, bf16[256,1536]{1,0:T(8,128)(2,1)} %copy-done.22, ...), custom_call_target="tpu_custom_call" | custom-call | flops 1000000000 | bytes 1000000 | tf_op jit(solution)/shard_map/outer_sum/pallas_call | solution.py:728
  343.2 30.1 %backward_slot.7 = (bf16[256,1536]{1,0:T(8,128)(2,1)}, bf16[256,3072]{1,0:T(8,128)(2,1)}, bf16[256,3456]{1,0:T(8,128)(2,1)}, f32[8,3328]{1,0:T(8,128)}) custom-call(s32[2]{0:T(128)} %pad_add_fusion.3.at_ref, bf16[256,1536]{1,0:T(8,128)(2,1)} %copy-done.6, ...), custom_call_target="tpu_custom_call", output_to_operand_aliasing={{1}: (16, {}), {2}: (17, {})} | custom-call | flops 1000000000 | bytes 1000000 | tf_op jit(solution)/shard_map/backward_slot/pallas_call | solution.py:593
  380.9 8.6 %outer_sum.6 = (bf16[384,3072]{1,0:T(8,128)(2,1)}, bf16[384,3072]{1,0:T(8,128)(2,1)}) custom-call(bf16[2,768,256]{2,1,0:T(8,128)(2,1)} %bitcast.65, bf16[2,768,256]{2,1,0:T(8,128)(2,1)} %collective-permute-done.11.sib_ref, bf16[256,3072]{1,0:T(8,128)(2,1)} %get-tuple-element.152.rest_0_, bf16[256,3072]{1,0:T(8,128)(2,1)} %get-tuple-element.153.rest_1_, ...), custom_call_target="tpu_custom_call" | custom-call | flops 1000000000 | bytes 1000000 | tf_op jit(solution)/shard_map/outer_sum/pallas_call | solution.py:728
  389.6 6.7 %collective-permute-done.14 = bf16[768,1536]{1,0:T(8,128)(2,1)} collective-permute-done((bf16[768,1536]{1,0:T(8,128)(2,1)}, bf16[768,1536]{1,0:T(8,128)(2,1)}, u32[]{:S(2)}, u32[]{:S(2)}) %collective-permute-start.14) | collective-permute-done | bytes 2359328 | tf_op jit(solution)/shard_map/ppermute | solution.py:743
  405.6 6.9 %outer_sum.7 = (bf16[384,1920]{1,0:T(8,128)(2,1)}, bf16[384,1920]{1,0:T(8,128)(2,1)}) custom-call(bf16[2,768,256]{2,1,0:T(8,128)(2,1)} %bitcast.66, bf16[2,768,256]{2,1,0:T(8,128)(2,1)} %collective-permute-done.11.sib_ref, bf16[256,3456]{1,0:T(8,128)(2,1)} %get-tuple-element.174.rest_0_, bf16[256,3456]{1,0:T(8,128)(2,1)} %get-tuple-element.163.rest_1_, ...), custom_call_target="tpu_custom_call" | custom-call | flops 1000000000 | bytes 1000000 | tf_op jit(solution)/shard_map/outer_sum/pallas_call | solution.py:728
  416.2 5.4 outer_sum.8
  421.6 29.2 %collective-permute-done.15 = bf16[384,3072]{1,0:T(8,128)(2,1)} collective-permute-done((bf16[384,3072]{1,0:T(8,128)(2,1)}, bf16[384,3072]{1,0:T(8,128)(2,1)}, u32[]{:S(2)}, u32[]{:S(2)}) %collective-permute-start.15) | collective-permute-done | bytes 2359328 | tf_op jit(solution)/shard_map/ppermute | solution.py:743
  457.2 4.6 outer_sum.9
  462.6 19.8 %collective-permute-done.20 = bf16[384,1920]{1,0:T(8,128)(2,1)} collective-permute-done((bf16[384,1920]{1,0:T(8,128)(2,1)}, bf16[384,1920]{1,0:T(8,128)(2,1)}, u32[]{:S(2)}, u32[]{:S(2)}) %collective-permute-start.20) | collective-permute-done | bytes 1474592 | tf_op jit(solution)/shard_map/ppermute | solution.py:743
  489.0 6.0 %collective-permute-done.24 = bf16[384,768]{1,0:T(8,128)(2,1)} collective-permute-done((bf16[384,768]{1,0:T(8,128)(2,1)}, bf16[384,768]{1,0:T(8,128)(2,1)}, u32[]{:S(2)}, u32[]{:S(2)}) %collective-permute-start.24) | collective-permute-done | bytes 589856 | tf_op jit(solution)/shard_map/ppermute | solution.py:743
  496.8 18.3 %collective-permute-done.23 = bf16[192,1920]{1,0:T(8,128)(2,1)S(1)} collective-permute-done((bf16[192,1920]{1,0:T(8,128)(2,1)S(1)}, bf16[192,1920]{1,0:T(8,128)(2,1)S(1)}, u32[]{:S(2)}, u32[]{:S(2)}) %collective-permute-start.23) | collective-permute-done | bytes 737312 | tf_op jit(solution)/shard_map/ppermute | solution.py:743
  522.9 4.2 collective-permute-done.28
  530.7 4.2 collective-permute-done.27
  (247 shorter events, 112.7 us)
Async XLA Ops:
  7.2 157.0 %all-gather.2.cloned.1.call-start = ((), (), s32[]{:S(2)}) async-start(), calls=%async_computation | async-start | bytes 31752192 | tf_op jit(solution)/shard_map/all_gather | solution.py:799
  184.0 22.7 %collective-permute-start.4 = (bf16[256,1536]{1,0:T(8,128)(2,1)}, bf16[256,1536]{1,0:T(8,128)(2,1)S(1)}, u32[]{:S(2)}, u32[]{:S(2)}) collective-permute-start(bf16[256,1536]{1,0:T(8,128)(2,1)} %get-tuple-element.96), channel_id=1, source_target_pairs={{0,16},{1,17},{2,18},{3,19},{4,20},{5,21},{6,22},{7,23},{8,24},{9,... | collective-permute-start | bytes 2359304 | tf_op jit(solution)/shard_map/ppermute | solution.py:828
  205.4 19.1 %collective-permute-start.5 = (bf16[256,1536]{1,0:T(8,128)(2,1)}, bf16[256,1536]{1,0:T(8,128)(2,1)S(1)}, u32[]{:S(2)}, u32[]{:S(2)}) collective-permute-start(bf16[256,1536]{1,0:T(8,128)(2,1)} %get-tuple-element.112), channel_id=1, source_target_pairs={{0,16},{1,17},{2,18},{3,19},{4,20},{5,21},{6,22},{7,23},{8,24},{9,... | collective-permute-start | bytes 2359304 | tf_op jit(solution)/shard_map/ppermute | solution.py:828
  229.9 67.0 %collective-permute-start.7 = (bf16[256,1536]{1,0:T(8,128)(2,1)}, bf16[256,1536]{1,0:T(8,128)(2,1)S(1)}, u32[]{:S(2)}, u32[]{:S(2)}) collective-permute-start(bf16[256,1536]{1,0:T(8,128)(2,1)} %get-tuple-element.129), channel_id=1, source_target_pairs={{16,0},{17,1},{18,2},{19,3},{20,4},{21,5},{22,6},{23,7},{24,8},{25... | collective-permute-start | bytes 2359304 | tf_op jit(solution)/shard_map/ppermute | solution.py:846
  234.2 93.7 %collective-permute-start.6 = (bf16[256,1536]{1,0:T(8,128)(2,1)}, bf16[256,1536]{1,0:T(8,128)(2,1)S(1)}, u32[]{:S(2)}, u32[]{:S(2)}) collective-permute-start(bf16[256,1536]{1,0:T(8,128)(2,1)} %get-tuple-element.128), channel_id=1, source_target_pairs={{16,0},{17,1},{18,2},{19,3},{20,4},{21,5},{22,6},{23,7},{24,8},{25... | collective-permute-start | bytes 2359304 | tf_op jit(solution)/shard_map/ppermute | solution.py:846
  241.9 91.2 %collective-permute-start.8 = (bf16[2,1536,256]{2,1,0:T(8,128)(2,1)}, bf16[2,1536,256]{2,1,0:T(8,128)(2,1)}, u32[]{:S(2)}, u32[]{:S(2)}) collective-permute-start(bf16[2,1536,256]{2,1,0:T(8,128)(2,1)} %bitcast.77), channel_id=1, source_target_pairs={{0,1},{1,0},{2,3},{3,2},{4,5},{5,4},{6,7},{7,6},{8,9},{9,8},{10,11... | collective-permute-start | bytes 4718600 | tf_op jit(solution)/shard_map/ppermute | solution.py:743
  342.7 53.6 %collective-permute-start.14 = (bf16[768,1536]{1,0:T(8,128)(2,1)}, bf16[768,1536]{1,0:T(8,128)(2,1)}, u32[]{:S(2)}, u32[]{:S(2)}) collective-permute-start(bf16[768,1536]{1,0:T(8,128)(2,1)} %get-tuple-element.143), channel_id=1, source_target_pairs={{0,4},{1,5},{2,6},{3,7},{4,0},{5,1},{6,2},{7,3},{8,12},{9,13},{10,... | collective-permute-start | bytes 7077896 | tf_op jit(solution)/shard_map/ppermute | solution.py:743
  343.2 37.7 %collective-permute-start.13 = (bf16[256,3072]{1,0:T(8,128)(2,1)}, bf16[256,3072]{1,0:T(8,128)(2,1)}, u32[]{:S(2)}, u32[]{:S(2)}) collective-permute-start(bf16[256,3072]{1,0:T(8,128)(2,1)} %get-tuple-element.153.rest_1_), channel_id=1, source_target_pairs={{0,1},{1,0},{2,3},{3,2},{4,5},{5,4},{6,7},{7,6},{8,9},{9,8},{10,11... | collective-permute-start | bytes 4718600 | tf_op jit(solution)/shard_map/ppermute | solution.py:743
  376.3 29.3 %collective-permute-start.17 = (bf16[256,3456]{1,0:T(8,128)(2,1)S(1)}, bf16[256,3456]{1,0:T(8,128)(2,1)}, u32[]{:S(2)}, u32[]{:S(2)}) collective-permute-start(bf16[256,3456]{1,0:T(8,128)(2,1)S(1)} %copy-done.1), channel_id=1, source_target_pairs={{0,1},{1,0},{2,3},{3,2},{4,5},{5,4},{6,7},{7,6},{8,9},{9,8},{10,11... | collective-permute-start | bytes 5308424 | tf_op jit(solution)/shard_map/ppermute | solution.py:743
  378.5 27.1 %collective-permute-start.16 = (bf16[256,3456]{1,0:T(8,128)(2,1)S(1)}, bf16[256,3456]{1,0:T(8,128)(2,1)}, u32[]{:S(2)}, u32[]{:S(2)}) collective-permute-start(bf16[256,3456]{1,0:T(8,128)(2,1)S(1)} %copy-done), channel_id=1, source_target_pairs={{0,1},{1,0},{2,3},{3,2},{4,5},{5,4},{6,7},{7,6},{8,9},{9,8},{10,11... | collective-permute-start | bytes 5308424 | tf_op jit(solution)/shard_map/ppermute | solution.py:743
  396.3 54.5 %collective-permute-start.15 = (bf16[384,3072]{1,0:T(8,128)(2,1)}, bf16[384,3072]{1,0:T(8,128)(2,1)}, u32[]{:S(2)}, u32[]{:S(2)}) collective-permute-start(bf16[384,3072]{1,0:T(8,128)(2,1)} %get-tuple-element.157), channel_id=1, source_target_pairs={{0,2},{1,3},{2,0},{3,1},{4,6},{5,7},{6,4},{7,5},{8,10},{9,11},{10,... | collective-permute-start | bytes 7077896 | tf_op jit(solution)/shard_map/ppermute | solution.py:743
  403.8 53.4 %collective-permute-start.21 = (bf16[384,1536]{1,0:T(8,128)(2,1)}, bf16[384,1536]{1,0:T(8,128)(2,1)}, u32[]{:S(2)}, u32[]{:S(2)}) collective-permute-start(bf16[384,1536]{1,0:T(8,128)(2,1)} %add_convert_fusion.1), channel_id=1, source_target_pairs={{0,8},{1,9},{2,10},{3,11},{4,12},{5,13},{6,14},{7,15},{8,0},{9,1},... | collective-permute-start | bytes 3538952 | tf_op jit(solution)/shard_map/ppermute | solution.py:743
  412.5 69.9 %collective-permute-start.20 = (bf16[384,1920]{1,0:T(8,128)(2,1)}, bf16[384,1920]{1,0:T(8,128)(2,1)}, u32[]{:S(2)}, u32[]{:S(2)}) collective-permute-start(bf16[384,1920]{1,0:T(8,128)(2,1)} %get-tuple-element.164), channel_id=1, source_target_pairs={{0,2},{1,3},{2,0},{3,1},{4,6},{5,7},{6,4},{7,5},{8,10},{9,11},{10,... | collective-permute-start | bytes 4423688 | tf_op jit(solution)/shard_map/ppermute | solution.py:743
  453.6 30.7 %collective-permute-start.19 = (bf16[192,3072]{1,0:T(8,128)(2,1)}, bf16[192,3072]{1,0:T(8,128)(2,1)}, u32[]{:S(2)}, u32[]{:S(2)}) collective-permute-start(bf16[192,3072]{1,0:T(8,128)(2,1)} %add_convert_fusion), channel_id=1, source_target_pairs={{0,4},{1,5},{2,6},{3,7},{4,0},{5,1},{6,2},{7,3},{8,12},{9,13},{10,... | collective-permute-start | bytes 3538952 | tf_op jit(solution)/shard_map/ppermute | solution.py:743
  456.0 39.0 %collective-permute-start.24 = (bf16[384,768]{1,0:T(8,128)(2,1)}, bf16[384,768]{1,0:T(8,128)(2,1)}, u32[]{:S(2)}, u32[]{:S(2)}) collective-permute-start(bf16[384,768]{1,0:T(8,128)(2,1)} %get-tuple-element.166), channel_id=1, source_target_pairs={{0,2},{1,3},{2,0},{3,1},{4,6},{5,7},{6,4},{7,5},{8,10},{9,11},{10,... | collective-permute-start | bytes 1769480 | tf_op jit(solution)/shard_map/ppermute | solution.py:743
  461.8 56.7 %collective-permute-start.26 = (bf16[384,768]{1,0:T(8,128)(2,1)}, bf16[384,768]{1,0:T(8,128)(2,1)S(1)}, u32[]{:S(2)}, u32[]{:S(2)}) collective-permute-start(bf16[384,768]{1,0:T(8,128)(2,1)} %get-tuple-element.176), channel_id=1, source_target_pairs={{0,2},{1,3},{2,0},{3,1},{4,6},{5,7},{6,4},{7,5},{8,10},{9,11},{10,... | collective-permute-start | bytes 1769480 | tf_op jit(solution)/shard_map/ppermute | solution.py:743
  483.7 31.5 %collective-permute-start.23 = (bf16[192,1920]{1,0:T(8,128)(2,1)S(1)}, bf16[192,1920]{1,0:T(8,128)(2,1)S(1)}, u32[]{:S(2)}, u32[]{:S(2)}) collective-permute-start(bf16[192,1920]{1,0:T(8,128)(2,1)S(1)} %add_convert_fusion.2), channel_id=1, source_target_pairs={{0,4},{1,5},{2,6},{3,7},{4,0},{5,1},{6,2},{7,3},{8,12},{9,13},{10,... | collective-permute-start | bytes 2211848 | tf_op jit(solution)/shard_map/ppermute | solution.py:743
  486.6 61.8 %collective-permute-start.22 = (bf16[96,3072]{1,0:T(8,128)(2,1)}, bf16[96,3072]{1,0:T(8,128)(2,1)}, u32[]{:S(2)}, u32[]{:S(2)}) collective-permute-start(bf16[96,3072]{1,0:T(8,128)(2,1)} %add_convert_fusion.4), channel_id=1, source_target_pairs={{0,8},{1,9},{2,10},{3,11},{4,12},{5,13},{6,14},{7,15},{8,0},{9,1},... | collective-permute-start | bytes 1769480 | tf_op jit(solution)/shard_map/ppermute | solution.py:743
  496.2 30.8 %collective-permute-start.28 = (bf16[192,768]{1,0:T(8,128)(2,1)S(1)}, bf16[192,768]{1,0:T(8,128)(2,1)S(1)}, u32[]{:S(2)}, u32[]{:S(2)}) collective-permute-start(bf16[192,768]{1,0:T(8,128)(2,1)S(1)} %add_convert_fusion.7), channel_id=1, source_target_pairs={{0,4},{1,5},{2,6},{3,7},{4,0},{5,1},{6,2},{7,3},{8,12},{9,13},{10,... | collective-permute-start | bytes 884744 | tf_op jit(solution)/shard_map/ppermute | solution.py:743
  516.3 20.2 %collective-permute-start.25 = (bf16[96,1920]{1,0:T(8,128)(2,1)S(1)}, bf16[96,1920]{1,0:T(8,128)(2,1)S(1)}, u32[]{:S(2)}, u32[]{:S(2)}) collective-permute-start(bf16[96,1920]{1,0:T(8,128)(2,1)S(1)} %add_convert_fusion.5), channel_id=1, source_target_pairs={{0,8},{1,9},{2,10},{3,11},{4,12},{5,13},{6,14},{7,15},{8,0},{9,1},... | collective-permute-start | bytes 1105928 | tf_op jit(solution)/shard_map/ppermute | solution.py:743
  518.5 16.3 %collective-permute-start.27 = (bf16[192,768]{1,0:T(8,128)(2,1)S(1)}, bf16[192,768]{1,0:T(8,128)(2,1)S(1)}, u32[]{:S(2)}, u32[]{:S(2)}) collective-permute-start(bf16[192,768]{1,0:T(8,128)(2,1)S(1)} %add_convert_fusion.6), channel_id=1, source_target_pairs={{0,4},{1,5},{2,6},{3,7},{4,0},{5,1},{6,2},{7,3},{8,12},{9,13},{10,... | collective-permute-start | bytes 884744 | tf_op jit(solution)/shard_map/ppermute | solution.py:743
  521.3 30.7 %collective-permute-start.31 = (bf16[192,1536]{1,0:T(8,128)(2,1)}, bf16[192,1536]{1,0:T(8,128)(2,1)}, u32[]{:S(2)}, u32[]{:S(2)}) collective-permute-start(bf16[192,1536]{1,0:T(8,128)(2,1)} %add_convert_fusion.3), channel_id=1, source_target_pairs={{0,2},{1,3},{2,0},{3,1},{4,6},{5,7},{6,4},{7,5},{8,10},{9,11},{10,... | collective-permute-start | bytes 1769480 | tf_op jit(solution)/shard_map/ppermute | solution.py:743
  528.0 11.0 %collective-permute-start.30 = (bf16[96,768]{1,0:T(8,128)(2,1)S(1)}, bf16[96,768]{1,0:T(8,128)(2,1)S(1)}, u32[]{:S(2)}, u32[]{:S(2)}) collective-permute-start(bf16[96,768]{1,0:T(8,128)(2,1)S(1)} %add_convert_fusion.9), channel_id=1, source_target_pairs={{0,8},{1,9},{2,10},{3,11},{4,12},{5,13},{6,14},{7,15},{8,0},{9,1},... | collective-permute-start | bytes 442376 | tf_op jit(solution)/shard_map/ppermute | solution.py:743
  535.6 11.6 %collective-permute-start.29 = (bf16[96,768]{1,0:T(8,128)(2,1)}, bf16[96,768]{1,0:T(8,128)(2,1)S(1)}, u32[]{:S(2)}, u32[]{:S(2)}) collective-permute-start(bf16[96,768]{1,0:T(8,128)(2,1)} %add_convert_fusion.8), channel_id=1, source_target_pairs={{0,8},{1,9},{2,10},{3,11},{4,12},{5,13},{6,14},{7,15},{8,0},{9,1},... | collective-permute-start | bytes 442376 | tf_op jit(solution)/shard_map/ppermute | solution.py:743
  (51 other events, 535.6 us)
Sparse Core Ops, SparseCore 0:
  10.3 153.8 all-gather.1

commit v6 on v5

--- a/solution.py
+++ b/solution.py
@@ -699,16 +699,23 @@
     return [a.reshape(micro, total // 2, rows) for a in parts]
 
 
-def outer_kernel(with_extra, own_ref, sib_ref, *rest):
+def outer_kernel(with_extra, picks, own_ref, sib_ref, *rest):
     rights, outs = rest[:-2], rest[-2:]
     micro, high = own_ref.shape[0], outs[0].shape[0]
+
+    def left_of(part):
+        size = high // len(picks[part])
+        rows = [
+            [ref[m, k * size : (k + 1) * size] for ref in (own_ref, sib_ref) for m in range(micro)] for k in picks[part]
+        ]
+        return jnp.concatenate([jnp.concatenate(row, axis=1) for row in rows], axis=0)
+
     if with_extra:
         extra_ref, rights = rights[-1], rights[:-1]
     right = jnp.concatenate([ref[...] for ref in rights], axis=0)
     for part, out_ref in enumerate(outs):
         rows = slice(part * high, (part + 1) * high)
-        left = jnp.concatenate([ref[m, rows] for ref in (own_ref, sib_ref) for m in range(micro)], axis=1)
-        total = nn_dot(left, right)
+        total = nn_dot(left_of(part), right)
         out_ref[...] = total.astype(BF16)
         if with_extra:
             extra = extra_ref[rows, :]
@@ -718,7 +725,7 @@
                 out_ref[:, -HALF:] = (total[:, -HALF:] + extra).astype(BF16)
 
 
-def outer_sum(own, sib, rights, start, stop, block, extra=None):
+def outer_sum(own, sib, rights, start, stop, block, extra=None, picks=((0,), (1,))):
     _, total, rows = own.shape
     low, steps = start // block, (stop - start) // block
     full = pl.BlockSpec(own.shape, lambda i: (0, 0, 0))
@@ -726,7 +733,7 @@
     made = jax.ShapeDtypeStruct((total // 2, stop - start), BF16)
     more = [] if extra is None else [extra]
     return pl.pallas_call(
-        functools.partial(outer_kernel, extra is not None),
+        functools.partial(outer_kernel, extra is not None, picks),
         grid=(steps,),
         in_specs=[full, full]
         + [pl.BlockSpec((rows, block), lambda i: (0, low + i)) for _ in rights]
@@ -737,6 +744,45 @@
         cost_estimate=pl.CostEstimate(flops=10**9, bytes_accessed=10**6, transcendentals=0),
         name="outer_sum",
     )(own, sib, *rights, *more)
+
+
+def listing(sizes, span):
+    return [-(-size // span) for size in sizes]
+
+
+def spread_sums_kernel(sizes, inner, width, lane, spot_ref, own_ref, sib_ref, out_ref):
+    total = own_ref[...] + sib_ref[...]
+    cols, spots = total.shape[1], spot_ref.shape[0]
+    depth, span = out_ref.shape[0] // spots, HALF - lane
+    keep = lax.broadcasted_iota(jnp.int32, (8, HALF), 1) >= lane
+    head = lax.broadcasted_iota(jnp.int32, (inner, HALF), 0) // HEAD_DIM
+    group = (head == lax.broadcasted_iota(jnp.int32, (inner, HALF), 1)).astype(F32)
+    skip = jnp.dot(total[:, :inner], group, precision=EXACT, preferred_element_type=F32)
+    shared = [total[:, width : width + HALF], total[:, width + HALF : width + 2 * HALF], skip]
+    shared = [jnp.where(keep, pltpu.roll(a, lane, 1), 0.0) for a in shared]
+    out_ref[...] = jnp.zeros_like(out_ref)
+    for spot in range(spots):
+        row = spot * depth
+        for size, low, high in ((sizes[0], 0, 5), (sizes[1], 5, 6), (sizes[2], 7, 8)):
+            for part in range(-(-size // span)):
+                start = spot_ref[spot] * size + part * span - lane
+                here = pltpu.roll(total, lax.rem(2 * cols - start, cols), 1)[:, :HALF]
+                out_ref[row : row + high - low, :] = jnp.where(keep, here, 0.0)[low:high]
+                row += high - low
+        for a, at in zip(shared, (7, 7, 6)):
+            out_ref[row : row + 1, :] = a[at : at + 1]
+            row += 1
+
+
+def spread_sums(spots, own, sib, sizes, inner, width, lane):
+    return pl.pallas_call(
+        functools.partial(spread_sums_kernel, sizes, inner, width, lane),
+        in_specs=[pl.BlockSpec(memory_space=pltpu.SMEM)] + [pl.BlockSpec(memory_space=pltpu.VMEM)] * 2,
+        out_shape=jax.ShapeDtypeStruct((width // 2, HALF), F32),
+        compiler_params=pltpu.CompilerParams(vmem_limit_bytes=VMEM),
+        cost_estimate=pl.CostEstimate(flops=0, bytes_accessed=0, transcendentals=0),
+        name="spread_sums",
+    )(spots, own, sib)
 
 
 def swap(values, axis, bit):
@@ -872,51 +918,49 @@
     returned[0], early_grads[-1] = lax.optimization_barrier((returned[0], early_grads[-1]))
     take_branch(0)
 
-    out_keep, out_send = outer_sum(out_own, out_sib, branch + branch_sib, 0, width, WIDE)
-    returned[0] = held(returned[0], out_send)
-    out_terms = [out_keep, swap(out_send, axis, out_order[0])]
+    half = width // 2
+    a_keep, a_send = outer_sum(out_own, out_sib, branch + branch_sib, 0, half, half)
+    branch[0] = held(branch[0], a_send)
+    every = range(count // 2)
+    b_keep, b_send = outer_sum(
+        out_own, out_sib, branch + branch_sib, half, width, half, picks=(every[::2], every[1::2])
+    )
+    returned[0], a_send, b_send = lax.optimization_barrier((returned[0], a_send, b_send))
+    out_a = [a_keep, swap(a_send, axis, line[0])]
+    out_b = [b_keep, swap(b_send, axis, 2)]
     early_grads[0], *grads[0], sums = run_backward(0, 0, 0, grads[0], sums, returned[0], block_input[0])
+    grads[0], out_a[-1], out_b[-1] = lax.optimization_barrier((grads[0], out_a[-1], out_b[-1]))
     z_sib[0], v_sib[0] = (swap(a, axis, 1) for a in grads[0])
+    for bit in line[1:]:
+        out_a, a_token = exchange(out_a, axis, bit)
+    out_b, b_token = exchange(out_b, axis, line[0])
     input_grads = jnp.stack([jnp.where(is_last, a, b) for a, b in zip(late_grads, early_grads)])
 
     z_rows = [a for a, _ in grads] + z_sib
     v_rows = [a for _, a in grads] + v_sib
     cut, block, end = 5 * 384, 384, inner + 3 * STATE
-    z_keep, z_send = outer_sum(in_own, in_sib, z_rows, 0, inner, 2 * WIDE)
-    (z_keep, z_send), out_terms[-1] = lax.optimization_barrier(((z_keep, z_send), out_terms[-1]))
-    token = z_send
-    for bit in out_order[1:-1]:
-        out_terms, token = exchange(out_terms, axis, bit)
-    sums, v_rows[0] = held((sums, v_rows[0]), token)
-    sums = sums + swap(sums, axis, 1)
-    per_owner = lambda rows: rows.reshape(-1, count, rows.shape[1] // count).transpose(1, 0, 2).reshape(count, -1)
-    skip_g = sums[6, :inner].reshape(heads, HEAD_DIM).sum(axis=1)
-    shared = jnp.concatenate([sums[7, width : width + heads], sums[7, width + HALF : width + HALF + heads], skip_g])
-    listed = jnp.concatenate(
-        [
-            per_owner(sums[:CONV]),
-            per_owner(sums[CONV : CONV + 1]),
-            per_owner(sums[7:8, :width]),
-            per_owner(sums[5:6, :inner]),
-            jnp.broadcast_to(shared, (count, shared.shape[0])),
-        ],
-        axis=1,
-    )
-    listed_cols = -(-listed.shape[1] // depth)
-    listed = jnp.pad(listed, ((0, 0), (0, listed_cols * depth - listed.shape[1]))).reshape(count, depth, listed_cols)
-    listed = jnp.take(listed, place ^ jnp.array(spots_of(in_order), jnp.int32), axis=0).reshape(width // 2, listed_cols)
+    z_rows[-micro] = held(z_rows[-micro], a_token, b_token)
+    half = inner // 2
+    z_pairs = [outer_sum(in_own, in_sib, z_rows, 0, half, WIDE)]
+    z_rows[-1] = held(z_rows[-1], z_pairs[0][1])
+    z_pairs.append(outer_sum(in_own, in_sib, z_rows, half, inner, WIDE))
+    out_b[-1] = held(out_b[-1], z_pairs[1][1])
+    for bit in line[1:]:
+        out_b, b_token = exchange(out_b, axis, bit)
+    chunks = [[keep, swap(send, axis, 2)] for keep, send in z_pairs]
+    sums, v_rows[0] = held((sums, v_rows[0]), b_token, out_a[-1])
     at_lane = (proj_cols - inner) % HALF
-    extra = jnp.pad(listed, ((0, 0), (at_lane, HALF - at_lane - listed_cols)))
+    per = [channels // count, inner // count, width // count]
+    in_spots = place ^ jnp.array(spots_of(in_order), jnp.int32)
+    extra = spread_sums(in_spots, sums, swap(sums, axis, 1), per, inner, width, at_lane)
     mid = end - 2 * block
-    pairs = [
-        (z_keep, z_send),
-        outer_sum(in_own, in_sib, v_rows, 0, cut, 640),
-        outer_sum(in_own, in_sib, v_rows, mid, end, block, extra),
-        outer_sum(in_own, in_sib, [held(v_rows[0], out_terms[-1])] + v_rows[1:], cut, mid, block),
-    ]
-    sends = [send for _, send in pairs]
-    chunks = [[keep, swap(send, axis, 2)] for keep, send in pairs]
-    token, out_came = sends[:-1], out_terms[-1]
+    pairs = [outer_sum(in_own, in_sib, v_rows, 0, cut, 640)]
+    v_rows[0] = held(v_rows[0], pairs[0][1], out_b[-1], chunks[0][-1])
+    pairs.append(outer_sum(in_own, in_sib, v_rows, mid, end, block, extra))
+    v_rows[0] = held(v_rows[0], pairs[1][1], chunks[1][-1])
+    pairs.append(outer_sum(in_own, in_sib, v_rows, cut, mid, block))
+    chunks += [[keep, swap(send, axis, 2)] for keep, send in pairs]
+    token = pairs[0][1]
     last = len(chunks) - 1
 
     def first_step(k, token):
@@ -932,30 +976,38 @@
 
     token = first_step(0, token)
     for k in range(1, last):
-        token = first_step(k, token)
-        token = other_steps(k - 1, (token, out_came) if k == 1 else token)
+        token = first_step(k, (token, chunks[0][-1]) if k == 2 else token)
+        token = other_steps(k - 1, token)
     token = first_step(last, token)
-    out_terms[-1] = held(out_terms[-1], token)
-    out_terms, _ = exchange(out_terms, axis, 2)
+    out_a[-1] = held(out_a[-1], token)
+    out_a, _ = exchange(out_a, axis, 2)
     token = other_steps(last - 1, token)
     token = other_steps(last, token)
-    out_grad = total_of(out_terms)
+    out_grad = jnp.concatenate([total_of(out_a), total_of(out_b)], axis=1)
     in_parts = [total_of(terms) for terms in chunks]
-    tail = in_parts[2]
+    tail = in_parts[3]
     own_cols = proj_cols - inner - mid
-    in_grad = jnp.concatenate([in_parts[0], in_parts[1], in_parts[3], tail[:, :own_cols]], axis=1)
-    own_list = tail[:, own_cols : own_cols + listed_cols].reshape(-1)
-    cuts = [0]
-    for size in sizes + [heads] * 3:
-        cuts.append(cuts[-1] + size)
-    lists = [own_list[a:b] for a, b in zip(cuts[:-1], cuts[1:])]
+    in_grad = jnp.concatenate([in_parts[0], in_parts[1], in_parts[2], in_parts[4], tail[:, :own_cols]], axis=1)
+    span = HALF - at_lane
+    tap_parts, gate_parts, norm_parts = listing(per, span)
+    rows_of = lambda low, high: tail[low:high, own_cols : own_cols + span]
+    cut_rows = [0, 5 * tap_parts, 5 * tap_parts + gate_parts, 5 * tap_parts + gate_parts + norm_parts]
+    taps_g = rows_of(0, cut_rows[1]).reshape(tap_parts, 5, span).transpose(1, 0, 2).reshape(5, -1)[:, : per[0]]
+    gate_g = rows_of(cut_rows[1], cut_rows[2]).reshape(1, -1)[:, : per[1]]
+    norm_g = rows_of(cut_rows[2], cut_rows[3]).reshape(1, -1)[:, : per[2]]
+    shared_g = rows_of(cut_rows[3], cut_rows[3] + 3)[:, :heads]
     return (
         outputs[None],
         input_grads[None],
         in_grad[None],
         out_grad[None],
-        lists[0].reshape(1, CONV, -1),
-        *[one[None] for one in lists[1:]],
+        taps_g[None, :CONV],
+        taps_g[CONV:],
+        norm_g,
+        gate_g,
+        shared_g[0:1],
+        shared_g[1:2],
+        shared_g[2:3],
     )
 
 

time: 572 us -> 564 us (0.986)
  waiting for transfers between devices: 295 us -> 263 us
  starting transfers between devices: 31.9 us -> 43.8 us
  Pallas kernels: 153 us -> 162 us
    ppermute x28 -> x34, waiting for transfers between devices: 101 us -> 67.8 us  [swap(): lax.ppermute(values, axis, [(a, a ^ bit) for a in range(lax.axis_size(axi...]
    ppermute x28 -> x34, starting transfers between devices: 26.6 us -> 38.5 us  [swap(): lax.ppermute(values, axis, [(a, a ^ bit) for a in range(lax.axis_size(axi...]
    pallas_call x5 -> x8, Pallas kernels: 34.2 us -> 44 us  [the longest x7 40.2 us: outer_sum(): pl.pallas_call(functools.partial(outer_kernel, extra is not None, picks),...]
    unnamed x2 -> x6, other arithmetic: 0.04 us -> 6.39 us
    convert_element_type x10 -> x14, other arithmetic: 15.5 us -> 17.9 us  [exchange(): sent = total_of([a[half:] for a in terms]).astype(BF16)]
  transfers between devices with their start and end apart: 33 -> 39, of which waited for: 18 -> 19; matrix products, arithmetic and copies ran while one was open for 10% -> 11% of each run, Pallas kernels for 21% -> 22%
where the time goes in v6:
time: 564 us; the launch traced here: 554 us
  waiting for transfers between devices  263 us (47%)
  Pallas kernels  162 us (29%)
  other arithmetic  46.7 us (8%)
  starting transfers between devices  43.8 us (8%)
  local copies, waits for them, and re-layouts  23.9 us (4%)
  between operations  15.2 us (3%)
    all_gather x1, waiting for transfers between devices, body(): lax.all_gather(pack(in_weight[0], out_weight[0], inner), axis, axis=0, ti...  127 us
    ppermute x34, waiting for transfers between devices, swap(): lax.ppermute(values, axis, [(a, a ^ bit) for a in range(lax.axis_size(axi...  67.8 us
    pallas_call x4, Pallas kernels, backward_slot(): pl.pallas_call(functools.partial(backward_kernel, place), in_specs=in_spe...  65 us
    ppermute x2, waiting for transfers between devices, body(): returned[m] = lax.ppermute(late_grads[m], 'section', [(1, 0)])  52 us
    pallas_call x4, Pallas kernels, forward_slot(): pl.pallas_call(functools.partial(forward_kernel, place), in_specs=in_spec...  42.5 us
    pallas_call x7, Pallas kernels, outer_sum(): pl.pallas_call(functools.partial(outer_kernel, extra is not None, picks),...  40.2 us
    ppermute x34, starting transfers between devices, swap(): lax.ppermute(values, axis, [(a, a ^ bit) for a in range(lax.axis_size(axi...  38.5 us
    convert_element_type x14, other arithmetic, exchange(): sent = total_of([a[half:] for a in terms]).astype(BF16)  17.9 us
  transfers between devices with their start and end apart: 39, of which 19 were waited for; matrix products, arithmetic and copies ran while one was open for 11% of the time, Pallas kernels for 22%

profile of v6, /device:TPU:8, one launch (start us, length us, event | category | flops | bytes accessed | tf_op | source)
XLA Modules:
  0.0 554.4 jit_solution(5099965411094983395)
XLA Ops:
  37.0 127.2 %all-gather.2.cloned.1.call-done.w_hbm = bf16[3072,4864]{1,0:T(8,128)(2,1)} async-done(((bf16[192,4864]{1,0:T(8,128)(2,1)}), bf16[3072,4864]{1,0:T(8,128)(2,1)}) %all-gather.2.cloned.1.call-update) | async-done | bytes 29884432 | tf_op jit(solution)/shard_map/all_gather | solution.py:845
  164.2 19.8 %forward_slot.4 = (bf16[4,256,1536]{2,1,0:T(8,128)(2,1)}, bf16[4,256,3072]{2,1,0:T(8,128)(2,1)}, f32[4,256,3072]{2,1,0:T(8,128)}, f32[4,256,3072]{2,1,0:T(8,128)...) custom-call(s32[2]{0:T(128)} %pad_add_fusion.3.at_ref, ...), custom_call_target="tpu_custom_call" | custom-call | flops 22000001024 | bytes 60000000 | tf_op jit(solution)/shard_map/forward_slot/pallas_call | solution.py:271
  185.4 20.0 %forward_slot.5 = (bf16[4,256,1536]{2,1,0:T(8,128)(2,1)}, bf16[4,256,3072]{2,1,0:T(8,128)(2,1)}, f32[4,256,3072]{2,1,0:T(8,128)}, f32[4,256,3072]{2,1,0:T(8,128)...) custom-call(s32[2]{0:T(128)} %pad_add_fusion.2.at_ref, ...), custom_call_target="tpu_custom_call", output_to_operand_aliasing={{0}: (9, {}), {1}: (10, {}), {2}: (11, {}), {3}: (12, {}), ... | custom-call | flops 22000001024 | bytes 60000000 | tf_op jit(solution)/shard_map/forward_slot/pallas_call | solution.py:271
  208.9 15.5 %collective-permute-done.5.u_hbm = bf16[256,1536]{1,0:T(8,128)(2,1)S(1)} collective-permute-done((bf16[256,1536]{1,0:T(8,128)(2,1)}, bf16[256,1536]{1,0:T(8,128)(2,1)S(1)}, u32[]{:S(2)}, u32[]{:S(2)}) %collective-permute-start.5) | collective-permute-done | bytes 786464 | tf_op jit(solution)/shard_map/ppermute | solution.py:874
  237.4 4.4 by_owner.2
  245.3 51.4 %collective-permute-done.7.g_hbm = bf16[256,1536]{1,0:T(8,128)(2,1)S(1)} collective-permute-done((bf16[256,1536]{1,0:T(8,128)(2,1)}, bf16[256,1536]{1,0:T(8,128)(2,1)S(1)}, u32[]{:S(2)}, u32[]{:S(2)}) %collective-permute-start.7) | collective-permute-done | bytes 786464 | tf_op jit(solution)/shard_map/ppermute | solution.py:892
  297.6 29.7 %backward_slot.6 = (bf16[256,1536]{1,0:T(8,128)(2,1)}, bf16[256,3072]{1,0:T(8,128)(2,1)}, bf16[256,3456]{1,0:T(8,128)(2,1)}, f32[8,3328]{1,0:T(8,128)}) custom-call(s32[2]{0:T(128)} %pad_add_fusion.2.at_ref, bf16[256,1536]{1,0:T(8,128)(2,1)} %copy-done.9, ...), custom_call_target="tpu_custom_call", output_to_operand_aliasing={{1}: (16, {}), {2}: (17, {})} | custom-call | flops 1000000000 | bytes 1000000 | tf_op jit(solution)/shard_map/backward_slot/pallas_call | solution.py:593
  334.0 5.9 %outer_sum.7 = (bf16[768,768]{1,0:T(8,128)(2,1)}, bf16[768,768]{1,0:T(8,128)(2,1)}) custom-call(bf16[2,1536,256]{2,1,0:T(8,128)(2,1)} %bitcast.63, bf16[2,1536,256]{2,1,0:T(8,128)(2,1)} %collective-permute-done.8.sib_ref, bf16[256,1536]{1,0:T(8,128)(2,1)} %copy-done.3, bf16[256,1536]{1,0:T(8,128)(2,1)} %copy-done.2, bf16[256,1536]{1,0:T(8,128)(2,1)} %copy-done.11, ...), custom_call_target="tpu_custom_call" | custom-call | flops 1000000000 | bytes 1000000 | tf_op jit(solution)/shard_map/outer_sum/pallas_call | solution.py:735
  339.9 5.9 %outer_sum.8 = (bf16[768,768]{1,0:T(8,128)(2,1)}, bf16[768,768]{1,0:T(8,128)(2,1)}) custom-call(bf16[2,1536,256]{2,1,0:T(8,128)(2,1)} %bitcast.64, bf16[2,1536,256]{2,1,0:T(8,128)(2,1)} %collective-permute-done.8.sib_ref, bf16[256,1536]{1,0:T(8,128)(2,1)} %copy-done.3, bf16[256,1536]{1,0:T(8,128)(2,1)} %copy-done.2, bf16[256,1536]{1,0:T(8,128)(2,1)} %copy-done.11, ...), custom_call_target="tpu_custom_call" | custom-call | flops 1000000000 | bytes 1000000 | tf_op jit(solution)/shard_map/outer_sum/pallas_call | solution.py:735
  348.0 29.9 %backward_slot.7 = (bf16[256,1536]{1,0:T(8,128)(2,1)}, bf16[256,3072]{1,0:T(8,128)(2,1)}, bf16[256,3456]{1,0:T(8,128)(2,1)}, f32[8,3328]{1,0:T(8,128)}) custom-call(s32[2]{0:T(128)} %pad_add_fusion.3.at_ref, bf16[256,1536]{1,0:T(8,128)(2,1)} %copy-done.8, ...), custom_call_target="tpu_custom_call", output_to_operand_aliasing={{1}: (16, {}), {2}: (17, {})} | custom-call | flops 1000000000 | bytes 1000000 | tf_op jit(solution)/shard_map/backward_slot/pallas_call | solution.py:593
  387.1 5.9 %outer_sum.9 = (bf16[384,1536]{1,0:T(8,128)(2,1)}, bf16[384,1536]{1,0:T(8,128)(2,1)}) custom-call(bf16[2,768,256]{2,1,0:T(8,128)(2,1)} %bitcast.58, bf16[2,768,256]{2,1,0:T(8,128)(2,1)} %collective-permute-done.11.sib_ref, bf16[256,3072]{1,0:T(8,128)(2,1)} %get-tuple-element.172.rest_0_, bf16[256,3072]{1,0:T(8,128)(2,1)} %get-tuple-element.173.rest_1_, ...), custom_call_target="tpu_custom_call" | custom-call | flops 1000000000 | bytes 1000000 | tf_op jit(solution)/shard_map/outer_sum/pallas_call | solution.py:735
  397.4 5.9 %outer_sum.10 = (bf16[384,1536]{1,0:T(8,128)(2,1)}, bf16[384,1536]{1,0:T(8,128)(2,1)}) custom-call(bf16[2,768,256]{2,1,0:T(8,128)(2,1)} %bitcast.59, bf16[2,768,256]{2,1,0:T(8,128)(2,1)} %collective-permute-done.11.sib_ref, bf16[256,3072]{1,0:T(8,128)(2,1)} %get-tuple-element.172.rest_0_, bf16[256,3072]{1,0:T(8,128)(2,1)} %get-tuple-element.173.rest_1_, ...), custom_call_target="tpu_custom_call" | custom-call | flops 1000000000 | bytes 1000000 | tf_op jit(solution)/shard_map/outer_sum/pallas_call | solution.py:735
  408.9 13.3 %collective-permute-done.18 = bf16[384,768]{1,0:T(8,128)(2,1)} collective-permute-done((bf16[384,768]{1,0:T(8,128)(2,1)S(1)}, bf16[384,768]{1,0:T(8,128)(2,1)}, u32[]{:S(2)}, u32[]{:S(2)}) %collective-permute-start.18) | collective-permute-done | bytes 589856 | tf_op jit(solution)/shard_map/ppermute | solution.py:789
  422.3 6.9 %outer_sum.11 = (bf16[384,1920]{1,0:T(8,128)(2,1)}, bf16[384,1920]{1,0:T(8,128)(2,1)}) custom-call(bf16[2,768,256]{2,1,0:T(8,128)(2,1)} %bitcast.60, bf16[2,768,256]{2,1,0:T(8,128)(2,1)} %collective-permute-done.11.sib_ref, bf16[256,3456]{1,0:T(8,128)(2,1)} %get-tuple-element.202.rest_0_, bf16[256,3456]{1,0:T(8,128)(2,1)} %get-tuple-element.187.rest_1_, ...), custom_call_target="tpu_custom_call" | custom-call | flops 1000000000 | bytes 1000000 | tf_op jit(solution)/shard_map/outer_sum/pallas_call | solution.py:735
  440.8 6.6 %collective-permute-done.22 = bf16[384,1536]{1,0:T(8,128)(2,1)} collective-permute-done((bf16[384,1536]{1,0:T(8,128)(2,1)}, bf16[384,1536]{1,0:T(8,128)(2,1)}, u32[]{:S(2)}, u32[]{:S(2)}) %collective-permute-start.22) | collective-permute-done | bytes 1179680 | tf_op jit(solution)/shard_map/ppermute | solution.py:789
  449.4 4.3 collective-permute-done.21
  455.7 3.8 collective-permute-start.23
  460.9 5.2 outer_sum.12
  466.8 4.6 outer_sum.13
  472.8 6.1 %collective-permute-done.25 = bf16[384,1920]{1,0:T(8,128)(2,1)S(1)} collective-permute-done((bf16[384,1920]{1,0:T(8,128)(2,1)}, bf16[384,1920]{1,0:T(8,128)(2,1)S(1)}, u32[]{:S(2)}, u32[]{:S(2)}) %collective-permute-start.25) | collective-permute-done | bytes 1474592 | tf_op jit(solution)/shard_map/ppermute | solution.py:789
  484.1 7.5 %collective-permute-done.30 = bf16[384,768]{1,0:T(8,128)(2,1)} collective-permute-done((bf16[384,768]{1,0:T(8,128)(2,1)}, bf16[384,768]{1,0:T(8,128)(2,1)}, u32[]{:S(2)}, u32[]{:S(2)}) %collective-permute-start.30) | collective-permute-done | bytes 589856 | tf_op jit(solution)/shard_map/ppermute | solution.py:789
  494.6 11.2 %collective-permute-done.26 = bf16[96,1536]{1,0:T(8,128)(2,1)S(1)} collective-permute-done((bf16[96,1536]{1,0:T(8,128)(2,1)S(1)}, bf16[96,1536]{1,0:T(8,128)(2,1)S(1)}, u32[]{:S(2)}, u32[]{:S(2)}) %collective-permute-start.26) | collective-permute-done | bytes 294944 | tf_op jit(solution)/shard_map/ppermute | solution.py:789
  514.1 5.5 collective-permute-start.36
  521.6 4.6 collective-permute-done.36
  (255 shorter events, 138.0 us)
Async XLA Ops:
  7.2 157.1 %all-gather.2.cloned.1.call-start = ((), (), s32[]{:S(2)}) async-start(), calls=%async_computation | async-start | bytes 31752192 | tf_op jit(solution)/shard_map/all_gather | solution.py:845
  184.0 22.7 %collective-permute-start.4 = (bf16[256,1536]{1,0:T(8,128)(2,1)}, bf16[256,1536]{1,0:T(8,128)(2,1)S(1)}, u32[]{:S(2)}, u32[]{:S(2)}) collective-permute-start(bf16[256,1536]{1,0:T(8,128)(2,1)} %get-tuple-element.110), channel_id=1, source_target_pairs={{0,16},{1,17},{2,18},{3,19},{4,20},{5,21},{6,22},{7,23},{8,24},{9,... | collective-permute-start | bytes 2359304 | tf_op jit(solution)/shard_map/ppermute | solution.py:874
  229.7 67.1 %collective-permute-start.7 = (bf16[256,1536]{1,0:T(8,128)(2,1)}, bf16[256,1536]{1,0:T(8,128)(2,1)S(1)}, u32[]{:S(2)}, u32[]{:S(2)}) collective-permute-start(bf16[256,1536]{1,0:T(8,128)(2,1)} %get-tuple-element.143), channel_id=1, source_target_pairs={{16,0},{17,1},{18,2},{19,3},{20,4},{21,5},{22,6},{23,7},{24,8},{25... | collective-permute-start | bytes 2359304 | tf_op jit(solution)/shard_map/ppermute | solution.py:892
  234.2 93.7 %collective-permute-start.6 = (bf16[256,1536]{1,0:T(8,128)(2,1)}, bf16[256,1536]{1,0:T(8,128)(2,1)S(1)}, u32[]{:S(2)}, u32[]{:S(2)}) collective-permute-start(bf16[256,1536]{1,0:T(8,128)(2,1)} %get-tuple-element.142), channel_id=1, source_target_pairs={{16,0},{17,1},{18,2},{19,3},{20,4},{21,5},{22,6},{23,7},{24,8},{25... | collective-permute-start | bytes 2359304 | tf_op jit(solution)/shard_map/ppermute | solution.py:892
  241.9 91.2 %collective-permute-start.8 = (bf16[2,1536,256]{2,1,0:T(8,128)(2,1)}, bf16[2,1536,256]{2,1,0:T(8,128)(2,1)}, u32[]{:S(2)}, u32[]{:S(2)}) collective-permute-start(bf16[2,1536,256]{2,1,0:T(8,128)(2,1)} %bitcast.73), channel_id=1, source_target_pairs={{0,1},{1,0},{2,3},{3,2},{4,5},{5,4},{6,7},{7,6},{8,9},{9,8},{10,11... | collective-permute-start | bytes 4718600 | tf_op jit(solution)/shard_map/ppermute | solution.py:789
  345.9 32.1 %collective-permute-start.12 = (bf16[768,768]{1,0:T(8,128)(2,1)}, bf16[768,768]{1,0:T(8,128)(2,1)S(1)}, u32[]{:S(2)}, u32[]{:S(2)}) collective-permute-start(bf16[768,768]{1,0:T(8,128)(2,1)} %get-tuple-element.170), channel_id=1, source_target_pairs={{0,4},{1,5},{2,6},{3,7},{4,0},{5,1},{6,2},{7,3},{8,12},{9,13},{10,... | collective-permute-start | bytes 3538952 | tf_op jit(solution)/shard_map/ppermute | solution.py:789
  346.4 31.6 %collective-permute-start.13 = (bf16[768,768]{1,0:T(8,128)(2,1)}, bf16[768,768]{1,0:T(8,128)(2,1)S(1)}, u32[]{:S(2)}, u32[]{:S(2)}) collective-permute-start(bf16[768,768]{1,0:T(8,128)(2,1)} %get-tuple-element.171), channel_id=1, source_target_pairs={{0,2},{1,3},{2,0},{3,1},{4,6},{5,7},{6,4},{7,5},{8,10},{9,11},{10,... | collective-permute-start | bytes 3538952 | tf_op jit(solution)/shard_map/ppermute | solution.py:789
  347.5 39.5 %collective-permute-start.11 = (bf16[2,768,256]{2,1,0:T(8,128)(2,1)}, bf16[2,768,256]{2,1,0:T(8,128)(2,1)}, u32[]{:S(2)}, u32[]{:S(2)}) collective-permute-start(bf16[2,768,256]{2,1,0:T(8,128)(2,1)} %bitcast.26), channel_id=1, source_target_pairs={{0,1},{1,0},{2,3},{3,2},{4,5},{5,4},{6,7},{7,6},{8,9},{9,8},{10,11... | collective-permute-start | bytes 2359304 | tf_op jit(solution)/shard_map/ppermute | solution.py:789
  347.5 39.5 %collective-permute-start.15 = (bf16[256,3072]{1,0:T(8,128)(2,1)}, bf16[256,3072]{1,0:T(8,128)(2,1)}, u32[]{:S(2)}, u32[]{:S(2)}) collective-permute-start(bf16[256,3072]{1,0:T(8,128)(2,1)} %get-tuple-element.173.rest_1_), channel_id=1, source_target_pairs={{0,1},{1,0},{2,3},{3,2},{4,5},{5,4},{6,7},{7,6},{8,9},{9,8},{10,11... | collective-permute-start | bytes 4718600 | tf_op jit(solution)/shard_map/ppermute | solution.py:789
  382.8 39.5 %collective-permute-start.20 = (bf16[256,3456]{1,0:T(8,128)(2,1)S(1)}, bf16[256,3456]{1,0:T(8,128)(2,1)}, u32[]{:S(2)}, u32[]{:S(2)}) collective-permute-start(bf16[256,3456]{1,0:T(8,128)(2,1)S(1)} %copy-done.1), channel_id=1, source_target_pairs={{0,1},{1,0},{2,3},{3,2},{4,5},{5,4},{6,7},{7,6},{8,9},{9,8},{10,11... | collective-permute-start | bytes 5308424 | tf_op jit(solution)/shard_map/ppermute | solution.py:789
  382.8 39.5 %collective-permute-start.19 = (bf16[256,3456]{1,0:T(8,128)(2,1)S(1)}, bf16[256,3456]{1,0:T(8,128)(2,1)}, u32[]{:S(2)}, u32[]{:S(2)}) collective-permute-start(bf16[256,3456]{1,0:T(8,128)(2,1)S(1)} %copy-done), channel_id=1, source_target_pairs={{0,1},{1,0},{2,3},{3,2},{4,5},{5,4},{6,7},{7,6},{8,9},{9,8},{10,11... | collective-permute-start | bytes 5308424 | tf_op jit(solution)/shard_map/ppermute | solution.py:789
  392.9 37.8 %collective-permute-start.16 = (bf16[384,1536]{1,0:T(8,128)(2,1)}, bf16[384,1536]{1,0:T(8,128)(2,1)}, u32[]{:S(2)}, u32[]{:S(2)}) collective-permute-start(bf16[384,1536]{1,0:T(8,128)(2,1)} %get-tuple-element.180), channel_id=1, source_target_pairs={{0,2},{1,3},{2,0},{3,1},{4,6},{5,7},{6,4},{7,5},{8,10},{9,11},{10,... | collective-permute-start | bytes 3538952 | tf_op jit(solution)/shard_map/ppermute | solution.py:789
  396.0 26.3 %collective-permute-start.18 = (bf16[384,768]{1,0:T(8,128)(2,1)S(1)}, bf16[384,768]{1,0:T(8,128)(2,1)}, u32[]{:S(2)}, u32[]{:S(2)}) collective-permute-start(bf16[384,768]{1,0:T(8,128)(2,1)S(1)} %add_convert_fusion.4), channel_id=1, source_target_pairs={{0,8},{1,9},{2,10},{3,11},{4,12},{5,13},{6,14},{7,15},{8,0},{9,1},... | collective-permute-start | bytes 1769480 | tf_op jit(solution)/shard_map/ppermute | solution.py:789
  404.5 42.9 %collective-permute-start.22 = (bf16[384,1536]{1,0:T(8,128)(2,1)}, bf16[384,1536]{1,0:T(8,128)(2,1)}, u32[]{:S(2)}, u32[]{:S(2)}) collective-permute-start(bf16[384,1536]{1,0:T(8,128)(2,1)} %get-tuple-element.184), channel_id=1, source_target_pairs={{0,2},{1,3},{2,0},{3,1},{4,6},{5,7},{6,4},{7,5},{8,10},{9,11},{10,... | collective-permute-start | bytes 3538952 | tf_op jit(solution)/shard_map/ppermute | solution.py:789
  429.2 49.7 %collective-permute-start.25 = (bf16[384,1920]{1,0:T(8,128)(2,1)}, bf16[384,1920]{1,0:T(8,128)(2,1)S(1)}, u32[]{:S(2)}, u32[]{:S(2)}) collective-permute-start(bf16[384,1920]{1,0:T(8,128)(2,1)} %get-tuple-element.188), channel_id=1, source_target_pairs={{0,2},{1,3},{2,0},{3,1},{4,6},{5,7},{6,4},{7,5},{8,10},{9,11},{10,... | collective-permute-start | bytes 4423688 | tf_op jit(solution)/shard_map/ppermute | solution.py:789
  432.1 21.6 %collective-permute-start.21 = (bf16[192,1536]{1,0:T(8,128)(2,1)S(1)}, bf16[192,1536]{1,0:T(8,128)(2,1)}, u32[]{:S(2)}, u32[]{:S(2)}) collective-permute-start(bf16[192,1536]{1,0:T(8,128)(2,1)S(1)} %add_convert_fusion.2), channel_id=1, source_target_pairs={{0,4},{1,5},{2,6},{3,7},{4,0},{5,1},{6,2},{7,3},{8,12},{9,13},{10,... | collective-permute-start | bytes 1769480 | tf_op jit(solution)/shard_map/ppermute | solution.py:789
  435.7 23.8 %collective-permute-start.28 = (bf16[192,768]{1,0:T(8,128)(2,1)}, bf16[192,768]{1,0:T(8,128)(2,1)S(1)}, u32[]{:S(2)}, u32[]{:S(2)}) collective-permute-start(bf16[192,768]{1,0:T(8,128)(2,1)} %add_convert_fusion.11), channel_id=1, source_target_pairs={{0,8},{1,9},{2,10},{3,11},{4,12},{5,13},{6,14},{7,15},{8,0},{9,1},... | collective-permute-start | bytes 884744 | tf_op jit(solution)/shard_map/ppermute | solution.py:789
  455.7 23.2 %collective-permute-start.23 = (bf16[96,1536]{1,0:T(8,128)(2,1)}, bf16[96,1536]{1,0:T(8,128)(2,1)S(1)}, u32[]{:S(2)}, u32[]{:S(2)}) collective-permute-start(bf16[96,1536]{1,0:T(8,128)(2,1)} %add_convert_fusion.10), channel_id=1, source_target_pairs={{0,8},{1,9},{2,10},{3,11},{4,12},{5,13},{6,14},{7,15},{8,0},{9,1},... | collective-permute-start | bytes 884744 | tf_op jit(solution)/shard_map/ppermute | solution.py:789
  466.1 25.5 %collective-permute-start.30 = (bf16[384,768]{1,0:T(8,128)(2,1)}, bf16[384,768]{1,0:T(8,128)(2,1)}, u32[]{:S(2)}, u32[]{:S(2)}) collective-permute-start(bf16[384,768]{1,0:T(8,128)(2,1)} %get-tuple-element.199), channel_id=1, source_target_pairs={{0,2},{1,3},{2,0},{3,1},{4,6},{5,7},{6,4},{7,5},{8,10},{9,11},{10,... | collective-permute-start | bytes 1769480 | tf_op jit(solution)/shard_map/ppermute | solution.py:789
  471.4 36.8 %collective-permute-start.32 = (bf16[384,768]{1,0:T(8,128)(2,1)}, bf16[384,768]{1,0:T(8,128)(2,1)S(1)}, u32[]{:S(2)}, u32[]{:S(2)}) collective-permute-start(bf16[384,768]{1,0:T(8,128)(2,1)} %get-tuple-element.204), channel_id=1, source_target_pairs={{0,2},{1,3},{2,0},{3,1},{4,6},{5,7},{6,4},{7,5},{8,10},{9,11},{10,... | collective-permute-start | bytes 1769480 | tf_op jit(solution)/shard_map/ppermute | solution.py:789
  479.1 27.9 %collective-permute-start.27 = (bf16[192,1920]{1,0:T(8,128)(2,1)S(1)}, bf16[192,1920]{1,0:T(8,128)(2,1)S(1)}, u32[]{:S(2)}, u32[]{:S(2)}) collective-permute-start(bf16[192,1920]{1,0:T(8,128)(2,1)S(1)} %add_convert_fusion), channel_id=1, source_target_pairs={{0,4},{1,5},{2,6},{3,7},{4,0},{5,1},{6,2},{7,3},{8,12},{9,13},{10,... | collective-permute-start | bytes 2211848 | tf_op jit(solution)/shard_map/ppermute | solution.py:789
  482.3 23.5 %collective-permute-start.26 = (bf16[96,1536]{1,0:T(8,128)(2,1)S(1)}, bf16[96,1536]{1,0:T(8,128)(2,1)S(1)}, u32[]{:S(2)}, u32[]{:S(2)}) collective-permute-start(bf16[96,1536]{1,0:T(8,128)(2,1)S(1)} %add_convert_fusion.9), channel_id=1, source_target_pairs={{0,8},{1,9},{2,10},{3,11},{4,12},{5,13},{6,14},{7,15},{8,0},{9,1},... | collective-permute-start | bytes 884744 | tf_op jit(solution)/shard_map/ppermute | solution.py:789
  508.1 34.4 %collective-permute-start.31 = (bf16[96,1920]{1,0:T(8,128)(2,1)}, bf16[96,1920]{1,0:T(8,128)(2,1)}, u32[]{:S(2)}, u32[]{:S(2)}) collective-permute-start(bf16[96,1920]{1,0:T(8,128)(2,1)} %add_convert_fusion.5), channel_id=1, source_target_pairs={{0,8},{1,9},{2,10},{3,11},{4,12},{5,13},{6,14},{7,15},{8,0},{9,1},... | collective-permute-start | bytes 1105928 | tf_op jit(solution)/shard_map/ppermute | solution.py:789
  509.1 26.9 %collective-permute-start.33 = (bf16[192,768]{1,0:T(8,128)(2,1)}, bf16[192,768]{1,0:T(8,128)(2,1)}, u32[]{:S(2)}, u32[]{:S(2)}) collective-permute-start(bf16[192,768]{1,0:T(8,128)(2,1)} %add_convert_fusion.7), channel_id=1, source_target_pairs={{0,4},{1,5},{2,6},{3,7},{4,0},{5,1},{6,2},{7,3},{8,12},{9,13},{10,... | collective-permute-start | bytes 884744 | tf_op jit(solution)/shard_map/ppermute | solution.py:789
  (63 other events, 600.8 us)
Sparse Core Ops, SparseCore 0:
  10.3 153.9 all-gather.1

commit v7 on v6

--- a/solution.py
+++ b/solution.py
@@ -877,7 +877,6 @@
             micro + m, numbers(m, 1), kept, arrived[m], w_all, view, norm, chan, chan_r, head_rows, gate, 2 * micro
         )
         second.append(h)
-    outputs = jnp.stack([jnp.where(section == 0, a, b) for a, b in zip(first, second)])
 
     def run_backward(place, m, stage, grads, sums, g, u):
         return backward_slot(
@@ -934,7 +933,6 @@
     for bit in line[1:]:
         out_a, a_token = exchange(out_a, axis, bit)
     out_b, b_token = exchange(out_b, axis, line[0])
-    input_grads = jnp.stack([jnp.where(is_last, a, b) for a, b in zip(late_grads, early_grads)])
 
     z_rows = [a for a, _ in grads] + z_sib
     v_rows = [a for _, a in grads] + v_sib
@@ -979,10 +977,14 @@
         token = first_step(k, (token, chunks[0][-1]) if k == 2 else token)
         token = other_steps(k - 1, token)
     token = first_step(last, token)
+    early_grads[0], second = held((early_grads[0], second), token)
+    outputs = jnp.stack([jnp.where(section == 0, a, b) for a, b in zip(first, second)])
+    input_grads = jnp.stack([jnp.where(is_last, a, b) for a, b in zip(late_grads, early_grads)])
     out_a[-1] = held(out_a[-1], token)
     out_a, _ = exchange(out_a, axis, 2)
     token = other_steps(last - 1, token)
     token = other_steps(last, token)
+    chunks[last - 1][-1] = held(chunks[last - 1][-1], token)
     out_grad = jnp.concatenate([total_of(out_a), total_of(out_b)], axis=1)
     in_parts = [total_of(terms) for terms in chunks]
     tail = in_parts[3]

time: 564 us -> 561 us (level)
  local copies, waits for them, and re-layouts: 23.9 us -> 17.5 us
    ppermute x34, waiting for transfers between devices: 67.8 us -> 75.5 us  [swap(): lax.ppermute(values, axis, [(a, a ^ bit) for a in range(lax.axis_size(axi...]
  transfers between devices with their start and end apart: 39 -> 39, of which waited for: 19 -> 19; matrix products, arithmetic and copies ran while one was open for 11% -> 10% of each run, Pallas kernels for 22% -> 23%
where the time goes in v7:
time: 561 us; the launch traced here: 550 us
  waiting for transfers between devices  268 us (48%)
  Pallas kernels  162 us (29%)
  other arithmetic  46 us (8%)
  starting transfers between devices  40.8 us (7%)
  local copies, waits for them, and re-layouts  17.5 us (3%)
  between operations  15.2 us (3%)
    all_gather x1, waiting for transfers between devices, body(): lax.all_gather(pack(in_weight[0], out_weight[0], inner), axis, axis=0, ti...  125 us
    ppermute x34, waiting for transfers between devices, swap(): lax.ppermute(values, axis, [(a, a ^ bit) for a in range(lax.axis_size(axi...  75.5 us
    pallas_call x4, Pallas kernels, backward_slot(): pl.pallas_call(functools.partial(backward_kernel, place), in_specs=in_spe...  65 us
    ppermute x2, waiting for transfers between devices, body(): returned[m] = lax.ppermute(late_grads[m], 'section', [(1, 0)])  52.7 us
    pallas_call x4, Pallas kernels, forward_slot(): pl.pallas_call(functools.partial(forward_kernel, place), in_specs=in_spec...  42.5 us
    pallas_call x7, Pallas kernels, outer_sum(): pl.pallas_call(functools.partial(outer_kernel, extra is not None, picks),...  40.3 us
    ppermute x34, starting transfers between devices, swap(): lax.ppermute(values, axis, [(a, a ^ bit) for a in range(lax.axis_size(axi...  35.5 us
    convert_element_type x14, other arithmetic, exchange(): sent = total_of([a[half:] for a in terms]).astype(BF16)  19 us
  transfers between devices with their start and end apart: 39, of which 19 were waited for; matrix products, arithmetic and copies ran while one was open for 10% of the time, Pallas kernels for 23%

profile of v7, /device:TPU:8, one launch (start us, length us, event | category | flops | bytes accessed | tf_op | source)
XLA Modules:
  0.0 550.3 jit_solution(4273881722439533675)
XLA Ops:
  30.0 3.9 collective-permute-start.3
  39.6 124.6 %all-gather.2.cloned.1.call-done.w_hbm = bf16[3072,4864]{1,0:T(8,128)(2,1)} async-done(((bf16[192,4864]{1,0:T(8,128)(2,1)}), bf16[3072,4864]{1,0:T(8,128)(2,1)}) %all-gather.2.cloned.1.call-update) | async-done | bytes 29884432 | tf_op jit(solution)/shard_map/all_gather | solution.py:845
  164.2 19.8 %forward_slot.4 = (bf16[4,256,1536]{2,1,0:T(8,128)(2,1)}, bf16[4,256,3072]{2,1,0:T(8,128)(2,1)}, f32[4,256,3072]{2,1,0:T(8,128)}, f32[4,256,3072]{2,1,0:T(8,128)...) custom-call(s32[2]{0:T(128)} %pad_add_fusion.3.at_ref, ...), custom_call_target="tpu_custom_call" | custom-call | flops 22000001024 | bytes 60000000 | tf_op jit(solution)/shard_map/forward_slot/pallas_call | solution.py:271
  185.4 20.0 %forward_slot.5 = (bf16[4,256,1536]{2,1,0:T(8,128)(2,1)}, bf16[4,256,3072]{2,1,0:T(8,128)(2,1)}, f32[4,256,3072]{2,1,0:T(8,128)}, f32[4,256,3072]{2,1,0:T(8,128)...) custom-call(s32[2]{0:T(128)} %pad_add_fusion.2.at_ref, ...), custom_call_target="tpu_custom_call", output_to_operand_aliasing={{0}: (9, {}), {1}: (10, {}), {2}: (11, {}), {3}: (12, {}), ... | custom-call | flops 22000001024 | bytes 60000000 | tf_op jit(solution)/shard_map/forward_slot/pallas_call | solution.py:271
  208.9 15.6 %collective-permute-done.5.u_hbm = bf16[256,1536]{1,0:T(8,128)(2,1)S(1)} collective-permute-done((bf16[256,1536]{1,0:T(8,128)(2,1)}, bf16[256,1536]{1,0:T(8,128)(2,1)S(1)}, u32[]{:S(2)}, u32[]{:S(2)}) %collective-permute-start.5) | collective-permute-done | bytes 786464 | tf_op jit(solution)/shard_map/ppermute | solution.py:874
  236.7 4.5 by_owner.2
  244.6 52.1 %collective-permute-done.7.g_hbm = bf16[256,1536]{1,0:T(8,128)(2,1)S(1)} collective-permute-done((bf16[256,1536]{1,0:T(8,128)(2,1)}, bf16[256,1536]{1,0:T(8,128)(2,1)S(1)}, u32[]{:S(2)}, u32[]{:S(2)}) %collective-permute-start.7) | collective-permute-done | bytes 786464 | tf_op jit(solution)/shard_map/ppermute | solution.py:891
  297.6 29.7 %backward_slot.6 = (bf16[256,1536]{1,0:T(8,128)(2,1)}, bf16[256,3072]{1,0:T(8,128)(2,1)}, bf16[256,3456]{1,0:T(8,128)(2,1)}, f32[8,3328]{1,0:T(8,128)}) custom-call(s32[2]{0:T(128)} %pad_add_fusion.2.at_ref, bf16[256,1536]{1,0:T(8,128)(2,1)} %copy-done.11, ...), custom_call_target="tpu_custom_call", output_to_operand_aliasing={{1}: (16, {}), {2}: (17, {})} | custom-call | flops 1000000000 | bytes 1000000 | tf_op jit(solution)/shard_map/backward_slot/pallas_call | solution.py:593
  333.9 5.9 %outer_sum.7 = (bf16[768,768]{1,0:T(8,128)(2,1)}, bf16[768,768]{1,0:T(8,128)(2,1)}) custom-call(bf16[2,1536,256]{2,1,0:T(8,128)(2,1)} %bitcast.63, bf16[2,1536,256]{2,1,0:T(8,128)(2,1)} %collective-permute-done.8.sib_ref, bf16[256,1536]{1,0:T(8,128)(2,1)} %copy-done.4, bf16[256,1536]{1,0:T(8,128)(2,1)} %copy-done.3, bf16[256,1536]{1,0:T(8,128)(2,1)} %copy-done.13, ...), custom_call_target="tpu_custom_call" | custom-call | flops 1000000000 | bytes 1000000 | tf_op jit(solution)/shard_map/outer_sum/pallas_call | solution.py:735
  339.9 5.9 %outer_sum.8 = (bf16[768,768]{1,0:T(8,128)(2,1)}, bf16[768,768]{1,0:T(8,128)(2,1)}) custom-call(bf16[2,1536,256]{2,1,0:T(8,128)(2,1)} %bitcast.64, bf16[2,1536,256]{2,1,0:T(8,128)(2,1)} %collective-permute-done.8.sib_ref, bf16[256,1536]{1,0:T(8,128)(2,1)} %copy-done.4, bf16[256,1536]{1,0:T(8,128)(2,1)} %copy-done.3, bf16[256,1536]{1,0:T(8,128)(2,1)} %copy-done.13, ...), custom_call_target="tpu_custom_call" | custom-call | flops 1000000000 | bytes 1000000 | tf_op jit(solution)/shard_map/outer_sum/pallas_call | solution.py:735
  347.5 30.0 %backward_slot.7 = (bf16[256,1536]{1,0:T(8,128)(2,1)}, bf16[256,3072]{1,0:T(8,128)(2,1)}, bf16[256,3456]{1,0:T(8,128)(2,1)}, f32[8,3328]{1,0:T(8,128)}) custom-call(s32[2]{0:T(128)} %pad_add_fusion.3.at_ref, bf16[256,1536]{1,0:T(8,128)(2,1)} %copy-done.10, ...), custom_call_target="tpu_custom_call", output_to_operand_aliasing={{1}: (16, {}), {2}: (17, {})} | custom-call | flops 1000000000 | bytes 1000000 | tf_op jit(solution)/shard_map/backward_slot/pallas_call | solution.py:593
  386.8 5.9 %outer_sum.9 = (bf16[384,1536]{1,0:T(8,128)(2,1)}, bf16[384,1536]{1,0:T(8,128)(2,1)}) custom-call(bf16[2,768,256]{2,1,0:T(8,128)(2,1)} %bitcast.58, bf16[2,768,256]{2,1,0:T(8,128)(2,1)} %copy-done.1, bf16[256,3072]{1,0:T(8,128)(2,1)} %get-tuple-element.179.rest_0_, bf16[256,3072]{1,0:T(8,128)(2,1)} %get-tuple-element.180.rest_1_, ...), custom_call_target="tpu_custom_call" | custom-call | flops 1000000000 | bytes 1000000 | tf_op jit(solution)/shard_map/outer_sum/pallas_call | solution.py:735
  396.5 5.9 %outer_sum.10 = (bf16[384,1536]{1,0:T(8,128)(2,1)}, bf16[384,1536]{1,0:T(8,128)(2,1)}) custom-call(bf16[2,768,256]{2,1,0:T(8,128)(2,1)} %bitcast.59, bf16[2,768,256]{2,1,0:T(8,128)(2,1)} %copy-done.1, bf16[256,3072]{1,0:T(8,128)(2,1)} %get-tuple-element.179.rest_0_, bf16[256,3072]{1,0:T(8,128)(2,1)} %get-tuple-element.180.rest_1_, ...), custom_call_target="tpu_custom_call" | custom-call | flops 1000000000 | bytes 1000000 | tf_op jit(solution)/shard_map/outer_sum/pallas_call | solution.py:735
  402.4 18.0 %collective-permute-done.14 = bf16[384,768]{1,0:T(8,128)(2,1)S(1)} collective-permute-done((bf16[384,768]{1,0:T(8,128)(2,1)}, bf16[384,768]{1,0:T(8,128)(2,1)S(1)}, u32[]{:S(2)}, u32[]{:S(2)}) %collective-permute-start.14) | collective-permute-done | bytes 589856 | tf_op jit(solution)/shard_map/ppermute | solution.py:789
  424.6 6.9 %outer_sum.11 = (bf16[384,1920]{1,0:T(8,128)(2,1)}, bf16[384,1920]{1,0:T(8,128)(2,1)}) custom-call(bf16[2,768,256]{2,1,0:T(8,128)(2,1)} %bitcast.60, bf16[2,768,256]{2,1,0:T(8,128)(2,1)} %copy-done.1, bf16[256,3456]{1,0:T(8,128)(2,1)} %get-tuple-element.194.rest_0_, bf16[256,3456]{1,0:T(8,128)(2,1)} %get-tuple-element.189.rest_1_, ...), custom_call_target="tpu_custom_call" | custom-call | flops 1000000000 | bytes 1000000 | tf_op jit(solution)/shard_map/outer_sum/pallas_call | solution.py:735
  435.8 3.8 spread_sums.1.rest_4_
  439.6 10.0 %collective-permute-done.23 = bf16[384,1536]{1,0:T(8,128)(2,1)} collective-permute-done((bf16[384,1536]{1,0:T(8,128)(2,1)}, bf16[384,1536]{1,0:T(8,128)(2,1)}, u32[]{:S(2)}, u32[]{:S(2)}) %collective-permute-start.23) | collective-permute-done | bytes 1179680 | tf_op jit(solution)/shard_map/ppermute | solution.py:789
  450.9 4.0 collective-permute-done.26
  460.8 5.2 outer_sum.12
  467.3 4.6 outer_sum.13
  472.7 8.6 %collective-permute-done.25 = bf16[384,1920]{1,0:T(8,128)(2,1)} collective-permute-done((bf16[384,1920]{1,0:T(8,128)(2,1)}, bf16[384,1920]{1,0:T(8,128)(2,1)}, u32[]{:S(2)}, u32[]{:S(2)}) %collective-permute-start.25) | collective-permute-done | bytes 1474592 | tf_op jit(solution)/shard_map/ppermute | solution.py:789
  486.3 7.6 %collective-permute-done.29 = bf16[384,768]{1,0:T(8,128)(2,1)} collective-permute-done((bf16[384,768]{1,0:T(8,128)(2,1)}, bf16[384,768]{1,0:T(8,128)(2,1)}, u32[]{:S(2)}, u32[]{:S(2)}) %collective-permute-start.29) | collective-permute-done | bytes 589856 | tf_op jit(solution)/shard_map/ppermute | solution.py:789
  498.7 8.8 %collective-permute-done.31 = bf16[96,1536]{1,0:T(8,128)(2,1)S(1)} collective-permute-done((bf16[96,1536]{1,0:T(8,128)(2,1)S(1)}, bf16[96,1536]{1,0:T(8,128)(2,1)S(1)}, u32[]{:S(2)}, u32[]{:S(2)}) %collective-permute-start.31) | collective-permute-done | bytes 294944 | tf_op jit(solution)/shard_map/ppermute | solution.py:789
  523.9 3.9 collective-permute-done.33
  (277 shorter events, 130.2 us)
Async XLA Ops:
  7.2 157.0 %all-gather.2.cloned.1.call-start = ((), (), s32[]{:S(2)}) async-start(), calls=%async_computation | async-start | bytes 31752192 | tf_op jit(solution)/shard_map/all_gather | solution.py:845
  184.0 22.7 %collective-permute-start.4 = (bf16[256,1536]{1,0:T(8,128)(2,1)}, bf16[256,1536]{1,0:T(8,128)(2,1)S(1)}, u32[]{:S(2)}, u32[]{:S(2)}) collective-permute-start(bf16[256,1536]{1,0:T(8,128)(2,1)} %get-tuple-element.114), channel_id=1, source_target_pairs={{0,16},{1,17},{2,18},{3,19},{4,20},{5,21},{6,22},{7,23},{8,24},{9,... | collective-permute-start | bytes 2359304 | tf_op jit(solution)/shard_map/ppermute | solution.py:874
  229.7 67.0 %collective-permute-start.7 = (bf16[256,1536]{1,0:T(8,128)(2,1)}, bf16[256,1536]{1,0:T(8,128)(2,1)S(1)}, u32[]{:S(2)}, u32[]{:S(2)}) collective-permute-start(bf16[256,1536]{1,0:T(8,128)(2,1)} %get-tuple-element.145), channel_id=1, source_target_pairs={{16,0},{17,1},{18,2},{19,3},{20,4},{21,5},{22,6},{23,7},{24,8},{25... | collective-permute-start | bytes 2359304 | tf_op jit(solution)/shard_map/ppermute | solution.py:891
  234.2 93.7 %collective-permute-start.6 = (bf16[256,1536]{1,0:T(8,128)(2,1)}, bf16[256,1536]{1,0:T(8,128)(2,1)S(1)}, u32[]{:S(2)}, u32[]{:S(2)}) collective-permute-start(bf16[256,1536]{1,0:T(8,128)(2,1)} %get-tuple-element.144), channel_id=1, source_target_pairs={{16,0},{17,1},{18,2},{19,3},{20,4},{21,5},{22,6},{23,7},{24,8},{25... | collective-permute-start | bytes 2359304 | tf_op jit(solution)/shard_map/ppermute | solution.py:891
  241.2 91.9 %collective-permute-start.8 = (bf16[2,1536,256]{2,1,0:T(8,128)(2,1)}, bf16[2,1536,256]{2,1,0:T(8,128)(2,1)}, u32[]{:S(2)}, u32[]{:S(2)}) collective-permute-start(bf16[2,1536,256]{2,1,0:T(8,128)(2,1)} %bitcast.73), channel_id=1, source_target_pairs={{0,1},{1,0},{2,3},{3,2},{4,5},{5,4},{6,7},{7,6},{8,9},{9,8},{10,11... | collective-permute-start | bytes 4718600 | tf_op jit(solution)/shard_map/ppermute | solution.py:789
  345.8 31.7 %collective-permute-start.12 = (bf16[768,768]{1,0:T(8,128)(2,1)}, bf16[768,768]{1,0:T(8,128)(2,1)}, u32[]{:S(2)}, u32[]{:S(2)}) collective-permute-start(bf16[768,768]{1,0:T(8,128)(2,1)} %get-tuple-element.174), channel_id=1, source_target_pairs={{0,4},{1,5},{2,6},{3,7},{4,0},{5,1},{6,2},{7,3},{8,12},{9,13},{10,... | collective-permute-start | bytes 3538952 | tf_op jit(solution)/shard_map/ppermute | solution.py:789
  346.3 31.2 %collective-permute-start.13 = (bf16[768,768]{1,0:T(8,128)(2,1)}, bf16[768,768]{1,0:T(8,128)(2,1)}, u32[]{:S(2)}, u32[]{:S(2)}) collective-permute-start(bf16[768,768]{1,0:T(8,128)(2,1)} %get-tuple-element.175), channel_id=1, source_target_pairs={{0,2},{1,3},{2,0},{3,1},{4,6},{5,7},{6,4},{7,5},{8,10},{9,11},{10,... | collective-permute-start | bytes 3538952 | tf_op jit(solution)/shard_map/ppermute | solution.py:789
  378.1 46.4 %collective-permute-start.19 = (bf16[256,3456]{1,0:T(8,128)(2,1)S(1)}, bf16[256,3456]{1,0:T(8,128)(2,1)}, u32[]{:S(2)}, u32[]{:S(2)}) collective-permute-start(bf16[256,3456]{1,0:T(8,128)(2,1)S(1)} %copy-done), channel_id=1, source_target_pairs={{0,1},{1,0},{2,3},{3,2},{4,5},{5,4},{6,7},{7,6},{8,9},{9,8},{10,11... | collective-permute-start | bytes 5308424 | tf_op jit(solution)/shard_map/ppermute | solution.py:789
  378.6 46.0 %collective-permute-start.18 = (bf16[256,3456]{1,0:T(8,128)(2,1)}, bf16[256,3456]{1,0:T(8,128)(2,1)}, u32[]{:S(2)}, u32[]{:S(2)}) collective-permute-start(bf16[256,3456]{1,0:T(8,128)(2,1)} %get-tuple-element.194.rest_0_), channel_id=1, source_target_pairs={{0,1},{1,0},{2,3},{3,2},{4,5},{5,4},{6,7},{7,6},{8,9},{9,8},{10,11... | collective-permute-start | bytes 5308424 | tf_op jit(solution)/shard_map/ppermute | solution.py:789
  392.7 39.5 %collective-permute-start.21 = (bf16[384,1536]{1,0:T(8,128)(2,1)}, bf16[384,1536]{1,0:T(8,128)(2,1)S(1)}, u32[]{:S(2)}, u32[]{:S(2)}) collective-permute-start(bf16[384,1536]{1,0:T(8,128)(2,1)} %get-tuple-element.184), channel_id=1, source_target_pairs={{0,2},{1,3},{2,0},{3,1},{4,6},{5,7},{6,4},{7,5},{8,10},{9,11},{10,... | collective-permute-start | bytes 3538952 | tf_op jit(solution)/shard_map/ppermute | solution.py:789
  393.6 26.8 %collective-permute-start.14 = (bf16[384,768]{1,0:T(8,128)(2,1)}, bf16[384,768]{1,0:T(8,128)(2,1)S(1)}, u32[]{:S(2)}, u32[]{:S(2)}) collective-permute-start(bf16[384,768]{1,0:T(8,128)(2,1)} %add_convert_fusion.4), channel_id=1, source_target_pairs={{0,4},{1,5},{2,6},{3,7},{4,0},{5,1},{6,2},{7,3},{8,12},{9,13},{10,... | collective-permute-start | bytes 1769480 | tf_op jit(solution)/shard_map/ppermute | solution.py:789
  395.1 28.6 %collective-permute-start.17 = (bf16[384,768]{1,0:T(8,128)(2,1)}, bf16[384,768]{1,0:T(8,128)(2,1)S(1)}, u32[]{:S(2)}, u32[]{:S(2)}) collective-permute-start(bf16[384,768]{1,0:T(8,128)(2,1)} %add_convert_fusion.3), channel_id=1, source_target_pairs={{0,8},{1,9},{2,10},{3,11},{4,12},{5,13},{6,14},{7,15},{8,0},{9,1},... | collective-permute-start | bytes 1769480 | tf_op jit(solution)/shard_map/ppermute | solution.py:789
  420.4 29.2 %collective-permute-start.23 = (bf16[384,1536]{1,0:T(8,128)(2,1)}, bf16[384,1536]{1,0:T(8,128)(2,1)}, u32[]{:S(2)}, u32[]{:S(2)}) collective-permute-start(bf16[384,1536]{1,0:T(8,128)(2,1)} %get-tuple-element.186), channel_id=1, source_target_pairs={{0,2},{1,3},{2,0},{3,1},{4,6},{5,7},{6,4},{7,5},{8,10},{9,11},{10,... | collective-permute-start | bytes 3538952 | tf_op jit(solution)/shard_map/ppermute | solution.py:789
  431.5 49.8 %collective-permute-start.25 = (bf16[384,1920]{1,0:T(8,128)(2,1)}, bf16[384,1920]{1,0:T(8,128)(2,1)}, u32[]{:S(2)}, u32[]{:S(2)}) collective-permute-start(bf16[384,1920]{1,0:T(8,128)(2,1)} %get-tuple-element.190), channel_id=1, source_target_pairs={{0,2},{1,3},{2,0},{3,1},{4,6},{5,7},{6,4},{7,5},{8,10},{9,11},{10,... | collective-permute-start | bytes 4423688 | tf_op jit(solution)/shard_map/ppermute | solution.py:789
  433.2 21.6 %collective-permute-start.26 = (bf16[192,1536]{1,0:T(8,128)(2,1)S(1)}, bf16[192,1536]{1,0:T(8,128)(2,1)}, u32[]{:S(2)}, u32[]{:S(2)}) collective-permute-start(bf16[192,1536]{1,0:T(8,128)(2,1)S(1)} %add_convert_fusion.2), channel_id=1, source_target_pairs={{0,4},{1,5},{2,6},{3,7},{4,0},{5,1},{6,2},{7,3},{8,12},{9,13},{10,... | collective-permute-start | bytes 1769480 | tf_op jit(solution)/shard_map/ppermute | solution.py:789
  435.7 23.7 %collective-permute-start.20 = (bf16[192,768]{1,0:T(8,128)(2,1)}, bf16[192,768]{1,0:T(8,128)(2,1)}, u32[]{:S(2)}, u32[]{:S(2)}) collective-permute-start(bf16[192,768]{1,0:T(8,128)(2,1)} %add_convert_fusion.11), channel_id=1, source_target_pairs={{0,8},{1,9},{2,10},{3,11},{4,12},{5,13},{6,14},{7,15},{8,0},{9,1},... | collective-permute-start | bytes 884744 | tf_op jit(solution)/shard_map/ppermute | solution.py:789
  456.8 24.4 %collective-permute-start.27 = (bf16[96,1536]{1,0:T(8,128)(2,1)}, bf16[96,1536]{1,0:T(8,128)(2,1)S(1)}, u32[]{:S(2)}, u32[]{:S(2)}) collective-permute-start(bf16[96,1536]{1,0:T(8,128)(2,1)} %add_convert_fusion.10), channel_id=1, source_target_pairs={{0,8},{1,9},{2,10},{3,11},{4,12},{5,13},{6,14},{7,15},{8,0},{9,1},... | collective-permute-start | bytes 884744 | tf_op jit(solution)/shard_map/ppermute | solution.py:789
  460.7 24.4 %collective-permute-start.30 = (bf16[192,1536]{1,0:T(8,128)(2,1)S(1)}, bf16[192,1536]{1,0:T(8,128)(2,1)}, u32[]{:S(2)}, u32[]{:S(2)}) collective-permute-start(bf16[192,1536]{1,0:T(8,128)(2,1)S(1)} %add_convert_fusion.1), channel_id=1, source_target_pairs={{0,4},{1,5},{2,6},{3,7},{4,0},{5,1},{6,2},{7,3},{8,12},{9,13},{10,... | collective-permute-start | bytes 1769480 | tf_op jit(solution)/shard_map/ppermute | solution.py:789
  466.0 27.9 %collective-permute-start.29 = (bf16[384,768]{1,0:T(8,128)(2,1)}, bf16[384,768]{1,0:T(8,128)(2,1)}, u32[]{:S(2)}, u32[]{:S(2)}) collective-permute-start(bf16[384,768]{1,0:T(8,128)(2,1)} %get-tuple-element.193), channel_id=1, source_target_pairs={{0,2},{1,3},{2,0},{3,1},{4,6},{5,7},{6,4},{7,5},{8,10},{9,11},{10,... | collective-permute-start | bytes 1769480 | tf_op jit(solution)/shard_map/ppermute | solution.py:789
  471.9 39.0 %collective-permute-start.24 = (bf16[384,768]{1,0:T(8,128)(2,1)}, bf16[384,768]{1,0:T(8,128)(2,1)S(1)}, u32[]{:S(2)}, u32[]{:S(2)}) collective-permute-start(bf16[384,768]{1,0:T(8,128)(2,1)} %get-tuple-element.196), channel_id=1, source_target_pairs={{0,2},{1,3},{2,0},{3,1},{4,6},{5,7},{6,4},{7,5},{8,10},{9,11},{10,... | collective-permute-start | bytes 1769480 | tf_op jit(solution)/shard_map/ppermute | solution.py:789
  482.6 26.0 %collective-permute-start.28 = (bf16[192,1920]{1,0:T(8,128)(2,1)S(1)}, bf16[192,1920]{1,0:T(8,128)(2,1)S(1)}, u32[]{:S(2)}, u32[]{:S(2)}) collective-permute-start(bf16[192,1920]{1,0:T(8,128)(2,1)S(1)} %add_convert_fusion), channel_id=1, source_target_pairs={{0,4},{1,5},{2,6},{3,7},{4,0},{5,1},{6,2},{7,3},{8,12},{9,13},{10,... | collective-permute-start | bytes 2211848 | tf_op jit(solution)/shard_map/ppermute | solution.py:789
  486.2 21.2 %collective-permute-start.31 = (bf16[96,1536]{1,0:T(8,128)(2,1)S(1)}, bf16[96,1536]{1,0:T(8,128)(2,1)S(1)}, u32[]{:S(2)}, u32[]{:S(2)}) collective-permute-start(bf16[96,1536]{1,0:T(8,128)(2,1)S(1)} %add_convert_fusion.9), channel_id=1, source_target_pairs={{0,8},{1,9},{2,10},{3,11},{4,12},{5,13},{6,14},{7,15},{8,0},{9,1},... | collective-permute-start | bytes 884744 | tf_op jit(solution)/shard_map/ppermute | solution.py:789
  494.9 22.7 %collective-permute-start.34 = (bf16[192,768]{1,0:T(8,128)(2,1)S(1)}, bf16[192,768]{1,0:T(8,128)(2,1)S(1)}, u32[]{:S(2)}, u32[]{:S(2)}) collective-permute-start(bf16[192,768]{1,0:T(8,128)(2,1)S(1)} %add_convert_fusion.8), channel_id=1, source_target_pairs={{0,4},{1,5},{2,6},{3,7},{4,0},{5,1},{6,2},{7,3},{8,12},{9,13},{10,... | collective-permute-start | bytes 884744 | tf_op jit(solution)/shard_map/ppermute | solution.py:789
  510.9 27.5 %collective-permute-start.32 = (bf16[96,1920]{1,0:T(8,128)(2,1)}, bf16[96,1920]{1,0:T(8,128)(2,1)}, u32[]{:S(2)}, u32[]{:S(2)}) collective-permute-start(bf16[96,1920]{1,0:T(8,128)(2,1)} %add_convert_fusion.5), channel_id=1, source_target_pairs={{0,8},{1,9},{2,10},{3,11},{4,12},{5,13},{6,14},{7,15},{8,0},{9,1},... | collective-permute-start | bytes 1105928 | tf_op jit(solution)/shard_map/ppermute | solution.py:789
  (73 other events, 707.3 us)
Sparse Core Ops, SparseCore 0:
  10.3 153.8 all-gather.1

commit v8 on v7

--- a/solution.py
+++ b/solution.py
@@ -746,6 +746,42 @@
     )(own, sib, *rights, *more)
 
 
+def out_kernel(picks, own_ref, sib_ref, *rest):
+    rights, outs = rest[:-4], rest[-4:]
+    micro, high = own_ref.shape[0], outs[0].shape[0]
+    right = jnp.concatenate([ref[...] for ref in rights], axis=0)
+
+    def fill(two):
+        for out_ref, spots in zip(outs[2 * two : 2 * two + 2], picks[two]):
+            size = high // len(spots)
+            rows = [
+                [ref[m, k * size : (k + 1) * size] for ref in (own_ref, sib_ref) for m in range(micro)] for k in spots
+            ]
+            left = jnp.concatenate([jnp.concatenate(row, axis=1) for row in rows], axis=0)
+            out_ref[...] = nn_dot(left, right).astype(BF16)
+
+    for two in range(2):
+        pl.when(pl.program_id(0) == two)(functools.partial(fill, two))
+
+
+def out_sums(own, sib, rights, picks):
+    _, total, rows = own.shape
+    half = rights[0].shape[1] // 2
+    full = pl.BlockSpec(own.shape, lambda i: (0, 0, 0))
+    out = pl.BlockSpec((total // 2, half), lambda i: (0, 0))
+    made = jax.ShapeDtypeStruct((total // 2, half), BF16)
+    return pl.pallas_call(
+        functools.partial(out_kernel, picks),
+        grid=(2,),
+        in_specs=[full, full] + [pl.BlockSpec((rows, half), lambda i: (0, i)) for _ in rights],
+        out_specs=[out] * 4,
+        out_shape=[made] * 4,
+        compiler_params=pltpu.CompilerParams(vmem_limit_bytes=VMEM),
+        cost_estimate=pl.CostEstimate(flops=10**9, bytes_accessed=10**6, transcendentals=0),
+        name="out_sums",
+    )(own, sib, *rights)
+
+
 def listing(sizes, span):
     return [-(-size // span) for size in sizes]
 
@@ -917,12 +953,9 @@
     returned[0], early_grads[-1] = lax.optimization_barrier((returned[0], early_grads[-1]))
     take_branch(0)
 
-    half = width // 2
-    a_keep, a_send = outer_sum(out_own, out_sib, branch + branch_sib, 0, half, half)
-    branch[0] = held(branch[0], a_send)
     every = range(count // 2)
-    b_keep, b_send = outer_sum(
-        out_own, out_sib, branch + branch_sib, half, width, half, picks=(every[::2], every[1::2])
+    a_keep, a_send, b_keep, b_send = out_sums(
+        out_own, out_sib, branch + branch_sib, (((0,), (1,)), (every[::2], every[1::2]))
     )
     returned[0], a_send, b_send = lax.optimization_barrier((returned[0], a_send, b_send))
     out_a = [a_keep, swap(a_send, axis, line[0])]
@@ -986,6 +1019,7 @@
     token = other_steps(last, token)
     chunks[last - 1][-1] = held(chunks[last - 1][-1], token)
     out_grad = jnp.concatenate([total_of(out_a), total_of(out_b)], axis=1)
+    chunks[last - 1][-1], chunks[last][-1] = held((chunks[last - 1][-1], chunks[last][-1]), out_grad)
     in_parts = [total_of(terms) for terms in chunks]
     tail = in_parts[3]
     own_cols = proj_cols - inner - mid

time: 561 us -> 559 us (level)
    pallas_call x7 -> x5, Pallas kernels: 40.3 us -> 28.5 us  [outer_sum(): pl.pallas_call(functools.partial(outer_kernel, extra is not None, picks),...]
    pallas_call x0 -> x1, Pallas kernels: none -> 10.1 us  [out_sums(): pl.pallas_call(functools.partial(out_kernel, picks), grid=(2,), in_specs=...]
  transfers between devices with their start and end apart: 39 -> 39, of which waited for: 19 -> 20; matrix products, arithmetic and copies ran while one was open for 10% -> 9% of each run, Pallas kernels for 23% -> 23%
where the time goes in v8:
time: 559 us; the launch traced here: 548 us
  waiting for transfers between devices  268 us (48%)
  Pallas kernels  161 us (29%)
  other arithmetic  44.7 us (8%)
  starting transfers between devices  42.4 us (8%)
  local copies, waits for them, and re-layouts  17 us (3%)
  between operations  15.3 us (3%)
    all_gather x1, waiting for transfers between devices, body(): lax.all_gather(pack(in_weight[0], out_weight[0], inner), axis, axis=0, ti...  125 us
    ppermute x34, waiting for transfers between devices, swap(): lax.ppermute(values, axis, [(a, a ^ bit) for a in range(lax.axis_size(axi...  75.4 us
    pallas_call x4, Pallas kernels, backward_slot(): pl.pallas_call(functools.partial(backward_kernel, place), in_specs=in_spe...  65 us
    ppermute x2, waiting for transfers between devices, body(): returned[m] = lax.ppermute(late_grads[m], 'section', [(1, 0)])  52.9 us
    pallas_call x4, Pallas kernels, forward_slot(): pl.pallas_call(functools.partial(forward_kernel, place), in_specs=in_spec...  42.5 us
    ppermute x34, starting transfers between devices, swap(): lax.ppermute(values, axis, [(a, a ^ bit) for a in range(lax.axis_size(axi...  37.1 us
    pallas_call x5, Pallas kernels, outer_sum(): pl.pallas_call(functools.partial(outer_kernel, extra is not None, picks),...  28.5 us
    convert_element_type x14, other arithmetic, exchange(): sent = total_of([a[half:] for a in terms]).astype(BF16)  19.2 us
  transfers between devices with their start and end apart: 39, of which 20 were waited for; matrix products, arithmetic and copies ran while one was open for 9% of the time, Pallas kernels for 23%

profile of v8, /device:TPU:8, one launch (start us, length us, event | category | flops | bytes accessed | tf_op | source)
XLA Modules:
  0.0 548.3 jit_solution(9905276729065121884)
XLA Ops:
  29.9 3.9 collective-permute-start.3
  39.6 124.6 %all-gather.2.cloned.1.call-done.w_hbm = bf16[3072,4864]{1,0:T(8,128)(2,1)} async-done(((bf16[192,4864]{1,0:T(8,128)(2,1)}), bf16[3072,4864]{1,0:T(8,128)(2,1)}) %all-gather.2.cloned.1.call-update) | async-done | bytes 29884432 | tf_op jit(solution)/shard_map/all_gather | solution.py:881
  164.2 19.8 %forward_slot.4 = (bf16[4,256,1536]{2,1,0:T(8,128)(2,1)}, bf16[4,256,3072]{2,1,0:T(8,128)(2,1)}, f32[4,256,3072]{2,1,0:T(8,128)}, f32[4,256,3072]{2,1,0:T(8,128)...) custom-call(s32[2]{0:T(128)} %pad_add_fusion.3.at_ref, ...), custom_call_target="tpu_custom_call" | custom-call | flops 22000001024 | bytes 60000000 | tf_op jit(solution)/shard_map/forward_slot/pallas_call | solution.py:271
  185.4 20.0 %forward_slot.5 = (bf16[4,256,1536]{2,1,0:T(8,128)(2,1)}, bf16[4,256,3072]{2,1,0:T(8,128)(2,1)}, f32[4,256,3072]{2,1,0:T(8,128)}, f32[4,256,3072]{2,1,0:T(8,128)...) custom-call(s32[2]{0:T(128)} %pad_add_fusion.2.at_ref, ...), custom_call_target="tpu_custom_call", output_to_operand_aliasing={{0}: (9, {}), {1}: (10, {}), {2}: (11, {}), {3}: (12, {}), ... | custom-call | flops 22000001024 | bytes 60000000 | tf_op jit(solution)/shard_map/forward_slot/pallas_call | solution.py:271
  208.9 15.5 %collective-permute-done.5.u_hbm = bf16[256,1536]{1,0:T(8,128)(2,1)S(1)} collective-permute-done((bf16[256,1536]{1,0:T(8,128)(2,1)}, bf16[256,1536]{1,0:T(8,128)(2,1)S(1)}, u32[]{:S(2)}, u32[]{:S(2)}) %collective-permute-start.5) | collective-permute-done | bytes 786464 | tf_op jit(solution)/shard_map/ppermute | solution.py:910
  236.7 4.4 by_owner.2
  244.5 52.2 %collective-permute-done.7.g_hbm = bf16[256,1536]{1,0:T(8,128)(2,1)S(1)} collective-permute-done((bf16[256,1536]{1,0:T(8,128)(2,1)}, bf16[256,1536]{1,0:T(8,128)(2,1)S(1)}, u32[]{:S(2)}, u32[]{:S(2)}) %collective-permute-start.7) | collective-permute-done | bytes 786464 | tf_op jit(solution)/shard_map/ppermute | solution.py:927
  297.6 29.7 %backward_slot.6 = (bf16[256,1536]{1,0:T(8,128)(2,1)}, bf16[256,3072]{1,0:T(8,128)(2,1)}, bf16[256,3456]{1,0:T(8,128)(2,1)}, f32[8,3328]{1,0:T(8,128)}) custom-call(s32[2]{0:T(128)} %pad_add_fusion.2.at_ref, bf16[256,1536]{1,0:T(8,128)(2,1)} %copy-done.9, ...), custom_call_target="tpu_custom_call", output_to_operand_aliasing={{1}: (16, {}), {2}: (17, {})} | custom-call | flops 1000000000 | bytes 1000000 | tf_op jit(solution)/shard_map/backward_slot/pallas_call | solution.py:593
  334.0 10.1 %out_sums.1 = (bf16[768,768]{1,0:T(8,128)(2,1)}, bf16[768,768]{1,0:T(8,128)(2,1)}, bf16[768,768]{1,0:T(8,128)(2,1)}, bf16[768,768]{1,0:T(8,128)(2,1)}) custom-call(bf16[2,1536,256]{2,1,0:T(8,128)(2,1)} %bitcast.63, bf16[2,1536,256]{2,1,0:T(8,128)(2,1)} %collective-permute-done.8.sib_ref, bf16[256,1536]{1,0:T(8,128)(2,1)} %copy-done.11, ...), custom_call_target="tpu_custom_call" | custom-call | flops 1000000000 | bytes 1000000 | tf_op jit(solution)/shard_map/out_sums/pallas_call | solution.py:773
  345.8 30.0 %backward_slot.7 = (bf16[256,1536]{1,0:T(8,128)(2,1)}, bf16[256,3072]{1,0:T(8,128)(2,1)}, bf16[256,3456]{1,0:T(8,128)(2,1)}, f32[8,3328]{1,0:T(8,128)}) custom-call(s32[2]{0:T(128)} %pad_add_fusion.3.at_ref, bf16[256,1536]{1,0:T(8,128)(2,1)} %copy-done.8, ...), custom_call_target="tpu_custom_call", output_to_operand_aliasing={{1}: (16, {}), {2}: (17, {})} | custom-call | flops 1000000000 | bytes 1000000 | tf_op jit(solution)/shard_map/backward_slot/pallas_call | solution.py:593
  385.2 5.9 %outer_sum.5 = (bf16[384,1536]{1,0:T(8,128)(2,1)}, bf16[384,1536]{1,0:T(8,128)(2,1)}) custom-call(bf16[2,768,256]{2,1,0:T(8,128)(2,1)} %bitcast.58, bf16[2,768,256]{2,1,0:T(8,128)(2,1)} %copy-done.1, bf16[256,3072]{1,0:T(8,128)(2,1)} %get-tuple-element.179.rest_0_, bf16[256,3072]{1,0:T(8,128)(2,1)} %get-tuple-element.180.rest_1_, ...), custom_call_target="tpu_custom_call" | custom-call | flops 1000000000 | bytes 1000000 | tf_op jit(solution)/shard_map/outer_sum/pallas_call | solution.py:735
  395.0 5.9 %outer_sum.6 = (bf16[384,1536]{1,0:T(8,128)(2,1)}, bf16[384,1536]{1,0:T(8,128)(2,1)}) custom-call(bf16[2,768,256]{2,1,0:T(8,128)(2,1)} %bitcast.59, bf16[2,768,256]{2,1,0:T(8,128)(2,1)} %copy-done.1, bf16[256,3072]{1,0:T(8,128)(2,1)} %get-tuple-element.179.rest_0_, bf16[256,3072]{1,0:T(8,128)(2,1)} %get-tuple-element.180.rest_1_, ...), custom_call_target="tpu_custom_call" | custom-call | flops 1000000000 | bytes 1000000 | tf_op jit(solution)/shard_map/outer_sum/pallas_call | solution.py:735
  400.9 18.0 %collective-permute-done.14 = bf16[384,768]{1,0:T(8,128)(2,1)S(1)} collective-permute-done((bf16[384,768]{1,0:T(8,128)(2,1)}, bf16[384,768]{1,0:T(8,128)(2,1)S(1)}, u32[]{:S(2)}, u32[]{:S(2)}) %collective-permute-start.14) | collective-permute-done | bytes 589856 | tf_op jit(solution)/shard_map/ppermute | solution.py:825
  422.9 6.9 %outer_sum.7 = (bf16[384,1920]{1,0:T(8,128)(2,1)}, bf16[384,1920]{1,0:T(8,128)(2,1)}) custom-call(bf16[2,768,256]{2,1,0:T(8,128)(2,1)} %bitcast.60, bf16[2,768,256]{2,1,0:T(8,128)(2,1)} %copy-done.1, bf16[256,3456]{1,0:T(8,128)(2,1)} %get-tuple-element.194.rest_0_, bf16[256,3456]{1,0:T(8,128)(2,1)} %get-tuple-element.189.rest_1_, ...), custom_call_target="tpu_custom_call" | custom-call | flops 1000000000 | bytes 1000000 | tf_op jit(solution)/shard_map/outer_sum/pallas_call | solution.py:735
  435.2 3.8 spread_sums.1.rest_4_
  439.0 9.1 %collective-permute-done.23 = bf16[384,1536]{1,0:T(8,128)(2,1)} collective-permute-done((bf16[384,1536]{1,0:T(8,128)(2,1)}, bf16[384,1536]{1,0:T(8,128)(2,1)}, u32[]{:S(2)}, u32[]{:S(2)}) %collective-permute-start.23) | collective-permute-done | bytes 1179680 | tf_op jit(solution)/shard_map/ppermute | solution.py:825
  450.3 4.2 collective-permute-done.26
  460.1 5.2 outer_sum.8
  466.6 4.6 outer_sum.9
  472.0 7.7 %collective-permute-done.25 = bf16[384,1920]{1,0:T(8,128)(2,1)} collective-permute-done((bf16[384,1920]{1,0:T(8,128)(2,1)}, bf16[384,1920]{1,0:T(8,128)(2,1)}, u32[]{:S(2)}, u32[]{:S(2)}) %collective-permute-start.25) | collective-permute-done | bytes 1474592 | tf_op jit(solution)/shard_map/ppermute | solution.py:825
  484.8 7.5 %collective-permute-done.29 = bf16[384,768]{1,0:T(8,128)(2,1)} collective-permute-done((bf16[384,768]{1,0:T(8,128)(2,1)}, bf16[384,768]{1,0:T(8,128)(2,1)}, u32[]{:S(2)}, u32[]{:S(2)}) %collective-permute-start.29) | collective-permute-done | bytes 589856 | tf_op jit(solution)/shard_map/ppermute | solution.py:825
  497.1 10.3 %collective-permute-done.31 = bf16[96,1536]{1,0:T(8,128)(2,1)S(1)} collective-permute-done((bf16[96,1536]{1,0:T(8,128)(2,1)S(1)}, bf16[96,1536]{1,0:T(8,128)(2,1)S(1)}, u32[]{:S(2)}, u32[]{:S(2)}) %collective-permute-start.31) | collective-permute-done | bytes 294944 | tf_op jit(solution)/shard_map/ppermute | solution.py:825
  517.3 4.1 collective-permute-start.35
  527.7 3.8 collective-permute-done.35
  (268 shorter events, 125.9 us)
Async XLA Ops:
  7.2 157.0 %all-gather.2.cloned.1.call-start = ((), (), s32[]{:S(2)}) async-start(), calls=%async_computation | async-start | bytes 31752192 | tf_op jit(solution)/shard_map/all_gather | solution.py:881
  184.0 22.7 %collective-permute-start.4 = (bf16[256,1536]{1,0:T(8,128)(2,1)}, bf16[256,1536]{1,0:T(8,128)(2,1)S(1)}, u32[]{:S(2)}, u32[]{:S(2)}) collective-permute-start(bf16[256,1536]{1,0:T(8,128)(2,1)} %get-tuple-element.115), channel_id=1, source_target_pairs={{0,16},{1,17},{2,18},{3,19},{4,20},{5,21},{6,22},{7,23},{8,24},{9,... | collective-permute-start | bytes 2359304 | tf_op jit(solution)/shard_map/ppermute | solution.py:910
  229.7 67.0 %collective-permute-start.7 = (bf16[256,1536]{1,0:T(8,128)(2,1)}, bf16[256,1536]{1,0:T(8,128)(2,1)S(1)}, u32[]{:S(2)}, u32[]{:S(2)}) collective-permute-start(bf16[256,1536]{1,0:T(8,128)(2,1)} %get-tuple-element.146), channel_id=1, source_target_pairs={{16,0},{17,1},{18,2},{19,3},{20,4},{21,5},{22,6},{23,7},{24,8},{25... | collective-permute-start | bytes 2359304 | tf_op jit(solution)/shard_map/ppermute | solution.py:927
  234.2 93.7 %collective-permute-start.6 = (bf16[256,1536]{1,0:T(8,128)(2,1)}, bf16[256,1536]{1,0:T(8,128)(2,1)S(1)}, u32[]{:S(2)}, u32[]{:S(2)}) collective-permute-start(bf16[256,1536]{1,0:T(8,128)(2,1)} %get-tuple-element.145), channel_id=1, source_target_pairs={{16,0},{17,1},{18,2},{19,3},{20,4},{21,5},{22,6},{23,7},{24,8},{25... | collective-permute-start | bytes 2359304 | tf_op jit(solution)/shard_map/ppermute | solution.py:927
  241.2 91.9 %collective-permute-start.8 = (bf16[2,1536,256]{2,1,0:T(8,128)(2,1)}, bf16[2,1536,256]{2,1,0:T(8,128)(2,1)}, u32[]{:S(2)}, u32[]{:S(2)}) collective-permute-start(bf16[2,1536,256]{2,1,0:T(8,128)(2,1)} %bitcast.72), channel_id=1, source_target_pairs={{0,1},{1,0},{2,3},{3,2},{4,5},{5,4},{6,7},{7,6},{8,9},{9,8},{10,11... | collective-permute-start | bytes 4718600 | tf_op jit(solution)/shard_map/ppermute | solution.py:825
  344.1 31.7 %collective-permute-start.12 = (bf16[768,768]{1,0:T(8,128)(2,1)}, bf16[768,768]{1,0:T(8,128)(2,1)}, u32[]{:S(2)}, u32[]{:S(2)}) collective-permute-start(bf16[768,768]{1,0:T(8,128)(2,1)} %get-tuple-element.174), channel_id=1, source_target_pairs={{0,4},{1,5},{2,6},{3,7},{4,0},{5,1},{6,2},{7,3},{8,12},{9,13},{10,... | collective-permute-start | bytes 3538952 | tf_op jit(solution)/shard_map/ppermute | solution.py:825
  344.7 31.2 %collective-permute-start.13 = (bf16[768,768]{1,0:T(8,128)(2,1)}, bf16[768,768]{1,0:T(8,128)(2,1)}, u32[]{:S(2)}, u32[]{:S(2)}) collective-permute-start(bf16[768,768]{1,0:T(8,128)(2,1)} %get-tuple-element.175), channel_id=1, source_target_pairs={{0,2},{1,3},{2,0},{3,1},{4,6},{5,7},{6,4},{7,5},{8,10},{9,11},{10,... | collective-permute-start | bytes 3538952 | tf_op jit(solution)/shard_map/ppermute | solution.py:825
  376.5 46.4 %collective-permute-start.19 = (bf16[256,3456]{1,0:T(8,128)(2,1)S(1)}, bf16[256,3456]{1,0:T(8,128)(2,1)}, u32[]{:S(2)}, u32[]{:S(2)}) collective-permute-start(bf16[256,3456]{1,0:T(8,128)(2,1)S(1)} %copy-done), channel_id=1, source_target_pairs={{0,1},{1,0},{2,3},{3,2},{4,5},{5,4},{6,7},{7,6},{8,9},{9,8},{10,11... | collective-permute-start | bytes 5308424 | tf_op jit(solution)/shard_map/ppermute | solution.py:825
  376.9 46.0 %collective-permute-start.18 = (bf16[256,3456]{1,0:T(8,128)(2,1)}, bf16[256,3456]{1,0:T(8,128)(2,1)}, u32[]{:S(2)}, u32[]{:S(2)}) collective-permute-start(bf16[256,3456]{1,0:T(8,128)(2,1)} %get-tuple-element.194.rest_0_), channel_id=1, source_target_pairs={{0,1},{1,0},{2,3},{3,2},{4,5},{5,4},{6,7},{7,6},{8,9},{9,8},{10,11... | collective-permute-start | bytes 5308424 | tf_op jit(solution)/shard_map/ppermute | solution.py:825
  391.1 39.5 %collective-permute-start.21 = (bf16[384,1536]{1,0:T(8,128)(2,1)}, bf16[384,1536]{1,0:T(8,128)(2,1)}, u32[]{:S(2)}, u32[]{:S(2)}) collective-permute-start(bf16[384,1536]{1,0:T(8,128)(2,1)} %get-tuple-element.184), channel_id=1, source_target_pairs={{0,2},{1,3},{2,0},{3,1},{4,6},{5,7},{6,4},{7,5},{8,10},{9,11},{10,... | collective-permute-start | bytes 3538952 | tf_op jit(solution)/shard_map/ppermute | solution.py:825
  392.0 26.8 %collective-permute-start.14 = (bf16[384,768]{1,0:T(8,128)(2,1)}, bf16[384,768]{1,0:T(8,128)(2,1)S(1)}, u32[]{:S(2)}, u32[]{:S(2)}) collective-permute-start(bf16[384,768]{1,0:T(8,128)(2,1)} %add_convert_fusion.4), channel_id=1, source_target_pairs={{0,4},{1,5},{2,6},{3,7},{4,0},{5,1},{6,2},{7,3},{8,12},{9,13},{10,... | collective-permute-start | bytes 1769480 | tf_op jit(solution)/shard_map/ppermute | solution.py:825
  393.5 28.5 %collective-permute-start.17 = (bf16[384,768]{1,0:T(8,128)(2,1)}, bf16[384,768]{1,0:T(8,128)(2,1)S(1)}, u32[]{:S(2)}, u32[]{:S(2)}) collective-permute-start(bf16[384,768]{1,0:T(8,128)(2,1)} %add_convert_fusion.3), channel_id=1, source_target_pairs={{0,8},{1,9},{2,10},{3,11},{4,12},{5,13},{6,14},{7,15},{8,0},{9,1},... | collective-permute-start | bytes 1769480 | tf_op jit(solution)/shard_map/ppermute | solution.py:825
  418.8 29.2 %collective-permute-start.23 = (bf16[384,1536]{1,0:T(8,128)(2,1)}, bf16[384,1536]{1,0:T(8,128)(2,1)}, u32[]{:S(2)}, u32[]{:S(2)}) collective-permute-start(bf16[384,1536]{1,0:T(8,128)(2,1)} %get-tuple-element.186), channel_id=1, source_target_pairs={{0,2},{1,3},{2,0},{3,1},{4,6},{5,7},{6,4},{7,5},{8,10},{9,11},{10,... | collective-permute-start | bytes 3538952 | tf_op jit(solution)/shard_map/ppermute | solution.py:825
  429.8 49.8 %collective-permute-start.25 = (bf16[384,1920]{1,0:T(8,128)(2,1)}, bf16[384,1920]{1,0:T(8,128)(2,1)}, u32[]{:S(2)}, u32[]{:S(2)}) collective-permute-start(bf16[384,1920]{1,0:T(8,128)(2,1)} %get-tuple-element.190), channel_id=1, source_target_pairs={{0,2},{1,3},{2,0},{3,1},{4,6},{5,7},{6,4},{7,5},{8,10},{9,11},{10,... | collective-permute-start | bytes 4423688 | tf_op jit(solution)/shard_map/ppermute | solution.py:825
  432.6 21.9 %collective-permute-start.26 = (bf16[192,1536]{1,0:T(8,128)(2,1)}, bf16[192,1536]{1,0:T(8,128)(2,1)}, u32[]{:S(2)}, u32[]{:S(2)}) collective-permute-start(bf16[192,1536]{1,0:T(8,128)(2,1)} %add_convert_fusion.2), channel_id=1, source_target_pairs={{0,4},{1,5},{2,6},{3,7},{4,0},{5,1},{6,2},{7,3},{8,12},{9,13},{10,... | collective-permute-start | bytes 1769480 | tf_op jit(solution)/shard_map/ppermute | solution.py:825
  435.0 23.9 %collective-permute-start.20 = (bf16[192,768]{1,0:T(8,128)(2,1)}, bf16[192,768]{1,0:T(8,128)(2,1)S(1)}, u32[]{:S(2)}, u32[]{:S(2)}) collective-permute-start(bf16[192,768]{1,0:T(8,128)(2,1)} %add_convert_fusion.11), channel_id=1, source_target_pairs={{0,8},{1,9},{2,10},{3,11},{4,12},{5,13},{6,14},{7,15},{8,0},{9,1},... | collective-permute-start | bytes 884744 | tf_op jit(solution)/shard_map/ppermute | solution.py:825
  456.4 23.3 %collective-permute-start.27 = (bf16[96,1536]{1,0:T(8,128)(2,1)}, bf16[96,1536]{1,0:T(8,128)(2,1)}, u32[]{:S(2)}, u32[]{:S(2)}) collective-permute-start(bf16[96,1536]{1,0:T(8,128)(2,1)} %add_convert_fusion.10), channel_id=1, source_target_pairs={{0,8},{1,9},{2,10},{3,11},{4,12},{5,13},{6,14},{7,15},{8,0},{9,1},... | collective-permute-start | bytes 884744 | tf_op jit(solution)/shard_map/ppermute | solution.py:825
  460.0 23.5 %collective-permute-start.30 = (bf16[192,1536]{1,0:T(8,128)(2,1)}, bf16[192,1536]{1,0:T(8,128)(2,1)}, u32[]{:S(2)}, u32[]{:S(2)}) collective-permute-start(bf16[192,1536]{1,0:T(8,128)(2,1)} %add_convert_fusion.1), channel_id=1, source_target_pairs={{0,4},{1,5},{2,6},{3,7},{4,0},{5,1},{6,2},{7,3},{8,12},{9,13},{10,... | collective-permute-start | bytes 1769480 | tf_op jit(solution)/shard_map/ppermute | solution.py:825
  465.3 27.0 %collective-permute-start.29 = (bf16[384,768]{1,0:T(8,128)(2,1)}, bf16[384,768]{1,0:T(8,128)(2,1)}, u32[]{:S(2)}, u32[]{:S(2)}) collective-permute-start(bf16[384,768]{1,0:T(8,128)(2,1)} %get-tuple-element.193), channel_id=1, source_target_pairs={{0,2},{1,3},{2,0},{3,1},{4,6},{5,7},{6,4},{7,5},{8,10},{9,11},{10,... | collective-permute-start | bytes 1769480 | tf_op jit(solution)/shard_map/ppermute | solution.py:825
  471.2 38.8 %collective-permute-start.24 = (bf16[384,768]{1,0:T(8,128)(2,1)}, bf16[384,768]{1,0:T(8,128)(2,1)S(1)}, u32[]{:S(2)}, u32[]{:S(2)}) collective-permute-start(bf16[384,768]{1,0:T(8,128)(2,1)} %get-tuple-element.196), channel_id=1, source_target_pairs={{0,2},{1,3},{2,0},{3,1},{4,6},{5,7},{6,4},{7,5},{8,10},{9,11},{10,... | collective-permute-start | bytes 1769480 | tf_op jit(solution)/shard_map/ppermute | solution.py:825
  481.0 27.5 %collective-permute-start.28 = (bf16[192,1920]{1,0:T(8,128)(2,1)S(1)}, bf16[192,1920]{1,0:T(8,128)(2,1)S(1)}, u32[]{:S(2)}, u32[]{:S(2)}) collective-permute-start(bf16[192,1920]{1,0:T(8,128)(2,1)S(1)} %add_convert_fusion), channel_id=1, source_target_pairs={{0,4},{1,5},{2,6},{3,7},{4,0},{5,1},{6,2},{7,3},{8,12},{9,13},{10,... | collective-permute-start | bytes 2211848 | tf_op jit(solution)/shard_map/ppermute | solution.py:825
  484.6 22.7 %collective-permute-start.31 = (bf16[96,1536]{1,0:T(8,128)(2,1)S(1)}, bf16[96,1536]{1,0:T(8,128)(2,1)S(1)}, u32[]{:S(2)}, u32[]{:S(2)}) collective-permute-start(bf16[96,1536]{1,0:T(8,128)(2,1)S(1)} %add_convert_fusion.9), channel_id=1, source_target_pairs={{0,8},{1,9},{2,10},{3,11},{4,12},{5,13},{6,14},{7,15},{8,0},{9,1},... | collective-permute-start | bytes 884744 | tf_op jit(solution)/shard_map/ppermute | solution.py:825
  493.4 23.0 %collective-permute-start.34 = (bf16[192,768]{1,0:T(8,128)(2,1)S(1)}, bf16[192,768]{1,0:T(8,128)(2,1)S(1)}, u32[]{:S(2)}, u32[]{:S(2)}) collective-permute-start(bf16[192,768]{1,0:T(8,128)(2,1)S(1)} %add_convert_fusion.8), channel_id=1, source_target_pairs={{0,4},{1,5},{2,6},{3,7},{4,0},{5,1},{6,2},{7,3},{8,12},{9,13},{10,... | collective-permute-start | bytes 884744 | tf_op jit(solution)/shard_map/ppermute | solution.py:825
  509.9 22.8 %collective-permute-start.32 = (bf16[96,1920]{1,0:T(8,128)(2,1)S(1)}, bf16[96,1920]{1,0:T(8,128)(2,1)S(1)}, u32[]{:S(2)}, u32[]{:S(2)}) collective-permute-start(bf16[96,1920]{1,0:T(8,128)(2,1)S(1)} %add_convert_fusion.5), channel_id=1, source_target_pairs={{0,8},{1,9},{2,10},{3,11},{4,12},{5,13},{6,14},{7,15},{8,0},{9,1},... | collective-permute-start | bytes 1105928 | tf_op jit(solution)/shard_map/ppermute | solution.py:825
  (69 other events, 705.1 us)
Sparse Core Ops, SparseCore 0:
  10.3 153.8 all-gather.1
